TPU v7x, 32 devices: a whole 2x2x4 slice. The times are simulated.
32 devices in a mesh: ctx: 8 (over z, x), wsh: 4 (over y, core).
Axes of the slice: x: 2, y: 2, z: 4, core: 2. Of those that a mesh axis runs over, the one named last changes fastest.
Arguments:
- tokens: bfloat16 [4, 2048, 1024], P('wsh', 'ctx'), may hold values from -6 to 6
- segments: int32 [4, 2048], P('wsh', 'ctx'), may hold values from 0 to 3, never falling along the last dimension, each value on 1 to 1024 neighbouring positions
- routes: int32 [4, 2048, 8], P('wsh', 'ctx'), may hold values from 0 to 15, all different within a row; in each aligned block of 256 rows (0 to 255, 256 to 511, ..., all dimensions but the last counted through in order) at most 192 rows name the same one
- gate_weights: float32 [4, 2048, 8], P('wsh', 'ctx'), may hold values from 0.05 to 0.25
- cotangent: bfloat16 [4, 2048, 1024], P('wsh', 'ctx'), may hold values from -6 to 6
- owners: int32 [54], replicated, may hold values from 0 to 79, as said below
- masters: float32 [80, 1024, 512], P('wsh', 'ctx'), may hold values from -8 to 8
- first_moments: float32 [80, 1024, 512], P('wsh', 'ctx'), may hold values from -16384 to 16384
- second_moments: float32 [80, 1024, 512], P('wsh', 'ctx'), may hold values from 0 to 32768, as said below
- norm_gains: float32 [2, 1024], replicated, may hold values from 0.5 to 1.5
- gain_first: float32 [2, 1024], replicated, may hold values from -32768 to 32768
- gain_second: float32 [2, 1024], replicated, may hold values from 0 to 131072, as said below
Outputs:
- output: bfloat16 [4, 2048, 1024], P('wsh', 'ctx')
- input_grad: float32 [4, 2048, 1024], P('wsh', 'ctx')
- new_masters: float32 [80, 1024, 512], P('wsh', 'ctx')
- new_first: float32 [80, 1024, 512], P('wsh', 'ctx')
- new_second: float32 [80, 1024, 512], P('wsh', 'ctx')
- new_gains: float32 [2, 1024], replicated
- new_gain_first: float32 [2, 1024], replicated
- new_gain_second: float32 [2, 1024], replicated
Inputs may be any that keep to these rules, and one draw needn't show every extreme that they name: `owners`: the entries are distinct; slot s belongs to index s // 20 of wsh; one index of wsh holds exactly 20 of the matrices. `segments`: documents are numbered in order within each sequence; each has at most 1024 positions and one of each sequence has exactly 1024. `routes`: the 8 experts of a position are distinct; among the 256 positions of one device no expert is named more than 192 times, and some expert is named 192 times. `second_moments`: every entry is positive. `gain_second`: every entry is positive.
All inputs are finite; a program needn't handle non-finite values.
Results may differ from a plain program's by a relative error of at most 0.024.
Values may be sent and summed in bfloat16 or wider, within the bound.
No kernel may reach another device: no remote copies, remote signals or barrier semaphores. Data moves between devices by JAX's collectives and lax.ppermute only.
A program may use at most 256 MiB of HBM per device.

v0:
```python
import jax
import jax.numpy as jnp
import numpy as np
from jax import lax
from jax.sharding import PartitionSpec as P

QH = 16
KVH = 8
HD = 64
TOPK = 8
REACH = 4
STEP = 7
CAP = 192


EPS_NORM = 1e-05
THETA = 10000.0
BETA_ONE = 0.5
BETA_TWO = 0.6
ADAM_EPS = 1e-08
DECAY = 0.1
GAIN_RATE = 0.3
NEG_BIG = -1e30


def from_behind(shard, axis, by):
    devices = lax.axis_size(axis)
    pairs = [(i, i + by) for i in range(devices) if 0 <= i + by < devices]
    return lax.ppermute(shard, axis, pairs)


def for_sending(shard):

    def short(part):
        return part.astype(jnp.bfloat16) if part.dtype == jnp.float32 else part

    return jax.tree.map(short, shard)


def normalize(values, gain_row):
    scale_row = lax.rsqrt(jnp.mean(values * values, axis=-1, keepdims=True) + EPS_NORM)
    return (values * scale_row * gain_row, scale_row)


def norm_back(values, scale_row, gain_row, grad_out):
    gain_grad = jnp.sum(grad_out * values * scale_row, axis=0)
    weighted = grad_out * gain_row
    grad_in = scale_row * weighted - values * scale_row**3 * jnp.mean(
        values * weighted, axis=-1, keepdims=True
    )
    return (grad_in, gain_grad)


def rotate_half(vector):
    half_width = vector.shape[-1] // 2
    return jnp.concatenate([-vector[..., half_width:], vector[..., :half_width]], axis=-1)


def rotary_tables(positions):
    inverse = THETA ** (-(jnp.arange(HD // 2, dtype=jnp.float32) * 2.0 / HD))
    angles = positions.astype(jnp.float32)[:, None] * inverse[None, :]
    cosine = jnp.concatenate([jnp.cos(angles), jnp.cos(angles)], axis=-1)[:, None, :]
    sine_table = jnp.concatenate([jnp.sin(angles), jnp.sin(angles)], axis=-1)[:, None, :]
    return (cosine, sine_table)


def rotary(vector, cosine, sine_table):
    return vector * cosine + rotate_half(vector) * sine_table


def rotary_back(grad_vec, cosine, sine_table):
    return grad_vec * cosine - rotate_half(grad_vec * sine_table)


def kind_rates(width, hidden):
    base_rate = 0.5 * width ** (-0.5)
    return jnp.array(
        [
            base_rate,
            base_rate,
            base_rate,
            2.0 * (2 * hidden) ** (-0.5),
            base_rate,
            base_rate,
            3.0 * hidden ** (-0.5),
            base_rate,
        ],
        jnp.float32,
    )


def slot_kinds(owners, slot_total):
    count = (owners.shape[0] - 6) // 3
    table = jnp.asarray(np.array([0, 0, 1, 2, 3, 3] + [4, 5, 6] * count, np.int32))
    return jnp.full((slot_total,), 7, jnp.int32).at[owners].set(table)


def adamw(weight, first, second, grad, rate, decay):
    first_new = BETA_ONE * first + (1.0 - BETA_ONE) * grad
    second_new = BETA_TWO * second + (1.0 - BETA_TWO) * grad * grad
    first_hat = first_new / (1.0 - BETA_ONE**STEP)
    second_hat = second_new / (1.0 - BETA_TWO**STEP)
    weight_new = weight - rate * (first_hat / (jnp.sqrt(second_hat) + ADAM_EPS) + decay * weight)
    return (weight_new, first_new, second_new)


def contract_first(left, right):
    return lax.dot_general(
        left, right, (((0,), (0,)), ((), ())), preferred_element_type=jnp.float32
    )


def contract_last(left, right):
    return lax.dot_general(
        left, right, (((1,), (1,)), ((), ())), preferred_element_type=jnp.float32
    )


def shards(
    tokens,
    segments,
    routes,
    gate_weights,
    cotangent,
    owners,
    masters,
    first_moments,
    second_moments,
    norm_gains,
    gain_first,
    gain_second,
):
    wsh_count = lax.axis_size("wsh")
    ctx_index = lax.axis_index("ctx")
    wsh_index = lax.axis_index("wsh")
    slot_count = masters.shape[0]
    slot_total = slot_count * wsh_count
    width = tokens.shape[2]
    hidden = masters.shape[2]
    seg_len = tokens.shape[1]
    matrix_count = owners.shape[0]
    experts_all = (matrix_count - 6) // 3
    experts_here = experts_all // wsh_count
    scale_score = HD ** (-0.5)
    tokens_f = tokens[0].astype(jnp.float32)
    seg_ids = segments[0]
    route_ids = routes[0]
    gate_vals = gate_weights[0]
    cot_rows = cotangent[0].astype(jnp.float32)
    every_slot = lax.all_gather(masters.astype(jnp.bfloat16), "wsh", axis=0, tiled=True)
    wanted = jnp.concatenate(
        [
            jnp.arange(6, dtype=jnp.int32),
            6 + 3 * experts_here * wsh_index + jnp.arange(3 * experts_here, dtype=jnp.int32),
        ]
    )
    weights_low = lax.all_gather(
        jnp.take(every_slot, jnp.take(owners, wanted), axis=0), "ctx", axis=1, tiled=True
    )
    local_experts = (weights_low.shape[0] - 6) // 3
    w_query = jnp.concatenate([weights_low[0], weights_low[1]], axis=1)
    w_key = weights_low[2]
    w_value = weights_low[3]
    w_out = jnp.concatenate([weights_low[4], weights_low[5]], axis=1)
    expert_w = weights_low[6:].reshape(local_experts, 3, width, hidden)
    w_gate = expert_w[:, 0]
    w_up = expert_w[:, 1]
    w_down = expert_w[:, 2]
    attn_norm, scale_one = normalize(tokens_f, norm_gains[0])
    attn_in = attn_norm.astype(jnp.bfloat16)
    queries = jnp.dot(attn_in, w_query, preferred_element_type=jnp.float32)
    keys_raw = jnp.dot(attn_in, w_key, preferred_element_type=jnp.float32)
    values_raw = jnp.dot(attn_in, w_value, preferred_element_type=jnp.float32)
    positions = ctx_index * seg_len + jnp.arange(seg_len, dtype=jnp.int32)
    cosine, sine_table = rotary_tables(positions)
    queries_turned = (
        rotary(queries.reshape(seg_len, QH, HD), cosine, sine_table)
        .astype(jnp.bfloat16)
        .reshape(seg_len, KVH, 2, HD)
    )
    keys_turned = rotary(keys_raw.reshape(seg_len, KVH, HD), cosine, sine_table).astype(
        jnp.bfloat16
    )
    values_low = values_raw.astype(jnp.bfloat16).reshape(seg_len, KVH, HD)
    seg_mark = (seg_ids + 1).astype(jnp.bfloat16)
    current = (keys_turned, values_low, seg_mark)
    blocks = [current]
    for hop in range(1, REACH + 1):
        current = from_behind((current[0], current[1], current[2]), "ctx", 1)
        blocks.append(current)

    def masked_scores(block, hop):
        key_blk = block[0]
        mark_blk = block[2]
        raw_scores = (
            jnp.einsum(
                "qgrd,kgd->grqk", queries_turned, key_blk, preferred_element_type=jnp.float32
            )
            * scale_score
        )
        key_pos = (ctx_index - hop) * seg_len + jnp.arange(seg_len, dtype=jnp.int32)
        allowed = (key_pos[None, :] <= positions[:, None]) & (
            mark_blk[None, :] == seg_mark[:, None]
        )
        return jnp.where(allowed, raw_scores, NEG_BIG)

    row_max = None
    row_sum = None
    for hop in range(REACH + 1):
        scores = masked_scores(blocks[hop], hop)
        block_max = jnp.max(scores, axis=-1)
        if hop == 0:
            new_max = block_max
            row_sum = jnp.sum(jnp.exp(scores - new_max[..., None]), axis=-1)
        else:
            new_max = jnp.maximum(row_max, block_max)
            row_sum = row_sum * jnp.exp(row_max - new_max) + jnp.sum(
                jnp.exp(scores - new_max[..., None]), axis=-1
            )
        row_max = new_max
    log_total = row_max + jnp.log(row_sum)
    mixed_low = jnp.zeros((seg_len, KVH, 2, HD), jnp.float32)
    mixed_tail = jnp.zeros((seg_len, KVH, 2, HD), jnp.float32)
    for hop in range(REACH + 1):
        probs = jnp.exp(masked_scores(blocks[hop], hop) - log_total[..., None])
        value_blk = blocks[hop][1]
        probs_head = probs.astype(jnp.bfloat16)
        probs_tail = (probs - probs_head.astype(jnp.float32)).astype(jnp.bfloat16)
        mixed_low = mixed_low + jnp.einsum(
            "grqk,kgd->qgrd", probs_head, value_blk, preferred_element_type=jnp.float32
        )
        mixed_tail = mixed_tail + jnp.einsum(
            "grqk,kgd->qgrd", probs_tail, value_blk, preferred_element_type=jnp.float32
        )
    mixed_full = mixed_low + mixed_tail
    attn_mix = mixed_low.reshape(seg_len, QH * HD).astype(jnp.bfloat16)
    attn_out = contract_last(attn_mix, w_out)
    resid_one = tokens_f + attn_out
    expert_norm, scale_two = normalize(resid_one, norm_gains[1])
    expert_in = expert_norm.astype(jnp.bfloat16)
    flat_routes = route_ids.reshape(seg_len * TOPK)
    expert_ids = jnp.arange(experts_all, dtype=jnp.int32)
    onehot_hits = (flat_routes[:, None] == expert_ids[None, :]).astype(jnp.int32)
    rank_in = jnp.sum((jnp.cumsum(onehot_hits, axis=0) - 1) * onehot_hits, axis=1)
    slot_ids = flat_routes * CAP + rank_in
    owner_rows = jnp.arange(seg_len * TOPK, dtype=jnp.int32) // TOPK

    def pack(rows_in):
        empty = jnp.zeros((experts_all * CAP, width), rows_in.dtype)
        return empty.at[slot_ids].set(rows_in).reshape(experts_all, CAP, width)

    send_rows = pack(expert_in[owner_rows])
    grad_send = pack(
        (gate_vals[:, :, None] * cot_rows[:, None, :])
        .astype(jnp.bfloat16)
        .reshape(seg_len * TOPK, width)
    )
    expert_rows = lax.all_to_all(send_rows, "wsh", split_axis=0, concat_axis=1, tiled=True)
    gate_pre = jnp.einsum("erd,edh->erh", expert_rows, w_gate, preferred_element_type=jnp.float32)
    up_pre = jnp.einsum("erd,edh->erh", expert_rows, w_up, preferred_element_type=jnp.float32)
    hidden_low = (jax.nn.silu(gate_pre) * up_pre).astype(jnp.bfloat16)
    result = jnp.einsum(
        "erh,edh->erd", hidden_low, w_down, preferred_element_type=jnp.float32
    ).astype(jnp.bfloat16)
    result, gate_pre, up_pre, hidden_low = (result, gate_pre, up_pre, hidden_low)
    returned = lax.all_to_all(result, "wsh", split_axis=1, concat_axis=0, tiled=True)
    grad_rows = lax.all_to_all(grad_send, "wsh", split_axis=0, concat_axis=1, tiled=True)
    grad_down = jnp.einsum(
        "erd,erh->edh", grad_rows, hidden_low, preferred_element_type=jnp.float32
    )
    grad_hidden = jnp.einsum("erd,edh->erh", grad_rows, w_down, preferred_element_type=jnp.float32)
    logistic = jax.nn.sigmoid(gate_pre)
    grad_gate_low = (grad_hidden * up_pre * logistic * (1.0 + gate_pre * (1.0 - logistic))).astype(
        jnp.bfloat16
    )
    grad_up_low = (grad_hidden * gate_pre * logistic).astype(jnp.bfloat16)
    grad_gate_w = jnp.einsum(
        "erd,erh->edh", expert_rows, grad_gate_low, preferred_element_type=jnp.float32
    )
    grad_up_w = jnp.einsum(
        "erd,erh->edh", expert_rows, grad_up_low, preferred_element_type=jnp.float32
    )
    grad_in_rows = jnp.einsum(
        "erh,edh->erd", grad_gate_low, w_gate, preferred_element_type=jnp.float32
    )
    grad_in_rows = grad_in_rows + jnp.einsum(
        "erh,edh->erd", grad_up_low, w_up, preferred_element_type=jnp.float32
    )
    grad_gate_w, grad_up_w, grad_down, grad_in_rows = (
        grad_gate_w,
        grad_up_w,
        grad_down,
        grad_in_rows,
    )
    row_grads = lax.all_to_all(
        grad_in_rows.astype(jnp.bfloat16), "wsh", split_axis=1, concat_axis=0, tiled=True
    ).astype(grad_in_rows.dtype)
    picked = (
        returned.reshape(experts_all * CAP, width)[slot_ids]
        .reshape(seg_len, TOPK, width)
        .astype(jnp.float32)
    )
    resid_two = resid_one + jnp.sum(gate_vals[:, :, None] * picked, axis=1)
    output = resid_two.astype(jnp.bfloat16)
    grad_expert_in = jnp.sum(
        row_grads.reshape(experts_all * CAP, width)[slot_ids].reshape(seg_len, TOPK, width), axis=1
    )
    norm_grad_two, gain_grad_two = norm_back(resid_one, scale_two, norm_gains[1], grad_expert_in)
    grad_resid = cot_rows + norm_grad_two
    grad_attn_low = grad_resid.astype(jnp.bfloat16)
    grad_w_out = contract_first(grad_attn_low, attn_mix)
    grad_mix_low = (
        jnp.dot(grad_attn_low, w_out, preferred_element_type=jnp.float32)
        .astype(jnp.bfloat16)
        .reshape(seg_len, KVH, 2, HD)
    )
    row_delta = jnp.transpose(
        jnp.sum(grad_mix_low.astype(jnp.float32) * mixed_full, axis=-1), (1, 2, 0)
    )
    grad_queries = jnp.zeros((seg_len, KVH, 2, HD), jnp.float32)
    remote = []
    for hop in range(REACH + 1):
        key_blk = blocks[hop][0]
        value_blk = blocks[hop][1]
        probs = jnp.exp(masked_scores(blocks[hop], hop) - log_total[..., None])
        grad_probs = jnp.einsum(
            "qgrd,kgd->grqk", grad_mix_low, value_blk, preferred_element_type=jnp.float32
        )
        grad_scores = (probs * (grad_probs - row_delta[..., None]) * scale_score).astype(
            jnp.bfloat16
        )
        grad_queries = grad_queries + jnp.einsum(
            "grqk,kgd->qgrd", grad_scores, key_blk, preferred_element_type=jnp.float32
        )
        grad_keys_hop = jnp.einsum(
            "grqk,qgrd->kgd", grad_scores, queries_turned, preferred_element_type=jnp.float32
        )
        grad_values_hop = jnp.einsum(
            "grqk,qgrd->kgd",
            probs.astype(jnp.bfloat16),
            grad_mix_low,
            preferred_element_type=jnp.float32,
        )
        remote.append((grad_keys_hop, grad_values_hop))
    grad_keys = remote[0][0]
    grad_values = remote[0][1]
    for hop in range(1, REACH + 1):
        arrived = from_behind(for_sending(remote[hop]), "ctx", -hop)
        grad_keys = grad_keys + arrived[0]
        grad_values = grad_values + arrived[1]
    grad_q_low = (
        rotary_back(grad_queries.reshape(seg_len, QH, HD), cosine, sine_table)
        .astype(jnp.bfloat16)
        .reshape(seg_len, QH * HD)
    )
    grad_k_low = (
        rotary_back(grad_keys, cosine, sine_table).astype(jnp.bfloat16).reshape(seg_len, hidden)
    )
    grad_v_low = grad_values.astype(jnp.bfloat16).reshape(seg_len, hidden)
    grad_w_query = contract_first(attn_in, grad_q_low)
    grad_w_key = contract_first(attn_in, grad_k_low)
    grad_w_value = contract_first(attn_in, grad_v_low)
    grad_attn_in = (
        contract_last(grad_q_low, w_query)
        + contract_last(grad_k_low, w_key)
        + contract_last(grad_v_low, w_value)
    )
    norm_grad_one, gain_grad_one = norm_back(tokens_f, scale_one, norm_gains[0], grad_attn_in)
    input_grad = grad_resid + norm_grad_one
    attn_grads = jnp.stack(
        [
            grad_w_query[:, :hidden],
            grad_w_query[:, hidden:],
            grad_w_key,
            grad_w_value,
            grad_w_out[:, :hidden],
            grad_w_out[:, hidden:],
        ]
    )
    expert_grads = jnp.stack([grad_gate_w, grad_up_w, grad_down], axis=1).reshape(-1, width, hidden)
    all_grads = jnp.concatenate([attn_grads, expert_grads], axis=0)
    summed = lax.psum_scatter(all_grads, "ctx", scatter_dimension=1, tiled=True)
    slot_buffer = (
        jnp.zeros((slot_total, summed.shape[1], hidden), jnp.float32)
        .at[jnp.take(owners, wanted)]
        .set(summed)
    )
    slot_grad = lax.psum_scatter(
        slot_buffer.astype(jnp.bfloat16), "wsh", scatter_dimension=0, tiled=True
    ).astype(jnp.float32)
    kinds_mine = lax.dynamic_slice_in_dim(
        slot_kinds(owners, slot_total), wsh_index * slot_count, slot_count
    )
    rates = kind_rates(width, hidden)[kinds_mine][:, None, None]
    new_masters, new_first, new_second = adamw(
        masters, first_moments, second_moments, slot_grad, rates, DECAY
    )
    gain_grad = lax.psum(jnp.stack([gain_grad_one, gain_grad_two]), ("ctx", "wsh"))
    new_gains, new_gain_first, new_gain_second = adamw(
        norm_gains, gain_first, gain_second, gain_grad, GAIN_RATE, 0.0
    )
    return (
        output[None],
        input_grad[None],
        new_masters,
        new_first,
        new_second,
        new_gains,
        new_gain_first,
        new_gain_second,
    )


def solution(mesh):
    return jax.shard_map(
        shards,
        mesh=mesh,
        in_specs=(
            P("wsh", "ctx", None),
            P("wsh", "ctx"),
            P("wsh", "ctx", None),
            P("wsh", "ctx", None),
            P("wsh", "ctx", None),
            P(),
            P("wsh", "ctx", None),
            P("wsh", "ctx", None),
            P("wsh", "ctx", None),
            P(),
            P(),
            P(),
        ),
        out_specs=(
            P("wsh", "ctx", None),
            P("wsh", "ctx", None),
            P("wsh", "ctx", None),
            P("wsh", "ctx", None),
            P("wsh", "ctx", None),
            P(),
            P(),
            P(),
        ),
        check_vma=False,
    )
```

profile of v0, /device:TPU:0, one launch (start us, length us, event | category | flops | bytes accessed | tf_op | source)
XLA Modules:
  0.0 1748.5 jit_solution(1947780251017787539)
XLA Ops:
  7.2 4.4 convert_element_type.296
  13.1 71.5 %all-gather.3.cloned.1.call-done = bf16[80,128,512]{2,1,0:T(8,128)(2,1)} async-done(((bf16[20,128,512]{2,1,0:T(8,128)(2,1)}), bf16[80,128,512]{2,1,0:T(8,128)(2,1)}) %all-gather.3.cloned.1.call-update) | async-done | bytes 10485776 | tf_op jit(solution)/shard_map/all_gather | solution.py:150
  84.7 4.7 gather_fusion
  91.1 3.4 collective-permute-start
  95.2 4.5 reduce-window.6
  100.9 14.4 scatter_custom_fusion.1
  115.3 5.4 all-to-all-start.2
  122.4 3.4 collective-permute-start.2
  127.1 4.1 collective-permute-start.4
  132.5 4.5 collective-permute-start.6
  139.0 314.7 %all-gather.5.cloned.1.call-done = bf16[18,1024,512]{2,1,0:T(8,128)(2,1)} async-done(((bf16[18,128,512]{2,1,0:T(8,128)(2,1)}), bf16[18,1024,512]{2,1,0:T(8,128)(2,1)}) %all-gather.5.cloned.1.call-update) | async-done | bytes 18874384 | tf_op jit(solution)/shard_map/all_gather | solution.py:157
  456.3 4.4 slice_bitcast_fusion.18
  462.4 2.6 copy.107
  464.9 2.5 fusion.112
  474.0 4.5 collective-permute-start.8
  480.6 4.5 collective-permute-start.3
  486.2 4.5 collective-permute-start.9
  491.9 5.0 collective-permute-start.5
  497.5 5.3 collective-permute-start.10
  503.6 5.3 collective-permute-start.7
  509.5 5.0 collective-permute-start.11
  529.0 28.6 %scatter_custom_fusion = bf16[3072,1024]{1,0:T(8,128)(2,1)} fusion(s32[2048]{0:T(1024)S(1)} %bitcast.709, bf16[256,1024]{1,0:T(8,128)(2,1)S(1)} %multiply_convert_fusion.3, s32[2048]{0:T(1024)} %broadcast_clamp_fusion.1, bf16[]{:T(256)} %constant.82.clone.1), kind=kCustom, calls=%fused_computation.54 | custom fusion | bytes 6291968 | tf_op jit(solution)/shard_map/scatter | solution.py:250
  557.7 5.4 all-to-all-start
  563.1 6.4 copy.124
  569.6 10.4 slice.130
  580.0 53.8 %all-to-all-done = bf16[16,192,1024]{2,1,0:T(8,128)(2,1)} async-done(((bf16[16,192,1024]{2,1,0:T(8,128)(2,1)}), bf16[16,192,1024]{2,1,0:T(8,128)(2,1)}, u32[]{:S(2)}, u32[]{:S(2)}) %all-to-all-start) | async-done | bytes 6291488 | tf_op jit(solution)/shard_map/all_to_all | solution.py:258
  633.8 3.7 copy.117
  637.5 5.0 copy-done.5
  642.5 5.3 fusion.25
  647.8 5.3 fusion.27
  653.1 13.1 multiply_convert_fusion
  666.2 8.9 fusion.24
  675.1 12.9 add_convert_fusion
  688.0 10.3 copy.125
  698.3 5.6 all-to-all-start.3
  704.7 3.6 fusion.48
  712.8 7.7 fusion.31
  720.4 10.4 copy.121
  730.8 43.8 %all-to-all-done.3 = bf16[4,768,1024]{2,0,1:T(4,128)(2,1)} async-done(((bf16[4,768,1024]{2,0,1:T(4,128)(2,1)}), bf16[4,768,1024]{2,0,1:T(4,128)(2,1)}, u32[]{:S(2)}, u32[]{:S(2)}) %all-to-all-start.3) | async-done | bytes 6291488 | tf_op jit(solution)/shard_map/all_to_all | solution.py:295
  774.6 5.2 all-to-all-start.1
  779.9 4.7 fusion.65
  784.7 7.1 convolution_bitcast_fusion
  791.8 9.4 convolution_bitcast_fusion.1
  801.2 9.5 convolution_bitcast_fusion.2
  810.7 8.6 pad_maximum_fusion
  819.3 8.8 copy.151
  828.1 9.6 copy.126
  837.7 16.3 gather_fusion.2
  854.0 5.5 bitcast_reduce_fusion
  859.9 7.7 copy.122
  867.6 14.7 gather_fusion.1
  882.4 4.9 fusion
  889.5 3.4 fusion.82
  929.8 13.8 collective-permute-done.15
  950.8 26.5 %collective-permute-done.19 = bf16[256,8,64]{0,2,1:T(8,128)(2,1)S(1)} collective-permute-done((bf16[256,8,64]{0,2,1:T(8,128)(2,1)S(1)}, bf16[256,8,64]{0,2,1:T(8,128)(2,1)S(1)}, u32[]{:S(2)}, u32[]{:S(2)}) %collective-permute-start.19) | collective-permute-done | bytes 262176 | tf_op jit(solution)/shard_map/ppermute | solution.py:29
  982.8 8.7 constant_dynamic-update-slice_fusion
  991.5 617.7 %reduce-scatter.3.cloned.1.call-done = f32[18,128,512]{2,1,0:T(8,128)} async-done(((f32[18,1024,512]{2,1,0:T(8,128)}), f32[18,128,512]{2,1,0:T(8,128)}) %reduce-scatter.3.cloned.1.call-update) | async-done | bytes 4718608 | tf_op jit(solution)/shard_map/reduce_scatter | solution.py:382
  1609.3 9.8 broadcast_in_dim.85
  1619.1 10.8 scatter_fusion
  1629.8 12.2 convert_element_type.373
  1645.9 2.9 fusion.59
  1653.1 38.8 %psum.7 = f32[2,1024]{1,0:T(2,128)S(1)} all-reduce(f32[2,1024]{1,0:T(2,128)S(1)} %pad_maximum_fusion.11), channel_id=1, replica_groups=mesh['ctx'=8,'wsh'=4] {'ctx','wsh'}, use_global_device_ids=true, to_apply=%region_28.30 | all-reduce | flops 2048 | bytes 16384 | tf_op jit(solution)/shard_map/psum | solution.py:398
  1693.9 33.6 %reduce-scatter.5.cloned.1.call-done = bf16[20,128,512]{2,1,0:T(8,128)(2,1)} async-done(((bf16[80,128,512]{2,1,0:T(8,128)(2,1)}), bf16[20,128,512]{2,1,0:T(8,128)(2,1)}) %reduce-scatter.5.cloned.1.call-update) | async-done | bytes 2621456 | tf_op jit(solution)/shard_map/reduce_scatter | solution.py:388
  1727.4 14.0 multiply_subtract_fusion
  (357 shorter events, 109.5 us)
Async XLA Ops:
  7.2 77.5 %all-gather.3.cloned.1.call-start = ((), (), s32[]{:S(2)}) async-start(), calls=%async_computation.6 | async-start | bytes 13107200 | tf_op jit(solution)/shard_map/all_gather | solution.py:150
  11.6 442.2 %all-gather.5.cloned.1.call-start = ((), (), s32[]{:S(2)}) async-start(), calls=%async_computation.7 | async-start | bytes 21233664 | tf_op jit(solution)/shard_map/all_gather | solution.py:157
  89.4 11.0 copy-start.75
  89.4 11.4 copy-start.32
  91.1 31.2 %collective-permute-start = (bf16[256]{0:T(256)(128)(2,1)S(1)}, bf16[256]{0:T(256)(128)(2,1)S(1)}, u32[]{:S(2)}, u32[]{:S(2)}) collective-permute-start(bf16[256]{0:T(256)(128)(2,1)S(1)} %convert_reduce_fusion), channel_id=1, source_target_pairs={{0,4},{4,8},{8,12},{12,16},{16,20},{20,24},{24,28},{1,5},{5,9},{9,... | collective-permute-start | bytes 1544 | tf_op jit(solution)/shard_map/ppermute | solution.py:29
  100.9 14.4 copy-start.80
  115.3 442.4 %all-to-all-start.2 = ((bf16[16,192,1024]{2,1,0:T(8,128)(2,1)}), bf16[16,192,1024]{2,1,0:T(8,128)(2,1)}, u32[]{:S(2)}, u32[]{:S(2)}) async-start(bf16[16,192,1024]{2,1,0:T(8,128)(2,1)} %bitcast.627), calls=%async_computation.2 | async-start | bytes 12582912 | tf_op jit(solution)/shard_map/all_to_all | solution.py:267
  120.9 357.6 %copy-start.37 = (f32[256,64]{0,1:T(8,128)}, f32[256,64]{0,1:T(8,128)S(1)}, u32[]{:S(2)}) copy-start(f32[256,64]{0,1:T(8,128)S(1)} %pad_maximum_fusion.10) | copy-start | bytes 196612
  120.9 357.6 %copy-start.28 = (f32[256,64]{0,1:T(8,128)}, f32[256,64]{0,1:T(8,128)S(1)}, u32[]{:S(2)}) copy-start(f32[256,64]{0,1:T(8,128)S(1)} %pad_maximum_fusion.9) | copy-start | bytes 196612
  121.7 347.9 %copy-start.73 = (f32[256]{0:T(256)}, f32[256]{0:T(256)S(1)}, u32[]{:S(2)}) copy-start(f32[256]{0:T(256)S(1)} %get-tuple-element.55) | copy-start | bytes 3076
  121.8 347.9 %copy-start.69 = (f32[1,1024]{1,0:T(1,128)}, f32[1,1024]{1,0:T(1,128)S(1)}, u32[]{:S(2)}) copy-start(f32[1,1024]{1,0:T(1,128)S(1)} %get-tuple-element.46) | copy-start | bytes 12292
  121.8 406.8 %copy-start.71 = (f32[1,1024]{1,0:T(1,128)}, f32[1,1024]{1,0:T(1,128)S(1)}, u32[]{:S(2)}) copy-start(f32[1,1024]{1,0:T(1,128)S(1)} %get-tuple-element.45) | copy-start | bytes 12292
  122.4 4.7 collective-permute-start.2
  127.1 5.4 collective-permute-start.4
  132.5 5.5 collective-permute-start.6
  139.0 385.8 %copy-start.39 = (pred[256,256]{0,1:T(8,128)(4,1)}, pred[256,256]{0,1:T(8,128)(4,1)S(1)}, u32[]{:S(2)}) copy-start(pred[256,256]{0,1:T(8,128)(4,1)S(1)} %get-tuple-element.49) | copy-start | bytes 196612
  469.7 8.9 copy-start.36
  469.7 9.1 copy-start.54
  471.7 8.8 copy-start.30
  471.7 8.9 collective-permute-start.1
  474.0 12.3 collective-permute-start.8
  478.7 36.9 %copy-start.3 = (bf16[256,16,64]{0,2,1:T(8,128)(2,1)}, bf16[256,16,64]{0,2,1:T(8,128)(2,1)S(1)}, u32[]{:S(2)}) copy-start(bf16[256,16,64]{0,2,1:T(8,128)(2,1)S(1)} %fusion.101) | copy-start | bytes 1572868
  479.6 40.8 %copy-start.18 = (f32[8,256,256,2]{2,1,3,0:T(8,128)}, f32[8,256,256,2]{2,1,3,0:T(8,128)S(1)}, u32[]{:S(2)}) copy-start(f32[8,256,256,2]{2,1,3,0:T(8,128)S(1)} %get-tuple-element.65) | copy-start | bytes 12582916
  480.6 23.0 %copy-start.46 = (bf16[256,8,64]{0,2,1:T(8,128)(2,1)}, bf16[256,8,64]{0,2,1:T(8,128)(2,1)S(1)}, u32[]{:S(2)}) copy-start(bf16[256,8,64]{0,2,1:T(8,128)(2,1)S(1)} %collective-permute-done.1) | copy-start | bytes 786436
  480.6 11.2 collective-permute-start.3
  486.2 35.2 %copy-start.59 = (bf16[256,8,64]{0,2,1:T(8,128)(2,1)}, bf16[256,8,64]{0,2,1:T(8,128)(2,1)S(1)}, u32[]{:S(2)}) copy-start(bf16[256,8,64]{0,2,1:T(8,128)(2,1)S(1)} %collective-permute-done.8) | copy-start | bytes 786436
  486.2 11.2 collective-permute-start.9
  491.6 29.9 %copy-start.8 = (f32[8,256,256,2]{2,1,3,0:T(8,128)}, f32[8,256,256,2]{2,1,3,0:T(8,128)S(1)}, u32[]{:S(2)}) copy-start(f32[8,256,256,2]{2,1,3,0:T(8,128)S(1)} %get-tuple-element.67) | copy-start | bytes 12582916
  491.9 23.4 %copy-start.48 = (bf16[256,8,64]{0,2,1:T(8,128)(2,1)}, bf16[256,8,64]{0,2,1:T(8,128)(2,1)S(1)}, u32[]{:S(2)}) copy-start(bf16[256,8,64]{0,2,1:T(8,128)(2,1)S(1)} %collective-permute-done.3) | copy-start | bytes 786436
  491.9 11.8 collective-permute-start.5
  497.5 25.1 %copy-start.62 = (bf16[256,8,64]{0,2,1:T(8,128)(2,1)}, bf16[256,8,64]{0,2,1:T(8,128)(2,1)S(1)}, u32[]{:S(2)}) copy-start(bf16[256,8,64]{0,2,1:T(8,128)(2,1)S(1)} %collective-permute-done.9) | copy-start | bytes 786436
  497.5 12.0 collective-permute-start.10
  503.6 19.0 %copy-start.11 = (f32[8,256,256,2]{2,1,3,0:T(8,128)}, f32[8,256,256,2]{2,1,3,0:T(8,128)S(1)}, u32[]{:S(2)}) copy-start(f32[8,256,256,2]{2,1,3,0:T(8,128)S(1)} %get-tuple-element.63) | copy-start | bytes 12582916
  503.6 12.8 copy-start.50
  503.6 12.0 collective-permute-start.7
  509.5 14.2 copy-start.65
  509.5 15.4 collective-permute-start.11
  528.5 29.2 %copy-start.82 = (f32[256]{0:T(256)}, f32[256]{0:T(256)S(1)}, u32[]{:S(2)}) copy-start(f32[256]{0:T(256)S(1)} %get-tuple-element.57) | copy-start | bytes 3076
  557.7 76.1 %all-to-all-start = ((bf16[16,192,1024]{2,1,0:T(8,128)(2,1)}), bf16[16,192,1024]{2,1,0:T(8,128)(2,1)}, u32[]{:S(2)}, u32[]{:S(2)}) async-start(bf16[16,192,1024]{2,1,0:T(8,128)(2,1)} %bitcast.628), calls=%async_computation | async-start | bytes 12582912 | tf_op jit(solution)/shard_map/all_to_all | solution.py:258
  633.8 8.7 copy-start.5
  637.5 10.3 copy-start.23
  698.3 76.3 %all-to-all-start.3 = ((bf16[4,768,1024]{2,0,1:T(4,128)(2,1)}), bf16[4,768,1024]{2,0,1:T(4,128)(2,1)}, u32[]{:S(2)}, u32[]{:S(2)}) async-start(bf16[4,768,1024]{2,0,1:T(4,128)(2,1)} %copy.125), calls=%async_computation.3 | async-start | bytes 12582912 | tf_op jit(solution)/shard_map/all_to_all | solution.py:295
  774.6 85.3 %all-to-all-start.1 = ((bf16[4,768,1024]{2,0,1:T(4,128)(2,1)}), bf16[4,768,1024]{2,0,1:T(4,128)(2,1)}, u32[]{:S(2)}, u32[]{:S(2)}) async-start(bf16[4,768,1024]{2,0,1:T(4,128)(2,1)} %copy.121), calls=%async_computation.1 | async-start | bytes 12582912 | tf_op jit(solution)/shard_map/all_to_all | solution.py:266
  779.9 829.4 %reduce-scatter.3.cloned.1.call-start = ((), (), s32[]{:S(2)}) async-start(), calls=%async_computation.8 | async-start | bytes 42467328 | tf_op jit(solution)/shard_map/reduce_scatter | solution.py:382
  867.6 14.7 copy-start.56
  917.6 65.0 %slice-start = ((s8[25165824]{0:T(1024)(128)(4,1)}), s8[4194304]{0:T(1024)(128)(4,1)S(1)}, s32[]{:S(2)}) async-start(s8[25165824]{0:T(1024)(128)(4,1)} %bitcast.608), calls=%async_computation.10 | async-start | bytes 8388608
  917.8 25.7 %collective-permute-start.15 = (bf16[256,8,64]{0,2,1:T(8,128)(2,1)S(1)}, bf16[256,8,64]{0,2,1:T(8,128)(2,1)S(1)}, u32[]{:S(2)}, u32[]{:S(2)}) collective-permute-start(bf16[256,8,64]{0,2,1:T(8,128)(2,1)S(1)} %fusion.86), channel_id=1, source_target_pairs={{16,0},{20,4},{24,8},{28,12},{17,1},{21,5},{25,9},{29,13},{18,2},{... | collective-permute-start | bytes 786440 | tf_op jit(solution)/shard_map/ppermute | solution.py:29
  919.4 25.5 %collective-permute-start.14 = (bf16[256,8,64]{0,2,1:T(8,128)(2,1)S(1)}, bf16[256,8,64]{0,2,1:T(8,128)(2,1)S(1)}, u32[]{:S(2)}, u32[]{:S(2)}) collective-permute-start(bf16[256,8,64]{0,2,1:T(8,128)(2,1)S(1)} %fusion.87), channel_id=1, source_target_pairs={{12,0},{16,4},{20,8},{24,12},{28,16},{13,1},{17,5},{21,9},{25,13},... | collective-permute-start | bytes 786440 | tf_op jit(solution)/shard_map/ppermute | solution.py:29
  920.7 25.5 %collective-permute-start.13 = (bf16[256,8,64]{0,2,1:T(8,128)(2,1)S(1)}, bf16[256,8,64]{0,2,1:T(8,128)(2,1)S(1)}, u32[]{:S(2)}, u32[]{:S(2)}) collective-permute-start(bf16[256,8,64]{0,2,1:T(8,128)(2,1)S(1)} %fusion.88), channel_id=1, source_target_pairs={{8,0},{12,4},{16,8},{20,12},{24,16},{28,20},{9,1},{13,5},{17,9},{2... | collective-permute-start | bytes 786440 | tf_op jit(solution)/shard_map/ppermute | solution.py:29
  922.0 25.7 %collective-permute-start.12 = (bf16[256,8,64]{0,2,1:T(8,128)(2,1)S(1)}, bf16[256,8,64]{0,2,1:T(8,128)(2,1)S(1)}, u32[]{:S(2)}, u32[]{:S(2)}) collective-permute-start(bf16[256,8,64]{0,2,1:T(8,128)(2,1)S(1)} %fusion.89), channel_id=1, source_target_pairs={{4,0},{8,4},{12,8},{16,12},{20,16},{24,20},{28,24},{5,1},{9,5},{13... | collective-permute-start | bytes 786440 | tf_op jit(solution)/shard_map/ppermute | solution.py:29
  923.3 54.0 %collective-permute-start.19 = (bf16[256,8,64]{0,2,1:T(8,128)(2,1)S(1)}, bf16[256,8,64]{0,2,1:T(8,128)(2,1)S(1)}, u32[]{:S(2)}, u32[]{:S(2)}) collective-permute-start(bf16[256,8,64]{0,2,1:T(8,128)(2,1)S(1)} %fusion.82), channel_id=1, source_target_pairs={{16,0},{20,4},{24,8},{28,12},{17,1},{21,5},{25,9},{29,13},{18,2},{... | collective-permute-start | bytes 786440 | tf_op jit(solution)/shard_map/ppermute | solution.py:29
  924.6 58.0 %slice-start.1 = ((s8[25165824]{0:T(1024)(128)(4,1)}), s8[4194304]{0:T(1024)(128)(4,1)S(1)}, s32[]{:S(2)}) async-start(s8[25165824]{0:T(1024)(128)(4,1)} %bitcast.608), calls=%async_computation.11 | async-start | bytes 8388608
  926.6 56.0 %slice-start.2 = ((s8[25165824]{0:T(1024)(128)(4,1)}), s8[4194304]{0:T(1024)(128)(4,1)S(1)}, s32[]{:S(2)}) async-start(s8[25165824]{0:T(1024)(128)(4,1)} %bitcast.608), calls=%async_computation.12 | async-start | bytes 8388608
  929.8 52.8 %slice-start.3 = ((s8[25165824]{0:T(1024)(128)(4,1)}), s8[4194304]{0:T(1024)(128)(4,1)S(1)}, s32[]{:S(2)}) async-start(s8[25165824]{0:T(1024)(128)(4,1)} %bitcast.608), calls=%async_computation.13 | async-start | bytes 8388608
  943.5 33.8 %collective-permute-start.18 = (bf16[256,8,64]{0,2,1:T(8,128)(2,1)S(1)}, bf16[256,8,64]{0,2,1:T(8,128)(2,1)S(1)}, u32[]{:S(2)}, u32[]{:S(2)}) collective-permute-start(bf16[256,8,64]{0,2,1:T(8,128)(2,1)S(1)} %fusion.83), channel_id=1, source_target_pairs={{12,0},{16,4},{20,8},{24,12},{28,16},{13,1},{17,5},{21,9},{25,13},... | collective-permute-start | bytes 786440 | tf_op jit(solution)/shard_map/ppermute | solution.py:29
  944.8 32.5 %collective-permute-start.17 = (bf16[256,8,64]{0,2,1:T(8,128)(2,1)S(1)}, bf16[256,8,64]{0,2,1:T(8,128)(2,1)S(1)}, u32[]{:S(2)}, u32[]{:S(2)}) collective-permute-start(bf16[256,8,64]{0,2,1:T(8,128)(2,1)S(1)} %fusion.84), channel_id=1, source_target_pairs={{8,0},{12,4},{16,8},{20,12},{24,16},{28,20},{9,1},{13,5},{17,9},{2... | collective-permute-start | bytes 786440 | tf_op jit(solution)/shard_map/ppermute | solution.py:29
  946.1 31.2 %collective-permute-start.16 = (bf16[256,8,64]{0,2,1:T(8,128)(2,1)S(1)}, bf16[256,8,64]{0,2,1:T(8,128)(2,1)S(1)}, u32[]{:S(2)}, u32[]{:S(2)}) collective-permute-start(bf16[256,8,64]{0,2,1:T(8,128)(2,1)S(1)} %fusion.85), channel_id=1, source_target_pairs={{4,0},{8,4},{12,8},{16,12},{20,16},{24,20},{28,24},{5,1},{9,5},{13... | collective-permute-start | bytes 786440 | tf_op jit(solution)/shard_map/ppermute | solution.py:29
  948.8 33.8 %slice-start.4 = ((s8[25165824]{0:T(1024)(128)(4,1)}), s8[4194304]{0:T(1024)(128)(4,1)S(1)}, s32[]{:S(2)}) async-start(s8[25165824]{0:T(1024)(128)(4,1)} %bitcast.608), calls=%async_computation.14 | async-start | bytes 8388608
  991.5 627.6 %copy-start.87 = (s32[18]{0:T(128)S(1)}, s32[18]{0:T(128)}, u32[]{:S(2)}) copy-start(s32[18]{0:T(128)} %copy-done.86) | copy-start | bytes 220
  991.5 736.0 %reduce-scatter.5.cloned.1.call-start = ((), (), s32[]{:S(2)}) async-start(), calls=%async_computation.9 | async-start | bytes 13107200 | tf_op jit(solution)/shard_map/reduce_scatter | solution.py:388
  1648.8 43.1 %copy-start.79 = (f32[2,1024]{1,0:T(2,128)S(1)}, f32[2,1024]{1,0:T(2,128)}, u32[]{:S(2)}) copy-start(f32[2,1024]{1,0:T(2,128)} %param.25) | copy-start | bytes 24580
  1648.8 43.1 %copy-start.84 = (f32[2,1024]{1,0:T(2,128)S(1)}, f32[2,1024]{1,0:T(2,128)}, u32[]{:S(2)}) copy-start(f32[2,1024]{1,0:T(2,128)} %param.26) | copy-start | bytes 24580
  1648.8 43.1 %copy-start.85 = (f32[2,1024]{1,0:T(2,128)S(1)}, f32[2,1024]{1,0:T(2,128)}, u32[]{:S(2)}) copy-start(f32[2,1024]{1,0:T(2,128)} %param.27) | copy-start | bytes 24580
  1648.8 43.8 %copy-start.88 = (f32[256]{0:T(256)S(1)}, f32[256]{0:T(256)}, u32[]{:S(2)}) copy-start(f32[256]{0:T(256)} %get-tuple-element.54) | copy-start | bytes 3076
  (63 other events, 220.2 us)
Sparse Core Ops, SparseCore 0:
  11.7 72.8 all-gather.2
  91.2 362.5 all-gather.4
  991.6 617.6 reduce-scatter.2
  1642.2 85.2 reduce-scatter.4
where the time goes:
time: 1760 us; the launch traced here: 1750 us
  waiting for transfers between devices  1180 us (67%)
  local copies, waits for them, and re-layouts  195 us (11%)
  matrix products  144 us (8%)
  other arithmetic  87.6 us (5%)
  starting transfers between devices  84.4 us (5%)
  blocking collectives  38.8 us (2%)
    reduce_scatter x1, waiting for transfers between devices, shards(): summed = lax.psum_scatter(all_grads, 'ctx', scatter_dimension=1, tiled=True)  618 us
    all_gather x1, waiting for transfers between devices, shards(): lax.all_gather(jnp.take(every_slot, jnp.take(owners, wanted), axis=0), 'c...  315 us
    all_gather x1, waiting for transfers between devices, shards(): lax.all_gather(masters.astype(jnp.bfloat16), 'wsh', axis=0, tiled=True)  71.5 us
    ppermute x20, starting transfers between devices, from_behind(): return lax.ppermute(shard, axis, pairs)  62.6 us
    all_to_all x1, waiting for transfers between devices, shards(): lax.all_to_all(send_rows, 'wsh', split_axis=0, concat_axis=1, tiled=True)  53.8 us
    ppermute x20, waiting for transfers between devices, from_behind(): return lax.ppermute(shard, axis, pairs)  46.9 us
    all_to_all x1, waiting for transfers between devices, shards(): lax.all_to_all(grad_in_rows.astype(jnp.bfloat16), 'wsh', split_axis=1, co...  43.8 us
    psum x1, blocking collectives, shards(): lax.psum(jnp.stack([gain_grad_one, gain_grad_two]), ('ctx', 'wsh'))  38.8 us
  transfers between devices with their start and end apart: 28, of which 17 were waited for; matrix products, arithmetic and copies ran while one was open for 13% of the time, Pallas kernels for 0%

commit v1 on v0

v1 whole, which is shorter than its diff:
```python
import jax
import jax.numpy as jnp
import numpy as np
from jax import lax
from jax.experimental import pallas as pl
from jax.experimental.pallas import tpu as pltpu
from jax.sharding import Mesh
from jax.sharding import PartitionSpec as P

QH = 16
KVH = 8
HD = 64
STEP = 7

EPS_NORM = 1e-05
THETA = 10000.0
BETA_ONE = 0.5
BETA_TWO = 0.6
ADAM_EPS = 1e-08
DECAY = 0.1
GAIN_RATE = 0.3
NEG_BIG = -1e30
PLANE = ("x", "y", "c")
WSH = ("y", "c")
BF = jnp.bfloat16
F32 = jnp.float32


def swap(value, axis):
    return lax.ppermute(value, axis, [(0, 1), (1, 0)])


def shift(value, by):
    count = lax.axis_size("z")
    pairs = [(i, i + by) for i in range(count) if 0 <= i + by < count]
    return lax.ppermute(value, "z", pairs)


def plane_gather(rows):
    half = rows.shape[0] // 2
    over_x = swap(rows, "x")
    over_y = swap(rows, "y")
    corner_top = swap(over_x[:half], "y")
    corner_low = swap(over_y[half:], "x")
    mine = jnp.concatenate([rows, over_x, over_y, corner_top, corner_low], axis=0)
    other = swap(mine, "c")
    return jnp.concatenate([mine, other], axis=0)


def plane_reduce(part):
    whole = part.shape[0]
    step = whole // 8
    half = step // 2
    got = swap(part[whole // 2 :], "c")
    total = part[: whole // 2].astype(F32) + got.astype(F32)
    own = total[:step]
    to_x = total[step : 2 * step]
    to_y = total[2 * step : 3 * step]
    corner = total[3 * step :].astype(BF)
    for_x = swap(corner[:half], "y").astype(F32)
    for_y = swap(corner[half:], "x").astype(F32)
    to_x = jnp.concatenate([to_x[:half] + for_x, to_x[half:]], axis=0).astype(BF)
    to_y = jnp.concatenate([to_y[:half], to_y[half:] + for_y], axis=0).astype(BF)
    return own + swap(to_x, "x").astype(F32) + swap(to_y, "y").astype(F32)


def sum_everywhere(value):
    for axis in ("c", "x", "y"):
        value = value + swap(value, axis)
    count = lax.axis_size("z")
    if count & (count - 1):
        return lax.psum(value, "z")
    stride = 1
    while stride < count:
        value = value + lax.ppermute(value, "z", [(i, i ^ stride) for i in range(count)])
        stride *= 2
    return value


def norm_scale(values):
    return lax.rsqrt(jnp.mean(values * values, axis=-1, keepdims=True) + EPS_NORM)


def norm_back(values, scale_row, gain_row, grad_out):
    gain_grad = jnp.sum(grad_out * values * scale_row, axis=0)
    weighted = grad_out * gain_row
    grad_in = scale_row * weighted - values * scale_row**3 * jnp.mean(
        values * weighted, axis=-1, keepdims=True
    )
    return (grad_in, gain_grad)


def kind_rates(width, hidden):
    base_rate = 0.5 * width ** (-0.5)
    return [
        base_rate,
        base_rate,
        base_rate,
        2.0 * (2 * hidden) ** (-0.5),
        base_rate,
        base_rate,
        3.0 * hidden ** (-0.5),
        base_rate,
    ]


def adamw(weight, first, second, grad, rate, decay):
    first_new = BETA_ONE * first + (1.0 - BETA_ONE) * grad
    second_new = BETA_TWO * second + (1.0 - BETA_TWO) * grad * grad
    first_hat = first_new / (1.0 - BETA_ONE**STEP)
    second_hat = second_new / (1.0 - BETA_TWO**STEP)
    weight_new = weight - rate * (first_hat / (jnp.sqrt(second_hat) + ADAM_EPS) + decay * weight)
    return (weight_new, first_new, second_new)


def dot_nn(left, right):
    return lax.dot_general(left, right, (((1,), (0,)), ((), ())), preferred_element_type=F32)


def dot_nt(left, right):
    return lax.dot_general(left, right, (((1,), (1,)), ((), ())), preferred_element_type=F32)


def dot_tn(left, right):
    return lax.dot_general(left, right, (((0,), (0,)), ((), ())), preferred_element_type=F32)


def turn(value, lane):
    low = (lane % HD) < (HD // 2)
    return jnp.where(
        low, -pltpu.roll(value, 2 * HD - HD // 2, 1), pltpu.roll(value, HD // 2, 1)
    )


def project_kernel(x_ref, w_ref, cos_ref, sin_ref, q_ref, kv_ref):
    both = dot_nn(x_ref[...], w_ref[...])
    cosine = cos_ref[0]
    sine = sin_ref[0]
    lane = lax.broadcasted_iota(jnp.int32, cosine.shape, 1)
    query = both[:, : 2 * HD]
    pair = both[:, 2 * HD :]
    q_ref[...] = (query * cosine + turn(query, lane) * sine).astype(BF)
    turned = pair * cosine + turn(pair, lane) * sine
    kv_ref[...] = jnp.where(lane < HD, turned, pair).astype(BF)


def project(x_rows, w_pair, cosine, sine, block):
    rows = x_rows.shape[0]
    width = w_pair.shape[0]
    table = pl.BlockSpec((1, block, 2 * HD), lambda i: (i % 2, 0, 0))
    return pl.pallas_call(
        project_kernel,
        grid=(rows // block,),
        in_specs=[
            pl.BlockSpec((block, width), lambda i: (i, 0)),
            pl.BlockSpec((width, 4 * HD), lambda i: (0, 0)),
            table,
            table,
        ],
        out_specs=[pl.BlockSpec((block, 2 * HD), lambda i: (i, 0))] * 2,
        out_shape=[jax.ShapeDtypeStruct((rows, 2 * HD), BF)] * 2,
        compiler_params=pltpu.CompilerParams(vmem_limit_bytes=32 * 2**20),
    )(x_rows, w_pair, cosine, sine)


def head_rows(rows, head, lane, high):
    if (head == 1) != high:
        rows = pltpu.roll(rows, HD, 1)
    keep = (lane >= HD) if high else (lane < HD)
    return jnp.where(keep, rows, jnp.zeros_like(rows))


def masks(info_ref, qseg_ref, kseg_ref, block, span):
    flip = info_ref[0]
    chunk = pl.program_id(1)
    key_at = lax.broadcasted_iota(jnp.int32, (span, 1), 0)
    query_at = lax.broadcasted_iota(jnp.int32, (1, block), 1)
    swapped = jnp.where(flip == 1, key_at ^ block, key_at)
    key_pos = jnp.where(key_at < 2 * block, swapped, -1)
    query_pos = query_at + block * jnp.where(flip == 1, 1 - chunk, chunk)
    return (key_pos <= query_pos) & (kseg_ref[0] == qseg_ref[0])


def attend_kernel(info_ref, q_ref, k0_ref, k1_ref, k2_ref, qseg_ref, kseg_ref, w_ref,
                  mix_ref, stat_ref, out_ref, kv_all):
    block = q_ref.shape[0]
    span = kv_all.shape[0]
    third = span // 3
    kv_all[:third] = k0_ref[...]
    kv_all[third : 2 * third] = k1_ref[...]
    kv_all[2 * third :] = k2_ref[...]
    pair = kv_all[...]
    allowed = masks(info_ref, qseg_ref, kseg_ref, block, span)
    lane = lax.broadcasted_iota(jnp.int32, (block, 2 * HD), 1)
    query = q_ref[...]
    mixed = []
    for head in range(2):
        scores = dot_nt(pair, head_rows(query, head, lane, False)) * HD ** (-0.5)
        scores = jnp.where(allowed, scores, NEG_BIG)
        top = jnp.max(scores, axis=0, keepdims=True)
        powers = jnp.exp(scores - top)
        total = jnp.sum(powers, axis=0, keepdims=True)
        stat_ref[0, 0, head : head + 1, :] = top + jnp.log(total)
        probs = (powers * (1.0 / total)).astype(BF)
        mixed.append(dot_tn(probs, pair))
    mix = jnp.where(lane < HD, pltpu.roll(mixed[0], HD, 1), mixed[1]).astype(BF)
    mix_ref[...] = mix
    out_ref[...] = dot_nt(mix, w_ref[...]).astype(BF)


def attend(info, query, kv, qseg, kseg, w_out, block):
    rows = query.shape[0]
    seqs = rows // (2 * block)
    width = w_out.shape[0]
    row_spec = pl.BlockSpec((block, 2 * HD), lambda s, i: (2 * s + i, 0))
    kv_spec = pl.BlockSpec((2 * block, 2 * HD), lambda s, i: (s, 0))
    return pl.pallas_call(
        attend_kernel,
        grid=(seqs, 2),
        in_specs=[
            pl.BlockSpec(memory_space=pltpu.SMEM),
            row_spec,
            kv_spec,
            kv_spec,
            kv_spec,
            pl.BlockSpec((1, 1, block), lambda s, i: (2 * s + i, 0, 0)),
            pl.BlockSpec((1, 6 * block, 1), lambda s, i: (s, 0, 0)),
            pl.BlockSpec((width, 2 * HD), lambda s, i: (0, 0)),
        ],
        out_specs=[
            row_spec,
            pl.BlockSpec((1, 1, 2, block), lambda s, i: (s, i, 0, 0)),
            pl.BlockSpec((block, width), lambda s, i: (2 * s + i, 0)),
        ],
        out_shape=[
            jax.ShapeDtypeStruct((rows, 2 * HD), BF),
            jax.ShapeDtypeStruct((seqs, 2, 2, block), F32),
            jax.ShapeDtypeStruct((rows, width), BF),
        ],
        scratch_shapes=[pltpu.VMEM((6 * block, 2 * HD), BF)],
        compiler_params=pltpu.CompilerParams(vmem_limit_bytes=48 * 2**20),
    )(info, query, *kv, qseg, kseg, w_out)


def attend_back_kernel(info_ref, q_ref, k0_ref, k1_ref, k2_ref, qseg_ref, kseg_ref, stat_ref,
                       dy_ref, w_ref, cos_ref, sin_ref,
                       dq_ref, dk0_ref, dk1_ref, dk2_ref, kv_all, sums):
    block = q_ref.shape[0]
    span = kv_all.shape[0]
    third = span // 3
    chunk = pl.program_id(1)

    @pl.when(chunk == 0)
    def _():
        sums[...] = jnp.zeros_like(sums)
        kv_all[:third] = k0_ref[...]
        kv_all[third : 2 * third] = k1_ref[...]
        kv_all[2 * third :] = k2_ref[...]

    pair = kv_all[...]
    allowed = masks(info_ref, qseg_ref, kseg_ref, block, span)
    lane = lax.broadcasted_iota(jnp.int32, (block, 2 * HD), 1)
    query = q_ref[...]
    grad_mix = dot_nn(dy_ref[...], w_ref[...]).astype(BF)
    grad_query = []
    for head in range(2):
        q_low = head_rows(query, head, lane, False)
        g_high = head_rows(grad_mix, head, lane, True)
        scores = dot_nt(pair, q_low) * HD ** (-0.5)
        stat = stat_ref[0, 0, head : head + 1, :]
        probs = jnp.where(allowed, jnp.exp(scores - stat), 0.0)
        grad_probs = dot_nt(pair, g_high)
        delta = jnp.sum(probs * grad_probs, axis=0, keepdims=True)
        grad_scores = (probs * (grad_probs - delta) * HD ** (-0.5)).astype(BF)
        sums[...] += dot_nn(grad_scores, q_low) + dot_nn(probs.astype(BF), g_high)
        grad_query.append(dot_tn(grad_scores, pair))
    grad_q = jnp.where(lane < HD, grad_query[0], pltpu.roll(grad_query[1], HD, 1))
    dq_ref[...] = (grad_q * cos_ref[0] - turn(grad_q * sin_ref[0], lane)).astype(BF)

    @pl.when(chunk == 1)
    def _():
        dk0_ref[...] = sums[:third]
        dk1_ref[...] = sums[third : 2 * third]
        dk2_ref[...] = sums[2 * third :].astype(BF)


def attend_back(info, query, kv, qseg, kseg, stat, grad_rows, w_out, cosine, sine, block):
    rows = query.shape[0]
    seqs = rows // (2 * block)
    width = w_out.shape[0]
    row_spec = pl.BlockSpec((block, 2 * HD), lambda s, i: (2 * s + i, 0))
    kv_spec = pl.BlockSpec((2 * block, 2 * HD), lambda s, i: (s, 0))
    table = pl.BlockSpec((1, block, 2 * HD), lambda s, i: (i, 0, 0))
    return pl.pallas_call(
        attend_back_kernel,
        grid=(seqs, 2),
        in_specs=[
            pl.BlockSpec(memory_space=pltpu.SMEM),
            row_spec,
            kv_spec,
            kv_spec,
            kv_spec,
            pl.BlockSpec((1, 1, block), lambda s, i: (2 * s + i, 0, 0)),
            pl.BlockSpec((1, 6 * block, 1), lambda s, i: (s, 0, 0)),
            pl.BlockSpec((1, 1, 2, block), lambda s, i: (s, i, 0, 0)),
            pl.BlockSpec((block, width), lambda s, i: (2 * s + i, 0)),
            pl.BlockSpec((width, 2 * HD), lambda s, i: (0, 0)),
            table,
            table,
        ],
        out_specs=[row_spec, kv_spec, kv_spec, kv_spec],
        out_shape=[
            jax.ShapeDtypeStruct((rows, 2 * HD), BF),
            jax.ShapeDtypeStruct((rows, 2 * HD), F32),
            jax.ShapeDtypeStruct((rows, 2 * HD), F32),
            jax.ShapeDtypeStruct((rows, 2 * HD), BF),
        ],
        scratch_shapes=[
            pltpu.VMEM((6 * block, 2 * HD), BF),
            pltpu.VMEM((6 * block, 2 * HD), F32),
        ],
        compiler_params=pltpu.CompilerParams(vmem_limit_bytes=56 * 2**20),
    )(info, query, *kv, qseg, kseg, stat, grad_rows, w_out, cosine, sine)


def key_back_kernel(a_ref, b_ref, cos_ref, sin_ref, out_ref):
    grad = a_ref[...] + b_ref[...].astype(F32)
    lane = lax.broadcasted_iota(jnp.int32, grad.shape, 1)
    turned = grad * cos_ref[0] - turn(grad * sin_ref[0], lane)
    out_ref[...] = jnp.where(lane < HD, turned, grad).astype(BF)


def key_back(here, arrived, cosine, sine, block):
    rows = here.shape[0]
    spec = pl.BlockSpec((block, 2 * HD), lambda i: (i, 0))
    table = pl.BlockSpec((1, block, 2 * HD), lambda i: (i % 2, 0, 0))
    return pl.pallas_call(
        key_back_kernel,
        grid=(rows // block,),
        in_specs=[spec, spec, table, table],
        out_specs=spec,
        out_shape=jax.ShapeDtypeStruct((rows, 2 * HD), BF),
    )(here, arrived, cosine, sine)


def shards(
    tokens,
    segments,
    routes,
    gate_weights,
    cotangent,
    owners,
    masters,
    first_moments,
    second_moments,
    norm_gains,
    gain_first,
    gain_second,
):
    z_index = lax.axis_index("z")
    x_index = lax.axis_index("x")
    w_index = lax.axis_index("y") * 2 + lax.axis_index("c")
    slot_count, row_count, hidden = masters.shape
    slot_total = slot_count * 4
    seg_len = tokens.shape[1]
    width = tokens.shape[2]
    matrix_count = owners.shape[0]
    experts = (matrix_count - 6) // 3
    group = experts // 2
    part = hidden // 4
    x_even = x_index == 0

    slot_ids = jnp.arange(slot_total, dtype=jnp.int32)
    hits = owners[None, :] == slot_ids[:, None]
    held = jnp.sum(hits * (jnp.arange(matrix_count, dtype=jnp.int32) + 1)[None, :], axis=1) - 1

    masters_low = masters.astype(BF)
    local_at = owners[:6] - slot_count * w_index
    local_ok = (local_at >= 0) & (local_at < slot_count)
    attn_mats = jnp.where(
        local_ok[:, None, None],
        jnp.take(masters_low, jnp.clip(local_at, 0, slot_count - 1), axis=0),
        jnp.zeros((), BF),
    )

    def by_head(mat, lanes):
        return jnp.transpose(mat.reshape(row_count, -1, lanes), (1, 0, 2))

    q_parts = jnp.concatenate([by_head(attn_mats[0], part), by_head(attn_mats[1], part)], axis=0)
    o_parts = jnp.concatenate([by_head(attn_mats[4], part), by_head(attn_mats[5], part)], axis=0)
    kv_parts = jnp.concatenate([by_head(attn_mats[2], HD), by_head(attn_mats[3], HD)], axis=2)
    attn_send = jnp.stack([q_parts, kv_parts, o_parts], axis=1)
    attn_got = lax.all_to_all(attn_send, PLANE, split_axis=0, concat_axis=0, tiled=True)
    attn_mine = jnp.sum(attn_got.reshape(2, 4, 3, row_count, part).astype(F32), axis=1).astype(BF)
    attn_mine = jnp.transpose(attn_mine, (0, 2, 1, 3)).reshape(2 * row_count, 3 * part)
    attn_w = lax.all_gather(attn_mine, "z", axis=0, tiled=True)
    w_pair = attn_w[:, : 2 * part]
    w_out = attn_w[:, 2 * part :]

    tokens_f = tokens[0].astype(F32)
    scale_one = norm_scale(tokens_f)
    attn_in = (tokens_f * scale_one * norm_gains[0]).astype(BF)
    expert_ids = jnp.arange(experts, dtype=jnp.int32)
    gates = jnp.sum(
        jnp.where(routes[0][:, :, None] == expert_ids[None, None, :], gate_weights[0][:, :, None], 0.0),
        axis=1,
    )
    gates_high = gates.astype(BF)
    gates_low = (gates - gates_high.astype(F32)).astype(BF)
    marks = (segments[0] + 1).astype(BF)[:, None]
    spare = jnp.zeros((seg_len, 128 - 2 * experts - 1), BF)
    packed = jnp.concatenate([attn_in, gates_high, gates_low, marks, spare], axis=1)
    packed_all = plane_gather(packed)
    x_all = packed_all[:, :width]
    gates_all = packed_all[:, width : width + experts].astype(F32) + packed_all[
        :, width + experts : width + 2 * experts
    ].astype(F32)
    my_gates = jnp.where(x_even, gates_all[:, :group], gates_all[:, group:])
    marks_all = packed_all[:, width + 2 * experts].astype(F32).reshape(-1, 128)
    marks_one = shift(marks_all, 1)
    marks_two = shift(marks_one, 1)
    seqs = 4
    qseg = marks_all.reshape(2 * seqs, 1, seg_len)
    kseg = jnp.concatenate(
        [m.reshape(seqs, 2 * seg_len) for m in (marks_all, marks_one, marks_two)], axis=1
    )[:, :, None]
    g_all = plane_gather(cotangent[0])

    bulk_send = jnp.transpose(masters_low.reshape(slot_count, row_count, 4, part), (2, 0, 1, 3))
    bulk_got = lax.all_to_all(bulk_send, WSH, split_axis=0, concat_axis=0, tiled=True).reshape(
        slot_total, row_count, part
    )
    order = np.array([[6 + 3 * (group * g + e) + k for k in range(3) for e in range(group)] for g in range(2)])
    picks = jnp.take(owners, jnp.asarray(order))
    picks_mine = jnp.where(x_even, picks[0], picks[1])
    picks_other = jnp.where(x_even, picks[1], picks[0])

    def pick(which):
        return jnp.transpose(jnp.take(bulk_got, which, axis=0), (1, 0, 2)).reshape(row_count, -1)

    rows_mine = pick(picks_mine)
    rows_got = swap(pick(picks_other), "x")
    pair_rows = jnp.where(
        x_even,
        jnp.concatenate([rows_mine, rows_got], axis=0),
        jnp.concatenate([rows_got, rows_mine], axis=0),
    )
    expert_w = lax.all_gather(pair_rows, "z", axis=0, tiled=True)
    cols = group * part
    w_gate = expert_w[:, :cols]
    w_up = expert_w[:, cols : 2 * cols]
    w_down = expert_w[:, 2 * cols :]

    inverse = THETA ** (-(jnp.arange(HD // 2, dtype=F32) * 2.0 / HD))
    at = jnp.arange(seg_len, dtype=jnp.int32)
    first_pos = z_index * 2 * seg_len + x_index * seg_len + at
    second_pos = z_index * 2 * seg_len + (1 - x_index) * seg_len + at
    positions = jnp.stack([first_pos, second_pos])
    angles = positions.astype(F32)[:, :, None] * inverse[None, None, :]
    cosine = jnp.tile(jnp.cos(angles), (1, 1, 4))
    sine = jnp.tile(jnp.sin(angles), (1, 1, 4))
    info = x_index.reshape(1).astype(jnp.int32)

    query, kv_zero = project(packed_all, w_pair, cosine, sine, seg_len)
    kv_one = shift(kv_zero, 1)
    kv_two = shift(kv_one, 1)
    kv = (kv_zero, kv_one, kv_two)
    attn_mix, stat, out_part = attend(info, query, kv, qseg, kseg, w_out, seg_len)
    resid_one = tokens_f + plane_reduce(out_part)
    scale_two = norm_scale(resid_one)
    expert_in = (resid_one * scale_two * norm_gains[1]).astype(BF)
    e_all = plane_gather(expert_in)

    gate_wide = jnp.broadcast_to(my_gates[:, :, None], (my_gates.shape[0], group, part)).reshape(
        -1, cols
    )
    gate_pre = dot_nn(e_all, w_gate)
    up_pre = dot_nn(e_all, w_up)
    logistic = jax.nn.sigmoid(gate_pre)
    active = gate_pre * logistic
    hidden_low = (active * up_pre * gate_wide).astype(BF)
    grad_hidden = dot_nn(g_all, w_down) * gate_wide
    grad_gate_low = (grad_hidden * up_pre * logistic * (1.0 + gate_pre * (1.0 - logistic))).astype(BF)
    grad_up_low = (grad_hidden * active).astype(BF)
    grad_in_part = (dot_nt(grad_gate_low, w_gate) + dot_nt(grad_up_low, w_up)).astype(BF)
    expert_grads = jnp.concatenate(
        [
            dot_tn(e_all, grad_gate_low).astype(BF),
            dot_tn(e_all, grad_up_low).astype(BF),
            dot_tn(g_all, hidden_low).astype(BF),
        ],
        axis=1,
    )
    expert_sum = lax.psum_scatter(expert_grads, "z", scatter_dimension=0, tiled=True)
    out_moe = dot_nt(hidden_low, w_down).astype(BF)
    grad_expert_in = plane_reduce(grad_in_part)
    resid_two = resid_one + plane_reduce(out_moe)
    output = resid_two.astype(BF)

    cot_rows = cotangent[0].astype(F32)
    norm_grad_two, gain_grad_two = norm_back(resid_one, scale_two, norm_gains[1], grad_expert_in)
    grad_resid = cot_rows + norm_grad_two
    dy_all = plane_gather(grad_resid.astype(BF))
    grad_w_out = dot_tn(dy_all, attn_mix)
    grad_q_low, dkv_zero, dkv_one, dkv_two = attend_back(
        info, query, kv, qseg, kseg, stat, dy_all, w_out, cosine, sine, seg_len
    )
    passed = shift(dkv_two, -1)
    passed = shift((dkv_one + passed.astype(F32)).astype(BF), -1)
    grad_kv_low = key_back(dkv_zero, passed, cosine, sine, seg_len)
    grad_both = jnp.concatenate([grad_q_low, grad_kv_low], axis=1)
    grad_w_pair = dot_tn(x_all, grad_both)
    grad_in_one = plane_reduce(dot_nt(grad_both, w_pair).astype(BF))
    norm_grad_one, gain_grad_one = norm_back(tokens_f, scale_one, norm_gains[0], grad_in_one)
    input_grad = grad_resid + norm_grad_one

    attn_grads = jnp.concatenate([grad_w_pair.astype(BF), grad_w_out.astype(BF)], axis=1)
    attn_sum = lax.psum_scatter(attn_grads, "z", scatter_dimension=0, tiled=True)
    attn_rows = jnp.broadcast_to(
        attn_sum.reshape(2, 1, row_count, 3 * part), (2, 4, row_count, 3 * part)
    ).reshape(8, row_count, 3 * part)
    attn_back = lax.all_to_all(attn_rows, PLANE, split_axis=0, concat_axis=0, tiled=True)
    q_back = jnp.transpose(attn_back[:, :, :part].reshape(2, 4, row_count, part), (0, 2, 1, 3)).reshape(2, row_count, hidden)
    o_back = jnp.transpose(attn_back[:, :, 2 * part :].reshape(2, 4, row_count, part), (0, 2, 1, 3)).reshape(2, row_count, hidden)
    k_back = jnp.transpose(attn_back[:, :, part : part + HD], (1, 0, 2)).reshape(1, row_count, hidden)
    v_back = jnp.transpose(attn_back[:, :, part + HD : 2 * part], (1, 0, 2)).reshape(1, row_count, hidden)
    attn_six = jnp.concatenate([q_back, k_back, v_back, o_back], axis=0)

    keep = lax.dynamic_slice_in_dim(expert_sum, x_index * row_count, row_count, axis=0)
    give = lax.dynamic_slice_in_dim(expert_sum, (1 - x_index) * row_count, row_count, axis=0)
    came = swap(give, "x")
    both_groups = jnp.stack([keep, came]).reshape(2, row_count, 3 * group, part)
    both_groups = jnp.transpose(both_groups, (0, 2, 1, 3)).reshape(6 * group, row_count, part)
    expert_of = (held - 6) // 3
    kind_of = (held - 6) % 3
    side = (expert_of // group) ^ x_index
    place = side * 3 * group + kind_of * group + expert_of % group
    is_expert = held >= 6
    slot_send = jnp.where(
        is_expert[:, None, None],
        jnp.take(both_groups, jnp.clip(place, 0, 6 * group - 1), axis=0),
        jnp.zeros((), BF),
    )
    slot_got = lax.all_to_all(slot_send, WSH, split_axis=0, concat_axis=0, tiled=True)
    expert_slot = jnp.transpose(
        slot_got.reshape(4, slot_count, row_count, part), (1, 2, 0, 3)
    ).reshape(slot_count, row_count, hidden)
    held_mine = lax.dynamic_slice_in_dim(held, w_index * slot_count, slot_count)
    attn_slot = jnp.take(attn_six, jnp.clip(held_mine, 0, 5), axis=0)
    is_attn = (held_mine >= 0) & (held_mine < 6)
    slot_grad = jnp.where(is_attn[:, None, None], attn_slot, expert_slot).astype(F32)
    table = jnp.asarray(np.array([7, 0, 0, 1, 2, 3, 3] + [4, 5, 6] * experts, np.int32))
    rates = jnp.take(jnp.asarray(kind_rates(width, hidden), F32), jnp.take(table, held_mine + 1))
    new_masters, new_first, new_second = adamw(
        masters, first_moments, second_moments, slot_grad, rates[:, None, None], DECAY
    )
    gain_grad = sum_everywhere(jnp.stack([gain_grad_one, gain_grad_two]))
    new_gains, new_gain_first, new_gain_second = adamw(
        norm_gains, gain_first, gain_second, gain_grad, GAIN_RATE, 0.0
    )
    return (
        output[None],
        input_grad[None],
        new_masters,
        new_first,
        new_second,
        new_gains,
        new_gain_first,
        new_gain_second,
    )


def solution(mesh):
    ctx, wsh = mesh.devices.shape
    fine = Mesh(mesh.devices.reshape(ctx // 2, 2, wsh // 2, 2), ("z", "x", "y", "c"))
    rows = P(WSH, ("z", "x"), None)
    marks = P(WSH, ("z", "x"))
    return jax.shard_map(
        shards,
        mesh=fine,
        in_specs=(rows, marks, rows, rows, rows, P(), rows, rows, rows, P(), P(), P()),
        out_specs=(rows, rows, rows, rows, rows, P(), P(), P()),
        check_vma=False,
    )
```

time: 1760 us -> 728 us (0.41)
  waiting for transfers between devices: 1180 us -> 238 us
  local copies, waits for them, and re-layouts: 195 us -> 82 us
  Pallas kernels: 0 us -> 71.7 us
  matrix products: 144 us -> 94.2 us
  starting transfers between devices: 84.4 us -> 113 us
  blocking collectives: 38.8 us -> 19.9 us
    reduce_scatter x2, waiting for transfers between devices: 651 us -> 0.67 us  [the longest x1 0.67 us: shards(): lax.psum_scatter(attn_grads, 'z', scatter_dimension=0, tiled=True)]
    all_gather x2 -> x1, waiting for transfers between devices: 386 us -> 0.01 us  [shards(): expert_w = lax.all_gather(pair_rows, 'z', axis=0, tiled=True)]
    ppermute x20 -> x53, waiting for transfers between devices: 46.9 us -> 235 us  [the longest x45 156 us: swap(): return lax.ppermute(value, axis, [(0, 1), (1, 0)])]
    all_to_all x4, waiting for transfers between devices: 97.6 us -> 2.25 us  [the longest x1 2.24 us: shards(): lax.all_to_all(attn_send, PLANE, split_axis=0, concat_axis=0, tiled=True)]
    pallas_call x0 -> x4, Pallas kernels: none -> 71.7 us  [the longest x1 31.5 us: attend_back(): pl.pallas_call(attend_back_kernel, grid=(seqs, 2), in_specs=[pl.BlockSpec...]
    dot_general x56 -> x12, matrix products: 144 us -> 94.2 us  [the longest x3 39.7 us: dot_nn(): lax.dot_general(left, right, (((1,), (0,)), ((), ())), preferred_element_...]
    scatter x3 -> x0, local copies, waits for them, and re-layouts: 40.3 us -> none  [the longest x1 28.6 us: pack(): return empty.at[slot_ids].set(rows_in).reshape(experts_all, CAP, width)]
    psum x1 -> x0, blocking collectives: 38.8 us -> none  [shards(): lax.psum(jnp.stack([gain_grad_one, gain_grad_two]), ('ctx', 'wsh'))]
  transfers between devices with their start and end apart: 28 -> 60, of which waited for: 17 -> 36; matrix products, arithmetic and copies ran while one was open for 13% -> 24% of each run, Pallas kernels for 0% -> 10%
where the time goes in v1:
time: 728 us; the launch traced here: 717 us
  waiting for transfers between devices  238 us (33%)
  starting transfers between devices  113 us (16%)
  matrix products  94.2 us (13%)
  other arithmetic  82.4 us (11%)
  local copies, waits for them, and re-layouts  82 us (11%)
  Pallas kernels  71.7 us (10%)
  blocking collectives  19.9 us (3%)
  between operations  15.6 us (2%)
    ppermute x45, waiting for transfers between devices, swap(): return lax.ppermute(value, axis, [(0, 1), (1, 0)])  156 us
    ppermute x6, waiting for transfers between devices, shift(): return lax.ppermute(value, 'z', pairs)  77 us
    ppermute x6, starting transfers between devices, shift(): return lax.ppermute(value, 'z', pairs)  45.5 us
    ppermute x45, starting transfers between devices, swap(): return lax.ppermute(value, axis, [(0, 1), (1, 0)])  45.2 us
    dot_general x3, matrix products, dot_nn(): lax.dot_general(left, right, (((1,), (0,)), ((), ())), preferred_element_...  39.7 us
    pallas_call x1, Pallas kernels, attend_back(): pl.pallas_call(attend_back_kernel, grid=(seqs, 2), in_specs=[pl.BlockSpec...  31.5 us
    dot_general x5, matrix products, dot_tn(): lax.dot_general(left, right, (((0,), (0,)), ((), ())), preferred_element_...  29.6 us
    pallas_call x1, Pallas kernels, attend(): pl.pallas_call(attend_kernel, grid=(seqs, 2), in_specs=[pl.BlockSpec(memo...  27.4 us
  transfers between devices with their start and end apart: 60, of which 36 were waited for; matrix products, arithmetic and copies ran while one was open for 24% of the time, Pallas kernels for 10%

profile of v1, /device:TPU:0, one launch (start us, length us, event | category | flops | bytes accessed | tf_op | source)
XLA Modules:
  0.0 717.4 jit_solution(12086028499726674417)
XLA Ops:
  14.0 2.9 collective-permute-start
  18.4 2.9 convert_element_type.221
  21.3 2.6 copy.167
  23.9 3.6 copy.168
  27.4 4.5 all-to-all-start.1
  45.9 23.7 %collective-permute-done.2 = bf16[128,1152]{1,0:T(8,128)(2,1)S(1)} collective-permute-done((bf16[128,1152]{1,0:T(8,128)(2,1)S(1)}, bf16[128,1152]{1,0:T(8,128)(2,1)S(1)}, u32[]{:S(2)}, u32[]{:S(2)}) %collective-permute-start.2) | collective-permute-done | bytes 294944 | tf_op jit(solution)/shard_map/ppermute | solution.py:30
  72.2 4.2 all-to-all-start
  76.5 3.2 copy.169
  90.0 19.9 %all_gather.6 = bf16[1024,384]{1,0:T(8,128)(2,1)S(1)} all-gather(bf16[256,384]{1,0:T(8,128)(2,1)S(1)} %bitcast.173), channel_id=1, replica_groups=mesh['z'=4,'x'=2,'y'=2,'c'=2] {'z'}, dimensions={0}, use_global_device_ids=true | all-gather | bytes 983040 | tf_op jit(solution)/shard_map/all_gather | solution.py:396
  110.0 2.7 gather_fusion.6
  115.2 3.0 maximum_select_fusion
  118.3 3.3 constant_dynamic-update-slice_fusion.5.x_ref
  121.5 6.7 shard_map.206
  128.3 2.4 collective-permute-start.5
  130.7 21.2 %collective-permute-done.5.k1_ref = bf16[2048,128]{1,0:T(8,128)(2,1)} collective-permute-done((bf16[2048,128]{1,0:T(8,128)(2,1)S(1)}, bf16[2048,128]{1,0:T(8,128)(2,1)}, u32[]{:S(2)}, u32[]{:S(2)}) %collective-permute-start.5) | collective-permute-done | bytes 524320 | tf_op jit(solution)/shard_map/ppermute | solution.py:36
  151.9 18.3 %collective-permute-start.6 = (bf16[2048,128]{1,0:T(8,128)(2,1)}, bf16[2048,128]{1,0:T(8,128)(2,1)}, u32[]{:S(2)}, u32[]{:S(2)}) collective-permute-start(bf16[2048,128]{1,0:T(8,128)(2,1)} %collective-permute-done.5.k1_ref), channel_id=1, source_target_pairs={{0,8},{8,16},{16,24},{1,9},{9,17},{17,25},{2,10},{10,18},{18,26},{... | collective-permute-start | bytes 1572872 | tf_op jit(solution)/shard_map/ppermute | solution.py:36
  171.6 3.7 collective-permute-start.7
  175.3 16.6 %collective-permute-done.7 = f32[16,128]{1,0:T(8,128)S(1)} collective-permute-done((f32[16,128]{1,0:T(8,128)S(1)}, f32[16,128]{1,0:T(8,128)S(1)}, u32[]{:S(2)}, u32[]{:S(2)}) %collective-permute-start.7) | collective-permute-done | bytes 8224 | tf_op jit(solution)/shard_map/ppermute | solution.py:36
  191.9 18.3 %collective-permute-start.8 = (f32[16,128]{1,0:T(8,128)S(1)}, f32[16,128]{1,0:T(8,128)S(1)}, u32[]{:S(2)}, u32[]{:S(2)}) collective-permute-start(f32[16,128]{1,0:T(8,128)S(1)} %collective-permute-done.7), channel_id=1, source_target_pairs={{0,8},{8,16},{16,24},{1,9},{9,17},{17,25},{2,10},{10,18},{18,26},{... | collective-permute-start | bytes 24584 | tf_op jit(solution)/shard_map/ppermute | solution.py:36
  215.2 27.4 %shard_map.207 = (bf16[2048,128]{1,0:T(8,128)(2,1)S(1)}, f32[4,2,2,256]{3,2,1,0:T(2,128)S(1)}, bf16[2048,1024]{1,0:T(8,128)(2,1)}) custom-call(s32[1]{0:T(128)} %bitcast.1.info_ref, bf16[2048,128]{1,0:T(8,128)(2,1)S(1)} %copy-done.5, bf16[2048,128]{1,0:T(8,128)(2,1)S(1)} %copy-done.7, bf16[2048,128]{1,0:T(8,128)(2,1)} %collective-permute-done.5.k1_ref, ...), custom_call_target="tpu_custom_call" | custom-call | tf_op jit(solution)/shard_map/pallas_call | solution.py:217
  246.0 2.9 collective-permute-done.9
  251.2 8.3 %collective-permute-done.25 = bf16[256,1024]{1,0:T(8,128)(2,1)S(1)} collective-permute-done((bf16[256,1024]{1,0:T(8,128)(2,1)S(1)}, bf16[256,1024]{1,0:T(8,128)(2,1)S(1)}, u32[]{:S(2)}, u32[]{:S(2)}) %collective-permute-start.25) | collective-permute-done | bytes 524320 | tf_op jit(solution)/shard_map/ppermute | solution.py:30
  261.7 3.6 collective-permute-done.10
  271.1 10.5 %collective-permute-done.11 = bf16[256,1024]{1,0:T(8,128)(2,1)S(1)} collective-permute-done((bf16[256,1024]{1,0:T(8,128)(2,1)S(1)}, bf16[256,1024]{1,0:T(8,128)(2,1)S(1)}, u32[]{:S(2)}, u32[]{:S(2)}) %collective-permute-start.11) | collective-permute-done | bytes 524320 | tf_op jit(solution)/shard_map/ppermute | solution.py:30
  285.8 9.9 %collective-permute-done.14 = bf16[256,1024]{1,0:T(8,128)(2,1)S(1)} collective-permute-done((bf16[256,1024]{1,0:T(8,128)(2,1)S(1)}, bf16[256,1024]{1,0:T(8,128)(2,1)S(1)}, u32[]{:S(2)}, u32[]{:S(2)}) %collective-permute-start.14) | collective-permute-done | bytes 524320 | tf_op jit(solution)/shard_map/ppermute | solution.py:30
  300.2 2.5 collective-permute-done.16
  310.0 10.8 %fusion.9 = f32[2048,1024]{1,0:T(8,128)} fusion(bf16[2048,1024]{1,0:T(8,128)(2,1)} %constant_dynamic-update-slice_fusion.16, bf16[1024,3072]{0,1:T(8,128)(2,1)} %all-gather.2.cloned.1.call-done), kind=kOutput, calls=%fused_computation.44 | convolution fusion | flops 4294967296 | bytes 14680064 | tf_op jit(solution)/shard_map/dot_general | solution.py:117
  320.7 11.0 %fusion.13 = f32[2048,1024]{1,0:T(8,128)} fusion(bf16[2048,1024]{1,0:T(8,128)(2,1)} %constant_dynamic-update-slice_fusion.16, bf16[1024,3072]{0,1:T(8,128)(2,1)} %all-gather.2.cloned.1.call-done), kind=kOutput, calls=%fused_computation.48 | convolution fusion | flops 4294967296 | bytes 14680064 | tf_op jit(solution)/shard_map/dot_general | solution.py:117
  331.8 6.3 broadcast_in_dim.155
  338.1 17.9 %multiply_convert_fusion = (bf16[2048,1024]{1,0:T(8,128)(2,1)}, bf16[2048,1024]{1,0:T(8,128)(2,1)}, bf16[2048,1024]{1,0:T(8,128)(2,1)}) fusion(f32[2048,1024]{1,0:T(8,128)} %fusion.13, f32[2048,1024]{1,0:T(8,128)} %fusion.9, f32[256,8,8,128]{3,2,1,0:T(8,128)} %bitcast.160, bf16[2048,1024]{1,0:T(8,128)(2,1)} %copy-done.32, ...), kind=kOutput, calls=%fused_computation.12 | convolution fusion | flops 4330618880 | bytes 44040192 | tf_op jit(solution)/shard_map/dot_general | solution.py:117
  356.0 7.4 %convolution_convert_fusion.1 = bf16[2048,1024]{1,0:T(8,128)(2,1)S(1)} fusion(bf16[2048,1024]{1,0:T(8,128)(2,1)} %get-tuple-element.54, bf16[1024,3072]{0,1:T(8,128)(2,1)} %all-gather.2.cloned.1.call-done), kind=kOutput, calls=%fused_computation.28 | convolution fusion | flops 4297064448 | bytes 10485760 | tf_op jit(solution)/shard_map/dot_general | solution.py:121
  368.5 7.6 %convolution_convert_fusion.4 = bf16[1024,1024]{0,1:T(8,128)(2,1)S(1)} fusion(bf16[2048,1024]{1,0:T(8,128)(2,1)} %constant_dynamic-update-slice_fusion.16, bf16[2048,1024]{1,0:T(8,128)(2,1)S(1)} %copy-done.43), kind=kOutput, calls=%fused_computation.40 | convolution fusion | flops 4296015872 | bytes 10485760 | tf_op jit(solution)/shard_map/dot_general | solution.py:125
  376.0 7.1 convolution_convert_fusion.3
  383.2 6.8 fusion.11
  390.0 8.3 %add_convert_fusion = bf16[2048,1024]{1,0:T(8,128)(2,1)S(1)} fusion(f32[2048,1024]{1,0:T(8,128)} %fusion.11, bf16[2048,1024]{1,0:T(8,128)(2,1)} %get-tuple-element.52, bf16[1024,3072]{0,1:T(8,128)(2,1)S(1)} %bitcast.197), kind=kOutput, calls=%fused_computation.11 | convolution fusion | flops 4299161600 | bytes 18874368 | tf_op jit(solution)/shard_map/dot_general | solution.py:121
  398.4 8.5 %convolution_convert_fusion.2 = bf16[1024,1024]{0,1:T(8,128)(2,1)S(1)} fusion(bf16[2048,1024]{1,0:T(8,128)(2,1)S(1)} %copy-done.33, bf16[2048,1024]{1,0:T(8,128)(2,1)} %get-tuple-element.54), kind=kOutput, calls=%fused_computation.38 | convolution fusion | flops 4296015872 | bytes 10485760 | tf_op jit(solution)/shard_map/dot_general | solution.py:125
  408.5 13.4 %pad_maximum_fusion = bf16[1024,3072]{0,1:T(8,128)(2,1)} fusion(bf16[1024,1024]{0,1:T(8,128)(2,1)S(1)} %convolution_convert_fusion.2, bf16[1024,1024]{0,1:T(8,128)(2,1)S(1)} %convolution_convert_fusion.3, bf16[1024,1024]{0,1:T(8,128)(2,1)S(1)} %convolution_convert_fusion.4), kind=kLoop, calls=%fused_computation.18 | loop fusion | flops 18874368 | bytes 12582912 | tf_op jit(solution)/shard_map/concatenate | solution.py:486
  422.0 3.5 fusion.57
  427.8 2.6 fusion.58
  444.0 8.6 %collective-permute-done.22 = bf16[256,1024]{1,0:T(8,128)(2,1)S(1)} collective-permute-done((bf16[256,1024]{1,0:T(8,128)(2,1)S(1)}, bf16[256,1024]{1,0:T(8,128)(2,1)S(1)}, u32[]{:S(2)}, u32[]{:S(2)}) %collective-permute-start.22) | collective-permute-done | bytes 524320 | tf_op jit(solution)/shard_map/ppermute | solution.py:30
  452.6 10.4 %collective-permute-done.32 = bf16[256,1024]{1,0:T(8,128)(2,1)S(1)} collective-permute-done((bf16[256,1024]{1,0:T(8,128)(2,1)S(1)}, bf16[256,1024]{1,0:T(8,128)(2,1)S(1)}, u32[]{:S(2)}, u32[]{:S(2)}) %collective-permute-start.32) | collective-permute-done | bytes 524320 | tf_op jit(solution)/shard_map/ppermute | solution.py:30
  467.1 11.0 %collective-permute-done.35 = bf16[256,1024]{1,0:T(8,128)(2,1)S(1)} collective-permute-done((bf16[256,1024]{1,0:T(8,128)(2,1)S(1)}, bf16[256,1024]{1,0:T(8,128)(2,1)S(1)}, u32[]{:S(2)}, u32[]{:S(2)}) %collective-permute-start.35) | collective-permute-done | bytes 524320 | tf_op jit(solution)/shard_map/ppermute | solution.py:30
  480.6 4.3 collective-permute-done.37
  485.9 4.1 collective-permute-done.39
  492.3 31.5 %shard_map.208 = (bf16[2048,128]{1,0:T(8,128)(2,1)}, f32[2048,128]{1,0:T(8,128)}, f32[2048,128]{1,0:T(8,128)}, bf16[2048,128]{1,0:T(8,128)(2,1)}) custom-call(s32[1]{0:T(128)} %bitcast.1.info_ref, bf16[2048,128]{1,0:T(8,128)(2,1)} %copy-done.4, bf16[2048,128]{1,0:T(8,128)(2,1)} %copy-done.6, bf16[2048,128]{1,0:T(8,128)(2,1)} %collective-permute-done.5.k1_ref, ...), custom_call_target="tpu_custom_call" | custom-call | tf_op jit(solution)/shard_map/pallas_call | solution.py:294
  525.2 23.4 %collective-permute-done.40 = bf16[2048,128]{1,0:T(8,128)(2,1)S(1)} collective-permute-done((bf16[2048,128]{1,0:T(8,128)(2,1)}, bf16[2048,128]{1,0:T(8,128)(2,1)S(1)}, u32[]{:S(2)}, u32[]{:S(2)}) %collective-permute-start.40) | collective-permute-done | bytes 524320 | tf_op jit(solution)/shard_map/ppermute | solution.py:36
  552.1 14.6 %collective-permute-done.41.b_ref = bf16[2048,128]{1,0:T(8,128)(2,1)} collective-permute-done((bf16[2048,128]{1,0:T(8,128)(2,1)}, bf16[2048,128]{1,0:T(8,128)(2,1)}, u32[]{:S(2)}, u32[]{:S(2)}) %collective-permute-start.41) | collective-permute-done | bytes 524320 | tf_op jit(solution)/shard_map/ppermute | solution.py:36
  566.7 6.2 shard_map.209
  579.8 3.0 convolution_convert_fusion.5
  582.8 3.5 fusion.15
  587.3 5.3 fusion.59
  596.4 5.0 collective-permute-done.43
  613.3 4.5 all-to-all-start.2
  622.3 14.6 %collective-permute-done.47 = bf16[128,3072]{0,1:T(8,128)(2,1)} collective-permute-done((bf16[128,3072]{0,1:T(8,128)(2,1)}, bf16[128,3072]{0,1:T(8,128)(2,1)}, u32[]{:S(2)}, u32[]{:S(2)}) %collective-permute-start.47) | collective-permute-done | bytes 786464 | tf_op jit(solution)/shard_map/ppermute | solution.py:30
  636.9 2.4 maximum_bitcast_fusion
  641.3 2.5 gather_fusion.5
  643.8 3.6 select_select_fusion
  647.4 4.5 all-to-all-start.3
  659.7 2.4 gather_fusion.4
  662.1 21.4 %collective-permute-done.50 = f32[2,1024]{1,0:T(2,128)S(1)} collective-permute-done((f32[2,1024]{1,0:T(2,128)S(1)}, f32[2,1024]{1,0:T(2,128)S(1)}, u32[]{:S(2)}, u32[]{:S(2)}) %collective-permute-start.50) | collective-permute-done | bytes 8224 | tf_op jit(solution)/shard_map/ppermute | solution.py:30
  687.1 2.9 collective-permute-start.52
  690.0 2.9 fusion.24
  693.6 8.2 %fusion.5 = (f32[20,128,512]{2,1,0:T(8,128)}, bf16[20,128,512]{2,1,0:T(8,128)(2,1)S(1)}) fusion(f32[20,128,512]{2,1,0:T(8,128)} %param.24, bf16[4,20,16,8,128]{4,3,2,1,0:T(8,128)(2,1)} %bitcast.80, bf16[20,128,512]{2,1,0:T(8,128)(2,1)} %gather_fusion.4, pred[20]{0:T(512)(128)(4,1)S(1)} %get-tuple-element.37, pred[20]{0:T(512)(128)(4,1)S(1)} %get-tuple-element.145), kind=kLoop, calls=%fused_computation.29 | loop fusion | flops 6553600 | bytes 18350120 | tf_op jit(solution)/shard_map/add | solution.py:108
  701.8 8.6 %multiply_subtract_fusion = (f32[20,128,512]{2,1,0:T(8,128)}, f32[20,128,512]{2,1,0:T(8,128)}) fusion(f32[20,128,512]{2,1,0:T(8,128)} %param.23, f32[20,128,512]{2,1,0:T(8,128)S(1)} %bitcast.157, bf16[20,128,512]{2,1,0:T(8,128)(2,1)S(1)} %get-tuple-element.34, f32[20]{0:T(128)S(1)} %and_select_fusion.7, f32[20,128,512]{2,1,0:T(8,128)} %param.25), kind=kLoop, calls=%fused_computation.20 | loop fusion | flops 18350080 | bytes 28835920 | tf_op jit(solution)/shard_map/sub | solution.py:112
  (348 shorter events, 152.4 us)
Async XLA Ops:
  14.0 23.0 %collective-permute-start = (bf16[256,1152]{1,0:T(8,128)(2,1)}, bf16[256,1152]{1,0:T(8,128)(2,1)}, u32[]{:S(2)}, u32[]{:S(2)}) collective-permute-start(bf16[256,1152]{1,0:T(8,128)(2,1)} %concatenate.98), channel_id=1, source_target_pairs={{0,4},{4,0},{1,5},{5,1},{2,6},{6,2},{3,7},{7,3},{8,12},{12,8},{9,1... | collective-permute-start | bytes 1769480 | tf_op jit(solution)/shard_map/ppermute | solution.py:30
  16.9 23.1 %collective-permute-start.1 = (bf16[256,1152]{1,0:T(8,128)(2,1)}, bf16[256,1152]{1,0:T(8,128)(2,1)}, u32[]{:S(2)}, u32[]{:S(2)}) collective-permute-start(bf16[256,1152]{1,0:T(8,128)(2,1)} %concatenate.98), channel_id=1, source_target_pairs={{0,2},{2,0},{1,3},{3,1},{4,6},{6,4},{5,7},{7,5},{8,10},{10,8},{9,1... | collective-permute-start | bytes 1769480 | tf_op jit(solution)/shard_map/ppermute | solution.py:30
  27.4 44.7 %all-to-all-start.1 = ((bf16[4,20,128,128]{2,3,1,0:T(8,128)(2,1)}), bf16[4,20,128,128]{2,3,1,0:T(8,128)(2,1)}, u32[]{:S(2)}, u32[]{:S(2)}) async-start(bf16[4,20,128,128]{2,3,1,0:T(8,128)(2,1)} %copy.168), calls=%async_computation.1 | async-start | bytes 5242880 | tf_op jit(solution)/shard_map/all_to_all | solution.py:430
  38.0 31.6 %collective-permute-start.2 = (bf16[128,1152]{1,0:T(8,128)(2,1)S(1)}, bf16[128,1152]{1,0:T(8,128)(2,1)S(1)}, u32[]{:S(2)}, u32[]{:S(2)}) collective-permute-start(bf16[128,1152]{1,0:T(8,128)(2,1)S(1)} %slice.350), channel_id=1, source_target_pairs={{0,2},{2,0},{1,3},{3,1},{4,6},{6,4},{5,7},{7,5},{8,10},{10,8},{9,1... | collective-permute-start | bytes 884744 | tf_op jit(solution)/shard_map/ppermute | solution.py:30
  41.0 29.5 %collective-permute-start.3 = (bf16[128,1152]{1,0:T(8,128)(2,1)S(1)}, bf16[128,1152]{1,0:T(8,128)(2,1)S(1)}, u32[]{:S(2)}, u32[]{:S(2)}) collective-permute-start(bf16[128,1152]{1,0:T(8,128)(2,1)S(1)} %slice.351), channel_id=1, source_target_pairs={{0,4},{4,0},{1,5},{5,1},{2,6},{6,2},{3,7},{7,3},{8,12},{12,8},{9,1... | collective-permute-start | bytes 884744 | tf_op jit(solution)/shard_map/ppermute | solution.py:30
  71.3 47.0 %collective-permute-start.4 = (bf16[1024,1152]{1,0:T(8,128)(2,1)}, bf16[1024,1152]{1,0:T(8,128)(2,1)}, u32[]{:S(2)}, u32[]{:S(2)}) collective-permute-start(bf16[1024,1152]{1,0:T(8,128)(2,1)} %get-tuple-element.120), channel_id=1, source_target_pairs={{0,1},{1,0},{2,3},{3,2},{4,5},{5,4},{6,7},{7,6},{8,9},{9,8},{10,11... | collective-permute-start | bytes 7077896 | tf_op jit(solution)/shard_map/ppermute | solution.py:30
  72.2 16.4 %all-to-all-start = ((bf16[8,3,128,128]{2,3,1,0:T(8,128)(2,1)}), bf16[8,3,128,128]{2,3,1,0:T(8,128)(2,1)}, u32[]{:S(2)}, u32[]{:S(2)}) async-start(bf16[8,3,128,128]{2,3,1,0:T(8,128)(2,1)} %copy.159), calls=%async_computation | async-start | bytes 1572864 | tf_op jit(solution)/shard_map/all_to_all | solution.py:393
  76.4 233.6 %all-gather.2.cloned.1.call-start = ((), (), s32[]{:S(2)}) async-start(), calls=%async_computation.6 | async-start | bytes 7864320 | tf_op jit(solution)/shard_map/all_gather | solution.py:448
  83.8 31.4 %collective-permute-start.19 = (bf16[128,3072]{0,1:T(8,128)(2,1)}, bf16[128,3072]{0,1:T(8,128)(2,1)}, u32[]{:S(2)}, u32[]{:S(2)}) collective-permute-start(bf16[128,3072]{0,1:T(8,128)(2,1)} %bitcast.34), channel_id=1, source_target_pairs={{0,4},{4,0},{1,5},{5,1},{2,6},{6,2},{3,7},{7,3},{8,12},{12,8},{9,1... | collective-permute-start | bytes 2359304 | tf_op jit(solution)/shard_map/ppermute | solution.py:30
  109.9 100.3 %copy-start.19 = (bf16[1024,384]{1,0:T(8,128)(2,1)}, bf16[1024,384]{1,0:T(8,128)(2,1)S(1)}, u32[]{:S(2)}) copy-start(bf16[1024,384]{1,0:T(8,128)(2,1)S(1)} %all_gather.6) | copy-start | bytes 2359300
  118.2 489.5 %reduce-scatter.5.cloned.1.call-start = ((), (), s32[]{:S(2)}) async-start(), calls=%async_computation.8 | async-start | bytes 7864320 | tf_op jit(solution)/shard_map/reduce_scatter | solution.py:494
  128.2 63.6 %copy-start.4 = (bf16[2048,128]{1,0:T(8,128)(2,1)}, bf16[2048,128]{1,0:T(8,128)(2,1)S(1)}, u32[]{:S(2)}) copy-start(bf16[2048,128]{1,0:T(8,128)(2,1)S(1)} %get-tuple-element.18.q_ref) | copy-start | bytes 1572868
  128.3 83.4 %copy-start.6 = (bf16[2048,128]{1,0:T(8,128)(2,1)}, bf16[2048,128]{1,0:T(8,128)(2,1)S(1)}, u32[]{:S(2)}) copy-start(bf16[2048,128]{1,0:T(8,128)(2,1)S(1)} %get-tuple-element.19.k0_ref) | copy-start | bytes 1572868
  128.3 23.6 %collective-permute-start.5 = (bf16[2048,128]{1,0:T(8,128)(2,1)S(1)}, bf16[2048,128]{1,0:T(8,128)(2,1)}, u32[]{:S(2)}, u32[]{:S(2)}) collective-permute-start(bf16[2048,128]{1,0:T(8,128)(2,1)S(1)} %get-tuple-element.19.k0_ref), channel_id=1, source_target_pairs={{0,8},{8,16},{16,24},{1,9},{9,17},{17,25},{2,10},{10,18},{18,26},{... | collective-permute-start | bytes 1572872 | tf_op jit(solution)/shard_map/ppermute | solution.py:36
  151.9 60.8 %collective-permute-start.6 = (bf16[2048,128]{1,0:T(8,128)(2,1)}, bf16[2048,128]{1,0:T(8,128)(2,1)}, u32[]{:S(2)}, u32[]{:S(2)}) collective-permute-start(bf16[2048,128]{1,0:T(8,128)(2,1)} %collective-permute-done.5.k1_ref), channel_id=1, source_target_pairs={{0,8},{8,16},{16,24},{1,9},{9,17},{17,25},{2,10},{10,18},{18,26},{... | collective-permute-start | bytes 1572872 | tf_op jit(solution)/shard_map/ppermute | solution.py:36
  171.6 71.0 %copy-start.8 = (f32[2048]{0:T(1024)}, f32[2048]{0:T(1024)S(1)}, u32[]{:S(2)}) copy-start(f32[2048]{0:T(1024)S(1)} %convert_reduce_fusion) | copy-start | bytes 24580
  171.6 20.2 %collective-permute-start.7 = (f32[16,128]{1,0:T(8,128)S(1)}, f32[16,128]{1,0:T(8,128)S(1)}, u32[]{:S(2)}, u32[]{:S(2)}) collective-permute-start(f32[16,128]{1,0:T(8,128)S(1)} %bitcast.153), channel_id=1, source_target_pairs={{0,8},{8,16},{16,24},{1,9},{9,17},{17,25},{2,10},{10,18},{18,26},{... | collective-permute-start | bytes 24584 | tf_op jit(solution)/shard_map/ppermute | solution.py:36
  191.9 19.7 %collective-permute-start.8 = (f32[16,128]{1,0:T(8,128)S(1)}, f32[16,128]{1,0:T(8,128)S(1)}, u32[]{:S(2)}, u32[]{:S(2)}) collective-permute-start(f32[16,128]{1,0:T(8,128)S(1)} %collective-permute-done.7), channel_id=1, source_target_pairs={{0,8},{8,16},{16,24},{1,9},{9,17},{17,25},{2,10},{10,18},{18,26},{... | collective-permute-start | bytes 24584 | tf_op jit(solution)/shard_map/ppermute | solution.py:36
  244.7 4.2 collective-permute-start.9
  244.8 14.8 %collective-permute-start.25 = (bf16[256,1024]{1,0:T(8,128)(2,1)S(1)}, bf16[256,1024]{1,0:T(8,128)(2,1)S(1)}, u32[]{:S(2)}, u32[]{:S(2)}) collective-permute-start(bf16[256,1024]{1,0:T(8,128)(2,1)S(1)} %bitcast.165), channel_id=1, source_target_pairs={{0,4},{4,0},{1,5},{5,1},{2,6},{6,2},{3,7},{7,3},{8,12},{12,8},{9,1... | collective-permute-start | bytes 1572872 | tf_op jit(solution)/shard_map/ppermute | solution.py:30
  244.8 15.9 %collective-permute-start.26 = (bf16[256,1024]{1,0:T(8,128)(2,1)S(1)}, bf16[256,1024]{1,0:T(8,128)(2,1)S(1)}, u32[]{:S(2)}, u32[]{:S(2)}) collective-permute-start(bf16[256,1024]{1,0:T(8,128)(2,1)S(1)} %bitcast.166), channel_id=1, source_target_pairs={{0,2},{2,0},{1,3},{3,1},{4,6},{6,4},{5,7},{7,5},{8,10},{10,8},{9,1... | collective-permute-start | bytes 1572872 | tf_op jit(solution)/shard_map/ppermute | solution.py:30
  250.0 15.2 %collective-permute-start.10 = (bf16[128,1024]{1,0:T(8,128)(2,1)S(1)}, bf16[128,1024]{1,0:T(8,128)(2,1)S(1)}, u32[]{:S(2)}, u32[]{:S(2)}) collective-permute-start(bf16[128,1024]{1,0:T(8,128)(2,1)S(1)} %get-tuple-element.83), channel_id=1, source_target_pairs={{0,2},{2,0},{1,3},{3,1},{4,6},{6,4},{5,7},{7,5},{8,10},{10,8},{9,1... | collective-permute-start | bytes 786440 | tf_op jit(solution)/shard_map/ppermute | solution.py:30
  251.2 14.1 %collective-permute-start.12 = (bf16[128,1024]{1,0:T(8,128)(2,1)S(1)}, bf16[128,1024]{1,0:T(8,128)(2,1)S(1)}, u32[]{:S(2)}, u32[]{:S(2)}) collective-permute-start(bf16[128,1024]{1,0:T(8,128)(2,1)S(1)} %get-tuple-element.84), channel_id=1, source_target_pairs={{0,4},{4,0},{1,5},{5,1},{2,6},{6,2},{3,7},{7,3},{8,12},{12,8},{9,1... | collective-permute-start | bytes 786440 | tf_op jit(solution)/shard_map/ppermute | solution.py:30
  259.6 11.3 %collective-permute-start.27 = (bf16[128,1024]{1,0:T(8,128)(2,1)S(1)}, bf16[128,1024]{1,0:T(8,128)(2,1)S(1)}, u32[]{:S(2)}, u32[]{:S(2)}) collective-permute-start(bf16[128,1024]{1,0:T(8,128)(2,1)S(1)} %slice.386), channel_id=1, source_target_pairs={{0,2},{2,0},{1,3},{3,1},{4,6},{6,4},{5,7},{7,5},{8,10},{10,8},{9,1... | collective-permute-start | bytes 786440 | tf_op jit(solution)/shard_map/ppermute | solution.py:30
  260.7 10.2 %collective-permute-start.28 = (bf16[128,1024]{1,0:T(8,128)(2,1)S(1)}, bf16[128,1024]{1,0:T(8,128)(2,1)S(1)}, u32[]{:S(2)}, u32[]{:S(2)}) collective-permute-start(bf16[128,1024]{1,0:T(8,128)(2,1)S(1)} %slice.387), channel_id=1, source_target_pairs={{0,4},{4,0},{1,5},{5,1},{2,6},{6,2},{3,7},{7,3},{8,12},{12,8},{9,1... | collective-permute-start | bytes 786440 | tf_op jit(solution)/shard_map/ppermute | solution.py:30
  265.5 16.1 %collective-permute-start.11 = (bf16[256,1024]{1,0:T(8,128)(2,1)S(1)}, bf16[256,1024]{1,0:T(8,128)(2,1)S(1)}, u32[]{:S(2)}, u32[]{:S(2)}) collective-permute-start(bf16[256,1024]{1,0:T(8,128)(2,1)S(1)} %pad_maximum_fusion.7), channel_id=1, source_target_pairs={{0,4},{4,0},{1,5},{5,1},{2,6},{6,2},{3,7},{7,3},{8,12},{12,8},{9,1... | collective-permute-start | bytes 1572872 | tf_op jit(solution)/shard_map/ppermute | solution.py:30
  267.5 14.0 %collective-permute-start.13 = (bf16[256,1024]{1,0:T(8,128)(2,1)S(1)}, bf16[256,1024]{1,0:T(8,128)(2,1)S(1)}, u32[]{:S(2)}, u32[]{:S(2)}) collective-permute-start(bf16[256,1024]{1,0:T(8,128)(2,1)S(1)} %pad_maximum_fusion.8), channel_id=1, source_target_pairs={{0,2},{2,0},{1,3},{3,1},{4,6},{6,4},{5,7},{7,5},{8,10},{10,8},{9,1... | collective-permute-start | bytes 1572872 | tf_op jit(solution)/shard_map/ppermute | solution.py:30
  271.0 33.4 %collective-permute-start.29 = (bf16[1024,1024]{1,0:T(8,128)(2,1)S(1)}, bf16[1024,1024]{1,0:T(8,128)(2,1)S(1)}, u32[]{:S(2)}, u32[]{:S(2)}) collective-permute-start(bf16[1024,1024]{1,0:T(8,128)(2,1)S(1)} %get-tuple-element.128), channel_id=1, source_target_pairs={{0,1},{1,0},{2,3},{3,2},{4,5},{5,4},{6,7},{7,6},{8,9},{9,8},{10,11... | collective-permute-start | bytes 6291464 | tf_op jit(solution)/shard_map/ppermute | solution.py:30
  282.1 13.5 %collective-permute-start.14 = (bf16[256,1024]{1,0:T(8,128)(2,1)S(1)}, bf16[256,1024]{1,0:T(8,128)(2,1)S(1)}, u32[]{:S(2)}, u32[]{:S(2)}) collective-permute-start(bf16[256,1024]{1,0:T(8,128)(2,1)S(1)} %get-tuple-element.47), channel_id=1, source_target_pairs={{0,4},{4,0},{1,5},{5,1},{2,6},{6,2},{3,7},{7,3},{8,12},{12,8},{9,1... | collective-permute-start | bytes 1572872 | tf_op jit(solution)/shard_map/ppermute | solution.py:30
  283.9 12.9 %collective-permute-start.15 = (bf16[256,1024]{1,0:T(8,128)(2,1)S(1)}, bf16[256,1024]{1,0:T(8,128)(2,1)S(1)}, u32[]{:S(2)}, u32[]{:S(2)}) collective-permute-start(bf16[256,1024]{1,0:T(8,128)(2,1)S(1)} %get-tuple-element.47), channel_id=1, source_target_pairs={{0,2},{2,0},{1,3},{3,1},{4,6},{6,4},{5,7},{7,5},{8,10},{10,8},{9,1... | collective-permute-start | bytes 1572872 | tf_op jit(solution)/shard_map/ppermute | solution.py:30
  295.7 7.0 collective-permute-start.16
  296.8 6.7 collective-permute-start.17
  304.3 4.2 collective-permute-start.18
  367.0 55.0 %collective-permute-start.20 = (bf16[1024,1024]{1,0:T(8,128)(2,1)}, bf16[1024,1024]{1,0:T(8,128)(2,1)}, u32[]{:S(2)}, u32[]{:S(2)}) collective-permute-start(bf16[1024,1024]{1,0:T(8,128)(2,1)} %slice.378), channel_id=1, source_target_pairs={{0,1},{1,0},{2,3},{3,2},{4,5},{5,4},{6,7},{7,6},{8,9},{9,8},{10,11... | collective-permute-start | bytes 6291464 | tf_op jit(solution)/shard_map/ppermute | solution.py:30
  408.4 19.4 %collective-permute-start.30 = (bf16[1024,1024]{1,0:T(8,128)(2,1)}, bf16[1024,1024]{1,0:T(8,128)(2,1)}, u32[]{:S(2)}, u32[]{:S(2)}) collective-permute-start(bf16[1024,1024]{1,0:T(8,128)(2,1)} %slice.389), channel_id=1, source_target_pairs={{0,1},{1,0},{2,3},{3,2},{4,5},{5,4},{6,7},{7,6},{8,9},{9,8},{10,11... | collective-permute-start | bytes 6291464 | tf_op jit(solution)/shard_map/ppermute | solution.py:30
  421.9 189.4 %reduce-scatter.3.cloned.1.call-start = ((), (), s32[]{:S(2)}) async-start(), calls=%async_computation.7 | async-start | bytes 983040 | tf_op jit(solution)/shard_map/reduce_scatter | solution.py:518
  425.6 9.2 %collective-permute-start.21 = (bf16[128,1024]{1,0:T(8,128)(2,1)S(1)}, bf16[128,1024]{1,0:T(8,128)(2,1)S(1)}, u32[]{:S(2)}, u32[]{:S(2)}) collective-permute-start(bf16[128,1024]{1,0:T(8,128)(2,1)S(1)} %get-tuple-element.79), channel_id=1, source_target_pairs={{0,2},{2,0},{1,3},{3,1},{4,6},{6,4},{5,7},{7,5},{8,10},{10,8},{9,1... | collective-permute-start | bytes 786440 | tf_op jit(solution)/shard_map/ppermute | solution.py:30
  426.6 9.2 %collective-permute-start.23 = (bf16[128,1024]{1,0:T(8,128)(2,1)S(1)}, bf16[128,1024]{1,0:T(8,128)(2,1)S(1)}, u32[]{:S(2)}, u32[]{:S(2)}) collective-permute-start(bf16[128,1024]{1,0:T(8,128)(2,1)S(1)} %get-tuple-element.80), channel_id=1, source_target_pairs={{0,4},{4,0},{1,5},{5,1},{2,6},{6,2},{3,7},{7,3},{8,12},{12,8},{9,1... | collective-permute-start | bytes 786440 | tf_op jit(solution)/shard_map/ppermute | solution.py:30
  430.5 9.9 %collective-permute-start.31 = (bf16[128,1024]{1,0:T(8,128)(2,1)S(1)}, bf16[128,1024]{1,0:T(8,128)(2,1)S(1)}, u32[]{:S(2)}, u32[]{:S(2)}) collective-permute-start(bf16[128,1024]{1,0:T(8,128)(2,1)S(1)} %get-tuple-element.75), channel_id=1, source_target_pairs={{0,2},{2,0},{1,3},{3,1},{4,6},{6,4},{5,7},{7,5},{8,10},{10,8},{9,1... | collective-permute-start | bytes 786440 | tf_op jit(solution)/shard_map/ppermute | solution.py:30
  431.6 9.8 %collective-permute-start.33 = (bf16[128,1024]{1,0:T(8,128)(2,1)S(1)}, bf16[128,1024]{1,0:T(8,128)(2,1)S(1)}, u32[]{:S(2)}, u32[]{:S(2)}) collective-permute-start(bf16[128,1024]{1,0:T(8,128)(2,1)S(1)} %get-tuple-element.76), channel_id=1, source_target_pairs={{0,4},{4,0},{1,5},{5,1},{2,6},{6,2},{3,7},{7,3},{8,12},{12,8},{9,1... | collective-permute-start | bytes 786440 | tf_op jit(solution)/shard_map/ppermute | solution.py:30
  436.0 16.7 %collective-permute-start.22 = (bf16[256,1024]{1,0:T(8,128)(2,1)S(1)}, bf16[256,1024]{1,0:T(8,128)(2,1)S(1)}, u32[]{:S(2)}, u32[]{:S(2)}) collective-permute-start(bf16[256,1024]{1,0:T(8,128)(2,1)S(1)} %pad_maximum_fusion.9), channel_id=1, source_target_pairs={{0,4},{4,0},{1,5},{5,1},{2,6},{6,2},{3,7},{7,3},{8,12},{12,8},{9,1... | collective-permute-start | bytes 1572872 | tf_op jit(solution)/shard_map/ppermute | solution.py:30
  437.2 15.4 %collective-permute-start.24 = (bf16[256,1024]{1,0:T(8,128)(2,1)S(1)}, bf16[256,1024]{1,0:T(8,128)(2,1)S(1)}, u32[]{:S(2)}, u32[]{:S(2)}) collective-permute-start(bf16[256,1024]{1,0:T(8,128)(2,1)S(1)} %pad_maximum_fusion.10), channel_id=1, source_target_pairs={{0,2},{2,0},{1,3},{3,1},{4,6},{6,4},{5,7},{7,5},{8,10},{10,8},{9,1... | collective-permute-start | bytes 1572872 | tf_op jit(solution)/shard_map/ppermute | solution.py:30
  441.6 21.4 %collective-permute-start.32 = (bf16[256,1024]{1,0:T(8,128)(2,1)S(1)}, bf16[256,1024]{1,0:T(8,128)(2,1)S(1)}, u32[]{:S(2)}, u32[]{:S(2)}) collective-permute-start(bf16[256,1024]{1,0:T(8,128)(2,1)S(1)} %pad_maximum_fusion.11), channel_id=1, source_target_pairs={{0,4},{4,0},{1,5},{5,1},{2,6},{6,2},{3,7},{7,3},{8,12},{12,8},{9,1... | collective-permute-start | bytes 1572872 | tf_op jit(solution)/shard_map/ppermute | solution.py:30
  442.9 20.1 %collective-permute-start.34 = (bf16[256,1024]{1,0:T(8,128)(2,1)S(1)}, bf16[256,1024]{1,0:T(8,128)(2,1)S(1)}, u32[]{:S(2)}, u32[]{:S(2)}) collective-permute-start(bf16[256,1024]{1,0:T(8,128)(2,1)S(1)} %pad_maximum_fusion.12), channel_id=1, source_target_pairs={{0,2},{2,0},{1,3},{3,1},{4,6},{6,4},{5,7},{7,5},{8,10},{10,8},{9,1... | collective-permute-start | bytes 1572872 | tf_op jit(solution)/shard_map/ppermute | solution.py:30
  464.9 13.2 %collective-permute-start.35 = (bf16[256,1024]{1,0:T(8,128)(2,1)S(1)}, bf16[256,1024]{1,0:T(8,128)(2,1)S(1)}, u32[]{:S(2)}, u32[]{:S(2)}) collective-permute-start(bf16[256,1024]{1,0:T(8,128)(2,1)S(1)} %get-tuple-element.40), channel_id=1, source_target_pairs={{0,4},{4,0},{1,5},{5,1},{2,6},{6,2},{3,7},{7,3},{8,12},{12,8},{9,1... | collective-permute-start | bytes 1572872 | tf_op jit(solution)/shard_map/ppermute | solution.py:30
  466.1 13.2 %collective-permute-start.36 = (bf16[256,1024]{1,0:T(8,128)(2,1)S(1)}, bf16[256,1024]{1,0:T(8,128)(2,1)S(1)}, u32[]{:S(2)}, u32[]{:S(2)}) collective-permute-start(bf16[256,1024]{1,0:T(8,128)(2,1)S(1)} %get-tuple-element.40), channel_id=1, source_target_pairs={{0,2},{2,0},{1,3},{3,1},{4,6},{6,4},{5,7},{7,5},{8,10},{10,8},{9,1... | collective-permute-start | bytes 1572872 | tf_op jit(solution)/shard_map/ppermute | solution.py:30
  478.1 6.8 collective-permute-start.37
  479.3 6.5 collective-permute-start.38
  485.8 4.2 collective-permute-start.39
  523.7 24.9 %collective-permute-start.40 = (bf16[2048,128]{1,0:T(8,128)(2,1)}, bf16[2048,128]{1,0:T(8,128)(2,1)S(1)}, u32[]{:S(2)}, u32[]{:S(2)}) collective-permute-start(bf16[2048,128]{1,0:T(8,128)(2,1)} %get-tuple-element.25), channel_id=1, source_target_pairs={{8,0},{16,8},{24,16},{9,1},{17,9},{25,17},{10,2},{18,10},{26,18},{... | collective-permute-start | bytes 1572872 | tf_op jit(solution)/shard_map/ppermute | solution.py:36
  550.7 16.0 %collective-permute-start.41 = (bf16[2048,128]{1,0:T(8,128)(2,1)}, bf16[2048,128]{1,0:T(8,128)(2,1)}, u32[]{:S(2)}, u32[]{:S(2)}) collective-permute-start(bf16[2048,128]{1,0:T(8,128)(2,1)} %add_convert_fusion.1), channel_id=1, source_target_pairs={{8,0},{16,8},{24,16},{9,1},{17,9},{25,17},{10,2},{18,10},{26,18},{... | collective-permute-start | bytes 1572872 | tf_op jit(solution)/shard_map/ppermute | solution.py:36
  578.8 8.5 %collective-permute-start.42 = (bf16[1024,1024]{1,0:T(8,128)(2,1)}, bf16[1024,1024]{1,0:T(8,128)(2,1)}, u32[]{:S(2)}, u32[]{:S(2)}) collective-permute-start(bf16[1024,1024]{1,0:T(8,128)(2,1)} %slice.400), channel_id=1, source_target_pairs={{0,1},{1,0},{2,3},{3,2},{4,5},{5,4},{6,7},{7,6},{8,9},{9,8},{10,11... | collective-permute-start | bytes 6291464 | tf_op jit(solution)/shard_map/ppermute | solution.py:30
  592.6 8.8 %collective-permute-start.43 = (bf16[128,1024]{1,0:T(8,128)(2,1)S(1)}, bf16[128,1024]{1,0:T(8,128)(2,1)S(1)}, u32[]{:S(2)}, u32[]{:S(2)}) collective-permute-start(bf16[128,1024]{1,0:T(8,128)(2,1)S(1)} %get-tuple-element.71), channel_id=1, source_target_pairs={{0,2},{2,0},{1,3},{3,1},{4,6},{6,4},{5,7},{7,5},{8,10},{10,8},{9,1... | collective-permute-start | bytes 786440 | tf_op jit(solution)/shard_map/ppermute | solution.py:30
  594.2 8.4 %collective-permute-start.45 = (bf16[128,1024]{1,0:T(8,128)(2,1)S(1)}, bf16[128,1024]{1,0:T(8,128)(2,1)S(1)}, u32[]{:S(2)}, u32[]{:S(2)}) collective-permute-start(bf16[128,1024]{1,0:T(8,128)(2,1)S(1)} %get-tuple-element.72), channel_id=1, source_target_pairs={{0,4},{4,0},{1,5},{5,1},{2,6},{6,2},{3,7},{7,3},{8,12},{12,8},{9,1... | collective-permute-start | bytes 786440 | tf_op jit(solution)/shard_map/ppermute | solution.py:30
  604.9 15.1 %collective-permute-start.44 = (bf16[256,1024]{1,0:T(8,128)(2,1)}, bf16[256,1024]{1,0:T(8,128)(2,1)S(1)}, u32[]{:S(2)}, u32[]{:S(2)}) collective-permute-start(bf16[256,1024]{1,0:T(8,128)(2,1)} %pad_maximum_fusion.13), channel_id=1, source_target_pairs={{0,4},{4,0},{1,5},{5,1},{2,6},{6,2},{3,7},{7,3},{8,12},{12,8},{9,1... | collective-permute-start | bytes 1572872 | tf_op jit(solution)/shard_map/ppermute | solution.py:30
  607.2 13.2 %collective-permute-start.46 = (bf16[256,1024]{1,0:T(8,128)(2,1)}, bf16[256,1024]{1,0:T(8,128)(2,1)S(1)}, u32[]{:S(2)}, u32[]{:S(2)}) collective-permute-start(bf16[256,1024]{1,0:T(8,128)(2,1)} %pad_maximum_fusion.14), channel_id=1, source_target_pairs={{0,2},{2,0},{1,3},{3,1},{4,6},{6,4},{5,7},{7,5},{8,10},{10,8},{9,1... | collective-permute-start | bytes 1572872 | tf_op jit(solution)/shard_map/ppermute | solution.py:30
  610.1 26.8 %collective-permute-start.47 = (bf16[128,3072]{0,1:T(8,128)(2,1)}, bf16[128,3072]{0,1:T(8,128)(2,1)}, u32[]{:S(2)}, u32[]{:S(2)}) collective-permute-start(bf16[128,3072]{0,1:T(8,128)(2,1)} %get-tuple-element.88), channel_id=1, source_target_pairs={{0,4},{4,0},{1,5},{5,1},{2,6},{6,2},{3,7},{7,3},{8,12},{12,8},{9,1... | collective-permute-start | bytes 2359304 | tf_op jit(solution)/shard_map/ppermute | solution.py:30
  613.3 34.1 %all-to-all-start.2 = ((bf16[8,128,384]{1,2,0:T(8,128)(2,1)}), bf16[8,128,384]{1,2,0:T(8,128)(2,1)}, u32[]{:S(2)}, u32[]{:S(2)}) async-start(bf16[8,128,384]{1,2,0:T(8,128)(2,1)} %bitcast.38), calls=%async_computation.3 | async-start | bytes 1572864 | tf_op jit(solution)/shard_map/all_to_all | solution.py:522
  647.4 46.2 %all-to-all-start.3 = ((bf16[80,128,128]{2,1,0:T(8,128)(2,1)}), bf16[80,128,128]{2,1,0:T(8,128)(2,1)}, u32[]{:S(2)}, u32[]{:S(2)}) async-start(bf16[80,128,128]{2,1,0:T(8,128)(2,1)} %select_select_fusion), calls=%async_computation.5 | async-start | bytes 5242880 | tf_op jit(solution)/shard_map/all_to_all | solution.py:544
  652.0 2.0 collective-permute-start.48
  654.0 3.7 collective-permute-start.49
  657.8 25.7 %collective-permute-start.50 = (f32[2,1024]{1,0:T(2,128)S(1)}, f32[2,1024]{1,0:T(2,128)S(1)}, u32[]{:S(2)}, u32[]{:S(2)}) collective-permute-start(f32[2,1024]{1,0:T(2,128)S(1)} %fusion.84), channel_id=1, source_target_pairs={{0,2},{2,0},{1,3},{3,1},{4,6},{6,4},{5,7},{7,5},{8,10},{10,8},{9,1... | collective-permute-start | bytes 24584 | tf_op jit(solution)/shard_map/ppermute | solution.py:30
  683.4 3.7 collective-permute-start.51
  687.1 5.8 collective-permute-start.52
  (45 other events, 771.4 us)
Sparse Core Ops, SparseCore 0:
  118.3 132.0 all-gather.1
  422.1 120.4 reduce-scatter.4
  587.4 23.9 reduce-scatter.2

commit v2 on v1

v2 whole, which is shorter than its diff:
```python
import jax
import jax.numpy as jnp
import numpy as np
from jax import lax
from jax.experimental import pallas as pl
from jax.experimental.pallas import tpu as pltpu
from jax.sharding import Mesh
from jax.sharding import PartitionSpec as P

QH = 16
KVH = 8
HD = 64
STEP = 7

EPS_NORM = 1e-05
THETA = 10000.0
BETA_ONE = 0.5
BETA_TWO = 0.6
ADAM_EPS = 1e-08
DECAY = 0.1
GAIN_RATE = 0.3
NEG_BIG = -1e30
PLANE = ("x", "y", "c")
WSH = ("y", "c")
BF = jnp.bfloat16
F32 = jnp.float32


def swap(value, axis):
    return lax.ppermute(value, axis, [(0, 1), (1, 0)])


def shift(value, by):
    count = lax.axis_size("z")
    pairs = [(i, i + by) for i in range(count) if 0 <= i + by < count]
    return lax.ppermute(value, "z", pairs)


def took(us):
    return pl.CostEstimate(flops=int(us * 1e9), bytes_accessed=2**20, transcendentals=0)


def vmem(mib):
    return pltpu.CompilerParams(vmem_limit_bytes=mib * 2**20)


def whole(shape):
    return pl.BlockSpec(shape, lambda *_: (0,) * len(shape))


def half_specs(block, width, rows, at):
    low = pl.BlockSpec((block, width), lambda *g: (jnp.minimum(at(*g), rows // 2 // block - 1), 0))
    high = pl.BlockSpec((block, width), lambda *g: (jnp.maximum(at(*g) - rows // 2 // block, 0), 0))
    return [low, high]


def after(value, *first):
    return lax.optimization_barrier((value, *first))[0]


def stack_kernel(*refs):
    at = 0
    for ref in refs[:-1]:
        refs[-1][at : at + ref.shape[0]] = ref[...]
        at += ref.shape[0]


def stack(pieces):
    shape = (sum(piece.shape[0] for piece in pieces), pieces[0].shape[1])
    return pl.pallas_call(
        stack_kernel,
        grid=(1,),
        in_specs=[whole(piece.shape) for piece in pieces],
        out_specs=whole(shape),
        out_shape=jax.ShapeDtypeStruct(shape, BF),
        cost_estimate=took(2),
        compiler_params=vmem(32),
    )(*pieces)


def plane_gather(rows, wait=lambda value: value, last=lambda value: value):
    half = rows.shape[0] // 2
    over_x = swap(rows, "x")
    over_y = swap(rows, "y")
    first, second = wait((over_x[:half], over_y[half:]))
    corner_top = swap(first, "y")
    corner_low = swap(second, "x")
    mine = stack([rows, over_x, over_y, corner_top, corner_low])
    return mine, swap(last(mine), "c")


def corner_kernel(kept_ref, got_ref, out_ref):
    out_ref[...] = (kept_ref[...].astype(F32) + got_ref[...].astype(F32)).astype(BF)


def corner_rows(kept, got):
    rows, width = kept.shape
    spec = pl.BlockSpec((rows // 4, width), lambda i: (3, 0))
    return pl.pallas_call(
        corner_kernel,
        grid=(1,),
        in_specs=[spec, spec],
        out_specs=whole((rows // 4, width)),
        out_shape=jax.ShapeDtypeStruct((rows // 4, width), BF),
        cost_estimate=took(2),
        compiler_params=vmem(32),
    )(kept, got)


def edge_kernel(kx_ref, gx_ref, ky_ref, gy_ref, fx_ref, fy_ref, x_ref, y_ref):
    half = fx_ref.shape[0]
    for kept, got, extra, out_ref, at in ((kx_ref, gx_ref, fx_ref, x_ref, 0), (ky_ref, gy_ref, fy_ref, y_ref, 1)):
        total = kept[...].astype(F32) + got[...].astype(F32)
        mine, rest = slice(at * half, (at + 1) * half), slice((1 - at) * half, (2 - at) * half)
        out_ref[mine] = (total[mine] + extra[...].astype(F32)).astype(BF)
        out_ref[rest] = total[rest].astype(BF)


def edge_rows(kept, got, for_x, for_y):
    rows, width = kept.shape
    step = rows // 4
    one, two = (pl.BlockSpec((step, width), lambda i, b=b: (b, 0)) for b in (1, 2))
    half = whole((step // 2, width))
    return pl.pallas_call(
        edge_kernel,
        grid=(1,),
        in_specs=[one, one, two, two, half, half],
        out_specs=[whole((step, width))] * 2,
        out_shape=[jax.ShapeDtypeStruct((step, width), BF)] * 2,
        cost_estimate=took(2),
        compiler_params=vmem(32),
    )(kept, got, kept, got, for_x, for_y)


def plane_reduce(kept, sent, waits=(None, None, None)):
    hold = [wait or (lambda value: value) for wait in waits]
    step = kept.shape[0] // 4
    half = step // 2
    got = swap(hold[0](sent), "c")
    corner = hold[1](corner_rows(kept, got))
    for_x = swap(corner[:half], "y")
    for_y = swap(corner[half:], "x")
    to_x, to_y = hold[2](edge_rows(kept, got, for_x, for_y))
    own = kept[:step].astype(F32) + got[:step].astype(F32)
    return own + swap(to_x, "x").astype(F32) + swap(to_y, "y").astype(F32)


def sum_everywhere(value):
    for axis in ("c", "x", "y"):
        value = value + swap(value, axis)
    count = lax.axis_size("z")
    if count & (count - 1):
        return lax.psum(value, "z")
    stride = 1
    while stride < count:
        value = value + lax.ppermute(value, "z", [(i, i ^ stride) for i in range(count)])
        stride *= 2
    return value


def norm_scale(values):
    return lax.rsqrt(jnp.mean(values * values, axis=-1, keepdims=True) + EPS_NORM)


def norm_back(values, scale_row, gain_row, grad_out):
    weighted = grad_out * gain_row
    grad_in = scale_row * weighted - values * scale_row**3 * jnp.mean(
        values * weighted, axis=-1, keepdims=True
    )
    return grad_in


def kind_rates(width, hidden):
    base_rate = 0.5 * width ** (-0.5)
    return [
        base_rate,
        base_rate,
        base_rate,
        2.0 * (2 * hidden) ** (-0.5),
        base_rate,
        base_rate,
        3.0 * hidden ** (-0.5),
        base_rate,
    ]


def adamw(weight, first, second, grad, rate, decay):
    first_new = BETA_ONE * first + (1.0 - BETA_ONE) * grad
    second_new = BETA_TWO * second + (1.0 - BETA_TWO) * grad * grad
    first_hat = first_new / (1.0 - BETA_ONE**STEP)
    second_hat = second_new / (1.0 - BETA_TWO**STEP)
    weight_new = weight - rate * (first_hat / (jnp.sqrt(second_hat) + ADAM_EPS) + decay * weight)
    return (weight_new, first_new, second_new)


def dot_nn(left, right):
    return lax.dot_general(left, right, (((1,), (0,)), ((), ())), preferred_element_type=F32)


def dot_nt(left, right):
    return lax.dot_general(left, right, (((1,), (1,)), ((), ())), preferred_element_type=F32)


def dot_tn(left, right):
    return lax.dot_general(left, right, (((0,), (0,)), ((), ())), preferred_element_type=F32)


def turn(value, lane):
    low = (lane % HD) < (HD // 2)
    return jnp.where(
        low, -pltpu.roll(value, 2 * HD - HD // 2, 1), pltpu.roll(value, HD // 2, 1)
    )

def choose(early, low_ref, high_ref):
    return jnp.where(early, low_ref[...], high_ref[...])


def attn_send_kernel(at_ref, ok_ref, *refs):
    mats, out_ref = refs[:6], refs[6]

    def read(m):
        return jnp.where(ok_ref[m] == 1, mats[m][0], 0.0).astype(BF)

    part = out_ref.shape[3]
    for side in range(2):
        for kind, m in ((0, side), (2, 4 + side)):
            mat = read(m)
            for j in range(4):
                out_ref[4 * side + j, kind] = mat[:, j * part : (j + 1) * part]
    keys, values = read(2), read(3)
    for h in range(8):
        both = (keys[:, h * HD : (h + 1) * HD], values[:, h * HD : (h + 1) * HD])
        out_ref[h, 1] = jnp.concatenate(both, axis=1)


def attn_send(masters, at, ok):
    _, rows, hidden = masters.shape
    part = hidden // 4
    specs = [pl.BlockSpec((1, rows, hidden), lambda i, at, ok, m=m: (at[m], 0, 0)) for m in range(6)]
    return pl.pallas_call(
        attn_send_kernel,
        grid_spec=pltpu.PrefetchScalarGridSpec(
            num_scalar_prefetch=2,
            grid=(1,),
            in_specs=specs,
            out_specs=pl.BlockSpec((8, 3, rows, part), lambda i, at, ok: (0, 0, 0, 0)),
        ),
        out_shape=jax.ShapeDtypeStruct((8, 3, rows, part), BF),
        cost_estimate=took(3),
        compiler_params=vmem(62),
    )(at, ok, *([masters] * 6))


def bulk_send_kernel(in_ref, *outs):
    part = outs[0].shape[3]
    rows = outs[0].shape[2]
    for h, out_ref in enumerate(outs):
        for j in range(4):
            piece = in_ref[:, h * rows : (h + 1) * rows, j * part : (j + 1) * part]
            out_ref[j] = piece.astype(BF)


def bulk_send(masters, halves):
    slots, rows, hidden = masters.shape
    step, part, piece = 5 if slots % 5 == 0 else 1, hidden // 4, rows // halves
    return pl.pallas_call(
        bulk_send_kernel,
        grid=(slots // step,),
        in_specs=[pl.BlockSpec((step, rows, hidden), lambda i: (i, 0, 0))],
        out_specs=[pl.BlockSpec((4, step, piece, part), lambda i: (0, i, 0, 0))] * halves,
        out_shape=[jax.ShapeDtypeStruct((4, slots, piece, part), BF)] * halves,
        cost_estimate=took(4),
        compiler_params=vmem(62),
    )(masters)


def pick_kernel(mine_ref, other_ref, in_ref, keep_ref, give_ref):
    part = in_ref.shape[2]
    for k in range(keep_ref.shape[1] // part):
        keep_ref[:, k * part : (k + 1) * part] = in_ref[mine_ref[k]]
        give_ref[:, k * part : (k + 1) * part] = in_ref[other_ref[k]]


def pick(mine, other, slots):
    total, rows, part = slots.shape
    count = mine.shape[0]
    wide = (rows, count * part)
    return pl.pallas_call(
        pick_kernel,
        grid_spec=pltpu.PrefetchScalarGridSpec(
            num_scalar_prefetch=2,
            grid=(1,),
            in_specs=[pl.BlockSpec((total, rows, part), lambda i, a, b: (0, 0, 0))],
            out_specs=[pl.BlockSpec(wide, lambda i, a, b: (0, 0))] * 2,
        ),
        out_shape=[jax.ShapeDtypeStruct(wide, BF)] * 2,
        cost_estimate=took(3),
        compiler_params=vmem(32),
    )(mine, other, slots)


def join_kernel(info_ref, *refs):
    out_ref = refs[-1]
    rows = refs[0].shape[0]
    half = out_ref.shape[0] // 2
    first = info_ref[0] == 0
    for h in range(len(refs) // 2):
        keep, got = refs[2 * h][...], refs[2 * h + 1][...]
        out_ref[h * rows : (h + 1) * rows] = jnp.where(first, keep, got)
        out_ref[half + h * rows : half + (h + 1) * rows] = jnp.where(first, got, keep)


def join(info, pieces):
    rows, wide = pieces[0].shape
    total = rows * len(pieces)
    return pl.pallas_call(
        join_kernel,
        grid=(1,),
        in_specs=[pl.BlockSpec(memory_space=pltpu.SMEM)] + [whole((rows, wide))] * len(pieces),
        out_specs=whole((total, wide)),
        out_shape=jax.ShapeDtypeStruct((total, wide), BF),
        cost_estimate=took(2),
        compiler_params=vmem(32),
    )(info, *pieces)


def pack_kernel(place_ref, side_ref, info_ref, total_ref, got_ref, out_ref):
    part = out_ref.shape[2]
    rows = out_ref.shape[1]
    mine = pl.ds(pl.multiple_of(info_ref[0] * rows, rows), rows)

    def one(s, carry):
        start = pl.multiple_of(place_ref[s] * part, part)

        @pl.when(side_ref[s] == 0)
        def _():
            out_ref[s] = total_ref[mine, pl.ds(start, part)]

        @pl.when(side_ref[s] == 1)
        def _():
            out_ref[s] = got_ref[:, pl.ds(start, part)]

        @pl.when(side_ref[s] == 2)
        def _():
            out_ref[s] = jnp.zeros((rows, part), BF)

        return carry

    lax.fori_loop(0, out_ref.shape[0], one, 0)


def pack(place, side, info, summed, got, part):
    rows, wide = got.shape
    total = place.shape[0]
    return pl.pallas_call(
        pack_kernel,
        grid_spec=pltpu.PrefetchScalarGridSpec(
            num_scalar_prefetch=3,
            grid=(1,),
            in_specs=[
                pl.BlockSpec((2 * rows, wide), lambda i, a, b, c: (0, 0)),
                pl.BlockSpec((rows, wide), lambda i, a, b, c: (0, 0)),
            ],
            out_specs=pl.BlockSpec((total, rows, part), lambda i, a, b, c: (0, 0, 0)),
        ),
        out_shape=jax.ShapeDtypeStruct((total, rows, part), BF),
        cost_estimate=took(3),
        compiler_params=vmem(32),
    )(place, side, info, summed, got)


def update_kernel(halves, held_ref, rate_ref, attn_ref, *refs):
    grads, (w_ref, m_ref, v_ref, w_out, m_out, v_out) = refs[:halves], refs[halves:]
    part = grads[0].shape[3]
    rows = grads[0].shape[2]
    everything = slice(0, halves * rows)

    def one(s, carry):
        slot = pl.program_id(0) * w_ref.shape[0] + s
        held = held_ref[slot]
        rate = rate_ref[slot]

        def write(at, lanes, grad):
            new_w, new_m, new_v = adamw(
                w_ref[s, at, lanes], m_ref[s, at, lanes], v_ref[s, at, lanes], grad, rate, DECAY
            )
            w_out[s, at, lanes] = new_w
            m_out[s, at, lanes] = new_m
            v_out[s, at, lanes] = new_v

        @pl.when((held < 0) | (held >= 6))
        def _():
            for h in range(halves):
                for j in range(4):
                    at, lanes = slice(h * rows, (h + 1) * rows), slice(j * part, (j + 1) * part)
                    write(at, lanes, grads[h][j, s].astype(F32))

        for m, side, kind in ((0, 0, 0), (1, 1, 0), (4, 0, 2), (5, 1, 2)):

            @pl.when(held == m)
            def _():
                for j in range(4):
                    grad = attn_ref[4 * side + j, :, kind * part : (kind + 1) * part]
                    write(everything, slice(j * part, (j + 1) * part), grad.astype(F32))

        for m, start in ((2, part), (3, part + HD)):

            @pl.when(held == m)
            def _():
                for j in range(4):
                    pieces = [attn_ref[2 * j + i, :, start : start + HD] for i in range(2)]
                    grad = jnp.concatenate(pieces, axis=1)
                    write(everything, slice(j * part, (j + 1) * part), grad.astype(F32))

        return carry

    lax.fori_loop(0, w_ref.shape[0], one, 0)


def update(held, rates, attn_back, grads, masters, first, second):
    slots, rows, hidden = masters.shape
    halves = len(grads)
    step = 4 if slots % 4 == 0 else 1
    smem = pl.BlockSpec(memory_space=pltpu.SMEM)
    spec = pl.BlockSpec((step, rows, hidden), lambda i: (i, 0, 0))
    grad_spec = pl.BlockSpec((4, step, rows // halves, hidden // 4), lambda i: (0, i, 0, 0))
    return pl.pallas_call(
        lambda *refs: update_kernel(halves, *refs),
        grid=(slots // step,),
        in_specs=[smem, smem, whole(attn_back.shape)] + [grad_spec] * halves + [spec] * 3,
        out_specs=[spec] * 3,
        out_shape=[jax.ShapeDtypeStruct(masters.shape, F32)] * 3,
        cost_estimate=took(12),
        compiler_params=vmem(62),
    )(held, rates, attn_back, *grads, masters, first, second)


def project_kernel(low_ref, high_ref, w_ref, cos_ref, sin_ref, q_ref, kv_ref):
    early = pl.program_id(0) < pl.num_programs(0) // 2
    both = dot_nn(choose(early, low_ref, high_ref), w_ref[...])
    cosine = cos_ref[0]
    sine = sin_ref[0]
    lane = lax.broadcasted_iota(jnp.int32, cosine.shape, 1)
    query = both[:, : 2 * HD]
    pair = both[:, 2 * HD :]
    q_ref[...] = (query * cosine + turn(query, lane) * sine).astype(BF)
    turned = pair * cosine + turn(pair, lane) * sine
    kv_ref[...] = jnp.where(lane < HD, turned, pair).astype(BF)


def project(x_low, x_high, w_pair, cosine, sine, block):
    rows = 2 * x_low.shape[0]
    width = w_pair.shape[0]
    table = pl.BlockSpec((1, block, 2 * HD), lambda i: (i % 2, 0, 0))
    return pl.pallas_call(
        project_kernel,
        grid=(rows // block,),
        in_specs=[
            *half_specs(block, width, rows, lambda i: i),
            whole((width, 4 * HD)),
            table,
            table,
        ],
        out_specs=[pl.BlockSpec((block, 2 * HD), lambda i: (i, 0))] * 2,
        out_shape=[jax.ShapeDtypeStruct((rows, 2 * HD), BF)] * 2,
        cost_estimate=took(6),
        compiler_params=vmem(32),
    )(x_low, x_high, w_pair, cosine, sine)


def head_rows(rows, head, lane, high):
    if (head == 1) != high:
        rows = pltpu.roll(rows, HD, 1)
    keep = (lane >= HD) if high else (lane < HD)
    return jnp.where(keep, rows, jnp.zeros_like(rows))


def masks(info_ref, qseg_ref, kseg, block, span):
    flip = info_ref[0]
    chunk = pl.program_id(1)
    key_at = lax.broadcasted_iota(jnp.int32, (span, 1), 0)
    query_at = lax.broadcasted_iota(jnp.int32, (1, block), 1)
    swapped = jnp.where(flip == 1, key_at ^ block, key_at)
    key_pos = jnp.where(key_at < 2 * block, swapped, -1)
    query_pos = query_at + block * jnp.where(flip == 1, 1 - chunk, chunk)
    return (key_pos <= query_pos) & (kseg == qseg_ref[0])


def load_pairs(refs, tails, kv_all, kv_turned, marks, kseg):
    third = kv_all.shape[0] // 3
    for i, (ref, tail) in enumerate(zip(refs, tails)):
        kv_all[i * third : (i + 1) * third] = ref[...]
        marks[i] = tail[...].astype(F32).reshape(marks.shape[1:])
        columns = marks[i, pl.program_id(0)].T
        for j in range(third // 128):
            at = i * third + j * 128
            kseg[at : at + 128] = columns[:, j : j + 1]
    kv_turned[...] = kv_all[...].T


def attend_kernel(info_ref, q_ref, k0_ref, k1_ref, k2_ref, t0_ref, t1_ref, t2_ref, qseg_ref,
                  w_ref, mix_ref, stat_ref, low_ref, high_ref, kv_all, kv_turned, marks, kseg):
    block = q_ref.shape[0]
    span = kv_all.shape[0]

    @pl.when(pl.program_id(1) == 0)
    def _():
        load_pairs((k0_ref, k1_ref, k2_ref), (t0_ref, t1_ref, t2_ref), kv_all, kv_turned, marks, kseg)

    allowed = masks(info_ref, qseg_ref, kseg[...], block, span)
    lane = lax.broadcasted_iota(jnp.int32, (block, 2 * HD), 1)
    query = q_ref[...] * jnp.asarray(HD**-0.5, BF)
    mixed = []
    for head in range(2):
        scores = dot_nt(kv_all[...], head_rows(query, head, lane, False))
        scores = jnp.where(allowed, scores, NEG_BIG)
        top = jnp.max(scores, axis=0, keepdims=True)
        powers = jnp.exp(scores - top)
        total = jnp.sum(powers, axis=0, keepdims=True)
        stat_ref[0, 0, head : head + 1, :] = top + jnp.log(total)
        probs = (powers * (1.0 / total)).astype(BF)
        mixed.append(dot_nn(kv_turned[...], probs)[HD:])
    mix = jnp.concatenate(mixed, axis=0).T.astype(BF)
    mix_ref[...] = mix
    out = dot_nt(mix, w_ref[...]).astype(BF)
    early = pl.program_id(0) < pl.num_programs(0) // 2

    @pl.when(early)
    def _():
        low_ref[...] = out

    @pl.when(jnp.logical_not(early))
    def _():
        high_ref[...] = out


def attend(info, query, kv, qseg, w_out, block):
    rows = query.shape[0]
    seqs = rows // (2 * block)
    width = w_out.shape[0]
    row_spec = pl.BlockSpec((block, 2 * HD), lambda s, i: (2 * s + i, 0))
    kv_spec = pl.BlockSpec((2 * block, 2 * HD), lambda s, i: (s, 0))
    tail_spec = pl.BlockSpec((8 * seqs, 2 * HD), lambda s, i: (rows // (8 * seqs), 0))
    return pl.pallas_call(
        attend_kernel,
        grid=(seqs, 2),
        in_specs=[
            pl.BlockSpec(memory_space=pltpu.SMEM),
            row_spec,
            kv_spec,
            kv_spec,
            kv_spec,
            tail_spec,
            tail_spec,
            tail_spec,
            pl.BlockSpec((1, 1, block), lambda s, i: (2 * s + i, 0, 0)),
            whole((width, 2 * HD)),
        ],
        out_specs=[
            row_spec,
            pl.BlockSpec((1, 1, 2, block), lambda s, i: (s, i, 0, 0)),
            *half_specs(block, width, rows, lambda s, i: 2 * s + i),
        ],
        out_shape=[
            jax.ShapeDtypeStruct((rows, 2 * HD), BF),
            jax.ShapeDtypeStruct((seqs, 2, 2, block), F32),
            *[jax.ShapeDtypeStruct((rows // 2, width), BF)] * 2,
        ],
        scratch_shapes=[
            pltpu.VMEM((6 * block, 2 * HD), BF),
            pltpu.VMEM((2 * HD, 6 * block), BF),
            pltpu.VMEM((3, seqs, 8, 128), F32),
            pltpu.VMEM((6 * block, 1), F32),
        ],
        cost_estimate=took(24),
        compiler_params=vmem(48),
    )(info, query, *kv, *kv, qseg, w_out)


def attend_back_kernel(info_ref, q_ref, k0_ref, k1_ref, k2_ref, t0_ref, t1_ref, t2_ref, qseg_ref,
                       stat_ref, dy_low, dy_high, mix_ref, w_ref, cos_ref, sin_ref,
                       dq_ref, dk0_ref, dk1_ref, dk2_ref, dw_ref,
                       kv_all, kv_turned, marks, kseg, sums, dw_sum):
    block = q_ref.shape[0]
    span = kv_all.shape[0]
    third = span // 3
    seq = pl.program_id(0)
    chunk = pl.program_id(1)

    @pl.when((chunk == 0) & (seq == 0))
    def _():
        dw_sum[...] = jnp.zeros_like(dw_sum)

    @pl.when(chunk == 0)
    def _():
        sums[...] = jnp.zeros_like(sums)
        load_pairs((k0_ref, k1_ref, k2_ref), (t0_ref, t1_ref, t2_ref), kv_all, kv_turned, marks, kseg)

    allowed = masks(info_ref, qseg_ref, kseg[...], block, span)
    lane = lax.broadcasted_iota(jnp.int32, (block, 2 * HD), 1)
    query = q_ref[...] * jnp.asarray(HD**-0.5, BF)
    grad_rows = choose(seq < pl.num_programs(0) // 2, dy_low, dy_high)
    dw_sum[...] += dot_tn(mix_ref[...], grad_rows)
    grad_mix = dot_nn(grad_rows, w_ref[...]).astype(BF)
    grad_query = []
    for head in range(2):
        q_low = head_rows(query, head, lane, False)
        g_high = head_rows(grad_mix, head, lane, True)
        scores = dot_nt(kv_all[...], q_low)
        stat = stat_ref[0, 0, head : head + 1, :]
        probs = jnp.where(allowed, jnp.exp(scores - stat), 0.0)
        grad_probs = dot_nt(kv_all[...], g_high)
        delta = jnp.sum(probs * grad_probs, axis=0, keepdims=True)
        grad_scores = (probs * (grad_probs - delta)).astype(BF)
        sums[...] += dot_nn(grad_scores, q_low) + dot_nn(probs.astype(BF), g_high)
        grad_query.append(dot_nn(kv_turned[...], grad_scores)[:HD])
    grad_q = jnp.concatenate(grad_query, axis=0).T * HD**-0.5
    dq_ref[...] = (grad_q * cos_ref[0] - turn(grad_q * sin_ref[0], lane)).astype(BF)

    @pl.when(chunk == 1)
    def _():
        dk0_ref[...] = sums[:third]
        dk1_ref[...] = sums[third : 2 * third]
        dk2_ref[...] = sums[2 * third :].astype(BF)

    @pl.when((chunk == 1) & (seq == pl.num_programs(0) - 1))
    def _():
        dw_ref[...] = dw_sum[...].T.astype(BF)


def attend_back(info, query, kv, qseg, stat, grad_rows, mix, w_out, cosine, sine, block):
    rows = query.shape[0]
    seqs = rows // (2 * block)
    width = w_out.shape[0]
    row_spec = pl.BlockSpec((block, 2 * HD), lambda s, i: (2 * s + i, 0))
    kv_spec = pl.BlockSpec((2 * block, 2 * HD), lambda s, i: (s, 0))
    tail_spec = pl.BlockSpec((8 * seqs, 2 * HD), lambda s, i: (rows // (8 * seqs), 0))
    table = pl.BlockSpec((1, block, 2 * HD), lambda s, i: (i, 0, 0))
    return pl.pallas_call(
        attend_back_kernel,
        grid=(seqs, 2),
        in_specs=[
            pl.BlockSpec(memory_space=pltpu.SMEM),
            row_spec,
            kv_spec,
            kv_spec,
            kv_spec,
            tail_spec,
            tail_spec,
            tail_spec,
            pl.BlockSpec((1, 1, block), lambda s, i: (2 * s + i, 0, 0)),
            pl.BlockSpec((1, 1, 2, block), lambda s, i: (s, i, 0, 0)),
            *half_specs(block, width, rows, lambda s, i: 2 * s + i),
            row_spec,
            whole((width, 2 * HD)),
            table,
            table,
        ],
        out_specs=[row_spec, kv_spec, kv_spec, kv_spec, whole((width, 2 * HD))],
        out_shape=[
            jax.ShapeDtypeStruct((rows, 2 * HD), BF),
            jax.ShapeDtypeStruct((rows, 2 * HD), F32),
            jax.ShapeDtypeStruct((rows, 2 * HD), F32),
            jax.ShapeDtypeStruct((rows, 2 * HD), BF),
            jax.ShapeDtypeStruct((width, 2 * HD), BF),
        ],
        scratch_shapes=[
            pltpu.VMEM((6 * block, 2 * HD), BF),
            pltpu.VMEM((2 * HD, 6 * block), BF),
            pltpu.VMEM((3, seqs, 8, 128), F32),
            pltpu.VMEM((6 * block, 1), F32),
            pltpu.VMEM((6 * block, 2 * HD), F32),
            pltpu.VMEM((2 * HD, width), F32),
        ],
        cost_estimate=took(28),
        compiler_params=vmem(56),
    )(info, query, *kv, *kv, qseg, stat, *grad_rows, mix, w_out, cosine, sine)


def project_back_kernel(dq_ref, a_ref, b_ref, x_low, x_high, w_ref, cos_ref, sin_ref, dout_ref,
                        low_ref, high_ref, dw_ref, gain_ref, dw_sum):
    step = pl.program_id(0)

    @pl.when(step == 0)
    def _():
        dw_sum[...] = jnp.zeros_like(dw_sum)
        gain_ref[...] = jnp.zeros_like(gain_ref)

    grad = a_ref[...] + b_ref[...].astype(F32)
    lane = lax.broadcasted_iota(jnp.int32, grad.shape, 1)
    turned = grad * cos_ref[0] - turn(grad * sin_ref[0], lane)
    pair = jnp.where(lane < HD, turned, grad).astype(BF)
    both = jnp.concatenate([dq_ref[...], pair], axis=1)
    grad_in = dot_nt(both, w_ref[...])
    early = step < pl.num_programs(0) // 2

    @pl.when(early)
    def _():
        low_ref[...] = grad_in.astype(BF)

    @pl.when(jnp.logical_not(early))
    def _():
        high_ref[...] = grad_in.astype(BF)

    x_rows = choose(early, x_low, x_high)
    dw_sum[...] += dot_tn(both, x_rows)
    weighted = grad_in * x_rows.astype(F32)
    gain_ref[...] += jnp.sum(weighted.reshape(-1, 8, weighted.shape[1]), axis=0)

    @pl.when(step == pl.num_programs(0) - 1)
    def _():
        dw_ref[:, : 4 * HD] = dw_sum[...].T.astype(BF)
        dw_ref[:, 4 * HD :] = dout_ref[...]


def project_back(grad_q, here, arrived, x_rows, w_pair, cosine, sine, grad_out, block):
    rows = here.shape[0]
    width, cols = w_pair.shape
    spec = pl.BlockSpec((block, 2 * HD), lambda i: (i, 0))
    table = pl.BlockSpec((1, block, 2 * HD), lambda i: (i % 2, 0, 0))
    return pl.pallas_call(
        project_back_kernel,
        grid=(rows // block,),
        in_specs=[
            *[spec] * 3,
            *half_specs(block, width, rows, lambda i: i),
            whole((width, cols)),
            table,
            table,
            whole(grad_out.shape),
        ],
        out_specs=[
            *half_specs(block, width, rows, lambda i: i),
            whole((width, 6 * HD)),
            whole((8, width)),
        ],
        out_shape=[
            *[jax.ShapeDtypeStruct((rows // 2, width), BF)] * 2,
            jax.ShapeDtypeStruct((width, 6 * HD), BF),
            jax.ShapeDtypeStruct((8, width), F32),
        ],
        scratch_shapes=[pltpu.VMEM((cols, width), F32)],
        cost_estimate=took(7),
        compiler_params=vmem(32),
    )(grad_q, here, arrived, *x_rows, w_pair, cosine, sine, grad_out)


def expert_kernel(part, e_low, e_high, g_low, g_high, gate_ref, w_ref,
                  act_ref, low_ref, high_ref, et_ref, gt_ref, e_ref, g_ref):
    rows = e_ref.shape[0]
    early = pl.program_id(0) < pl.num_programs(0) // 2
    e_ref[...] = choose(early, e_low, e_high)
    g_ref[...] = choose(early, g_low, g_high)
    cols = w_ref.shape[1] // 3
    step = 2 * part
    lane = lax.broadcasted_iota(jnp.int32, (rows, step), 1)
    for j in range(cols // step):
        at = j * step
        gate = jnp.where(lane < part, gate_ref[:, 2 * j : 2 * j + 1], gate_ref[:, 2 * j + 1 : 2 * j + 2])
        pre = dot_nn(e_ref[...], w_ref[:, at : at + step])
        up = dot_nn(e_ref[...], w_ref[:, cols + at : cols + at + step])
        grad = dot_nn(g_ref[...], w_ref[:, 2 * cols + at : 2 * cols + at + step]) * gate
        logistic = 1.0 / (1.0 + jnp.exp(-pre))
        active = pre * logistic
        act_ref[:, at : at + step] = (
            grad * up * logistic * (1.0 + pre * (1.0 - logistic))
        ).astype(BF)
        act_ref[:, cols + at : cols + at + step] = (grad * active).astype(BF)
        act_ref[:, 2 * cols + at : 2 * cols + at + step] = (active * up * gate).astype(BF)
    et_ref[...] = e_ref[...].T
    gt_ref[...] = g_ref[...].T
    dx = dot_nt(act_ref[:, : 2 * cols], w_ref[:, : 2 * cols]).astype(BF)

    @pl.when(early)
    def _():
        low_ref[...] = dx

    @pl.when(jnp.logical_not(early))
    def _():
        high_ref[...] = dx


def expert_rows(e_rows, g_rows, gates, weights, part, block):
    rows, width = 2 * e_rows[0].shape[0], e_rows[0].shape[1]
    wide = weights.shape[1]
    return pl.pallas_call(
        lambda *refs: expert_kernel(part, *refs),
        grid=(rows // block,),
        in_specs=[
            *half_specs(block, width, rows, lambda i: i) * 2,
            pl.BlockSpec((block, gates.shape[1]), lambda i: (i, 0)),
            whole(weights.shape),
        ],
        out_specs=[
            pl.BlockSpec((block, wide), lambda i: (i, 0)),
            *half_specs(block, width, rows, lambda i: i),
            *[pl.BlockSpec((width, block), lambda i: (0, i))] * 2,
        ],
        out_shape=[
            jax.ShapeDtypeStruct((rows, wide), BF),
            *[jax.ShapeDtypeStruct((rows // 2, width), BF)] * 2,
            *[jax.ShapeDtypeStruct((width, rows), BF)] * 2,
        ],
        scratch_shapes=[pltpu.VMEM((block, width), BF)] * 2,
        cost_estimate=took(28),
        compiler_params=vmem(56),
    )(*e_rows, *g_rows, gates, weights)


def expert_grad_kernel(e_ref, g_ref, act_ref, out_ref):
    step = pl.program_id(0)
    count = 2 * (pl.num_programs(0) // 3)

    @pl.when(step < count)
    def _():
        out_ref[...] = dot_nn(e_ref[...].reshape(-1, act_ref.shape[0]), act_ref[...]).astype(BF)

    @pl.when(step >= count)
    def _():
        out_ref[...] = dot_nn(g_ref[...].reshape(-1, act_ref.shape[0]), act_ref[...]).astype(BF)


def expert_grads(e_turned, g_turned, act, half, halves, piece, step):
    width, rows = e_turned.shape
    wide = act.shape[1]
    count = width // halves // piece
    spec = pl.BlockSpec((count, 1, piece, rows), lambda i: (0, half, 0, 0))
    split = (count, halves, piece, rows)
    return pl.pallas_call(
        expert_grad_kernel,
        grid=(wide // step,),
        in_specs=[spec, spec, pl.BlockSpec((rows, step), lambda i: (0, i))],
        out_specs=pl.BlockSpec((count * piece, step), lambda i: (0, i)),
        out_shape=jax.ShapeDtypeStruct((count * piece, wide), BF),
        cost_estimate=took(9),
        compiler_params=vmem(48),
    )(e_turned.reshape(split), g_turned.reshape(split), act)


def expert_out_kernel(act_ref, w_ref, low_ref, high_ref):
    out = dot_nt(act_ref[...], w_ref[...]).astype(BF)
    early = pl.program_id(0) < pl.num_programs(0) // 2

    @pl.when(early)
    def _():
        low_ref[...] = out

    @pl.when(jnp.logical_not(early))
    def _():
        high_ref[...] = out


def expert_out(act, weights, block):
    rows, wide = act.shape
    width = weights.shape[0]
    cols = wide // 3
    return pl.pallas_call(
        expert_out_kernel,
        grid=(rows // block,),
        in_specs=[
            pl.BlockSpec((block, cols), lambda i: (i, 2)),
            pl.BlockSpec((width, cols), lambda i: (0, 2)),
        ],
        out_specs=half_specs(block, width, rows, lambda i: i),
        out_shape=[jax.ShapeDtypeStruct((rows // 2, width), BF)] * 2,
        cost_estimate=took(7),
        compiler_params=vmem(48),
    )(act, weights)


def shards(
    tokens,
    segments,
    routes,
    gate_weights,
    cotangent,
    owners,
    masters,
    first_moments,
    second_moments,
    norm_gains,
    gain_first,
    gain_second,
):
    z_index = lax.axis_index("z")
    x_index = lax.axis_index("x")
    w_index = lax.axis_index("y") * 2 + lax.axis_index("c")
    slot_count, row_count, hidden = masters.shape
    slot_total = slot_count * 4
    seg_len = tokens.shape[1]
    width = tokens.shape[2]
    ctx_count = width // row_count
    matrix_count = owners.shape[0]
    experts = (matrix_count - 6) // 3
    group = experts // 2
    part = hidden // 4
    halves = 2 if row_count % 32 == 0 else 1
    piece = row_count // halves
    x_even = x_index == 0
    info = x_index.reshape(1).astype(jnp.int32)

    slot_ids = jnp.arange(slot_total, dtype=jnp.int32)
    hits = owners[None, :] == slot_ids[:, None]
    held = jnp.sum(hits * (jnp.arange(matrix_count, dtype=jnp.int32) + 1)[None, :], axis=1) - 1

    local_at = owners[:6] - slot_count * w_index
    local_ok = (local_at >= 0) & (local_at < slot_count)
    attn_sent = attn_send(masters, jnp.clip(local_at, 0, slot_count - 1), local_ok.astype(jnp.int32))
    bulk = bulk_send(masters, halves)
    attn_got = lax.all_to_all(attn_sent, PLANE, split_axis=0, concat_axis=0, tiled=True)
    attn_got = after(attn_got, *bulk)
    attn_mine = jnp.sum(attn_got.reshape(2, 4, 3, row_count, part).astype(F32), axis=1).astype(BF)
    attn_mine = jnp.transpose(attn_mine, (0, 2, 1, 3)).reshape(2 * row_count, 3 * part)
    attn_w = lax.all_gather(attn_mine, "z", axis=0, tiled=True)
    w_pair = attn_w[:, : 2 * part]
    w_out = attn_w[:, 2 * part :]

    order = np.array([[6 + 3 * (group * g + e) + k for k in range(3) for e in range(group)] for g in range(2)])
    picks = jnp.take(owners, jnp.asarray(order))
    picks_mine = jnp.where(x_even, picks[0], picks[1])
    picks_other = jnp.where(x_even, picks[1], picks[0])
    pieces = []
    arrived = []
    got = attn_got
    for send in bulk:
        got = lax.all_to_all(after(send, got), WSH, split_axis=0, concat_axis=0, tiled=True)
        arrived.append(got)
        keep, give = pick(picks_mine, picks_other, got.reshape(slot_total, piece, part))
        pieces += [keep, swap(give, "x")]
    joined = join(info, pieces)
    expert_w = lax.all_gather(after(joined, attn_w), "z", axis=0, tiled=True)

    gains = norm_gains
    tokens_f = tokens[0].astype(F32)
    cot_low = cotangent[0]
    scale_one = norm_scale(tokens_f)
    attn_in = (tokens_f * scale_one * gains[0]).astype(BF)
    expert_ids = jnp.arange(experts, dtype=jnp.int32)
    gates = jnp.sum(
        jnp.where(routes[0][:, :, None] == expert_ids[None, None, :], gate_weights[0][:, :, None], 0.0),
        axis=1,
    )
    gates_high = gates.astype(BF)
    gates_low = (gates - gates_high.astype(F32)).astype(BF)
    marks = (segments[0] + 1).astype(BF)[:, None]
    spare = jnp.zeros((seg_len, 128 - 2 * experts - 1), BF)
    packed = jnp.concatenate([attn_in, gates_high, gates_low, marks, spare], axis=1)
    packed_all = plane_gather(
        after(packed, attn_got), lambda sent: after(sent, attn_w, arrived[0])
    )
    extras = jnp.concatenate([rows[:, width:] for rows in packed_all], axis=0)
    gates_all = extras[:, :experts].astype(F32) + extras[:, experts : 2 * experts].astype(F32)
    my_gates = jnp.where(x_even, gates_all[:, :group], gates_all[:, group:])
    seqs = 4
    rows_all = seqs * 2 * seg_len
    marks_all = extras[:, 2 * experts].reshape(seqs, -1, 128)
    marks_tail = jnp.pad(marks_all, ((0, 0), (0, 8 - marks_all.shape[1]), (0, 0))).reshape(-1, 128)

    inverse = THETA ** (-(jnp.arange(HD // 2, dtype=F32) * 2.0 / HD))
    at = jnp.arange(seg_len, dtype=jnp.int32)
    first_pos = z_index * 2 * seg_len + x_index * seg_len + at
    second_pos = z_index * 2 * seg_len + (1 - x_index) * seg_len + at
    positions = jnp.stack([first_pos, second_pos])
    angles = positions.astype(F32)[:, :, None] * inverse[None, None, :]
    cosine = jnp.tile(jnp.cos(angles), (1, 1, 4))
    sine = jnp.tile(jnp.sin(angles), (1, 1, 4))

    query, kv_low = project(*packed_all, w_pair, cosine, sine, seg_len)
    kv_zero = jnp.concatenate([kv_low, marks_tail], axis=0)
    g_all = plane_gather(after(cot_low, kv_zero))
    kv_one = shift(kv_zero, 1)
    kv_two = shift(kv_one, 1)
    kv = (kv_zero, kv_one, kv_two)
    qseg = marks_all.astype(F32).reshape(2 * seqs, 1, seg_len)
    attn_mix, stat, out_low, out_high = attend(
        info, after(query, joined), kv, qseg, w_out, seg_len
    )
    resid_one = tokens_f + plane_reduce(out_low, out_high)
    scale_two = norm_scale(resid_one)
    expert_in = (resid_one * scale_two * gains[1]).astype(BF)
    e_all = plane_gather(expert_in)

    act, grad_in_low, grad_in_high, e_turned, g_turned = expert_rows(e_all, g_all, my_gates, expert_w, part, 2 * seg_len)
    parts = []

    def weight_grads(h, then):
        grads = expert_grads(e_turned, g_turned, after(act, then), h, halves, piece, 4 * part)
        parts.append(grads)
        return after(then, grads)

    waits = [None, lambda sent: weight_grads(0, sent), None]
    if halves == 2:
        waits[2] = lambda sent: (weight_grads(1, sent[0]), sent[1])
    grad_expert_in = plane_reduce(grad_in_low, grad_in_high, waits)

    cot_rows = cot_low.astype(F32)
    norm_grad_two = norm_back(resid_one, scale_two, gains[1], grad_expert_in)
    gain_grad_two = jnp.sum(grad_expert_in * resid_one * scale_two, axis=0)
    grad_resid = cot_rows + norm_grad_two
    expert_of = (held - 6) // 3
    kind_of = (held - 6) % 3
    place = jnp.where(held >= 6, kind_of * group + expert_of % group, 0)
    side = jnp.where(held >= 6, (expert_of // group) ^ x_index, 2)

    def pack_slots(total, *first):
        give = lax.dynamic_slice_in_dim(total, (1 - x_index) * piece, piece, axis=0)
        return pack(place, side, info, total, after(swap(give, "x"), *first), part)

    def to_owners(send):
        got = lax.all_to_all(send, WSH, split_axis=0, concat_axis=0, tiled=True)
        return got.reshape(4, slot_count, piece, part)

    sums = [lax.psum_scatter(parts[0], "z", scatter_dimension=0, tiled=True)]
    dy_all = after(plane_gather(grad_resid.astype(BF)), *sums)
    if halves == 2:
        sums.append(lax.psum_scatter(after(parts[1], *sums), "z", scatter_dimension=0, tiled=True))
    grad_q_low, dkv_zero, dkv_one, dkv_two, grad_w_out = attend_back(
        info, query, kv, qseg, stat, dy_all, attn_mix, w_out, cosine, sine, seg_len
    )
    passed_one = shift(dkv_two, -1)
    packs = [pack_slots(sums[0], grad_q_low)]
    slot_grads = [to_owners(packs[0])]
    moe_low, moe_high = expert_out(after(act, grad_q_low, packs[0]), expert_w, 2 * seg_len)
    passed_one = after(passed_one, moe_high, *sums)
    passed = shift((dkv_one + passed_one.astype(F32)).astype(BF), -1)
    resid_two = resid_one + plane_reduce(
        moe_low,
        moe_high,
        (None, lambda sent: after(sent, passed_one), None),
    )
    output = (resid_two.astype(BF))
    if halves == 2:
        packs.append(pack_slots(after(sums[1], slot_grads[0])))
        slot_grads.append(to_owners(packs[1]))
    grad_one_low, grad_one_high, attn_grads, gain_part = project_back(
        grad_q_low, after(dkv_zero, *packs), passed, packed_all, w_pair, cosine, sine, grad_w_out, seg_len
    )
    grad_in_one = plane_reduce(
        grad_one_low, grad_one_high, (None, lambda sent: after(sent, *slot_grads), None)
    )
    gain_grad_one = jnp.sum(gain_part, axis=0) / gains[0]
    norm_grad_one = norm_back(tokens_f, scale_one, gains[0], grad_in_one)
    input_grad = (grad_resid + norm_grad_one)

    attn_sum = lax.psum_scatter(attn_grads, "z", scatter_dimension=0, tiled=True)
    attn_rows = jnp.broadcast_to(
        after(attn_sum, *slot_grads).reshape(2, 1, row_count, 3 * part), (2, 4, row_count, 3 * part)
    ).reshape(8, row_count, 3 * part)
    attn_back = lax.all_to_all(attn_rows, PLANE, split_axis=0, concat_axis=0, tiled=True)

    held_mine = lax.dynamic_slice_in_dim(held, w_index * slot_count, slot_count)
    table = jnp.asarray(np.array([7, 0, 0, 1, 2, 3, 3] + [4, 5, 6] * experts, np.int32))
    rates = jnp.take(jnp.asarray(kind_rates(width, hidden), F32), jnp.take(table, held_mine + 1))
    new_masters, new_first, new_second = update(
        held_mine, rates, attn_back, slot_grads, masters, first_moments, second_moments
    )
    gain_grad = (sum_everywhere(after(jnp.stack([gain_grad_one, gain_grad_two]), attn_sum)))
    new_gains, new_gain_first, new_gain_second = adamw(
        norm_gains, gain_first, gain_second, gain_grad, GAIN_RATE, 0.0
    )
    return (
        output[None],
        input_grad[None],
        new_masters,
        new_first,
        new_second,
        new_gains,
        new_gain_first,
        new_gain_second,
    )


def solution(mesh):
    ctx, wsh = mesh.devices.shape
    fine = Mesh(mesh.devices.reshape(ctx // 2, 2, wsh // 2, 2), ("z", "x", "y", "c"))
    rows = P(WSH, ("z", "x"), None)
    marks = P(WSH, ("z", "x"))
    return jax.shard_map(
        shards,
        mesh=fine,
        in_specs=(rows, marks, rows, rows, rows, P(), rows, rows, rows, P(), P(), P()),
        out_specs=(rows, rows, rows, rows, rows, P(), P(), P()),
        check_vma=False,
    )
```

time: 728 us -> 546 us (0.75)
  Pallas kernels: 71.7 us -> 184 us
  matrix products: 94.2 us -> 0 us
  other arithmetic: 82.4 us -> 23 us
  local copies, waits for them, and re-layouts: 82 us -> 27.4 us
  waiting for transfers between devices: 238 us -> 186 us
  starting transfers between devices: 113 us -> 83.2 us
    pallas_call x2 -> x26, Pallas kernels: 12.9 us -> 126 us  [the longest x1 32.1 us: expert_rows(): pl.pallas_call(lambda *refs: expert_kernel(part, *refs), grid=(rows // bl...]
    dot_general x12 -> x0, matrix products: 94.2 us -> none  [the longest x3 39.7 us: dot_nn(): lax.dot_general(left, right, (((1,), (0,)), ((), ())), preferred_element_...]
    ppermute x6 -> x4, waiting for transfers between devices: 77 us -> 23.3 us  [shift(): return lax.ppermute(value, 'z', pairs)]
    ppermute x6 -> x4, starting transfers between devices: 45.5 us -> 11.6 us  [shift(): return lax.ppermute(value, 'z', pairs)]
    ppermute x45 -> x47, waiting for transfers between devices: 156 us -> 127 us  [swap(): return lax.ppermute(value, axis, [(0, 1), (1, 0)])]
    all_gather x1, waiting for transfers between devices: 0.01 us -> 17.3 us  [shards(): expert_w = lax.all_gather(after(joined, attn_w), 'z', axis=0, tiled=True)]
    concatenate x11 -> x1, other arithmetic: 16.4 us -> 0.04 us  [shards(): kv_zero = jnp.concatenate([kv_low, marks_tail], axis=0)]
    another operation x12 -> x1, other arithmetic: 14.4 us -> 0.01 us  [shards(): jnp.stack([gain_grad_one, gain_grad_two])]
  transfers between devices with their start and end apart: 60 -> 63, of which waited for: 36 -> 38; matrix products, arithmetic and copies ran while one was open for 24% -> 5% of each run, Pallas kernels for 10% -> 25%
where the time goes in v2:
time: 546 us; the launch traced here: 539 us
  waiting for transfers between devices  186 us (34%)
  Pallas kernels  184 us (34%)
  starting transfers between devices  83.2 us (15%)
  local copies, waits for them, and re-layouts  27.4 us (5%)
  other arithmetic  23 us (4%)
  blocking collectives  20.3 us (4%)
  between operations  15.3 us (3%)
    ppermute x47, waiting for transfers between devices, swap(): return lax.ppermute(value, axis, [(0, 1), (1, 0)])  127 us
    ppermute x47, starting transfers between devices, swap(): return lax.ppermute(value, axis, [(0, 1), (1, 0)])  44.7 us
    pallas_call x1, Pallas kernels, expert_rows(): pl.pallas_call(lambda *refs: expert_kernel(part, *refs), grid=(rows // bl...  32.1 us
    pallas_call x1, Pallas kernels, attend_back(): pl.pallas_call(attend_back_kernel, grid=(seqs, 2), in_specs=[pl.BlockSpec...  31.3 us
    pallas_call x1, Pallas kernels, attend(): pl.pallas_call(attend_kernel, grid=(seqs, 2), in_specs=[pl.BlockSpec(memo...  27.1 us
    pallas_call x2, Pallas kernels, expert_grads(): pl.pallas_call(expert_grad_kernel, grid=(wide // step,), in_specs=[spec,...  24.1 us
    ppermute x4, waiting for transfers between devices, shift(): return lax.ppermute(value, 'z', pairs)  23.3 us
    all_gather x1, blocking collectives, shards(): attn_w = lax.all_gather(attn_mine, 'z', axis=0, tiled=True)  20.3 us
  transfers between devices with their start and end apart: 63, of which 38 were waited for; matrix products, arithmetic and copies ran while one was open for 5% of the time, Pallas kernels for 25%

profile of v2, /device:TPU:0, one launch (start us, length us, event | category | flops | bytes accessed | tf_op | source)
XLA Modules:
  0.0 539.2 jit_solution(3424525347345805426)
XLA Ops:
  9.5 3.5 shard_map.206
  13.0 5.1 all-to-all-start
  19.4 4.6 shard_map.207
  24.0 5.7 %all-to-all-done = bf16[8,3,128,128]{3,2,1,0:T(8,128)(2,1)S(1)} async-done(((bf16[8,3,128,128]{3,2,1,0:T(8,128)(2,1)}), bf16[8,3,128,128]{3,2,1,0:T(8,128)(2,1)S(1)}, u32[]{:S(2)}, u32[]{:S(2)}) %all-to-all-start) | async-done | bytes 786464 | tf_op jit(solution)/shard_map/all_to_all | solution.py:910
  29.7 3.5 all-to-all-start.1
  36.3 2.0 collective-permute-start.1
  39.8 20.3 %all_gather.6 = bf16[1024,384]{1,0:T(8,128)(2,1)} all-gather(bf16[256,384]{1,0:T(8,128)(2,1)S(1)} %bitcast.59), channel_id=1, replica_groups=mesh['z'=4,'x'=2,'y'=2,'c'=2] {'z'}, dimensions={0}, use_global_device_ids=true | all-gather | bytes 983040 | tf_op jit(solution)/shard_map/all_gather | solution.py:914
  60.1 3.0 collective-permute-done.1.refs_2_
  65.7 6.7 %collective-permute-done.2.refs_3_ = bf16[128,1152]{1,0:T(8,128)(2,1)S(1)} collective-permute-done((bf16[128,1152]{1,0:T(8,128)(2,1)S(1)}, bf16[128,1152]{1,0:T(8,128)(2,1)S(1)}, u32[]{:S(2)}, u32[]{:S(2)}) %collective-permute-start.2) | collective-permute-done | bytes 294944 | tf_op jit(solution)/shard_map/ppermute | solution.py:30
  73.0 1.7 shard_map.208.low_ref.x_low
  77.0 3.6 all-to-all-start.2
  84.3 6.7 %shard_map.209 = (bf16[2048,128]{1,0:T(8,128)(2,1)S(1)}, bf16[2048,128]{1,0:T(8,128)(2,1)S(1)}) custom-call(bf16[1024,1152]{1,0:T(8,128)(2,1)} %shard_map.208.low_ref.x_low, bf16[1024,1152]{1,0:T(8,128)(2,1)} %collective-permute-done.4.high_ref.x_high, bf16[1024,256]{1,0:T(8,128)(2,1)S(1)} %slice.167.w_ref, f32[2,256,128]{2,1,0:T(8,128)S(1)} %copy.71.cos_ref, ...), custom_call_target="tpu_custom_call" | custom-call | flops 6000000000 | bytes 1048576 | tf_op jit(solution)/shard_map/pallas_call | solution.py:455
  91.1 4.3 collective-permute-start.7
  100.4 6.2 %collective-permute-done.7.k1_ref.t1_ref = bf16[2080,128]{1,0:T(8,128)(2,1)} collective-permute-done((bf16[2080,128]{1,0:T(8,128)(2,1)S(1)}, bf16[2080,128]{1,0:T(8,128)(2,1)}, u32[]{:S(2)}, u32[]{:S(2)}) %collective-permute-start.7) | collective-permute-done | bytes 532512 | tf_op jit(solution)/shard_map/ppermute | solution.py:36
  106.6 4.5 collective-permute-start.8
  112.1 5.4 collective-permute-done.6.refs_3_
  119.2 3.4 collective-permute-done.8.k2_ref.t2_ref
  122.6 27.1 %shard_map.213 = (bf16[2048,128]{1,0:T(8,128)(2,1)S(1)}, f32[4,2,2,256]{3,2,1,0:T(2,128)S(1)}, bf16[1024,1024]{1,0:T(8,128)(2,1)S(1)}, bf16[1024,1024]{1,0:T(8,128)(2,1)}) custom-call(s32[1]{0:T(128)} %bitcast.1.info_ref, bf16[2048,128]{1,0:T(8,128)(2,1)S(1)} %copy-done.31, bf16[2080,128]{1,0:T(8,128)(2,1)S(1)} %pad_maximum_fusion.k0_ref.t0_ref, ...), custom_call_target="tpu_custom_call" | custom-call | flops 24000000000 | bytes 1048576 | tf_op jit(solution)/shard_map/pallas_call | solution.py:544
  149.9 4.4 collective-permute-done.9.got_ref.gx_ref.gy_ref
  157.1 5.7 %collective-permute-done.10.fx_ref = bf16[128,1024]{1,0:T(8,128)(2,1)S(1)} collective-permute-done((bf16[128,1024]{1,0:T(8,128)(2,1)S(1)}, bf16[128,1024]{1,0:T(8,128)(2,1)S(1)}, u32[]{:S(2)}, u32[]{:S(2)}) %collective-permute-start.10) | collective-permute-done | bytes 262176 | tf_op jit(solution)/shard_map/ppermute | solution.py:30
  168.2 10.8 %collective-permute-done.12 = bf16[256,1024]{1,0:T(8,128)(2,1)S(1)} collective-permute-done((bf16[256,1024]{1,0:T(8,128)(2,1)S(1)}, bf16[256,1024]{1,0:T(8,128)(2,1)S(1)}, u32[]{:S(2)}, u32[]{:S(2)}) %collective-permute-start.12) | collective-permute-done | bytes 524320 | tf_op jit(solution)/shard_map/ppermute | solution.py:30
  182.6 7.6 %collective-permute-done.19.refs_1_ = bf16[256,1024]{1,0:T(8,128)(2,1)S(1)} collective-permute-done((bf16[256,1024]{1,0:T(8,128)(2,1)S(1)}, bf16[256,1024]{1,0:T(8,128)(2,1)S(1)}, u32[]{:S(2)}, u32[]{:S(2)}) %collective-permute-start.19) | collective-permute-done | bytes 524320 | tf_op jit(solution)/shard_map/ppermute | solution.py:30
  192.7 8.8 %collective-permute-done.14.refs_1_ = bf16[256,1024]{1,0:T(8,128)(2,1)S(1)} collective-permute-done((bf16[256,1024]{1,0:T(8,128)(2,1)S(1)}, bf16[256,1024]{1,0:T(8,128)(2,1)S(1)}, u32[]{:S(2)}, u32[]{:S(2)}) %collective-permute-start.14) | collective-permute-done | bytes 524320 | tf_op jit(solution)/shard_map/ppermute | solution.py:30
  203.9 4.6 collective-permute-done.21.refs_3_
  208.8 3.1 collective-permute-done.16.refs_3_
  216.5 17.3 %all-gather.2.cloned.1.call-done.refs_5_.w_ref = bf16[1024,3072]{1,0:T(8,128)(2,1)} async-done(((bf16[256,3072]{1,0:T(8,128)(2,1)}), bf16[1024,3072]{1,0:T(8,128)(2,1)}) %all-gather.2.cloned.1.call-update) | async-done | bytes 6291472 | tf_op jit(solution)/shard_map/all_gather | solution.py:931
  233.7 32.1 %shard_map.218 = (bf16[2048,3072]{1,0:T(8,128)(2,1)}, bf16[1024,1024]{1,0:T(8,128)(2,1)}, bf16[1024,1024]{1,0:T(8,128)(2,1)}, bf16[1024,2048]{1,0:T(8,128)(2,1)}, bf16[1024,2048]{1,0:T(8,128)(2,1)}) custom-call(bf16[1024,1024]{1,0:T(8,128)(2,1)} %copy-done.24, bf16[1024,1024]{1,0:T(8,128)(2,1)} %collective-permute-done.18.refs_1_, ...), custom_call_target="tpu_custom_call" | custom-call | flops 28000000000 | bytes 1048576 | tf_op jit(solution)/shard_map/pallas_call | solution.py:786
  266.0 4.3 collective-permute-done.24.got_ref.gx_ref.gy_ref
  270.3 2.3 copy-done
  272.8 11.4 %shard_map.220 = bf16[512,3072]{1,0:T(8,128)(2,1)S(1)} custom-call(bf16[8,2,64,2048]{3,2,1,0:T(8,128)(2,1)} %bitcast.72, bf16[8,2,64,2048]{3,2,1,0:T(8,128)(2,1)} %bitcast.74, bf16[2048,3072]{1,0:T(8,128)(2,1)} %get-tuple-element.110.act_ref), custom_call_target="tpu_custom_call" | custom-call | flops 8999999488 | bytes 1048576 | tf_op jit(solution)/shard_map/pallas_call | solution.py:829
  284.3 1.7 copy-done.8
  289.0 5.4 %collective-permute-done.25.fx_ref = bf16[128,1024]{1,0:T(8,128)(2,1)S(1)} collective-permute-done((bf16[128,1024]{1,0:T(8,128)(2,1)S(1)}, bf16[128,1024]{1,0:T(8,128)(2,1)S(1)}, u32[]{:S(2)}, u32[]{:S(2)}) %collective-permute-start.25) | collective-permute-done | bytes 262176 | tf_op jit(solution)/shard_map/ppermute | solution.py:30
  295.7 1.6 copy-done.3
  298.4 12.6 %shard_map.222 = bf16[512,3072]{1,0:T(8,128)(2,1)} custom-call(bf16[8,2,64,2048]{3,2,1,0:T(8,128)(2,1)} %bitcast.73, bf16[8,2,64,2048]{3,2,1,0:T(8,128)(2,1)} %bitcast.75, bf16[2048,3072]{1,0:T(8,128)(2,1)} %get-tuple-element.110.act_ref), custom_call_target="tpu_custom_call" | custom-call | flops 8999999488 | bytes 1048576 | tf_op jit(solution)/shard_map/pallas_call | solution.py:829
  313.1 11.1 %collective-permute-done.27 = bf16[256,1024]{1,0:T(8,128)(2,1)S(1)} collective-permute-done((bf16[256,1024]{1,0:T(8,128)(2,1)}, bf16[256,1024]{1,0:T(8,128)(2,1)S(1)}, u32[]{:S(2)}, u32[]{:S(2)}) %collective-permute-start.27) | collective-permute-done | bytes 524320 | tf_op jit(solution)/shard_map/ppermute | solution.py:30
  325.1 1.9 multiply_reduce_fusion
  327.0 2.6 fusion.16
  330.9 10.5 %collective-permute-done.29.refs_1_ = bf16[256,1024]{1,0:T(8,128)(2,1)S(1)} collective-permute-done((bf16[256,1024]{1,0:T(8,128)(2,1)S(1)}, bf16[256,1024]{1,0:T(8,128)(2,1)S(1)}, u32[]{:S(2)}, u32[]{:S(2)}) %collective-permute-start.29) | collective-permute-done | bytes 524320 | tf_op jit(solution)/shard_map/ppermute | solution.py:30
  342.4 1.6 collective-permute-start.32
  344.1 3.8 collective-permute-done.31.refs_3_
  349.3 4.0 collective-permute-done.33.dy_high
  353.4 1.6 collective-permute-start.34
  355.0 31.3 %shard_map.224 = (bf16[2048,128]{1,0:T(8,128)(2,1)}, f32[2048,128]{1,0:T(8,128)}, f32[2048,128]{1,0:T(8,128)}, bf16[2048,128]{1,0:T(8,128)(2,1)}, bf16[1024,128]{1,0:T(8,128)(2,1)}) custom-call(s32[1]{0:T(128)} %bitcast.1.info_ref, bf16[2048,128]{1,0:T(8,128)(2,1)} %copy-done.30, bf16[2080,128]{1,0:T(8,128)(2,1)} %copy-done.9, ...), custom_call_target="tpu_custom_call" | custom-call | flops 28000000000 | bytes 1048576 | tf_op jit(solution)/shard_map/pallas_call | solution.py:639
  386.4 4.3 shard_map.225
  390.7 3.7 all-to-all-start.3
  395.7 8.5 %shard_map.226 = (bf16[1024,1024]{1,0:T(8,128)(2,1)S(1)}, bf16[1024,1024]{1,0:T(8,128)(2,1)}) custom-call(bf16[2048,3072]{1,0:T(8,128)(2,1)} %get-tuple-element.110.act_ref, bf16[1024,3072]{1,0:T(8,128)(2,1)} %all-gather.2.cloned.1.call-done.refs_5_.w_ref), custom_call_target="tpu_custom_call" | custom-call | flops 7000000000 | bytes 1048576 | tf_op jit(solution)/shard_map/pallas_call | solution.py:857
  406.0 10.8 %collective-permute-done.36 = bf16[2048,128]{1,0:T(8,128)(2,1)S(1)} collective-permute-done((bf16[2048,128]{1,0:T(8,128)(2,1)S(1)}, bf16[2048,128]{1,0:T(8,128)(2,1)S(1)}, u32[]{:S(2)}, u32[]{:S(2)}) %collective-permute-start.36) | collective-permute-done | bytes 524320 | tf_op jit(solution)/shard_map/ppermute | solution.py:36
  422.6 6.7 %collective-permute-done.41.got_ref = bf16[64,3072]{1,0:T(8,128)(2,1)S(1)} collective-permute-done((bf16[64,3072]{1,0:T(8,128)(2,1)S(1)}, bf16[64,3072]{1,0:T(8,128)(2,1)S(1)}, u32[]{:S(2)}, u32[]{:S(2)}) %collective-permute-start.41) | collective-permute-done | bytes 393248 | tf_op jit(solution)/shard_map/ppermute | solution.py:30
  429.3 4.5 shard_map.229
  433.8 3.0 collective-permute-done.42.b_ref
  436.8 9.4 %shard_map.230 = (bf16[1024,1024]{1,0:T(8,128)(2,1)S(1)}, bf16[1024,1024]{1,0:T(8,128)(2,1)S(1)}, bf16[1024,384]{1,0:T(8,128)(2,1)}, f32[8,1024]{1,0:T(8,128)S(1)}) custom-call(bf16[2048,128]{1,0:T(8,128)(2,1)S(1)} %copy-done.32, f32[2048,128]{1,0:T(8,128)S(1)} %copy-done.29, bf16[2048,128]{1,0:T(8,128)(2,1)S(1)} %collective-permute-done.42.b_ref, ...), custom_call_target="tpu_custom_call" | custom-call | flops 7000000000 | bytes 1048576 | tf_op jit(solution)/shard_map/pallas_call | solution.py:721
  453.5 4.3 all-to-all-start.4
  457.9 12.5 %reduce-scatter.8.cloned.1.call-done = bf16[256,384]{1,0:T(8,128)(2,1)} async-done(((bf16[1024,384]{1,0:T(8,128)(2,1)}), bf16[256,384]{1,0:T(8,128)(2,1)}) %reduce-scatter.8.cloned.1.call-update) | async-done | bytes 196624 | tf_op jit(solution)/shard_map/reduce_scatter | solution.py:1045
  476.8 1.6 copy-done.7
  478.4 2.2 shard_map.228
  484.2 4.2 all-to-all-start.5
  488.5 2.3 collective-permute-start.52
  492.1 1.9 collective-permute-start.44
  495.5 5.7 %collective-permute-done.40 = bf16[256,1024]{1,0:T(8,128)(2,1)} collective-permute-done((bf16[256,1024]{1,0:T(8,128)(2,1)S(1)}, bf16[256,1024]{1,0:T(8,128)(2,1)}, u32[]{:S(2)}, u32[]{:S(2)}) %collective-permute-start.40) | collective-permute-done | bytes 524320 | tf_op jit(solution)/shard_map/ppermute | solution.py:30
  501.3 2.6 fusion.10
  504.5 3.9 collective-permute-done.44.fx_ref
  511.5 15.6 %shard_map.233 = (f32[20,128,512]{2,1,0:T(8,128)}, f32[20,128,512]{2,1,0:T(8,128)}, f32[20,128,512]{2,1,0:T(8,128)}) custom-call(s32[20]{0:T(128)} %copy-done.70, f32[20]{0:T(128)} %and_select_fusion.refs_1_, bf16[8,128,384]{2,1,0:T(8,128)(2,1)} %all-to-all-done.5.refs_2_, bf16[4,20,64,128]{3,2,1,0:T(8,128)(2,1)} %bitcast.54, ...), custom_call_target="tpu_custom_call" | custom-call | flops 12000000000 | bytes 1048576 | tf_op jit(solution)/shard_map/pallas_call | solution.py:427
  527.1 2.0 fusion.7
  529.2 3.0 fusion.6
  (326 shorter events, 91.7 us)
Async XLA Ops:
  13.0 16.7 %all-to-all-start = ((bf16[8,3,128,128]{3,2,1,0:T(8,128)(2,1)}), bf16[8,3,128,128]{3,2,1,0:T(8,128)(2,1)S(1)}, u32[]{:S(2)}, u32[]{:S(2)}) async-start(bf16[8,3,128,128]{3,2,1,0:T(8,128)(2,1)} %shard_map.206), calls=%async_computation | async-start | bytes 1572864 | tf_op jit(solution)/shard_map/all_to_all | solution.py:910
  29.7 34.2 %all-to-all-start.1 = ((bf16[4,20,64,128]{3,2,1,0:T(8,128)(2,1)}), bf16[4,20,64,128]{3,2,1,0:T(8,128)(2,1)S(1)}, u32[]{:S(2)}, u32[]{:S(2)}) async-start(bf16[4,20,64,128]{3,2,1,0:T(8,128)(2,1)} %get-tuple-element.76), calls=%async_computation.1 | async-start | bytes 2621440 | tf_op jit(solution)/shard_map/all_to_all | solution.py:926
  34.8 25.3 %collective-permute-start = (bf16[256,1152]{1,0:T(8,128)(2,1)S(1)}, bf16[256,1152]{1,0:T(8,128)(2,1)S(1)}, u32[]{:S(2)}, u32[]{:S(2)}) collective-permute-start(bf16[256,1152]{1,0:T(8,128)(2,1)S(1)} %concatenate.13.refs_0_), channel_id=1, source_target_pairs={{0,4},{4,0},{1,5},{5,1},{2,6},{6,2},{3,7},{7,3},{8,12},{12,8},{9,1... | collective-permute-start | bytes 1769480 | tf_op jit(solution)/shard_map/ppermute | solution.py:30
  36.3 26.8 %collective-permute-start.1 = (bf16[256,1152]{1,0:T(8,128)(2,1)S(1)}, bf16[256,1152]{1,0:T(8,128)(2,1)S(1)}, u32[]{:S(2)}, u32[]{:S(2)}) collective-permute-start(bf16[256,1152]{1,0:T(8,128)(2,1)S(1)} %concatenate.13.refs_0_), channel_id=1, source_target_pairs={{0,2},{2,0},{1,3},{3,1},{4,6},{6,4},{5,7},{7,5},{8,10},{10,8},{9,1... | collective-permute-start | bytes 1769480 | tf_op jit(solution)/shard_map/ppermute | solution.py:30
  63.9 8.6 %collective-permute-start.2 = (bf16[128,1152]{1,0:T(8,128)(2,1)S(1)}, bf16[128,1152]{1,0:T(8,128)(2,1)S(1)}, u32[]{:S(2)}, u32[]{:S(2)}) collective-permute-start(bf16[128,1152]{1,0:T(8,128)(2,1)S(1)} %slice.165), channel_id=1, source_target_pairs={{0,2},{2,0},{1,3},{3,1},{4,6},{6,4},{5,7},{7,5},{8,10},{10,8},{9,1... | collective-permute-start | bytes 884744 | tf_op jit(solution)/shard_map/ppermute | solution.py:30
  64.2 8.8 %collective-permute-start.3 = (bf16[128,1152]{1,0:T(8,128)(2,1)}, bf16[128,1152]{1,0:T(8,128)(2,1)S(1)}, u32[]{:S(2)}, u32[]{:S(2)}) collective-permute-start(bf16[128,1152]{1,0:T(8,128)(2,1)} %slice.166), channel_id=1, source_target_pairs={{0,4},{4,0},{1,5},{5,1},{2,6},{6,2},{3,7},{7,3},{8,12},{12,8},{9,1... | collective-permute-start | bytes 884744 | tf_op jit(solution)/shard_map/ppermute | solution.py:30
  74.7 6.9 %collective-permute-start.4 = (bf16[1024,1152]{1,0:T(8,128)(2,1)}, bf16[1024,1152]{1,0:T(8,128)(2,1)}, u32[]{:S(2)}, u32[]{:S(2)}) collective-permute-start(bf16[1024,1152]{1,0:T(8,128)(2,1)} %shard_map.208.low_ref.x_low), channel_id=1, source_target_pairs={{0,1},{1,0},{2,3},{3,2},{4,5},{5,4},{6,7},{7,6},{8,9},{9,8},{10,11... | collective-permute-start | bytes 7077896 | tf_op jit(solution)/shard_map/ppermute | solution.py:30
  77.0 22.1 %all-to-all-start.2 = ((bf16[4,20,64,128]{3,2,1,0:T(8,128)(2,1)}), bf16[4,20,64,128]{3,2,1,0:T(8,128)(2,1)S(1)}, u32[]{:S(2)}, u32[]{:S(2)}) async-start(bf16[4,20,64,128]{3,2,1,0:T(8,128)(2,1)} %get-tuple-element.82), calls=%async_computation.2 | async-start | bytes 2621440 | tf_op jit(solution)/shard_map/all_to_all | solution.py:926
  80.6 153.2 %all-gather.2.cloned.1.call-start = ((), (), s32[]{:S(2)}) async-start(), calls=%async_computation.9 | async-start | bytes 7864320 | tf_op jit(solution)/shard_map/all_gather | solution.py:931
  91.1 15.5 %collective-permute-start.7 = (bf16[2080,128]{1,0:T(8,128)(2,1)S(1)}, bf16[2080,128]{1,0:T(8,128)(2,1)}, u32[]{:S(2)}, u32[]{:S(2)}) collective-permute-start(bf16[2080,128]{1,0:T(8,128)(2,1)S(1)} %pad_maximum_fusion.k0_ref.t0_ref), channel_id=1, source_target_pairs={{0,8},{8,16},{16,24},{1,9},{9,17},{17,25},{2,10},{10,18},{18,26},{... | collective-permute-start | bytes 1597448 | tf_op jit(solution)/shard_map/ppermute | solution.py:36
  97.6 14.5 %collective-permute-start.5 = (bf16[64,3072]{1,0:T(8,128)(2,1)}, bf16[64,3072]{1,0:T(8,128)(2,1)S(1)}, u32[]{:S(2)}, u32[]{:S(2)}) collective-permute-start(bf16[64,3072]{1,0:T(8,128)(2,1)} %get-tuple-element.81), channel_id=1, source_target_pairs={{0,4},{4,0},{1,5},{5,1},{2,6},{6,2},{3,7},{7,3},{8,12},{12,8},{9,1... | collective-permute-start | bytes 1179656 | tf_op jit(solution)/shard_map/ppermute | solution.py:30
  99.8 17.7 %collective-permute-start.6 = (bf16[64,3072]{1,0:T(8,128)(2,1)S(1)}, bf16[64,3072]{1,0:T(8,128)(2,1)S(1)}, u32[]{:S(2)}, u32[]{:S(2)}) collective-permute-start(bf16[64,3072]{1,0:T(8,128)(2,1)S(1)} %get-tuple-element.84), channel_id=1, source_target_pairs={{0,4},{4,0},{1,5},{5,1},{2,6},{6,2},{3,7},{7,3},{8,12},{12,8},{9,1... | collective-permute-start | bytes 1179656 | tf_op jit(solution)/shard_map/ppermute | solution.py:30
  106.6 16.0 %collective-permute-start.8 = (bf16[2080,128]{1,0:T(8,128)(2,1)}, bf16[2080,128]{1,0:T(8,128)(2,1)S(1)}, u32[]{:S(2)}, u32[]{:S(2)}) collective-permute-start(bf16[2080,128]{1,0:T(8,128)(2,1)} %collective-permute-done.7.k1_ref.t1_ref), channel_id=1, source_target_pairs={{0,8},{8,16},{16,24},{1,9},{9,17},{17,25},{2,10},{10,18},{18,26},{... | collective-permute-start | bytes 1597448 | tf_op jit(solution)/shard_map/ppermute | solution.py:36
  118.7 230.4 %reduce-scatter.4.cloned.1.call-start = ((), (), s32[]{:S(2)}) async-start(), calls=%async_computation.10 | async-start | bytes 3932160 | tf_op jit(solution)/shard_map/reduce_scatter | solution.py:1013
  149.8 4.4 collective-permute-start.9
  154.4 8.4 %collective-permute-start.10 = (bf16[128,1024]{1,0:T(8,128)(2,1)S(1)}, bf16[128,1024]{1,0:T(8,128)(2,1)S(1)}, u32[]{:S(2)}, u32[]{:S(2)}) collective-permute-start(bf16[128,1024]{1,0:T(8,128)(2,1)S(1)} %get-tuple-element.155), channel_id=1, source_target_pairs={{0,2},{2,0},{1,3},{3,1},{4,6},{6,4},{5,7},{7,5},{8,10},{10,8},{9,1... | collective-permute-start | bytes 786440 | tf_op jit(solution)/shard_map/ppermute | solution.py:30
  155.7 8.1 %collective-permute-start.11 = (bf16[128,1024]{1,0:T(8,128)(2,1)S(1)}, bf16[128,1024]{1,0:T(8,128)(2,1)S(1)}, u32[]{:S(2)}, u32[]{:S(2)}) collective-permute-start(bf16[128,1024]{1,0:T(8,128)(2,1)S(1)} %get-tuple-element.154), channel_id=1, source_target_pairs={{0,4},{4,0},{1,5},{5,1},{2,6},{6,2},{3,7},{7,3},{8,12},{12,8},{9,1... | collective-permute-start | bytes 786440 | tf_op jit(solution)/shard_map/ppermute | solution.py:30
  164.1 14.9 %collective-permute-start.12 = (bf16[256,1024]{1,0:T(8,128)(2,1)S(1)}, bf16[256,1024]{1,0:T(8,128)(2,1)S(1)}, u32[]{:S(2)}, u32[]{:S(2)}) collective-permute-start(bf16[256,1024]{1,0:T(8,128)(2,1)S(1)} %get-tuple-element.89), channel_id=1, source_target_pairs={{0,4},{4,0},{1,5},{5,1},{2,6},{6,2},{3,7},{7,3},{8,12},{12,8},{9,1... | collective-permute-start | bytes 1572872 | tf_op jit(solution)/shard_map/ppermute | solution.py:30
  165.6 14.9 %collective-permute-start.13 = (bf16[256,1024]{1,0:T(8,128)(2,1)S(1)}, bf16[256,1024]{1,0:T(8,128)(2,1)S(1)}, u32[]{:S(2)}, u32[]{:S(2)}) collective-permute-start(bf16[256,1024]{1,0:T(8,128)(2,1)S(1)} %get-tuple-element.90), channel_id=1, source_target_pairs={{0,2},{2,0},{1,3},{3,1},{4,6},{6,4},{5,7},{7,5},{8,10},{10,8},{9,1... | collective-permute-start | bytes 1572872 | tf_op jit(solution)/shard_map/ppermute | solution.py:30
  166.4 23.8 %collective-permute-start.19 = (bf16[256,1024]{1,0:T(8,128)(2,1)S(1)}, bf16[256,1024]{1,0:T(8,128)(2,1)S(1)}, u32[]{:S(2)}, u32[]{:S(2)}) collective-permute-start(bf16[256,1024]{1,0:T(8,128)(2,1)S(1)} %bitcast.48), channel_id=1, source_target_pairs={{0,4},{4,0},{1,5},{5,1},{2,6},{6,2},{3,7},{7,3},{8,12},{12,8},{9,1... | collective-permute-start | bytes 1572872 | tf_op jit(solution)/shard_map/ppermute | solution.py:30
  167.0 24.7 %collective-permute-start.20 = (bf16[256,1024]{1,0:T(8,128)(2,1)S(1)}, bf16[256,1024]{1,0:T(8,128)(2,1)S(1)}, u32[]{:S(2)}, u32[]{:S(2)}) collective-permute-start(bf16[256,1024]{1,0:T(8,128)(2,1)S(1)} %bitcast.49), channel_id=1, source_target_pairs={{0,2},{2,0},{1,3},{3,1},{4,6},{6,4},{5,7},{7,5},{8,10},{10,8},{9,1... | collective-permute-start | bytes 1572872 | tf_op jit(solution)/shard_map/ppermute | solution.py:30
  181.1 20.3 %collective-permute-start.14 = (bf16[256,1024]{1,0:T(8,128)(2,1)S(1)}, bf16[256,1024]{1,0:T(8,128)(2,1)S(1)}, u32[]{:S(2)}, u32[]{:S(2)}) collective-permute-start(bf16[256,1024]{1,0:T(8,128)(2,1)S(1)} %multiply_convert_fusion.refs_0_), channel_id=1, source_target_pairs={{0,4},{4,0},{1,5},{5,1},{2,6},{6,2},{3,7},{7,3},{8,12},{12,8},{9,1... | collective-permute-start | bytes 1572872 | tf_op jit(solution)/shard_map/ppermute | solution.py:30
  181.8 21.1 %collective-permute-start.15 = (bf16[256,1024]{1,0:T(8,128)(2,1)S(1)}, bf16[256,1024]{1,0:T(8,128)(2,1)S(1)}, u32[]{:S(2)}, u32[]{:S(2)}) collective-permute-start(bf16[256,1024]{1,0:T(8,128)(2,1)S(1)} %multiply_convert_fusion.refs_0_), channel_id=1, source_target_pairs={{0,2},{2,0},{1,3},{3,1},{4,6},{6,4},{5,7},{7,5},{8,10},{10,8},{9,1... | collective-permute-start | bytes 1572872 | tf_op jit(solution)/shard_map/ppermute | solution.py:30
  190.2 18.3 %collective-permute-start.21 = (bf16[128,1024]{1,0:T(8,128)(2,1)S(1)}, bf16[128,1024]{1,0:T(8,128)(2,1)S(1)}, u32[]{:S(2)}, u32[]{:S(2)}) collective-permute-start(bf16[128,1024]{1,0:T(8,128)(2,1)S(1)} %slice.178), channel_id=1, source_target_pairs={{0,2},{2,0},{1,3},{3,1},{4,6},{6,4},{5,7},{7,5},{8,10},{10,8},{9,1... | collective-permute-start | bytes 786440 | tf_op jit(solution)/shard_map/ppermute | solution.py:30
  191.7 16.8 %collective-permute-start.22 = (bf16[128,1024]{1,0:T(8,128)(2,1)S(1)}, bf16[128,1024]{1,0:T(8,128)(2,1)S(1)}, u32[]{:S(2)}, u32[]{:S(2)}) collective-permute-start(bf16[128,1024]{1,0:T(8,128)(2,1)S(1)} %slice.179), channel_id=1, source_target_pairs={{0,4},{4,0},{1,5},{5,1},{2,6},{6,2},{3,7},{7,3},{8,12},{12,8},{9,1... | collective-permute-start | bytes 786440 | tf_op jit(solution)/shard_map/ppermute | solution.py:30
  201.5 10.4 %collective-permute-start.16 = (bf16[128,1024]{1,0:T(8,128)(2,1)S(1)}, bf16[128,1024]{1,0:T(8,128)(2,1)S(1)}, u32[]{:S(2)}, u32[]{:S(2)}) collective-permute-start(bf16[128,1024]{1,0:T(8,128)(2,1)S(1)} %slice.176), channel_id=1, source_target_pairs={{0,2},{2,0},{1,3},{3,1},{4,6},{6,4},{5,7},{7,5},{8,10},{10,8},{9,1... | collective-permute-start | bytes 786440 | tf_op jit(solution)/shard_map/ppermute | solution.py:30
  202.9 9.0 %collective-permute-start.17 = (bf16[128,1024]{1,0:T(8,128)(2,1)S(1)}, bf16[128,1024]{1,0:T(8,128)(2,1)S(1)}, u32[]{:S(2)}, u32[]{:S(2)}) collective-permute-start(bf16[128,1024]{1,0:T(8,128)(2,1)S(1)} %slice.177), channel_id=1, source_target_pairs={{0,4},{4,0},{1,5},{5,1},{2,6},{6,2},{3,7},{7,3},{8,12},{12,8},{9,1... | collective-permute-start | bytes 786440 | tf_op jit(solution)/shard_map/ppermute | solution.py:30
  208.7 5.1 collective-permute-start.23
  212.1 4.4 collective-permute-start.18
  265.9 4.4 collective-permute-start.24
  286.0 130.8 %reduce-scatter.6.cloned.1.call-start = ((), (), s32[]{:S(2)}) async-start(), calls=%async_computation.11 | async-start | bytes 3932160 | tf_op jit(solution)/shard_map/reduce_scatter | solution.py:1016
  286.1 8.4 %collective-permute-start.25 = (bf16[128,1024]{1,0:T(8,128)(2,1)S(1)}, bf16[128,1024]{1,0:T(8,128)(2,1)S(1)}, u32[]{:S(2)}, u32[]{:S(2)}) collective-permute-start(bf16[128,1024]{1,0:T(8,128)(2,1)S(1)} %get-tuple-element.153), channel_id=1, source_target_pairs={{0,2},{2,0},{1,3},{3,1},{4,6},{6,4},{5,7},{7,5},{8,10},{10,8},{9,1... | collective-permute-start | bytes 786440 | tf_op jit(solution)/shard_map/ppermute | solution.py:30
  287.6 8.1 %collective-permute-start.26 = (bf16[128,1024]{1,0:T(8,128)(2,1)S(1)}, bf16[128,1024]{1,0:T(8,128)(2,1)S(1)}, u32[]{:S(2)}, u32[]{:S(2)}) collective-permute-start(bf16[128,1024]{1,0:T(8,128)(2,1)S(1)} %get-tuple-element.152), channel_id=1, source_target_pairs={{0,4},{4,0},{1,5},{5,1},{2,6},{6,2},{3,7},{7,3},{8,12},{12,8},{9,1... | collective-permute-start | bytes 786440 | tf_op jit(solution)/shard_map/ppermute | solution.py:30
  311.0 13.1 %collective-permute-start.27 = (bf16[256,1024]{1,0:T(8,128)(2,1)}, bf16[256,1024]{1,0:T(8,128)(2,1)S(1)}, u32[]{:S(2)}, u32[]{:S(2)}) collective-permute-start(bf16[256,1024]{1,0:T(8,128)(2,1)} %copy-done.26), channel_id=1, source_target_pairs={{0,4},{4,0},{1,5},{5,1},{2,6},{6,2},{3,7},{7,3},{8,12},{12,8},{9,1... | collective-permute-start | bytes 1572872 | tf_op jit(solution)/shard_map/ppermute | solution.py:30
  312.4 12.6 %collective-permute-start.28 = (bf16[256,1024]{1,0:T(8,128)(2,1)S(1)}, bf16[256,1024]{1,0:T(8,128)(2,1)S(1)}, u32[]{:S(2)}, u32[]{:S(2)}) collective-permute-start(bf16[256,1024]{1,0:T(8,128)(2,1)S(1)} %get-tuple-element.104), channel_id=1, source_target_pairs={{0,2},{2,0},{1,3},{3,1},{4,6},{6,4},{5,7},{7,5},{8,10},{10,8},{9,1... | collective-permute-start | bytes 1572872 | tf_op jit(solution)/shard_map/ppermute | solution.py:30
  329.5 11.8 %collective-permute-start.29 = (bf16[256,1024]{1,0:T(8,128)(2,1)S(1)}, bf16[256,1024]{1,0:T(8,128)(2,1)S(1)}, u32[]{:S(2)}, u32[]{:S(2)}) collective-permute-start(bf16[256,1024]{1,0:T(8,128)(2,1)S(1)} %get-tuple-element.144.refs_0_), channel_id=1, source_target_pairs={{0,4},{4,0},{1,5},{5,1},{2,6},{6,2},{3,7},{7,3},{8,12},{12,8},{9,1... | collective-permute-start | bytes 1572872 | tf_op jit(solution)/shard_map/ppermute | solution.py:30
  330.1 12.3 %collective-permute-start.30 = (bf16[256,1024]{1,0:T(8,128)(2,1)S(1)}, bf16[256,1024]{1,0:T(8,128)(2,1)S(1)}, u32[]{:S(2)}, u32[]{:S(2)}) collective-permute-start(bf16[256,1024]{1,0:T(8,128)(2,1)S(1)} %get-tuple-element.144.refs_0_), channel_id=1, source_target_pairs={{0,2},{2,0},{1,3},{3,1},{4,6},{6,4},{5,7},{7,5},{8,10},{10,8},{9,1... | collective-permute-start | bytes 1572872 | tf_op jit(solution)/shard_map/ppermute | solution.py:30
  341.4 6.4 %collective-permute-start.31 = (bf16[128,1024]{1,0:T(8,128)(2,1)S(1)}, bf16[128,1024]{1,0:T(8,128)(2,1)S(1)}, u32[]{:S(2)}, u32[]{:S(2)}) collective-permute-start(bf16[128,1024]{1,0:T(8,128)(2,1)S(1)} %slice.185), channel_id=1, source_target_pairs={{0,2},{2,0},{1,3},{3,1},{4,6},{6,4},{5,7},{7,5},{8,10},{10,8},{9,1... | collective-permute-start | bytes 786440 | tf_op jit(solution)/shard_map/ppermute | solution.py:30
  342.4 6.4 %collective-permute-start.32 = (bf16[128,1024]{1,0:T(8,128)(2,1)S(1)}, bf16[128,1024]{1,0:T(8,128)(2,1)S(1)}, u32[]{:S(2)}, u32[]{:S(2)}) collective-permute-start(bf16[128,1024]{1,0:T(8,128)(2,1)S(1)} %slice.186), channel_id=1, source_target_pairs={{0,4},{4,0},{1,5},{5,1},{2,6},{6,2},{3,7},{7,3},{8,12},{12,8},{9,1... | collective-permute-start | bytes 786440 | tf_op jit(solution)/shard_map/ppermute | solution.py:30
  349.0 4.4 collective-permute-start.33
  353.4 33.0 %collective-permute-start.34 = (bf16[64,3072]{1,0:T(8,128)(2,1)S(1)}, bf16[64,3072]{1,0:T(8,128)(2,1)S(1)}, u32[]{:S(2)}, u32[]{:S(2)}) collective-permute-start(bf16[64,3072]{1,0:T(8,128)(2,1)S(1)} %constant_dynamic-slice_fusion.1), channel_id=1, source_target_pairs={{0,4},{4,0},{1,5},{5,1},{2,6},{6,2},{3,7},{7,3},{8,12},{12,8},{9,1... | collective-permute-start | bytes 1179656 | tf_op jit(solution)/shard_map/ppermute | solution.py:30
  390.7 26.1 %all-to-all-start.3 = ((bf16[80,64,128]{2,1,0:T(8,128)(2,1)}), bf16[80,64,128]{2,1,0:T(8,128)(2,1)S(1)}, u32[]{:S(2)}, u32[]{:S(2)}) async-start(bf16[80,64,128]{2,1,0:T(8,128)(2,1)} %shard_map.225), calls=%async_computation.5 | async-start | bytes 2621440 | tf_op jit(solution)/shard_map/all_to_all | solution.py:1010
  394.4 76.1 %reduce-scatter.8.cloned.1.call-start = ((), (), s32[]{:S(2)}) async-start(), calls=%async_computation.12 | async-start | bytes 983040 | tf_op jit(solution)/shard_map/reduce_scatter | solution.py:1045
  394.4 22.3 %collective-permute-start.36 = (bf16[2048,128]{1,0:T(8,128)(2,1)S(1)}, bf16[2048,128]{1,0:T(8,128)(2,1)S(1)}, u32[]{:S(2)}, u32[]{:S(2)}) collective-permute-start(bf16[2048,128]{1,0:T(8,128)(2,1)S(1)} %copy-done.72), channel_id=1, source_target_pairs={{8,0},{16,8},{24,16},{9,1},{17,9},{25,17},{10,2},{18,10},{26,18},{... | collective-permute-start | bytes 1572872 | tf_op jit(solution)/shard_map/ppermute | solution.py:36
  405.6 42.9 %collective-permute-start.35 = (bf16[1024,1024]{1,0:T(8,128)(2,1)}, bf16[1024,1024]{1,0:T(8,128)(2,1)}, u32[]{:S(2)}, u32[]{:S(2)}) collective-permute-start(bf16[1024,1024]{1,0:T(8,128)(2,1)} %get-tuple-element.112), channel_id=1, source_target_pairs={{0,1},{1,0},{2,3},{3,2},{4,5},{5,4},{6,7},{7,6},{8,9},{9,8},{10,11... | collective-permute-start | bytes 6291464 | tf_op jit(solution)/shard_map/ppermute | solution.py:30
  418.1 11.2 %collective-permute-start.41 = (bf16[64,3072]{1,0:T(8,128)(2,1)S(1)}, bf16[64,3072]{1,0:T(8,128)(2,1)S(1)}, u32[]{:S(2)}, u32[]{:S(2)}) collective-permute-start(bf16[64,3072]{1,0:T(8,128)(2,1)S(1)} %constant_dynamic-slice_fusion), channel_id=1, source_target_pairs={{0,4},{4,0},{1,5},{5,1},{2,6},{6,2},{3,7},{7,3},{8,12},{12,8},{9,1... | collective-permute-start | bytes 1179656 | tf_op jit(solution)/shard_map/ppermute | solution.py:30
  421.1 15.7 %collective-permute-start.42 = (bf16[2048,128]{1,0:T(8,128)(2,1)S(1)}, bf16[2048,128]{1,0:T(8,128)(2,1)S(1)}, u32[]{:S(2)}, u32[]{:S(2)}) collective-permute-start(bf16[2048,128]{1,0:T(8,128)(2,1)S(1)} %add_convert_fusion), channel_id=1, source_target_pairs={{8,0},{16,8},{24,16},{9,1},{17,9},{25,17},{10,2},{18,10},{26,18},{... | collective-permute-start | bytes 1572872 | tf_op jit(solution)/shard_map/ppermute | solution.py:36
  447.6 60.8 %copy-start.4 = (bf16[1024,1024]{1,0:T(8,128)(2,1)}, bf16[1024,1024]{1,0:T(8,128)(2,1)S(1)}, u32[]{:S(2)}) copy-start(bf16[1024,1024]{1,0:T(8,128)(2,1)S(1)} %get-tuple-element.124.kept_ref.kx_ref.ky_ref) | copy-start | bytes 6291460
  447.6 43.2 %collective-permute-start.43 = (bf16[1024,1024]{1,0:T(8,128)(2,1)}, bf16[1024,1024]{1,0:T(8,128)(2,1)}, u32[]{:S(2)}, u32[]{:S(2)}) collective-permute-start(bf16[1024,1024]{1,0:T(8,128)(2,1)} %copy-done.21), channel_id=1, source_target_pairs={{0,1},{1,0},{2,3},{3,2},{4,5},{5,4},{6,7},{7,6},{8,9},{9,8},{10,11... | collective-permute-start | bytes 6291464 | tf_op jit(solution)/shard_map/ppermute | solution.py:30
  451.3 25.5 %collective-permute-start.37 = (bf16[128,1024]{1,0:T(8,128)(2,1)S(1)}, bf16[128,1024]{1,0:T(8,128)(2,1)S(1)}, u32[]{:S(2)}, u32[]{:S(2)}) collective-permute-start(bf16[128,1024]{1,0:T(8,128)(2,1)S(1)} %get-tuple-element.151), channel_id=1, source_target_pairs={{0,2},{2,0},{1,3},{3,1},{4,6},{6,4},{5,7},{7,5},{8,10},{10,8},{9,1... | collective-permute-start | bytes 786440 | tf_op jit(solution)/shard_map/ppermute | solution.py:30
  452.8 24.0 %collective-permute-start.38 = (bf16[128,1024]{1,0:T(8,128)(2,1)S(1)}, bf16[128,1024]{1,0:T(8,128)(2,1)S(1)}, u32[]{:S(2)}, u32[]{:S(2)}) collective-permute-start(bf16[128,1024]{1,0:T(8,128)(2,1)S(1)} %get-tuple-element.150), channel_id=1, source_target_pairs={{0,4},{4,0},{1,5},{5,1},{2,6},{6,2},{3,7},{7,3},{8,12},{12,8},{9,1... | collective-permute-start | bytes 786440 | tf_op jit(solution)/shard_map/ppermute | solution.py:30
  453.5 29.7 %all-to-all-start.4 = ((bf16[80,64,128]{2,1,0:T(8,128)(2,1)}), bf16[80,64,128]{2,1,0:T(8,128)(2,1)}, u32[]{:S(2)}, u32[]{:S(2)}) async-start(bf16[80,64,128]{2,1,0:T(8,128)(2,1)} %shard_map.229), calls=%async_computation.6 | async-start | bytes 2621440 | tf_op jit(solution)/shard_map/all_to_all | solution.py:1010
  470.5 1.2 collective-permute-start.48
  471.6 3.7 collective-permute-start.49
  475.3 7.3 %collective-permute-start.50 = (f32[2,1024]{1,0:T(2,128)S(1)}, f32[2,1024]{1,0:T(2,128)S(1)}, u32[]{:S(2)}, u32[]{:S(2)}) collective-permute-start(f32[2,1024]{1,0:T(2,128)S(1)} %add.274), channel_id=1, source_target_pairs={{0,2},{2,0},{1,3},{3,1},{4,6},{6,4},{5,7},{7,5},{8,10},{10,8},{9,1... | collective-permute-start | bytes 24584 | tf_op jit(solution)/shard_map/ppermute | solution.py:30
  480.6 14.9 %collective-permute-start.39 = (bf16[256,1024]{1,0:T(8,128)(2,1)}, bf16[256,1024]{1,0:T(8,128)(2,1)S(1)}, u32[]{:S(2)}, u32[]{:S(2)}) collective-permute-start(bf16[256,1024]{1,0:T(8,128)(2,1)} %get-tuple-element.117), channel_id=1, source_target_pairs={{0,4},{4,0},{1,5},{5,1},{2,6},{6,2},{3,7},{7,3},{8,12},{12,8},{9,1... | collective-permute-start | bytes 1572872 | tf_op jit(solution)/shard_map/ppermute | solution.py:30
  482.1 19.2 %collective-permute-start.40 = (bf16[256,1024]{1,0:T(8,128)(2,1)S(1)}, bf16[256,1024]{1,0:T(8,128)(2,1)}, u32[]{:S(2)}, u32[]{:S(2)}) collective-permute-start(bf16[256,1024]{1,0:T(8,128)(2,1)S(1)} %get-tuple-element.118), channel_id=1, source_target_pairs={{0,2},{2,0},{1,3},{3,1},{4,6},{6,4},{5,7},{7,5},{8,10},{10,8},{9,1... | collective-permute-start | bytes 1572872 | tf_op jit(solution)/shard_map/ppermute | solution.py:30
  482.6 5.8 %collective-permute-start.51 = (f32[2,1024]{1,0:T(2,128)S(1)}, f32[2,1024]{1,0:T(2,128)S(1)}, u32[]{:S(2)}, u32[]{:S(2)}) collective-permute-start(f32[2,1024]{1,0:T(2,128)S(1)} %add.275), channel_id=1, source_target_pairs={{0,8},{8,0},{16,24},{24,16},{1,9},{9,1},{17,25},{25,17},{2,10},{10... | collective-permute-start | bytes 24584 | tf_op jit(solution)/shard_map/ppermute | solution.py:156
  484.2 27.3 %all-to-all-start.5 = ((bf16[8,128,384]{2,1,0:T(8,128)(2,1)}), bf16[8,128,384]{2,1,0:T(8,128)(2,1)}, u32[]{:S(2)}, u32[]{:S(2)}) async-start(bf16[8,128,384]{2,1,0:T(8,128)(2,1)} %bitcast.53), calls=%async_computation.8 | async-start | bytes 1572864 | tf_op jit(solution)/shard_map/all_to_all | solution.py:1049
  488.5 15.4 %collective-permute-start.52 = (f32[2,1024]{1,0:T(2,128)S(1)}, f32[2,1024]{1,0:T(2,128)S(1)}, u32[]{:S(2)}, u32[]{:S(2)}) collective-permute-start(f32[2,1024]{1,0:T(2,128)S(1)} %add.276), channel_id=1, source_target_pairs={{0,16},{8,24},{16,0},{24,8},{1,17},{9,25},{17,1},{25,9},{2,18},{10... | collective-permute-start | bytes 24584 | tf_op jit(solution)/shard_map/ppermute | solution.py:156
  492.1 16.3 %collective-permute-start.44 = (bf16[128,1024]{1,0:T(8,128)(2,1)S(1)}, bf16[128,1024]{1,0:T(8,128)(2,1)S(1)}, u32[]{:S(2)}, u32[]{:S(2)}) collective-permute-start(bf16[128,1024]{1,0:T(8,128)(2,1)S(1)} %get-tuple-element.149), channel_id=1, source_target_pairs={{0,2},{2,0},{1,3},{3,1},{4,6},{6,4},{5,7},{7,5},{8,10},{10,8},{9,1... | collective-permute-start | bytes 786440 | tf_op jit(solution)/shard_map/ppermute | solution.py:30
  494.0 14.4 %collective-permute-start.45 = (bf16[128,1024]{1,0:T(8,128)(2,1)S(1)}, bf16[128,1024]{1,0:T(8,128)(2,1)S(1)}, u32[]{:S(2)}, u32[]{:S(2)}) collective-permute-start(bf16[128,1024]{1,0:T(8,128)(2,1)S(1)} %get-tuple-element.148), channel_id=1, source_target_pairs={{0,4},{4,0},{1,5},{5,1},{2,6},{6,2},{3,7},{7,3},{8,12},{12,8},{9,1... | collective-permute-start | bytes 786440 | tf_op jit(solution)/shard_map/ppermute | solution.py:30
  509.9 17.2 %collective-permute-start.46 = (bf16[256,1024]{1,0:T(8,128)(2,1)S(1)}, bf16[256,1024]{1,0:T(8,128)(2,1)}, u32[]{:S(2)}, u32[]{:S(2)}) collective-permute-start(bf16[256,1024]{1,0:T(8,128)(2,1)S(1)} %get-tuple-element.127), channel_id=1, source_target_pairs={{0,4},{4,0},{1,5},{5,1},{2,6},{6,2},{3,7},{7,3},{8,12},{12,8},{9,1... | collective-permute-start | bytes 1572872 | tf_op jit(solution)/shard_map/ppermute | solution.py:30
  510.5 16.6 %collective-permute-start.47 = (bf16[256,1024]{1,0:T(8,128)(2,1)S(1)}, bf16[256,1024]{1,0:T(8,128)(2,1)}, u32[]{:S(2)}, u32[]{:S(2)}) collective-permute-start(bf16[256,1024]{1,0:T(8,128)(2,1)S(1)} %get-tuple-element.128), channel_id=1, source_target_pairs={{0,2},{2,0},{1,3},{3,1},{4,6},{6,4},{5,7},{7,5},{8,10},{10,8},{9,1... | collective-permute-start | bytes 1572872 | tf_op jit(solution)/shard_map/ppermute | solution.py:30
  (72 other events, 611.1 us)
Sparse Core Ops, SparseCore 0:
  118.9 114.8 all-gather.1
  286.1 58.4 reduce-scatter.3
  349.3 63.7 reduce-scatter.5
  447.7 22.6 reduce-scatter.7

commit v3 on v2

--- a/solution.py
+++ b/solution.py
@@ -54,6 +54,10 @@
     return [low, high]
 
 
+def together(*values):
+    return lax.optimization_barrier(values)
+
+
 def after(value, *first):
     return lax.optimization_barrier((value, *first))[0]
 
@@ -102,7 +106,7 @@
         in_specs=[spec, spec],
         out_specs=whole((rows // 4, width)),
         out_shape=jax.ShapeDtypeStruct((rows // 4, width), BF),
-        cost_estimate=took(2),
+        cost_estimate=took(1),
         compiler_params=vmem(32),
     )(kept, got)
 
@@ -143,19 +147,6 @@
     to_x, to_y = hold[2](edge_rows(kept, got, for_x, for_y))
     own = kept[:step].astype(F32) + got[:step].astype(F32)
     return own + swap(to_x, "x").astype(F32) + swap(to_y, "y").astype(F32)
-
-
-def sum_everywhere(value):
-    for axis in ("c", "x", "y"):
-        value = value + swap(value, axis)
-    count = lax.axis_size("z")
-    if count & (count - 1):
-        return lax.psum(value, "z")
-    stride = 1
-    while stride < count:
-        value = value + lax.ppermute(value, "z", [(i, i ^ stride) for i in range(count)])
-        stride *= 2
-    return value
 
 
 def norm_scale(values):
@@ -251,107 +242,119 @@
     )(at, ok, *([masters] * 6))
 
 
-def bulk_send_kernel(in_ref, *outs):
-    part = outs[0].shape[3]
-    rows = outs[0].shape[2]
-    for h, out_ref in enumerate(outs):
-        for j in range(4):
-            piece = in_ref[:, h * rows : (h + 1) * rows, j * part : (j + 1) * part]
-            out_ref[j] = piece.astype(BF)
-
-
-def bulk_send(masters, halves):
+def bulk_send_kernel(info_ref, in_ref, *outs):
+    part = outs[0].shape[2]
+    for d, out_ref in enumerate(outs):
+        start = pl.multiple_of((info_ref[1] ^ d) * part, part)
+        out_ref[...] = in_ref[:, :, pl.ds(start, part)].astype(BF)
+
+
+def bulk_send(info, masters):
     slots, rows, hidden = masters.shape
-    step, part, piece = 5 if slots % 5 == 0 else 1, hidden // 4, rows // halves
+    step, part = 5 if slots % 5 == 0 else 1, hidden // 4
     return pl.pallas_call(
         bulk_send_kernel,
         grid=(slots // step,),
-        in_specs=[pl.BlockSpec((step, rows, hidden), lambda i: (i, 0, 0))],
-        out_specs=[pl.BlockSpec((4, step, piece, part), lambda i: (0, i, 0, 0))] * halves,
-        out_shape=[jax.ShapeDtypeStruct((4, slots, piece, part), BF)] * halves,
+        in_specs=[
+            pl.BlockSpec(memory_space=pltpu.SMEM),
+            pl.BlockSpec((step, rows, hidden), lambda i: (i, 0, 0)),
+        ],
+        out_specs=[pl.BlockSpec((step, rows, part), lambda i: (i, 0, 0))] * 4,
+        out_shape=[jax.ShapeDtypeStruct((slots, rows, part), BF)] * 4,
         cost_estimate=took(4),
         compiler_params=vmem(62),
-    )(masters)
-
-
-def pick_kernel(mine_ref, other_ref, in_ref, keep_ref, give_ref):
-    part = in_ref.shape[2]
-    for k in range(keep_ref.shape[1] // part):
-        keep_ref[:, k * part : (k + 1) * part] = in_ref[mine_ref[k]]
-        give_ref[:, k * part : (k + 1) * part] = in_ref[other_ref[k]]
-
-
-def pick(mine, other, slots):
-    total, rows, part = slots.shape
-    count = mine.shape[0]
-    wide = (rows, count * part)
+    )(info, masters)
+
+
+def over_wsh(arrays):
+    across = [(i, i ^ 3) for i in range(4)]
+    return [arrays[0], swap(arrays[1], "c"), swap(arrays[2], "y"), lax.ppermute(arrays[3], WSH, across)]
+
+
+def pick_kernel(at_ref, *refs):
+    slots, outs, held = refs[:4], refs[4:-1], refs[-1]
+    count = slots[0].shape[0]
+    part = held.shape[2]
+    for d in range(4):
+        held[d * count : (d + 1) * count] = slots[d][...]
+    for i, out_ref in enumerate(outs):
+        number = out_ref.shape[1] // part
+        for k in range(number):
+            out_ref[:, k * part : (k + 1) * part] = held[at_ref[i * number + k]]
+
+
+def pick(places, slots, parts):
+    count, rows, part = slots[0].shape
+    wide = (rows, places.shape[0] // parts * part)
     return pl.pallas_call(
         pick_kernel,
         grid_spec=pltpu.PrefetchScalarGridSpec(
-            num_scalar_prefetch=2,
+            num_scalar_prefetch=1,
             grid=(1,),
-            in_specs=[pl.BlockSpec((total, rows, part), lambda i, a, b: (0, 0, 0))],
-            out_specs=[pl.BlockSpec(wide, lambda i, a, b: (0, 0))] * 2,
+            in_specs=[pl.BlockSpec((count, rows, part), lambda i, a: (0, 0, 0))] * 4,
+            out_specs=[pl.BlockSpec(wide, lambda i, a: (0, 0))] * parts,
+            scratch_shapes=[pltpu.VMEM((4 * count, rows, part), BF)],
         ),
-        out_shape=[jax.ShapeDtypeStruct(wide, BF)] * 2,
+        out_shape=[jax.ShapeDtypeStruct(wide, BF)] * parts,
         cost_estimate=took(3),
-        compiler_params=vmem(32),
-    )(mine, other, slots)
+        compiler_params=vmem(62),
+    )(places, *slots)
 
 
 def join_kernel(info_ref, *refs):
-    out_ref = refs[-1]
-    rows = refs[0].shape[0]
-    half = out_ref.shape[0] // 2
+    count = len(refs) // 2
+    keeps, gots, out_ref = refs[:count], refs[count:-1], refs[-1]
+    rows, wide = keeps[0].shape
     first = info_ref[0] == 0
-    for h in range(len(refs) // 2):
-        keep, got = refs[2 * h][...], refs[2 * h + 1][...]
-        out_ref[h * rows : (h + 1) * rows] = jnp.where(first, keep, got)
-        out_ref[half + h * rows : half + (h + 1) * rows] = jnp.where(first, got, keep)
-
-
-def join(info, pieces):
-    rows, wide = pieces[0].shape
-    total = rows * len(pieces)
+    for i in range(count):
+        keep, got, lanes = keeps[i][...], gots[i][...], slice(i * wide, (i + 1) * wide)
+        out_ref[:rows, lanes] = jnp.where(first, keep, got)
+        out_ref[rows:, lanes] = jnp.where(first, got, keep)
+
+
+def join(info, keeps, gots):
+    rows, wide = keeps[0].shape
+    shape = (2 * rows, wide * len(keeps))
     return pl.pallas_call(
         join_kernel,
         grid=(1,),
-        in_specs=[pl.BlockSpec(memory_space=pltpu.SMEM)] + [whole((rows, wide))] * len(pieces),
-        out_specs=whole((total, wide)),
-        out_shape=jax.ShapeDtypeStruct((total, wide), BF),
-        cost_estimate=took(2),
+        in_specs=[pl.BlockSpec(memory_space=pltpu.SMEM)] + [whole((rows, wide))] * (2 * len(keeps)),
+        out_specs=whole(shape),
+        out_shape=jax.ShapeDtypeStruct(shape, BF),
+        cost_estimate=took(1.5),
         compiler_params=vmem(32),
-    )(info, *pieces)
-
-
-def pack_kernel(place_ref, side_ref, info_ref, total_ref, got_ref, out_ref):
-    part = out_ref.shape[2]
-    rows = out_ref.shape[1]
+    )(info, *keeps, *gots)
+
+
+def pack_kernel(place_ref, side_ref, info_ref, total_ref, got_ref, *outs):
+    count, rows, part = outs[0].shape
     mine = pl.ds(pl.multiple_of(info_ref[0] * rows, rows), rows)
-
-    def one(s, carry):
-        start = pl.multiple_of(place_ref[s] * part, part)
-
-        @pl.when(side_ref[s] == 0)
-        def _():
-            out_ref[s] = total_ref[mine, pl.ds(start, part)]
-
-        @pl.when(side_ref[s] == 1)
-        def _():
-            out_ref[s] = got_ref[:, pl.ds(start, part)]
-
-        @pl.when(side_ref[s] == 2)
-        def _():
-            out_ref[s] = jnp.zeros((rows, part), BF)
-
-        return carry
-
-    lax.fori_loop(0, out_ref.shape[0], one, 0)
+    for d, out_ref in enumerate(outs):
+
+        def one(j, carry):
+            s = (info_ref[1] ^ d) * count + j
+            lanes = pl.ds(pl.multiple_of(place_ref[s] * part, part), part)
+
+            @pl.when(side_ref[s] == 0)
+            def _():
+                out_ref[j] = total_ref[mine, lanes]
+
+            @pl.when(side_ref[s] == 1)
+            def _():
+                out_ref[j] = got_ref[:, lanes]
+
+            @pl.when(side_ref[s] == 2)
+            def _():
+                out_ref[j] = jnp.zeros((rows, part), BF)
+
+            return carry
+
+        lax.fori_loop(0, count, one, 0)
 
 
 def pack(place, side, info, summed, got, part):
     rows, wide = got.shape
-    total = place.shape[0]
+    shape = (place.shape[0] // 4, rows, part)
     return pl.pallas_call(
         pack_kernel,
         grid_spec=pltpu.PrefetchScalarGridSpec(
@@ -361,78 +364,110 @@
                 pl.BlockSpec((2 * rows, wide), lambda i, a, b, c: (0, 0)),
                 pl.BlockSpec((rows, wide), lambda i, a, b, c: (0, 0)),
             ],
-            out_specs=pl.BlockSpec((total, rows, part), lambda i, a, b, c: (0, 0, 0)),
+            out_specs=[pl.BlockSpec(shape, lambda i, a, b, c: (0, 0, 0))] * 4,
         ),
-        out_shape=jax.ShapeDtypeStruct((total, rows, part), BF),
-        cost_estimate=took(3),
+        out_shape=[jax.ShapeDtypeStruct(shape, BF)] * 4,
+        cost_estimate=took(4),
         compiler_params=vmem(32),
     )(place, side, info, summed, got)
 
 
-def update_kernel(halves, held_ref, rate_ref, attn_ref, *refs):
-    grads, (w_ref, m_ref, v_ref, w_out, m_out, v_out) = refs[:halves], refs[halves:]
-    part = grads[0].shape[3]
-    rows = grads[0].shape[2]
-    everything = slice(0, halves * rows)
+def update_kernel(info_ref, rate_ref, *refs):
+    grads, (w_ref, m_ref, v_ref, w_out, m_out, v_out) = refs[:-6], refs[-6:]
+    part = grads[0].shape[2]
+    rows = grads[0].shape[1]
 
     def one(s, carry):
-        slot = pl.program_id(0) * w_ref.shape[0] + s
-        held = held_ref[slot]
-        rate = rate_ref[slot]
-
-        def write(at, lanes, grad):
-            new_w, new_m, new_v = adamw(
-                w_ref[s, at, lanes], m_ref[s, at, lanes], v_ref[s, at, lanes], grad, rate, DECAY
+        rate = rate_ref[pl.program_id(0) * w_ref.shape[0] + s]
+        for i, grad_ref in enumerate(grads):
+            lanes = pl.ds(pl.multiple_of((info_ref[1] ^ (i % 4)) * part, part), part)
+            at = slice((i // 4) * rows, (i // 4 + 1) * rows)
+            w_out[s, at, lanes], m_out[s, at, lanes], v_out[s, at, lanes] = adamw(
+                w_ref[s, at, lanes],
+                m_ref[s, at, lanes],
+                v_ref[s, at, lanes],
+                grad_ref[s].astype(F32),
+                rate,
+                DECAY,
             )
-            w_out[s, at, lanes] = new_w
-            m_out[s, at, lanes] = new_m
-            v_out[s, at, lanes] = new_v
-
-        @pl.when((held < 0) | (held >= 6))
-        def _():
-            for h in range(halves):
-                for j in range(4):
-                    at, lanes = slice(h * rows, (h + 1) * rows), slice(j * part, (j + 1) * part)
-                    write(at, lanes, grads[h][j, s].astype(F32))
-
-        for m, side, kind in ((0, 0, 0), (1, 1, 0), (4, 0, 2), (5, 1, 2)):
-
-            @pl.when(held == m)
-            def _():
-                for j in range(4):
-                    grad = attn_ref[4 * side + j, :, kind * part : (kind + 1) * part]
-                    write(everything, slice(j * part, (j + 1) * part), grad.astype(F32))
-
-        for m, start in ((2, part), (3, part + HD)):
-
-            @pl.when(held == m)
-            def _():
-                for j in range(4):
-                    pieces = [attn_ref[2 * j + i, :, start : start + HD] for i in range(2)]
-                    grad = jnp.concatenate(pieces, axis=1)
-                    write(everything, slice(j * part, (j + 1) * part), grad.astype(F32))
-
         return carry
 
     lax.fori_loop(0, w_ref.shape[0], one, 0)
 
 
-def update(held, rates, attn_back, grads, masters, first, second):
+def update(info, rates, grads, masters, first, second):
     slots, rows, hidden = masters.shape
-    halves = len(grads)
     step = 4 if slots % 4 == 0 else 1
     smem = pl.BlockSpec(memory_space=pltpu.SMEM)
     spec = pl.BlockSpec((step, rows, hidden), lambda i: (i, 0, 0))
-    grad_spec = pl.BlockSpec((4, step, rows // halves, hidden // 4), lambda i: (0, i, 0, 0))
-    return pl.pallas_call(
-        lambda *refs: update_kernel(halves, *refs),
+    grad_spec = pl.BlockSpec((step, *grads[0].shape[1:]), lambda i: (i, 0, 0))
+    return pl.pallas_call(
+        update_kernel,
         grid=(slots // step,),
-        in_specs=[smem, smem, whole(attn_back.shape)] + [grad_spec] * halves + [spec] * 3,
+        in_specs=[smem, smem] + [grad_spec] * len(grads) + [spec] * 3,
         out_specs=[spec] * 3,
         out_shape=[jax.ShapeDtypeStruct(masters.shape, F32)] * 3,
-        cost_estimate=took(12),
+        cost_estimate=took(14),
         compiler_params=vmem(62),
-    )(held, rates, attn_back, *grads, masters, first, second)
+    )(info, rates, *grads, masters, first, second)
+
+
+def update_attn_kernel(slot_ref, held_ref, rate_ref, attn_ref, *refs):
+    (w_ref, m_ref, v_ref), olds, news = refs[:3], refs[3:6], refs[6:]
+    step = pl.program_id(0)
+    held = held_ref[step]
+    rate = rate_ref[step]
+    part = w_ref.shape[2] // 4
+
+    def write(j, grad):
+        lanes = slice(j * part, (j + 1) * part)
+        results = adamw(
+            w_ref[0, :, lanes], m_ref[0, :, lanes], v_ref[0, :, lanes], grad.astype(F32), rate, DECAY
+        )
+        for new_ref, result in zip(news, results):
+            new_ref[0, :, lanes] = result
+
+    @pl.when(held < 0)
+    def _():
+        for old_ref, new_ref in zip(olds, news):
+            new_ref[...] = old_ref[...]
+
+    for m, side, kind in ((0, 0, 0), (1, 1, 0), (4, 0, 2), (5, 1, 2)):
+
+        @pl.when(held == m)
+        def _():
+            for j in range(4):
+                write(j, attn_ref[4 * side + j, :, kind * part : (kind + 1) * part])
+
+    for m, start in ((2, part), (3, part + HD)):
+
+        @pl.when(held == m)
+        def _():
+            for j in range(4):
+                pieces = [attn_ref[2 * j + i, :, start : start + HD] for i in range(2)]
+                write(j, jnp.concatenate(pieces, axis=1))
+
+
+def update_attn(slots, held, rates, attn_back, masters, first, second, new):
+    _, rows, hidden = masters.shape
+    spec = pl.BlockSpec((1, rows, hidden), lambda i, at, held: (at[i], 0, 0))
+    return pl.pallas_call(
+        update_attn_kernel,
+        grid_spec=pltpu.PrefetchScalarGridSpec(
+            num_scalar_prefetch=2,
+            grid=(slots.shape[0],),
+            in_specs=[
+                pl.BlockSpec(memory_space=pltpu.SMEM),
+                pl.BlockSpec(attn_back.shape, lambda i, at, held: (0, 0, 0)),
+                *[spec] * 6,
+            ],
+            out_specs=[spec] * 3,
+        ),
+        out_shape=[jax.ShapeDtypeStruct(masters.shape, F32)] * 3,
+        input_output_aliases={7: 0, 8: 1, 9: 2},
+        cost_estimate=took(5),
+        compiler_params=vmem(62),
+    )(slots, held, rates, attn_back, masters, first, second, *new)
 
 
 def project_kernel(low_ref, high_ref, w_ref, cos_ref, sin_ref, q_ref, kv_ref):
@@ -448,16 +483,16 @@
     kv_ref[...] = jnp.where(lane < HD, turned, pair).astype(BF)
 
 
-def project(x_low, x_high, w_pair, cosine, sine, block):
+def project(x_low, x_high, weights, cosine, sine, block):
     rows = 2 * x_low.shape[0]
-    width = w_pair.shape[0]
+    width = weights.shape[0]
     table = pl.BlockSpec((1, block, 2 * HD), lambda i: (i % 2, 0, 0))
     return pl.pallas_call(
         project_kernel,
         grid=(rows // block,),
         in_specs=[
             *half_specs(block, width, rows, lambda i: i),
-            whole((width, 4 * HD)),
+            pl.BlockSpec((width, 4 * HD), lambda i: (0, 0)),
             table,
             table,
         ],
@@ -465,7 +500,7 @@
         out_shape=[jax.ShapeDtypeStruct((rows, 2 * HD), BF)] * 2,
         cost_estimate=took(6),
         compiler_params=vmem(32),
-    )(x_low, x_high, w_pair, cosine, sine)
+    )(x_low, x_high, weights, cosine, sine)
 
 
 def head_rows(rows, head, lane, high):
@@ -534,10 +569,10 @@
         high_ref[...] = out
 
 
-def attend(info, query, kv, qseg, w_out, block):
+def attend(info, query, kv, qseg, weights, block):
     rows = query.shape[0]
     seqs = rows // (2 * block)
-    width = w_out.shape[0]
+    width = weights.shape[0]
     row_spec = pl.BlockSpec((block, 2 * HD), lambda s, i: (2 * s + i, 0))
     kv_spec = pl.BlockSpec((2 * block, 2 * HD), lambda s, i: (s, 0))
     tail_spec = pl.BlockSpec((8 * seqs, 2 * HD), lambda s, i: (rows // (8 * seqs), 0))
@@ -554,7 +589,7 @@
             tail_spec,
             tail_spec,
             pl.BlockSpec((1, 1, block), lambda s, i: (2 * s + i, 0, 0)),
-            whole((width, 2 * HD)),
+            pl.BlockSpec((width, 2 * HD), lambda s, i: (0, 2)),
         ],
         out_specs=[
             row_spec,
@@ -573,8 +608,8 @@
             pltpu.VMEM((6 * block, 1), F32),
         ],
         cost_estimate=took(24),
-        compiler_params=vmem(48),
-    )(info, query, *kv, *kv, qseg, w_out)
+        compiler_params=vmem(62),
+    )(info, query, *kv, *kv, qseg, weights)
 
 
 def attend_back_kernel(info_ref, q_ref, k0_ref, k1_ref, k2_ref, t0_ref, t1_ref, t2_ref, qseg_ref,
@@ -628,10 +663,10 @@
         dw_ref[...] = dw_sum[...].T.astype(BF)
 
 
-def attend_back(info, query, kv, qseg, stat, grad_rows, mix, w_out, cosine, sine, block):
+def attend_back(info, query, kv, qseg, stat, grad_rows, mix, weights, cosine, sine, block):
     rows = query.shape[0]
     seqs = rows // (2 * block)
-    width = w_out.shape[0]
+    width = weights.shape[0]
     row_spec = pl.BlockSpec((block, 2 * HD), lambda s, i: (2 * s + i, 0))
     kv_spec = pl.BlockSpec((2 * block, 2 * HD), lambda s, i: (s, 0))
     tail_spec = pl.BlockSpec((8 * seqs, 2 * HD), lambda s, i: (rows // (8 * seqs), 0))
@@ -652,7 +687,7 @@
             pl.BlockSpec((1, 1, 2, block), lambda s, i: (s, i, 0, 0)),
             *half_specs(block, width, rows, lambda s, i: 2 * s + i),
             row_spec,
-            whole((width, 2 * HD)),
+            pl.BlockSpec((width, 2 * HD), lambda s, i: (0, 2)),
             table,
             table,
         ],
@@ -673,8 +708,8 @@
             pltpu.VMEM((2 * HD, width), F32),
         ],
         cost_estimate=took(28),
-        compiler_params=vmem(56),
-    )(info, query, *kv, *kv, qseg, stat, *grad_rows, mix, w_out, cosine, sine)
+        compiler_params=vmem(62),
+    )(info, query, *kv, *kv, qseg, stat, *grad_rows, mix, weights, cosine, sine)
 
 
 def project_back_kernel(dq_ref, a_ref, b_ref, x_low, x_high, w_ref, cos_ref, sin_ref, dout_ref,
@@ -713,9 +748,9 @@
         dw_ref[:, 4 * HD :] = dout_ref[...]
 
 
-def project_back(grad_q, here, arrived, x_rows, w_pair, cosine, sine, grad_out, block):
+def project_back(grad_q, here, arrived, x_rows, weights, cosine, sine, grad_out, block):
     rows = here.shape[0]
-    width, cols = w_pair.shape
+    width, cols = weights.shape[0], 4 * HD
     spec = pl.BlockSpec((block, 2 * HD), lambda i: (i, 0))
     table = pl.BlockSpec((1, block, 2 * HD), lambda i: (i % 2, 0, 0))
     return pl.pallas_call(
@@ -724,7 +759,7 @@
         in_specs=[
             *[spec] * 3,
             *half_specs(block, width, rows, lambda i: i),
-            whole((width, cols)),
+            pl.BlockSpec((width, cols), lambda i: (0, 0)),
             table,
             table,
             whole(grad_out.shape),
@@ -740,15 +775,18 @@
             jax.ShapeDtypeStruct((8, width), F32),
         ],
         scratch_shapes=[pltpu.VMEM((cols, width), F32)],
-        cost_estimate=took(7),
-        compiler_params=vmem(32),
-    )(grad_q, here, arrived, *x_rows, w_pair, cosine, sine, grad_out)
-
-
-def expert_kernel(part, e_low, e_high, g_low, g_high, gate_ref, w_ref,
-                  act_ref, low_ref, high_ref, et_ref, gt_ref, e_ref, g_ref):
-    rows = e_ref.shape[0]
-    early = pl.program_id(0) < pl.num_programs(0) // 2
+        cost_estimate=took(10),
+        compiler_params=vmem(62),
+    )(grad_q, here, arrived, *x_rows, weights, cosine, sine, grad_out)
+
+
+def expert_kernel(part, piece, halves, e_low, e_high, g_low, g_high, gate_ref, w_ref, *refs):
+    low_ref, high_ref, hidden_ref = refs[:3]
+    grads, (e_ref, g_ref, act_ref, sums) = refs[3 : 3 + halves], refs[3 + halves :]
+    rows, width = e_ref.shape
+    step_id = pl.program_id(0)
+    last = pl.num_programs(0) - 1
+    early = step_id < pl.num_programs(0) // 2
     e_ref[...] = choose(early, e_low, e_high)
     g_ref[...] = choose(early, g_low, g_high)
     cols = w_ref.shape[1] // 3
@@ -767,8 +805,7 @@
         ).astype(BF)
         act_ref[:, cols + at : cols + at + step] = (grad * active).astype(BF)
         act_ref[:, 2 * cols + at : 2 * cols + at + step] = (active * up * gate).astype(BF)
-    et_ref[...] = e_ref[...].T
-    gt_ref[...] = g_ref[...].T
+    hidden_ref[...] = act_ref[:, 2 * cols :]
     dx = dot_nt(act_ref[:, : 2 * cols], w_ref[:, : 2 * cols]).astype(BF)
 
     @pl.when(early)
@@ -779,62 +816,63 @@
     def _():
         high_ref[...] = dx
 
-
-def expert_rows(e_rows, g_rows, gates, weights, part, block):
+    e_turned = e_ref[...].T
+    g_turned = g_ref[...].T
+    chunk = 2 * step
+
+    @pl.when(step_id == 0)
+    def _():
+        for at in range(0, 3 * cols, chunk):
+            left = e_turned if at < 2 * cols else g_turned
+            sums[:, at : at + chunk] = dot_nn(left, act_ref[:, at : at + chunk])
+
+    @pl.when((step_id > 0) & (step_id < last))
+    def _():
+        for at in range(0, 3 * cols, chunk):
+            left = e_turned if at < 2 * cols else g_turned
+            sums[:, at : at + chunk] += dot_nn(left, act_ref[:, at : at + chunk])
+
+    @pl.when(step_id == last)
+    def _():
+        for at in range(0, 3 * cols, chunk):
+            left = e_turned if at < 2 * cols else g_turned
+            total = (sums[:, at : at + chunk] + dot_nn(left, act_ref[:, at : at + chunk])).astype(BF)
+            for i in range(width // piece):
+                out_ref = grads[i % halves]
+                to = (i // halves) * piece
+                out_ref[to : to + piece, at : at + chunk] = total[i * piece : (i + 1) * piece]
+
+
+def expert_rows(e_rows, g_rows, gates, weights, part, piece, halves, block):
     rows, width = 2 * e_rows[0].shape[0], e_rows[0].shape[1]
     wide = weights.shape[1]
-    return pl.pallas_call(
-        lambda *refs: expert_kernel(part, *refs),
+    once = pl.Buffered(1)
+    return pl.pallas_call(
+        lambda *refs: expert_kernel(part, piece, halves, *refs),
         grid=(rows // block,),
         in_specs=[
             *half_specs(block, width, rows, lambda i: i) * 2,
             pl.BlockSpec((block, gates.shape[1]), lambda i: (i, 0)),
-            whole(weights.shape),
+            pl.BlockSpec(weights.shape, lambda i: (0, 0), pipeline_mode=once),
         ],
         out_specs=[
-            pl.BlockSpec((block, wide), lambda i: (i, 0)),
             *half_specs(block, width, rows, lambda i: i),
-            *[pl.BlockSpec((width, block), lambda i: (0, i))] * 2,
+            pl.BlockSpec((block, wide // 3), lambda i: (i, 0)),
+            *[pl.BlockSpec((width // halves, wide), lambda i: (0, 0), pipeline_mode=once)] * halves,
         ],
         out_shape=[
-            jax.ShapeDtypeStruct((rows, wide), BF),
             *[jax.ShapeDtypeStruct((rows // 2, width), BF)] * 2,
-            *[jax.ShapeDtypeStruct((width, rows), BF)] * 2,
-        ],
-        scratch_shapes=[pltpu.VMEM((block, width), BF)] * 2,
-        cost_estimate=took(28),
-        compiler_params=vmem(56),
+            jax.ShapeDtypeStruct((rows, wide // 3), BF),
+            *[jax.ShapeDtypeStruct((width // halves, wide), BF)] * halves,
+        ],
+        scratch_shapes=[
+            *[pltpu.VMEM((block, width), BF)] * 2,
+            pltpu.VMEM((block, wide), BF),
+            pltpu.VMEM((width, wide), F32),
+        ],
+        cost_estimate=took(45),
+        compiler_params=vmem(62),
     )(*e_rows, *g_rows, gates, weights)
-
-
-def expert_grad_kernel(e_ref, g_ref, act_ref, out_ref):
-    step = pl.program_id(0)
-    count = 2 * (pl.num_programs(0) // 3)
-
-    @pl.when(step < count)
-    def _():
-        out_ref[...] = dot_nn(e_ref[...].reshape(-1, act_ref.shape[0]), act_ref[...]).astype(BF)
-
-    @pl.when(step >= count)
-    def _():
-        out_ref[...] = dot_nn(g_ref[...].reshape(-1, act_ref.shape[0]), act_ref[...]).astype(BF)
-
-
-def expert_grads(e_turned, g_turned, act, half, halves, piece, step):
-    width, rows = e_turned.shape
-    wide = act.shape[1]
-    count = width // halves // piece
-    spec = pl.BlockSpec((count, 1, piece, rows), lambda i: (0, half, 0, 0))
-    split = (count, halves, piece, rows)
-    return pl.pallas_call(
-        expert_grad_kernel,
-        grid=(wide // step,),
-        in_specs=[spec, spec, pl.BlockSpec((rows, step), lambda i: (0, i))],
-        out_specs=pl.BlockSpec((count * piece, step), lambda i: (0, i)),
-        out_shape=jax.ShapeDtypeStruct((count * piece, wide), BF),
-        cost_estimate=took(9),
-        compiler_params=vmem(48),
-    )(e_turned.reshape(split), g_turned.reshape(split), act)
 
 
 def expert_out_kernel(act_ref, w_ref, low_ref, high_ref):
@@ -851,20 +889,19 @@
 
 
 def expert_out(act, weights, block):
-    rows, wide = act.shape
+    rows, cols = act.shape
     width = weights.shape[0]
-    cols = wide // 3
     return pl.pallas_call(
         expert_out_kernel,
         grid=(rows // block,),
         in_specs=[
-            pl.BlockSpec((block, cols), lambda i: (i, 2)),
+            pl.BlockSpec((block, cols), lambda i: (i, 0)),
             pl.BlockSpec((width, cols), lambda i: (0, 2)),
         ],
         out_specs=half_specs(block, width, rows, lambda i: i),
         out_shape=[jax.ShapeDtypeStruct((rows // 2, width), BF)] * 2,
-        cost_estimate=took(7),
-        compiler_params=vmem(48),
+        cost_estimate=took(8),
+        compiler_params=vmem(62),
     )(act, weights)
 
 
@@ -897,7 +934,7 @@
     halves = 2 if row_count % 32 == 0 else 1
     piece = row_count // halves
     x_even = x_index == 0
-    info = x_index.reshape(1).astype(jnp.int32)
+    info = jnp.stack([x_index, w_index]).astype(jnp.int32)
 
     slot_ids = jnp.arange(slot_total, dtype=jnp.int32)
     hits = owners[None, :] == slot_ids[:, None]
@@ -906,29 +943,16 @@
     local_at = owners[:6] - slot_count * w_index
     local_ok = (local_at >= 0) & (local_at < slot_count)
     attn_sent = attn_send(masters, jnp.clip(local_at, 0, slot_count - 1), local_ok.astype(jnp.int32))
-    bulk = bulk_send(masters, halves)
+    bulk = bulk_send(info, masters)
     attn_got = lax.all_to_all(attn_sent, PLANE, split_axis=0, concat_axis=0, tiled=True)
-    attn_got = after(attn_got, *bulk)
+    attn_got, *bulk = together(attn_got, *bulk)
     attn_mine = jnp.sum(attn_got.reshape(2, 4, 3, row_count, part).astype(F32), axis=1).astype(BF)
     attn_mine = jnp.transpose(attn_mine, (0, 2, 1, 3)).reshape(2 * row_count, 3 * part)
-    attn_w = lax.all_gather(attn_mine, "z", axis=0, tiled=True)
-    w_pair = attn_w[:, : 2 * part]
-    w_out = attn_w[:, 2 * part :]
 
     order = np.array([[6 + 3 * (group * g + e) + k for k in range(3) for e in range(group)] for g in range(2)])
     picks = jnp.take(owners, jnp.asarray(order))
-    picks_mine = jnp.where(x_even, picks[0], picks[1])
-    picks_other = jnp.where(x_even, picks[1], picks[0])
-    pieces = []
-    arrived = []
-    got = attn_got
-    for send in bulk:
-        got = lax.all_to_all(after(send, got), WSH, split_axis=0, concat_axis=0, tiled=True)
-        arrived.append(got)
-        keep, give = pick(picks_mine, picks_other, got.reshape(slot_total, piece, part))
-        pieces += [keep, swap(give, "x")]
-    joined = join(info, pieces)
-    expert_w = lax.all_gather(after(joined, attn_w), "z", axis=0, tiled=True)
+    picks = jnp.stack([jnp.where(x_even, picks[0], picks[1]), jnp.where(x_even, picks[1], picks[0])])
+    places = ((picks // slot_count) ^ w_index) * slot_count + picks % slot_count
 
     gains = norm_gains
     tokens_f = tokens[0].astype(F32)
@@ -945,9 +969,26 @@
     marks = (segments[0] + 1).astype(BF)[:, None]
     spare = jnp.zeros((seg_len, 128 - 2 * experts - 1), BF)
     packed = jnp.concatenate([attn_in, gates_high, gates_low, marks, spare], axis=1)
-    packed_all = plane_gather(
-        after(packed, attn_got), lambda sent: after(sent, attn_w, arrived[0])
-    )
+
+    across = [(i, i ^ 3) for i in range(4)]
+    half = seg_len // 2
+    packed = after(packed, attn_got)
+    over_x, over_y, from_y, attn_w = together(
+        swap(packed, "x"),
+        swap(packed, "y"),
+        swap(bulk[2], "y"),
+        lax.all_gather(attn_mine, "z", axis=0, tiled=True),
+    )
+    corner, from_c, from_corner = together(
+        swap(over_y, "x"),
+        swap(bulk[1], "c"),
+        lax.ppermute(after(bulk[3], from_y), WSH, across),
+    )
+    mine = stack([packed, over_x, over_y, corner])
+    other, *picked = together(
+        swap(mine, "c"), *pick(places.reshape(-1), [bulk[0], from_c, from_y, from_corner], 2)
+    )
+    packed_all = (mine, other)
     extras = jnp.concatenate([rows[:, width:] for rows in packed_all], axis=0)
     gates_all = extras[:, :experts].astype(F32) + extras[:, experts : 2 * experts].astype(F32)
     my_gates = jnp.where(x_even, gates_all[:, :group], gates_all[:, group:])
@@ -965,33 +1006,27 @@
     cosine = jnp.tile(jnp.cos(angles), (1, 1, 4))
     sine = jnp.tile(jnp.sin(angles), (1, 1, 4))
 
-    query, kv_low = project(*packed_all, w_pair, cosine, sine, seg_len)
+    query, kv_low = project(*packed_all, attn_w, cosine, sine, seg_len)
     kv_zero = jnp.concatenate([kv_low, marks_tail], axis=0)
-    g_all = plane_gather(after(cot_low, kv_zero))
-    kv_one = shift(kv_zero, 1)
-    kv_two = shift(kv_one, 1)
+    kv_one, got_rows = together(shift(kv_zero, 1), swap(picked[1], "x"))
+    joined = join(info, picked[:1], [got_rows])
+    expert_w = lax.all_gather(joined, "z", axis=0, tiled=True)
+    kv_two = shift(after(kv_one, joined), 1)
+    g_all = plane_gather(after(cot_low, joined))
     kv = (kv_zero, kv_one, kv_two)
     qseg = marks_all.astype(F32).reshape(2 * seqs, 1, seg_len)
     attn_mix, stat, out_low, out_high = attend(
-        info, after(query, joined), kv, qseg, w_out, seg_len
+        info, query, kv, qseg, attn_w, seg_len
     )
     resid_one = tokens_f + plane_reduce(out_low, out_high)
     scale_two = norm_scale(resid_one)
     expert_in = (resid_one * scale_two * gains[1]).astype(BF)
     e_all = plane_gather(expert_in)
 
-    act, grad_in_low, grad_in_high, e_turned, g_turned = expert_rows(e_all, g_all, my_gates, expert_w, part, 2 * seg_len)
-    parts = []
-
-    def weight_grads(h, then):
-        grads = expert_grads(e_turned, g_turned, after(act, then), h, halves, piece, 4 * part)
-        parts.append(grads)
-        return after(then, grads)
-
-    waits = [None, lambda sent: weight_grads(0, sent), None]
-    if halves == 2:
-        waits[2] = lambda sent: (weight_grads(1, sent[0]), sent[1])
-    grad_expert_in = plane_reduce(grad_in_low, grad_in_high, waits)
+    grad_in_low, grad_in_high, hidden_low, *parts = expert_rows(
+        e_all, g_all, my_gates, expert_w, part, piece, halves, 2 * seg_len
+    )
+    grad_expert_in = plane_reduce(grad_in_low, grad_in_high)
 
     cot_rows = cot_low.astype(F32)
     norm_grad_two = norm_back(resid_one, scale_two, gains[1], grad_expert_in)
@@ -1002,59 +1037,97 @@
     place = jnp.where(held >= 6, kind_of * group + expert_of % group, 0)
     side = jnp.where(held >= 6, (expert_of // group) ^ x_index, 2)
 
-    def pack_slots(total, *first):
+    def over(total):
         give = lax.dynamic_slice_in_dim(total, (1 - x_index) * piece, piece, axis=0)
-        return pack(place, side, info, total, after(swap(give, "x"), *first), part)
-
-    def to_owners(send):
-        got = lax.all_to_all(send, WSH, split_axis=0, concat_axis=0, tiled=True)
-        return got.reshape(4, slot_count, piece, part)
-
-    sums = [lax.psum_scatter(parts[0], "z", scatter_dimension=0, tiled=True)]
-    dy_all = after(plane_gather(grad_resid.astype(BF)), *sums)
-    if halves == 2:
-        sums.append(lax.psum_scatter(after(parts[1], *sums), "z", scatter_dimension=0, tiled=True))
-    grad_q_low, dkv_zero, dkv_one, dkv_two, grad_w_out = attend_back(
-        info, query, kv, qseg, stat, dy_all, attn_mix, w_out, cosine, sine, seg_len
-    )
-    passed_one = shift(dkv_two, -1)
-    packs = [pack_slots(sums[0], grad_q_low)]
-    slot_grads = [to_owners(packs[0])]
-    moe_low, moe_high = expert_out(after(act, grad_q_low, packs[0]), expert_w, 2 * seg_len)
-    passed_one = after(passed_one, moe_high, *sums)
-    passed = shift((dkv_one + passed_one.astype(F32)).astype(BF), -1)
-    resid_two = resid_one + plane_reduce(
-        moe_low,
-        moe_high,
-        (None, lambda sent: after(sent, passed_one), None),
-    )
-    output = (resid_two.astype(BF))
-    if halves == 2:
-        packs.append(pack_slots(after(sums[1], slot_grads[0])))
-        slot_grads.append(to_owners(packs[1]))
-    grad_one_low, grad_one_high, attn_grads, gain_part = project_back(
-        grad_q_low, after(dkv_zero, *packs), passed, packed_all, w_pair, cosine, sine, grad_w_out, seg_len
-    )
-    grad_in_one = plane_reduce(
-        grad_one_low, grad_one_high, (None, lambda sent: after(sent, *slot_grads), None)
-    )
-    gain_grad_one = jnp.sum(gain_part, axis=0) / gains[0]
-    norm_grad_one = norm_back(tokens_f, scale_one, gains[0], grad_in_one)
-    input_grad = (grad_resid + norm_grad_one)
-
-    attn_sum = lax.psum_scatter(attn_grads, "z", scatter_dimension=0, tiled=True)
-    attn_rows = jnp.broadcast_to(
-        after(attn_sum, *slot_grads).reshape(2, 1, row_count, 3 * part), (2, 4, row_count, 3 * part)
-    ).reshape(8, row_count, 3 * part)
-    attn_back = lax.all_to_all(attn_rows, PLANE, split_axis=0, concat_axis=0, tiled=True)
+        return swap(give, "x")
 
     held_mine = lax.dynamic_slice_in_dim(held, w_index * slot_count, slot_count)
     table = jnp.asarray(np.array([7, 0, 0, 1, 2, 3, 3] + [4, 5, 6] * experts, np.int32))
     rates = jnp.take(jnp.asarray(kind_rates(width, hidden), F32), jnp.take(table, held_mine + 1))
-    new_masters, new_first, new_second = update(
-        held_mine, rates, attn_back, slot_grads, masters, first_moments, second_moments
-    )
-    gain_grad = (sum_everywhere(after(jnp.stack([gain_grad_one, gain_grad_two]), attn_sum)))
+
+    sums = [lax.psum_scatter(parts[0], "z", scatter_dimension=0, tiled=True)]
+    dy = grad_resid.astype(BF)
+    over_x, over_y, moe = together(
+        swap(dy, "x"), swap(dy, "y"), expert_out(after(hidden_low, dy), expert_w, 2 * seg_len)
+    )
+    corner_top, corner_low, moe_got = together(
+        swap(over_x[:half], "y"), swap(over_y[half:], "x"), swap(moe[1], "c")
+    )
+    dy_mine = stack([dy, over_x, over_y, corner_top, corner_low])
+    dy_other, moe_corner = together(swap(dy_mine, "c"), corner_rows(moe[0], moe_got))
+    dy_all = after((dy_mine, dy_other), *sums)
+    if halves == 2:
+        sums.append(lax.psum_scatter(after(parts[1], *sums), "z", scatter_dimension=0, tiled=True))
+    back = attend_back(info, query, kv, qseg, stat, dy_all, attn_mix, attn_w, cosine, sine, seg_len)
+    (grad_q_low, dkv_zero, dkv_one, dkv_two, grad_w_out), got_rows, moe_x, moe_y = together(
+        back, over(sums[0]), swap(moe_corner[:half], "y"), swap(moe_corner[half:], "x")
+    )
+    to_x, to_y = edge_rows(moe[0], moe_got, moe_x, moe_y)
+
+    first_half = pack(place, side, info, sums[0], got_rows, part)
+    passed_one, slot_grads, out_x, out_y = together(
+        shift(dkv_two, -1), over_wsh(first_half), swap(to_x, "x"), swap(to_y, "y")
+    )
+    passing = (dkv_one + passed_one.astype(F32)).astype(BF)
+    passed, *got_rows = together(shift(passing, -1), *[over(total) for total in sums[1:]])
+    if halves == 2:
+        second_half = pack(place, side, info, sums[1], got_rows[0], part)
+        passed = after(passed, *second_half)
+        slot_grads = slot_grads + over_wsh(second_half)
+    grad_low, grad_high, attn_grads, gain_part = project_back(
+        grad_q_low, dkv_zero, passed, packed_all, attn_w, cosine, sine, grad_w_out, seg_len
+    )
+
+    hops = [("x", 1), ("z", 0), *[("z", k) for k in range(1, lax.axis_size("z").bit_length() - 1)], ("y", 1), ("c", 1)]
+
+    def hop(value, at):
+        axis, k = hops[at]
+        if axis != "z":
+            return value + swap(value, axis)
+        return value + lax.ppermute(value, "z", [(i, i ^ (1 << k)) for i in range(lax.axis_size("z"))])
+
+    gain_grad = jnp.stack([jnp.sum(gain_part, axis=0) / gains[0], gain_grad_two])
+    grad_got = swap(grad_high, "c")
+    grad_corner = corner_rows(grad_low, grad_got)
+    attn_sum, grad_x, grad_y, gain_grad, slot_grads = together(
+        lax.psum_scatter(attn_grads, "z", scatter_dimension=0, tiled=True),
+        swap(grad_corner[:half], "y"),
+        swap(grad_corner[half:], "x"),
+        hop(after(gain_grad, grad_corner), 0),
+        slot_grads,
+    )
+
+    attn_rows = jnp.broadcast_to(
+        attn_sum.reshape(2, 1, row_count, 3 * part), (2, 4, row_count, 3 * part)
+    ).reshape(8, row_count, 3 * part)
+    to_x, to_y = edge_rows(grad_low, grad_got, grad_x, grad_y)
+    attn_back, last_x, last_y, gain_grad, new = together(
+        lax.all_to_all(attn_rows, PLANE, split_axis=0, concat_axis=0, tiled=True),
+        swap(to_x, "x"),
+        swap(to_y, "y"),
+        hop(hop(gain_grad, 1), 2),
+        update(info, rates, slot_grads, masters, first_moments, second_moments),
+    )
+    for at in range(3, len(hops)):
+        gain_grad = hop(gain_grad, at)
+
+    def own(kept, got, *rest):
+        total = kept[:seg_len].astype(F32) + got[:seg_len].astype(F32)
+        return total + sum(value.astype(F32) for value in rest)
+
+    output = (resid_one + own(moe[0], moe_got, out_x, out_y)).astype(BF)
+    grad_in_one = own(grad_low, grad_got, last_x, last_y)
+    input_grad = grad_resid + norm_back(tokens_f, scale_one, gains[0], grad_in_one)
+    rank = jnp.cumsum(local_ok.astype(jnp.int32)) - 1
+    count = rank[5] + 1
+    wanted = jnp.minimum(jnp.arange(6, dtype=jnp.int32), count - 1)
+    chosen = local_ok[None, :] & (rank[None, :] == wanted[:, None])
+    attn_slots = jnp.sum(jnp.where(chosen, local_at[None, :], 0), axis=1)
+    attn_held = jnp.sum(jnp.where(chosen, jnp.arange(6, dtype=jnp.int32)[None, :] + 1, 0), axis=1) - 1
+    attn_rates = jnp.take(rates, attn_slots)
+    new_masters, new_first, new_second = update_attn(
+        attn_slots, attn_held, attn_rates, attn_back, masters, first_moments, second_moments, new
+    )
     new_gains, new_gain_first, new_gain_second = adamw(
         norm_gains, gain_first, gain_second, gain_grad, GAIN_RATE, 0.0
     )

time: 546 us -> 538 us (0.985)
  starting transfers between devices: 83.2 us -> 64.6 us
  Pallas kernels: 184 us -> 191 us
    all_to_all x4 -> x0, starting transfers between devices: 15.1 us -> none  [the longest x2 7.98 us: to_owners(): got = lax.all_to_all(send, WSH, split_axis=0, concat_axis=0, tiled=True)]
    ppermute x2 -> x5, waiting for transfers between devices: 0.01 us -> 12.3 us  [the longest x2 11 us: over_wsh(): lax.ppermute(arrays[3], WSH, across)]
    ppermute x4, waiting for transfers between devices: 23.3 us -> 35.5 us  [shift(): return lax.ppermute(value, 'z', pairs)]
    all_gather x1, waiting for transfers between devices: 17.3 us -> 6.43 us  [shards(): expert_w = lax.all_gather(joined, 'z', axis=0, tiled=True)]
    reduce_scatter x1, waiting for transfers between devices: 12.5 us -> 3.95 us  [shards(): lax.psum_scatter(attn_grads, 'z', scatter_dimension=0, tiled=True)]
    ppermute x47 -> x51, starting transfers between devices: 44.7 us -> 40.9 us  [swap(): return lax.ppermute(value, axis, [(0, 1), (1, 0)])]
    unnamed x147 -> x153, local copies, waits for them, and re-layouts: 16.2 us -> 13.2 us
    ppermute x47 -> x51, waiting for transfers between devices: 127 us -> 126 us  [swap(): return lax.ppermute(value, axis, [(0, 1), (1, 0)])]
  transfers between devices with their start and end apart: 63 -> 66, of which waited for: 38 -> 34; matrix products, arithmetic and copies ran while one was open for 5% -> 6% of each run, Pallas kernels for 25% -> 22%
where the time goes in v3:
time: 538 us; the launch traced here: 532 us
  Pallas kernels  191 us (36%)
  waiting for transfers between devices  189 us (35%)
  starting transfers between devices  64.6 us (12%)
  local copies, waits for them, and re-layouts  26.1 us (5%)
  other arithmetic  25.5 us (5%)
  blocking collectives  19.8 us (4%)
  between operations  15.4 us (3%)
    ppermute x51, waiting for transfers between devices, swap(): return lax.ppermute(value, axis, [(0, 1), (1, 0)])  126 us
    pallas_call x1, Pallas kernels, expert_rows(): pl.pallas_call(lambda *refs: expert_kernel(part, piece, halves, *refs), g...  49.8 us
    ppermute x51, starting transfers between devices, swap(): return lax.ppermute(value, axis, [(0, 1), (1, 0)])  40.9 us
    ppermute x4, waiting for transfers between devices, shift(): return lax.ppermute(value, 'z', pairs)  35.5 us
    pallas_call x1, Pallas kernels, attend_back(): pl.pallas_call(attend_back_kernel, grid=(seqs, 2), in_specs=[pl.BlockSpec...  31.5 us
    pallas_call x1, Pallas kernels, attend(): pl.pallas_call(attend_kernel, grid=(seqs, 2), in_specs=[pl.BlockSpec(memo...  28.1 us
    all_gather x1, blocking collectives, shards(): lax.all_gather(attn_mine, 'z', axis=0, tiled=True)  19.8 us
    pallas_call x1, Pallas kernels, update(): pl.pallas_call(update_kernel, grid=(slots // step,), in_specs=[smem, smem...  15.6 us
  transfers between devices with their start and end apart: 66, of which 34 were waited for; matrix products, arithmetic and copies ran while one was open for 6% of the time, Pallas kernels for 22%

profile of v3, /device:TPU:0, one launch (start us, length us, event | category | flops | bytes accessed | tf_op | source)
XLA Modules:
  0.0 531.6 jit_solution(13570041647307742910)
XLA Ops:
  9.4 3.4 shard_map.206
  12.8 5.7 %all-to-all-start = ((bf16[8,3,128,128]{3,2,1,0:T(8,128)(2,1)}), bf16[8,3,128,128]{3,2,1,0:T(8,128)(2,1)S(1)}, u32[]{:S(2)}, u32[]{:S(2)}) async-start(bf16[8,3,128,128]{3,2,1,0:T(8,128)(2,1)} %shard_map.206), calls=%async_computation | async-start | bytes 1572864 | tf_op jit(solution)/shard_map/all_to_all | solution.py:947
  20.4 4.8 shard_map.207
  25.2 4.9 all-to-all-done
  34.8 19.8 %all_gather.6.w_ref = bf16[1024,384]{1,0:T(8,128)(2,1)S(1)} all-gather(bf16[256,384]{1,0:T(8,128)(2,1)S(1)} %bitcast.60), channel_id=1, replica_groups=mesh['z'=4,'x'=2,'y'=2,'c'=2] {'z'}, dimensions={0}, use_global_device_ids=true | all-gather | bytes 983040 | tf_op jit(solution)/shard_map/all_gather | solution.py:980
  54.6 4.7 collective-permute-done.1.refs_2_
  60.1 15.0 %collective-permute-done.3.refs_3_ = bf16[256,1152]{1,0:T(8,128)(2,1)S(1)} collective-permute-done((bf16[256,1152]{1,0:T(8,128)(2,1)S(1)}, bf16[256,1152]{1,0:T(8,128)(2,1)S(1)}, u32[]{:S(2)}, u32[]{:S(2)}) %collective-permute-start.3) | collective-permute-done | bytes 589856 | tf_op jit(solution)/shard_map/ppermute | solution.py:30
  76.3 1.7 shard_map.208.low_ref.x_low
  80.5 1.7 slice.156
  82.2 4.1 shard_map.209
  89.3 6.8 %shard_map.210 = (bf16[2048,128]{1,0:T(8,128)(2,1)S(1)}, bf16[2048,128]{1,0:T(8,128)(2,1)S(1)}) custom-call(bf16[1024,1152]{1,0:T(8,128)(2,1)} %shard_map.208.low_ref.x_low, bf16[1024,1152]{1,0:T(8,128)(2,1)} %collective-permute-done.6.high_ref.x_high, bf16[1024,384]{1,0:T(8,128)(2,1)S(1)} %all_gather.6.w_ref, f32[2,256,128]{2,1,0:T(8,128)S(1)} %copy.74.cos_ref, ...), custom_call_target="tpu_custom_call" | custom-call | flops 6000000000 | bytes 1048576 | tf_op jit(solution)/shard_map/pallas_call | solution.py:490
  96.1 3.6 collective-permute-start.7
  99.8 11.7 %collective-permute-done.7.k1_ref.t1_ref = bf16[2080,128]{1,0:T(8,128)(2,1)S(1)} collective-permute-done((bf16[2080,128]{1,0:T(8,128)(2,1)S(1)}, bf16[2080,128]{1,0:T(8,128)(2,1)S(1)}, u32[]{:S(2)}, u32[]{:S(2)}) %collective-permute-start.7) | collective-permute-done | bytes 532512 | tf_op jit(solution)/shard_map/ppermute | solution.py:36
  111.5 1.8 shard_map.211
  113.3 4.4 collective-permute-start.9
  119.3 11.3 %collective-permute-done.9.k2_ref.t2_ref = bf16[2080,128]{1,0:T(8,128)(2,1)S(1)} collective-permute-done((bf16[2080,128]{1,0:T(8,128)(2,1)S(1)}, bf16[2080,128]{1,0:T(8,128)(2,1)S(1)}, u32[]{:S(2)}, u32[]{:S(2)}) %collective-permute-start.9) | collective-permute-done | bytes 532512 | tf_op jit(solution)/shard_map/ppermute | solution.py:36
  131.4 28.1 %shard_map.212 = (bf16[2048,128]{1,0:T(8,128)(2,1)}, f32[4,2,2,256]{3,2,1,0:T(2,128)}, bf16[1024,1024]{1,0:T(8,128)(2,1)}, bf16[1024,1024]{1,0:T(8,128)(2,1)}) custom-call(s32[2]{0:T(128)} %pad_add_fusion.1.info_ref, bf16[2048,128]{1,0:T(8,128)(2,1)} %copy-done.19, bf16[2080,128]{1,0:T(8,128)(2,1)} %copy-done.38, bf16[2080,128]{1,0:T(8,128)(2,1)} %copy-done.70, ...), custom_call_target="tpu_custom_call" | custom-call | flops 24000000000 | bytes 1048576 | tf_op jit(solution)/shard_map/pallas_call | solution.py:579
  159.6 4.4 collective-permute-done.10.got_ref.gx_ref.gy_ref
  163.9 1.6 copy-done.7
  166.3 7.8 %collective-permute-done.11.fx_ref = bf16[128,1024]{1,0:T(8,128)(2,1)S(1)} collective-permute-done((bf16[128,1024]{1,0:T(8,128)(2,1)S(1)}, bf16[128,1024]{1,0:T(8,128)(2,1)S(1)}, u32[]{:S(2)}, u32[]{:S(2)}) %collective-permute-start.11) | collective-permute-done | bytes 262176 | tf_op jit(solution)/shard_map/ppermute | solution.py:30
  174.5 1.7 collective-permute-start.14
  176.7 1.6 collective-permute-start.20
  178.6 10.8 %collective-permute-done.14 = bf16[256,1024]{1,0:T(8,128)(2,1)S(1)} collective-permute-done((bf16[256,1024]{1,0:T(8,128)(2,1)S(1)}, bf16[256,1024]{1,0:T(8,128)(2,1)S(1)}, u32[]{:S(2)}, u32[]{:S(2)}) %collective-permute-start.14) | collective-permute-done | bytes 524320 | tf_op jit(solution)/shard_map/ppermute | solution.py:30
  189.4 1.7 collective-permute-done.13
  192.6 9.7 %collective-permute-done.20.refs_1_ = bf16[256,1024]{1,0:T(8,128)(2,1)S(1)} collective-permute-done((bf16[256,1024]{1,0:T(8,128)(2,1)S(1)}, bf16[256,1024]{1,0:T(8,128)(2,1)S(1)}, u32[]{:S(2)}, u32[]{:S(2)}) %collective-permute-start.20) | collective-permute-done | bytes 524320 | tf_op jit(solution)/shard_map/ppermute | solution.py:30
  203.3 10.3 %collective-permute-done.15.refs_1_ = bf16[256,1024]{1,0:T(8,128)(2,1)S(1)} collective-permute-done((bf16[256,1024]{1,0:T(8,128)(2,1)S(1)}, bf16[256,1024]{1,0:T(8,128)(2,1)S(1)}, u32[]{:S(2)}, u32[]{:S(2)}) %collective-permute-start.15) | collective-permute-done | bytes 524320 | tf_op jit(solution)/shard_map/ppermute | solution.py:30
  214.5 3.0 collective-permute-done.22.refs_3_
  217.5 1.7 collective-permute-done.23.refs_4_
  219.4 2.1 collective-permute-done.17.refs_3_
  227.1 6.4 %all-gather.2.cloned.1.call-done.refs_5_.w_ref = bf16[1024,3072]{1,0:T(8,128)(2,1)} async-done(((bf16[256,3072]{1,0:T(8,128)(2,1)}), bf16[1024,3072]{1,0:T(8,128)(2,1)}) %all-gather.2.cloned.1.call-update) | async-done | bytes 6291472 | tf_op jit(solution)/shard_map/all_gather | solution.py:1013
  233.5 49.8 %shard_map.217 = (bf16[1024,1024]{1,0:T(8,128)(2,1)}, bf16[1024,1024]{1,0:T(8,128)(2,1)}, bf16[2048,1024]{1,0:T(8,128)(2,1)}, bf16[512,3072]{1,0:T(8,128)(2,1)}, bf16[512,3072]{1,0:T(8,128)(2,1)}) custom-call(bf16[1024,1024]{1,0:T(8,128)(2,1)} %copy-done.15, bf16[1024,1024]{1,0:T(8,128)(2,1)} %collective-permute-done.19.refs_1_, ...), custom_call_target="tpu_custom_call" | custom-call | flops 44999999488 | bytes 1048576 | tf_op jit(solution)/shard_map/pallas_call | solution.py:850
  283.5 4.4 collective-permute-done.25.got_ref.gx_ref.gy_ref
  289.2 1.6 collective-permute-start.26
  292.3 5.4 %collective-permute-done.26.fx_ref = bf16[128,1024]{1,0:T(8,128)(2,1)S(1)} collective-permute-done((bf16[128,1024]{1,0:T(8,128)(2,1)S(1)}, bf16[128,1024]{1,0:T(8,128)(2,1)S(1)}, u32[]{:S(2)}, u32[]{:S(2)}) %collective-permute-start.26) | collective-permute-done | bytes 262176 | tf_op jit(solution)/shard_map/ppermute | solution.py:30
  298.9 1.5 shard_map.219
  302.4 10.9 %collective-permute-done.29 = bf16[256,1024]{1,0:T(8,128)(2,1)S(1)} collective-permute-done((bf16[256,1024]{1,0:T(8,128)(2,1)S(1)}, bf16[256,1024]{1,0:T(8,128)(2,1)S(1)}, u32[]{:S(2)}, u32[]{:S(2)}) %collective-permute-start.29) | collective-permute-done | bytes 524320 | tf_op jit(solution)/shard_map/ppermute | solution.py:30
  313.7 2.1 multiply_reduce_fusion
  315.8 2.6 fusion.21
  321.2 9.1 %shard_map.220 = (bf16[1024,1024]{1,0:T(8,128)(2,1)}, bf16[1024,1024]{1,0:T(8,128)(2,1)}) custom-call(bf16[2048,1024]{1,0:T(8,128)(2,1)} %get-tuple-element.168.act_ref, bf16[1024,3072]{1,0:T(8,128)(2,1)} %all-gather.2.cloned.1.call-done.refs_5_.w_ref), custom_call_target="tpu_custom_call" | custom-call | flops 8000000000 | bytes 1048576 | tf_op jit(solution)/shard_map/pallas_call | solution.py:894
  333.5 6.7 %collective-permute-done.32.refs_3_ = bf16[128,1024]{1,0:T(8,128)(2,1)S(1)} collective-permute-done((bf16[128,1024]{1,0:T(8,128)(2,1)S(1)}, bf16[128,1024]{1,0:T(8,128)(2,1)S(1)}, u32[]{:S(2)}, u32[]{:S(2)}) %collective-permute-start.32) | collective-permute-done | bytes 262176 | tf_op jit(solution)/shard_map/ppermute | solution.py:30
  345.8 1.6 copy-done.5
  352.8 31.5 %shard_map.223 = (bf16[2048,128]{1,0:T(8,128)(2,1)}, f32[2048,128]{1,0:T(8,128)}, f32[2048,128]{1,0:T(8,128)}, bf16[2048,128]{1,0:T(8,128)(2,1)}, bf16[1024,128]{1,0:T(8,128)(2,1)}) custom-call(s32[2]{0:T(128)} %pad_add_fusion.1.info_ref, bf16[2048,128]{1,0:T(8,128)(2,1)} %copy-done.19, bf16[2080,128]{1,0:T(8,128)(2,1)} %copy-done.38, ...), custom_call_target="tpu_custom_call" | custom-call | flops 28000000000 | bytes 1048576 | tf_op jit(solution)/shard_map/pallas_call | solution.py:674
  385.6 3.6 shard_map.224
  393.6 19.1 %collective-permute-done.41.refs_2_ = bf16[20,64,128]{2,1,0:T(8,128)(2,1)S(1)} collective-permute-done((bf16[20,64,128]{2,1,0:T(8,128)(2,1)S(1)}, bf16[20,64,128]{2,1,0:T(8,128)(2,1)S(1)}, u32[]{:S(2)}, u32[]{:S(2)}) %collective-permute-start.41) | collective-permute-done | bytes 327712 | tf_op jit(solution)/shard_map/ppermute | solution.py:30
  412.7 5.6 %collective-permute-done.42.refs_3_ = bf16[20,64,128]{2,1,0:T(8,128)(2,1)S(1)} collective-permute-done((bf16[20,64,128]{2,1,0:T(8,128)(2,1)S(1)}, bf16[20,64,128]{2,1,0:T(8,128)(2,1)S(1)}, u32[]{:S(2)}, u32[]{:S(2)}) %collective-permute-start.42) | collective-permute-done | bytes 327712 | tf_op jit(solution)/shard_map/ppermute | solution.py:271
  421.6 1.5 collective-permute-start.46
  423.9 12.5 %collective-permute-done.45.b_ref = bf16[2048,128]{1,0:T(8,128)(2,1)S(1)} collective-permute-done((bf16[2048,128]{1,0:T(8,128)(2,1)S(1)}, bf16[2048,128]{1,0:T(8,128)(2,1)S(1)}, u32[]{:S(2)}, u32[]{:S(2)}) %collective-permute-start.45) | collective-permute-done | bytes 524320 | tf_op jit(solution)/shard_map/ppermute | solution.py:36
  437.7 4.6 shard_map.226
  443.0 11.4 %shard_map.227 = (bf16[1024,1024]{1,0:T(8,128)(2,1)}, bf16[1024,1024]{1,0:T(8,128)(2,1)}, bf16[1024,384]{1,0:T(8,128)(2,1)}, f32[8,1024]{1,0:T(8,128)}) custom-call(bf16[2048,128]{1,0:T(8,128)(2,1)} %get-tuple-element.202.dq_ref, f32[2048,128]{1,0:T(8,128)} %get-tuple-element.203.a_ref, bf16[2048,128]{1,0:T(8,128)(2,1)} %copy-done.72, ...), custom_call_target="tpu_custom_call" | custom-call | flops 10000000000 | bytes 1048576 | tf_op jit(solution)/shard_map/pallas_call | solution.py:756
  462.3 1.5 collective-permute-start.50
  467.5 2.4 fusion.10
  470.5 5.4 %collective-permute-done.53.refs_7_ = bf16[20,64,128]{2,1,0:T(8,128)(2,1)} collective-permute-done((bf16[20,64,128]{2,1,0:T(8,128)(2,1)S(1)}, bf16[20,64,128]{2,1,0:T(8,128)(2,1)}, u32[]{:S(2)}, u32[]{:S(2)}) %collective-permute-start.53) | collective-permute-done | bytes 327712 | tf_op jit(solution)/shard_map/ppermute | solution.py:271
  476.0 4.0 reduce-scatter.8.cloned.1.call-done
  479.9 1.8 collective-permute-done.48.fx_ref
  481.7 1.9 broadcast_in_dim.94
  483.6 4.2 all-to-all-start.1
  487.8 1.8 collective-permute-start.56
  489.7 2.2 shard_map.229
  491.8 1.8 collective-permute-start.54
  493.7 1.5 collective-permute-start.55
  495.2 15.6 %shard_map.230 = (f32[20,128,512]{2,1,0:T(8,128)}, f32[20,128,512]{2,1,0:T(8,128)}, f32[20,128,512]{2,1,0:T(8,128)}) custom-call(s32[2]{0:T(128)} %pad_add_fusion.1.info_ref, f32[20]{0:T(128)} %copy-done.25, bf16[20,64,128]{2,1,0:T(8,128)(2,1)} %copy-done.20, bf16[20,64,128]{2,1,0:T(8,128)(2,1)} %copy-done.73, bf16[20,64,128]{2,1,0:T(8,128)(2,1)} %copy-done.74, ...), custom_call_target="tpu_custom_call" | custom-call | flops 14000000000 | bytes 1048576 | tf_op jit(solution)/shard_map/pallas_call | solution.py:404
  512.9 6.1 %shard_map.231 = (f32[20,128,512]{2,1,0:T(8,128)}, f32[20,128,512]{2,1,0:T(8,128)}, f32[20,128,512]{2,1,0:T(8,128)}) custom-call(s32[6]{0:T(128)} %copy-done.57, s32[6]{0:T(128)} %broadcast_add_fusion.held_ref, f32[6]{0:T(128)} %and_select_fusion.rate_ref, ...), custom_call_target="tpu_custom_call", output_to_operand_aliasing={{0}: (7, {}), {1}: (8, {}), {2}: (9, {})} | custom-call | flops 5000000000 | bytes 1048576 | tf_op jit(solution)/shard_map/pallas_call | solution.py:454
  519.0 1.7 fusion.7
  521.3 2.7 fusion.6
  (350 shorter events, 79.8 us)
Async XLA Ops:
  12.8 17.3 %all-to-all-start = ((bf16[8,3,128,128]{3,2,1,0:T(8,128)(2,1)}), bf16[8,3,128,128]{3,2,1,0:T(8,128)(2,1)S(1)}, u32[]{:S(2)}, u32[]{:S(2)}) async-start(bf16[8,3,128,128]{3,2,1,0:T(8,128)(2,1)} %shard_map.206), calls=%async_computation | async-start | bytes 1572864 | tf_op jit(solution)/shard_map/all_to_all | solution.py:947
  18.5 215.0 %all-gather.2.cloned.1.call-start = ((), (), s32[]{:S(2)}) async-start(), calls=%async_computation.5 | async-start | bytes 7864320 | tf_op jit(solution)/shard_map/all_gather | solution.py:1013
  30.2 29.1 %collective-permute-start.2 = (bf16[20,128,128]{2,1,0:T(8,128)(2,1)}, bf16[20,128,128]{2,1,0:T(8,128)(2,1)}, u32[]{:S(2)}, u32[]{:S(2)}) collective-permute-start(bf16[20,128,128]{2,1,0:T(8,128)(2,1)} %get-tuple-element.136), channel_id=1, source_target_pairs={{0,2},{2,0},{1,3},{3,1},{4,6},{6,4},{5,7},{7,5},{8,10},{10,8},{9,1... | collective-permute-start | bytes 1966088 | tf_op jit(solution)/shard_map/ppermute | solution.py:30
  32.3 22.3 %collective-permute-start = (bf16[256,1152]{1,0:T(8,128)(2,1)S(1)}, bf16[256,1152]{1,0:T(8,128)(2,1)S(1)}, u32[]{:S(2)}, u32[]{:S(2)}) collective-permute-start(bf16[256,1152]{1,0:T(8,128)(2,1)S(1)} %concatenate.13.refs_0_), channel_id=1, source_target_pairs={{0,4},{4,0},{1,5},{5,1},{2,6},{6,2},{3,7},{7,3},{8,12},{12,8},{9,1... | collective-permute-start | bytes 1769480 | tf_op jit(solution)/shard_map/ppermute | solution.py:30
  32.9 26.4 %collective-permute-start.1 = (bf16[256,1152]{1,0:T(8,128)(2,1)S(1)}, bf16[256,1152]{1,0:T(8,128)(2,1)S(1)}, u32[]{:S(2)}, u32[]{:S(2)}) collective-permute-start(bf16[256,1152]{1,0:T(8,128)(2,1)S(1)} %concatenate.13.refs_0_), channel_id=1, source_target_pairs={{0,2},{2,0},{1,3},{3,1},{4,6},{6,4},{5,7},{7,5},{8,10},{10,8},{9,1... | collective-permute-start | bytes 1769480 | tf_op jit(solution)/shard_map/ppermute | solution.py:30
  34.7 25.4 %collective-permute-start.4 = (bf16[20,128,128]{2,1,0:T(8,128)(2,1)}, bf16[20,128,128]{2,1,0:T(8,128)(2,1)S(1)}, u32[]{:S(2)}, u32[]{:S(2)}) collective-permute-start(bf16[20,128,128]{2,1,0:T(8,128)(2,1)} %get-tuple-element.139), channel_id=1, source_target_pairs={{0,1},{1,0},{2,3},{3,2},{4,5},{5,4},{6,7},{7,6},{8,9},{9,8},{10,11... | collective-permute-start | bytes 1966088 | tf_op jit(solution)/shard_map/ppermute | solution.py:30
  59.3 17.0 %collective-permute-start.5 = (bf16[20,128,128]{2,1,0:T(8,128)(2,1)S(1)}, bf16[20,128,128]{2,1,0:T(8,128)(2,1)S(1)}, u32[]{:S(2)}, u32[]{:S(2)}) collective-permute-start(bf16[20,128,128]{2,1,0:T(8,128)(2,1)S(1)} %copy-done.69), channel_id=1, source_target_pairs={{0,3},{1,2},{2,1},{3,0},{4,7},{5,6},{6,5},{7,4},{8,11},{9,10},{10,... | collective-permute-start | bytes 1966088 | tf_op jit(solution)/shard_map/ppermute | solution.py:985
  59.3 15.8 %collective-permute-start.3 = (bf16[256,1152]{1,0:T(8,128)(2,1)S(1)}, bf16[256,1152]{1,0:T(8,128)(2,1)S(1)}, u32[]{:S(2)}, u32[]{:S(2)}) collective-permute-start(bf16[256,1152]{1,0:T(8,128)(2,1)S(1)} %collective-permute-done.1.refs_2_), channel_id=1, source_target_pairs={{0,4},{4,0},{1,5},{5,1},{2,6},{6,2},{3,7},{7,3},{8,12},{12,8},{9,1... | collective-permute-start | bytes 1769480 | tf_op jit(solution)/shard_map/ppermute | solution.py:30
  78.0 8.2 %collective-permute-start.6 = (bf16[1024,1152]{1,0:T(8,128)(2,1)}, bf16[1024,1152]{1,0:T(8,128)(2,1)}, u32[]{:S(2)}, u32[]{:S(2)}) collective-permute-start(bf16[1024,1152]{1,0:T(8,128)(2,1)} %shard_map.208.low_ref.x_low), channel_id=1, source_target_pairs={{0,1},{1,0},{2,3},{3,2},{4,5},{5,4},{6,7},{7,6},{8,9},{9,8},{10,11... | collective-permute-start | bytes 7077896 | tf_op jit(solution)/shard_map/ppermute | solution.py:30
  88.7 22.8 %collective-permute-start.8 = (bf16[128,3072]{1,0:T(8,128)(2,1)}, bf16[128,3072]{1,0:T(8,128)(2,1)S(1)}, u32[]{:S(2)}, u32[]{:S(2)}) collective-permute-start(bf16[128,3072]{1,0:T(8,128)(2,1)} %get-tuple-element.153), channel_id=1, source_target_pairs={{0,4},{4,0},{1,5},{5,1},{2,6},{6,2},{3,7},{7,3},{8,12},{12,8},{9,1... | collective-permute-start | bytes 2359304 | tf_op jit(solution)/shard_map/ppermute | solution.py:30
  96.1 15.3 %collective-permute-start.7 = (bf16[2080,128]{1,0:T(8,128)(2,1)S(1)}, bf16[2080,128]{1,0:T(8,128)(2,1)S(1)}, u32[]{:S(2)}, u32[]{:S(2)}) collective-permute-start(bf16[2080,128]{1,0:T(8,128)(2,1)S(1)} %pad_maximum_fusion.k0_ref.t0_ref), channel_id=1, source_target_pairs={{0,8},{8,16},{16,24},{1,9},{9,17},{17,25},{2,10},{10,18},{18,26},{... | collective-permute-start | bytes 1597448 | tf_op jit(solution)/shard_map/ppermute | solution.py:36
  113.3 17.3 %collective-permute-start.9 = (bf16[2080,128]{1,0:T(8,128)(2,1)S(1)}, bf16[2080,128]{1,0:T(8,128)(2,1)S(1)}, u32[]{:S(2)}, u32[]{:S(2)}) collective-permute-start(bf16[2080,128]{1,0:T(8,128)(2,1)S(1)} %collective-permute-done.7.k1_ref.t1_ref), channel_id=1, source_target_pairs={{0,8},{8,16},{16,24},{1,9},{9,17},{17,25},{2,10},{10,18},{18,26},{... | collective-permute-start | bytes 1597448 | tf_op jit(solution)/shard_map/ppermute | solution.py:36
  118.8 225.4 %reduce-scatter.4.cloned.1.call-start = ((), (), s32[]{:S(2)}) async-start(), calls=%async_computation.6 | async-start | bytes 3932160 | tf_op jit(solution)/shard_map/reduce_scatter | solution.py:1048
  159.5 4.4 collective-permute-start.10
  165.7 8.4 %collective-permute-start.11 = (bf16[128,1024]{1,0:T(8,128)(2,1)S(1)}, bf16[128,1024]{1,0:T(8,128)(2,1)S(1)}, u32[]{:S(2)}, u32[]{:S(2)}) collective-permute-start(bf16[128,1024]{1,0:T(8,128)(2,1)S(1)} %get-tuple-element.274), channel_id=1, source_target_pairs={{0,2},{2,0},{1,3},{3,1},{4,6},{6,4},{5,7},{7,5},{8,10},{10,8},{9,1... | collective-permute-start | bytes 786440 | tf_op jit(solution)/shard_map/ppermute | solution.py:30
  165.8 8.4 %collective-permute-start.12 = (bf16[128,1024]{1,0:T(8,128)(2,1)S(1)}, bf16[128,1024]{1,0:T(8,128)(2,1)S(1)}, u32[]{:S(2)}, u32[]{:S(2)}) collective-permute-start(bf16[128,1024]{1,0:T(8,128)(2,1)S(1)} %get-tuple-element.273), channel_id=1, source_target_pairs={{0,4},{4,0},{1,5},{5,1},{2,6},{6,2},{3,7},{7,3},{8,12},{12,8},{9,1... | collective-permute-start | bytes 786440 | tf_op jit(solution)/shard_map/ppermute | solution.py:30
  174.5 14.9 %collective-permute-start.14 = (bf16[256,1024]{1,0:T(8,128)(2,1)S(1)}, bf16[256,1024]{1,0:T(8,128)(2,1)S(1)}, u32[]{:S(2)}, u32[]{:S(2)}) collective-permute-start(bf16[256,1024]{1,0:T(8,128)(2,1)S(1)} %get-tuple-element.161), channel_id=1, source_target_pairs={{0,2},{2,0},{1,3},{3,1},{4,6},{6,4},{5,7},{7,5},{8,10},{10,8},{9,1... | collective-permute-start | bytes 1572872 | tf_op jit(solution)/shard_map/ppermute | solution.py:30
  176.2 14.9 %collective-permute-start.13 = (bf16[256,1024]{1,0:T(8,128)(2,1)S(1)}, bf16[256,1024]{1,0:T(8,128)(2,1)S(1)}, u32[]{:S(2)}, u32[]{:S(2)}) collective-permute-start(bf16[256,1024]{1,0:T(8,128)(2,1)S(1)} %get-tuple-element.160), channel_id=1, source_target_pairs={{0,4},{4,0},{1,5},{5,1},{2,6},{6,2},{3,7},{7,3},{8,12},{12,8},{9,1... | collective-permute-start | bytes 1572872 | tf_op jit(solution)/shard_map/ppermute | solution.py:30
  176.7 25.7 %collective-permute-start.20 = (bf16[256,1024]{1,0:T(8,128)(2,1)S(1)}, bf16[256,1024]{1,0:T(8,128)(2,1)S(1)}, u32[]{:S(2)}, u32[]{:S(2)}) collective-permute-start(bf16[256,1024]{1,0:T(8,128)(2,1)S(1)} %bitcast.54), channel_id=1, source_target_pairs={{0,4},{4,0},{1,5},{5,1},{2,6},{6,2},{3,7},{7,3},{8,12},{12,8},{9,1... | collective-permute-start | bytes 1572872 | tf_op jit(solution)/shard_map/ppermute | solution.py:30
  178.3 24.5 %collective-permute-start.21 = (bf16[256,1024]{1,0:T(8,128)(2,1)S(1)}, bf16[256,1024]{1,0:T(8,128)(2,1)S(1)}, u32[]{:S(2)}, u32[]{:S(2)}) collective-permute-start(bf16[256,1024]{1,0:T(8,128)(2,1)S(1)} %bitcast.55), channel_id=1, source_target_pairs={{0,2},{2,0},{1,3},{3,1},{4,6},{6,4},{5,7},{7,5},{8,10},{10,8},{9,1... | collective-permute-start | bytes 1572872 | tf_op jit(solution)/shard_map/ppermute | solution.py:30
  191.8 21.8 %collective-permute-start.15 = (bf16[256,1024]{1,0:T(8,128)(2,1)S(1)}, bf16[256,1024]{1,0:T(8,128)(2,1)S(1)}, u32[]{:S(2)}, u32[]{:S(2)}) collective-permute-start(bf16[256,1024]{1,0:T(8,128)(2,1)S(1)} %multiply_convert_fusion.refs_0_), channel_id=1, source_target_pairs={{0,4},{4,0},{1,5},{5,1},{2,6},{6,2},{3,7},{7,3},{8,12},{12,8},{9,1... | collective-permute-start | bytes 1572872 | tf_op jit(solution)/shard_map/ppermute | solution.py:30
  192.3 21.8 %collective-permute-start.16 = (bf16[256,1024]{1,0:T(8,128)(2,1)S(1)}, bf16[256,1024]{1,0:T(8,128)(2,1)S(1)}, u32[]{:S(2)}, u32[]{:S(2)}) collective-permute-start(bf16[256,1024]{1,0:T(8,128)(2,1)S(1)} %multiply_convert_fusion.refs_0_), channel_id=1, source_target_pairs={{0,2},{2,0},{1,3},{3,1},{4,6},{6,4},{5,7},{7,5},{8,10},{10,8},{9,1... | collective-permute-start | bytes 1572872 | tf_op jit(solution)/shard_map/ppermute | solution.py:30
  202.4 15.2 %collective-permute-start.22 = (bf16[128,1024]{1,0:T(8,128)(2,1)S(1)}, bf16[128,1024]{1,0:T(8,128)(2,1)S(1)}, u32[]{:S(2)}, u32[]{:S(2)}) collective-permute-start(bf16[128,1024]{1,0:T(8,128)(2,1)S(1)} %slice.164), channel_id=1, source_target_pairs={{0,2},{2,0},{1,3},{3,1},{4,6},{6,4},{5,7},{7,5},{8,10},{10,8},{9,1... | collective-permute-start | bytes 786440 | tf_op jit(solution)/shard_map/ppermute | solution.py:30
  202.8 16.4 %collective-permute-start.23 = (bf16[128,1024]{1,0:T(8,128)(2,1)S(1)}, bf16[128,1024]{1,0:T(8,128)(2,1)S(1)}, u32[]{:S(2)}, u32[]{:S(2)}) collective-permute-start(bf16[128,1024]{1,0:T(8,128)(2,1)S(1)} %slice.165), channel_id=1, source_target_pairs={{0,4},{4,0},{1,5},{5,1},{2,6},{6,2},{3,7},{7,3},{8,12},{12,8},{9,1... | collective-permute-start | bytes 786440 | tf_op jit(solution)/shard_map/ppermute | solution.py:30
  213.6 7.9 %collective-permute-start.17 = (bf16[128,1024]{1,0:T(8,128)(2,1)S(1)}, bf16[128,1024]{1,0:T(8,128)(2,1)S(1)}, u32[]{:S(2)}, u32[]{:S(2)}) collective-permute-start(bf16[128,1024]{1,0:T(8,128)(2,1)S(1)} %slice.162), channel_id=1, source_target_pairs={{0,2},{2,0},{1,3},{3,1},{4,6},{6,4},{5,7},{7,5},{8,10},{10,8},{9,1... | collective-permute-start | bytes 786440 | tf_op jit(solution)/shard_map/ppermute | solution.py:30
  214.0 8.5 %collective-permute-start.18 = (bf16[128,1024]{1,0:T(8,128)(2,1)S(1)}, bf16[128,1024]{1,0:T(8,128)(2,1)S(1)}, u32[]{:S(2)}, u32[]{:S(2)}) collective-permute-start(bf16[128,1024]{1,0:T(8,128)(2,1)S(1)} %slice.163), channel_id=1, source_target_pairs={{0,4},{4,0},{1,5},{5,1},{2,6},{6,2},{3,7},{7,3},{8,12},{12,8},{9,1... | collective-permute-start | bytes 786440 | tf_op jit(solution)/shard_map/ppermute | solution.py:30
  219.3 5.0 collective-permute-start.24
  222.7 4.4 collective-permute-start.19
  283.4 4.6 collective-permute-start.25
  283.5 137.1 %reduce-scatter.6.cloned.1.call-start = ((), (), s32[]{:S(2)}) async-start(), calls=%async_computation.7 | async-start | bytes 3932160 | tf_op jit(solution)/shard_map/reduce_scatter | solution.py:1060
  289.2 8.4 %collective-permute-start.26 = (bf16[128,1024]{1,0:T(8,128)(2,1)S(1)}, bf16[128,1024]{1,0:T(8,128)(2,1)S(1)}, u32[]{:S(2)}, u32[]{:S(2)}) collective-permute-start(bf16[128,1024]{1,0:T(8,128)(2,1)S(1)} %get-tuple-element.272), channel_id=1, source_target_pairs={{0,2},{2,0},{1,3},{3,1},{4,6},{6,4},{5,7},{7,5},{8,10},{10,8},{9,1... | collective-permute-start | bytes 786440 | tf_op jit(solution)/shard_map/ppermute | solution.py:30
  290.8 8.1 %collective-permute-start.27 = (bf16[128,1024]{1,0:T(8,128)(2,1)S(1)}, bf16[128,1024]{1,0:T(8,128)(2,1)S(1)}, u32[]{:S(2)}, u32[]{:S(2)}) collective-permute-start(bf16[128,1024]{1,0:T(8,128)(2,1)S(1)} %get-tuple-element.271), channel_id=1, source_target_pairs={{0,4},{4,0},{1,5},{5,1},{2,6},{6,2},{3,7},{7,3},{8,12},{12,8},{9,1... | collective-permute-start | bytes 786440 | tf_op jit(solution)/shard_map/ppermute | solution.py:30
  300.4 13.0 %collective-permute-start.29 = (bf16[256,1024]{1,0:T(8,128)(2,1)S(1)}, bf16[256,1024]{1,0:T(8,128)(2,1)S(1)}, u32[]{:S(2)}, u32[]{:S(2)}) collective-permute-start(bf16[256,1024]{1,0:T(8,128)(2,1)S(1)} %get-tuple-element.166), channel_id=1, source_target_pairs={{0,2},{2,0},{1,3},{3,1},{4,6},{6,4},{5,7},{7,5},{8,10},{10,8},{9,1... | collective-permute-start | bytes 1572872 | tf_op jit(solution)/shard_map/ppermute | solution.py:30
  301.0 12.7 %collective-permute-start.28 = (bf16[256,1024]{1,0:T(8,128)(2,1)S(1)}, bf16[256,1024]{1,0:T(8,128)(2,1)S(1)}, u32[]{:S(2)}, u32[]{:S(2)}) collective-permute-start(bf16[256,1024]{1,0:T(8,128)(2,1)S(1)} %get-tuple-element.165), channel_id=1, source_target_pairs={{0,4},{4,0},{1,5},{5,1},{2,6},{6,2},{3,7},{7,3},{8,12},{12,8},{9,1... | collective-permute-start | bytes 1572872 | tf_op jit(solution)/shard_map/ppermute | solution.py:30
  318.4 12.0 %collective-permute-start.30 = (bf16[256,1024]{1,0:T(8,128)(2,1)S(1)}, bf16[256,1024]{1,0:T(8,128)(2,1)S(1)}, u32[]{:S(2)}, u32[]{:S(2)}) collective-permute-start(bf16[256,1024]{1,0:T(8,128)(2,1)S(1)} %get-tuple-element.263.refs_0_), channel_id=1, source_target_pairs={{0,4},{4,0},{1,5},{5,1},{2,6},{6,2},{3,7},{7,3},{8,12},{12,8},{9,1... | collective-permute-start | bytes 1572872 | tf_op jit(solution)/shard_map/ppermute | solution.py:30
  319.8 11.6 %collective-permute-start.31 = (bf16[256,1024]{1,0:T(8,128)(2,1)S(1)}, bf16[256,1024]{1,0:T(8,128)(2,1)S(1)}, u32[]{:S(2)}, u32[]{:S(2)}) collective-permute-start(bf16[256,1024]{1,0:T(8,128)(2,1)S(1)} %get-tuple-element.263.refs_0_), channel_id=1, source_target_pairs={{0,2},{2,0},{1,3},{3,1},{4,6},{6,4},{5,7},{7,5},{8,10},{10,8},{9,1... | collective-permute-start | bytes 1572872 | tf_op jit(solution)/shard_map/ppermute | solution.py:30
  331.4 10.0 %collective-permute-start.34 = (bf16[1024,1024]{1,0:T(8,128)(2,1)}, bf16[1024,1024]{1,0:T(8,128)(2,1)S(1)}, u32[]{:S(2)}, u32[]{:S(2)}) collective-permute-start(bf16[1024,1024]{1,0:T(8,128)(2,1)} %get-tuple-element.174), channel_id=1, source_target_pairs={{0,1},{1,0},{2,3},{3,2},{4,5},{5,4},{6,7},{7,6},{8,9},{9,8},{10,11... | collective-permute-start | bytes 6291464 | tf_op jit(solution)/shard_map/ppermute | solution.py:30
  331.5 8.8 %collective-permute-start.32 = (bf16[128,1024]{1,0:T(8,128)(2,1)S(1)}, bf16[128,1024]{1,0:T(8,128)(2,1)S(1)}, u32[]{:S(2)}, u32[]{:S(2)}) collective-permute-start(bf16[128,1024]{1,0:T(8,128)(2,1)S(1)} %slice.136), channel_id=1, source_target_pairs={{0,2},{2,0},{1,3},{3,1},{4,6},{6,4},{5,7},{7,5},{8,10},{10,8},{9,1... | collective-permute-start | bytes 786440 | tf_op jit(solution)/shard_map/ppermute | solution.py:30
  332.9 8.5 %collective-permute-start.33 = (bf16[128,1024]{1,0:T(8,128)(2,1)S(1)}, bf16[128,1024]{1,0:T(8,128)(2,1)S(1)}, u32[]{:S(2)}, u32[]{:S(2)}) collective-permute-start(bf16[128,1024]{1,0:T(8,128)(2,1)S(1)} %slice.137), channel_id=1, source_target_pairs={{0,4},{4,0},{1,5},{5,1},{2,6},{6,2},{3,7},{7,3},{8,12},{12,8},{9,1... | collective-permute-start | bytes 786440 | tf_op jit(solution)/shard_map/ppermute | solution.py:30
  344.2 5.7 %collective-permute-start.35 = (bf16[1024,1024]{1,0:T(8,128)(2,1)}, bf16[1024,1024]{1,0:T(8,128)(2,1)}, u32[]{:S(2)}, u32[]{:S(2)}) collective-permute-start(bf16[1024,1024]{1,0:T(8,128)(2,1)} %shard_map.221.dy_low), channel_id=1, source_target_pairs={{0,1},{1,0},{2,3},{3,2},{4,5},{5,4},{6,7},{7,6},{8,9},{9,8},{10,11... | collective-permute-start | bytes 6291464 | tf_op jit(solution)/shard_map/ppermute | solution.py:30
  344.2 135.7 %reduce-scatter.8.cloned.1.call-start = ((), (), s32[]{:S(2)}) async-start(), calls=%async_computation.8 | async-start | bytes 983040 | tf_op jit(solution)/shard_map/reduce_scatter | solution.py:1093
  349.3 35.0 %collective-permute-start.36 = (bf16[64,3072]{1,0:T(8,128)(2,1)}, bf16[64,3072]{1,0:T(8,128)(2,1)S(1)}, u32[]{:S(2)}, u32[]{:S(2)}) collective-permute-start(bf16[64,3072]{1,0:T(8,128)(2,1)} %constant_dynamic-slice_fusion.1), channel_id=1, source_target_pairs={{0,4},{4,0},{1,5},{5,1},{2,6},{6,2},{3,7},{7,3},{8,12},{12,8},{9,1... | collective-permute-start | bytes 1179656 | tf_op jit(solution)/shard_map/ppermute | solution.py:30
  350.6 33.6 %collective-permute-start.37 = (bf16[128,1024]{1,0:T(8,128)(2,1)}, bf16[128,1024]{1,0:T(8,128)(2,1)S(1)}, u32[]{:S(2)}, u32[]{:S(2)}) collective-permute-start(bf16[128,1024]{1,0:T(8,128)(2,1)} %get-tuple-element.270), channel_id=1, source_target_pairs={{0,2},{2,0},{1,3},{3,1},{4,6},{6,4},{5,7},{7,5},{8,10},{10,8},{9,1... | collective-permute-start | bytes 786440 | tf_op jit(solution)/shard_map/ppermute | solution.py:30
  351.3 33.0 %collective-permute-start.38 = (bf16[128,1024]{1,0:T(8,128)(2,1)S(1)}, bf16[128,1024]{1,0:T(8,128)(2,1)S(1)}, u32[]{:S(2)}, u32[]{:S(2)}) collective-permute-start(bf16[128,1024]{1,0:T(8,128)(2,1)S(1)} %get-tuple-element.269), channel_id=1, source_target_pairs={{0,4},{4,0},{1,5},{5,1},{2,6},{6,2},{3,7},{7,3},{8,12},{12,8},{9,1... | collective-permute-start | bytes 786440 | tf_op jit(solution)/shard_map/ppermute | solution.py:30
  384.3 34.0 %collective-permute-start.39 = (bf16[2048,128]{1,0:T(8,128)(2,1)}, bf16[2048,128]{1,0:T(8,128)(2,1)S(1)}, u32[]{:S(2)}, u32[]{:S(2)}) collective-permute-start(bf16[2048,128]{1,0:T(8,128)(2,1)} %get-tuple-element.190), channel_id=1, source_target_pairs={{8,0},{16,8},{24,16},{9,1},{17,9},{25,17},{10,2},{18,10},{26,18},{... | collective-permute-start | bytes 1572872 | tf_op jit(solution)/shard_map/ppermute | solution.py:36
  390.3 28.0 %collective-permute-start.43 = (bf16[256,1024]{1,0:T(8,128)(2,1)S(1)}, bf16[256,1024]{1,0:T(8,128)(2,1)S(1)}, u32[]{:S(2)}, u32[]{:S(2)}) collective-permute-start(bf16[256,1024]{1,0:T(8,128)(2,1)S(1)} %get-tuple-element.198), channel_id=1, source_target_pairs={{0,4},{4,0},{1,5},{5,1},{2,6},{6,2},{3,7},{7,3},{8,12},{12,8},{9,1... | collective-permute-start | bytes 1572872 | tf_op jit(solution)/shard_map/ppermute | solution.py:30
  390.9 27.4 %collective-permute-start.44 = (bf16[256,1024]{1,0:T(8,128)(2,1)S(1)}, bf16[256,1024]{1,0:T(8,128)(2,1)S(1)}, u32[]{:S(2)}, u32[]{:S(2)}) collective-permute-start(bf16[256,1024]{1,0:T(8,128)(2,1)S(1)} %get-tuple-element.199), channel_id=1, source_target_pairs={{0,2},{2,0},{1,3},{3,1},{4,6},{6,4},{5,7},{7,5},{8,10},{10,8},{9,1... | collective-permute-start | bytes 1572872 | tf_op jit(solution)/shard_map/ppermute | solution.py:30
  392.3 20.4 %collective-permute-start.41 = (bf16[20,64,128]{2,1,0:T(8,128)(2,1)S(1)}, bf16[20,64,128]{2,1,0:T(8,128)(2,1)S(1)}, u32[]{:S(2)}, u32[]{:S(2)}) collective-permute-start(bf16[20,64,128]{2,1,0:T(8,128)(2,1)S(1)} %get-tuple-element.194), channel_id=1, source_target_pairs={{0,2},{2,0},{1,3},{3,1},{4,6},{6,4},{5,7},{7,5},{8,10},{10,8},{9,1... | collective-permute-start | bytes 983048 | tf_op jit(solution)/shard_map/ppermute | solution.py:30
  393.0 25.3 %collective-permute-start.42 = (bf16[20,64,128]{2,1,0:T(8,128)(2,1)S(1)}, bf16[20,64,128]{2,1,0:T(8,128)(2,1)S(1)}, u32[]{:S(2)}, u32[]{:S(2)}) collective-permute-start(bf16[20,64,128]{2,1,0:T(8,128)(2,1)S(1)} %get-tuple-element.195), channel_id=1, source_target_pairs={{0,3},{1,2},{2,1},{3,0},{4,7},{5,6},{6,5},{7,4},{8,11},{9,10},{10,... | collective-permute-start | bytes 983048 | tf_op jit(solution)/shard_map/ppermute | solution.py:271
  419.2 17.2 %collective-permute-start.45 = (bf16[2048,128]{1,0:T(8,128)(2,1)S(1)}, bf16[2048,128]{1,0:T(8,128)(2,1)S(1)}, u32[]{:S(2)}, u32[]{:S(2)}) collective-permute-start(bf16[2048,128]{1,0:T(8,128)(2,1)S(1)} %add_convert_fusion), channel_id=1, source_target_pairs={{8,0},{16,8},{24,16},{9,1},{17,9},{25,17},{10,2},{18,10},{26,18},{... | collective-permute-start | bytes 1572872 | tf_op jit(solution)/shard_map/ppermute | solution.py:36
  421.6 14.8 %collective-permute-start.46 = (bf16[64,3072]{1,0:T(8,128)(2,1)S(1)}, bf16[64,3072]{1,0:T(8,128)(2,1)S(1)}, u32[]{:S(2)}, u32[]{:S(2)}) collective-permute-start(bf16[64,3072]{1,0:T(8,128)(2,1)S(1)} %constant_dynamic-slice_fusion), channel_id=1, source_target_pairs={{0,4},{4,0},{1,5},{5,1},{2,6},{6,2},{3,7},{7,3},{8,12},{12,8},{9,1... | collective-permute-start | bytes 1179656 | tf_op jit(solution)/shard_map/ppermute | solution.py:30
  454.5 6.4 %collective-permute-start.47 = (bf16[1024,1024]{1,0:T(8,128)(2,1)}, bf16[1024,1024]{1,0:T(8,128)(2,1)}, u32[]{:S(2)}, u32[]{:S(2)}) collective-permute-start(bf16[1024,1024]{1,0:T(8,128)(2,1)} %get-tuple-element.217), channel_id=1, source_target_pairs={{0,1},{1,0},{2,3},{3,2},{4,5},{5,4},{6,7},{7,6},{8,9},{9,8},{10,11... | collective-permute-start | bytes 6291464 | tf_op jit(solution)/shard_map/ppermute | solution.py:30
  459.0 11.6 %collective-permute-start.51 = (bf16[20,64,128]{2,1,0:T(8,128)(2,1)}, bf16[20,64,128]{2,1,0:T(8,128)(2,1)}, u32[]{:S(2)}, u32[]{:S(2)}) collective-permute-start(bf16[20,64,128]{2,1,0:T(8,128)(2,1)} %get-tuple-element.211), channel_id=1, source_target_pairs={{0,1},{1,0},{2,3},{3,2},{4,5},{5,4},{6,7},{7,6},{8,9},{9,8},{10,11... | collective-permute-start | bytes 983048 | tf_op jit(solution)/shard_map/ppermute | solution.py:30
  459.4 11.1 %collective-permute-start.52 = (bf16[20,64,128]{2,1,0:T(8,128)(2,1)S(1)}, bf16[20,64,128]{2,1,0:T(8,128)(2,1)}, u32[]{:S(2)}, u32[]{:S(2)}) collective-permute-start(bf16[20,64,128]{2,1,0:T(8,128)(2,1)S(1)} %get-tuple-element.212), channel_id=1, source_target_pairs={{0,2},{2,0},{1,3},{3,1},{4,6},{6,4},{5,7},{7,5},{8,10},{10,8},{9,1... | collective-permute-start | bytes 983048 | tf_op jit(solution)/shard_map/ppermute | solution.py:30
  460.9 15.1 %collective-permute-start.53 = (bf16[20,64,128]{2,1,0:T(8,128)(2,1)S(1)}, bf16[20,64,128]{2,1,0:T(8,128)(2,1)}, u32[]{:S(2)}, u32[]{:S(2)}) collective-permute-start(bf16[20,64,128]{2,1,0:T(8,128)(2,1)S(1)} %get-tuple-element.213), channel_id=1, source_target_pairs={{0,3},{1,2},{2,1},{3,0},{4,7},{5,6},{6,5},{7,4},{8,11},{9,10},{10,... | collective-permute-start | bytes 983048 | tf_op jit(solution)/shard_map/ppermute | solution.py:271
  462.3 3.7 collective-permute-start.50
  464.6 17.2 %collective-permute-start.48 = (bf16[128,1024]{1,0:T(8,128)(2,1)}, bf16[128,1024]{1,0:T(8,128)(2,1)S(1)}, u32[]{:S(2)}, u32[]{:S(2)}) collective-permute-start(bf16[128,1024]{1,0:T(8,128)(2,1)} %get-tuple-element.268), channel_id=1, source_target_pairs={{0,2},{2,0},{1,3},{3,1},{4,6},{6,4},{5,7},{7,5},{8,10},{10,8},{9,1... | collective-permute-start | bytes 786440 | tf_op jit(solution)/shard_map/ppermute | solution.py:30
  466.0 15.7 %collective-permute-start.49 = (bf16[128,1024]{1,0:T(8,128)(2,1)S(1)}, bf16[128,1024]{1,0:T(8,128)(2,1)S(1)}, u32[]{:S(2)}, u32[]{:S(2)}) collective-permute-start(bf16[128,1024]{1,0:T(8,128)(2,1)S(1)} %get-tuple-element.267), channel_id=1, source_target_pairs={{0,4},{4,0},{1,5},{5,1},{2,6},{6,2},{3,7},{7,3},{8,12},{12,8},{9,1... | collective-permute-start | bytes 786440 | tf_op jit(solution)/shard_map/ppermute | solution.py:30
  483.6 27.3 %all-to-all-start.1 = ((bf16[8,128,384]{2,1,0:T(8,128)(2,1)}), bf16[8,128,384]{2,1,0:T(8,128)(2,1)}, u32[]{:S(2)}, u32[]{:S(2)}) async-start(bf16[8,128,384]{2,1,0:T(8,128)(2,1)} %bitcast.21), calls=%async_computation.4 | async-start | bytes 1572864 | tf_op jit(solution)/shard_map/all_to_all | solution.py:1105
  487.8 7.3 %collective-permute-start.56 = (f32[2,1024]{1,0:T(2,128)S(1)}, f32[2,1024]{1,0:T(2,128)S(1)}, u32[]{:S(2)}, u32[]{:S(2)}) collective-permute-start(f32[2,1024]{1,0:T(2,128)S(1)} %copy-done.47), channel_id=1, source_target_pairs={{0,8},{8,0},{16,24},{24,16},{1,9},{9,1},{17,25},{25,17},{2,10},{10... | collective-permute-start | bytes 24584 | tf_op jit(solution)/shard_map/ppermute | solution.py:1087
  491.8 19.1 %collective-permute-start.54 = (bf16[256,1024]{1,0:T(8,128)(2,1)}, bf16[256,1024]{1,0:T(8,128)(2,1)S(1)}, u32[]{:S(2)}, u32[]{:S(2)}) collective-permute-start(bf16[256,1024]{1,0:T(8,128)(2,1)} %get-tuple-element.228), channel_id=1, source_target_pairs={{0,4},{4,0},{1,5},{5,1},{2,6},{6,2},{3,7},{7,3},{8,12},{12,8},{9,1... | collective-permute-start | bytes 1572872 | tf_op jit(solution)/shard_map/ppermute | solution.py:30
  493.7 17.2 %collective-permute-start.55 = (bf16[256,1024]{1,0:T(8,128)(2,1)S(1)}, bf16[256,1024]{1,0:T(8,128)(2,1)S(1)}, u32[]{:S(2)}, u32[]{:S(2)}) collective-permute-start(bf16[256,1024]{1,0:T(8,128)(2,1)S(1)} %get-tuple-element.229), channel_id=1, source_target_pairs={{0,2},{2,0},{1,3},{3,1},{4,6},{6,4},{5,7},{7,5},{8,10},{10,8},{9,1... | collective-permute-start | bytes 1572872 | tf_op jit(solution)/shard_map/ppermute | solution.py:30
  495.1 15.7 %collective-permute-start.57 = (f32[2,1024]{1,0:T(2,128)S(1)}, f32[2,1024]{1,0:T(2,128)S(1)}, u32[]{:S(2)}, u32[]{:S(2)}) collective-permute-start(f32[2,1024]{1,0:T(2,128)S(1)} %add.315), channel_id=1, source_target_pairs={{0,16},{8,24},{16,0},{24,8},{1,17},{9,25},{17,1},{25,9},{2,18},{10... | collective-permute-start | bytes 24584 | tf_op jit(solution)/shard_map/ppermute | solution.py:1087
  511.7 9.1 %collective-permute-start.58 = (f32[2,1024]{1,0:T(2,128)S(1)}, f32[2,1024]{1,0:T(2,128)S(1)}, u32[]{:S(2)}, u32[]{:S(2)}) collective-permute-start(f32[2,1024]{1,0:T(2,128)S(1)} %add.316), channel_id=1, source_target_pairs={{0,2},{2,0},{1,3},{3,1},{4,6},{6,4},{5,7},{7,5},{8,10},{10,8},{9,1... | collective-permute-start | bytes 24584 | tf_op jit(solution)/shard_map/ppermute | solution.py:30
  (78 other events, 733.2 us)
Sparse Core Ops, SparseCore 0:
  118.9 114.6 all-gather.1
  283.6 58.5 reduce-scatter.3
  345.1 71.3 reduce-scatter.5
  457.3 22.6 reduce-scatter.7

commit v4 on v3

--- a/solution.py
+++ b/solution.py
@@ -326,50 +326,48 @@
     )(info, *keeps, *gots)
 
 
-def pack_kernel(place_ref, side_ref, info_ref, total_ref, got_ref, *outs):
+def pack_kernel(place_ref, side_ref, info_ref, *refs):
+    totals, gots, outs, held = refs[:2], refs[2:4], refs[4:-1], refs[-1]
     count, rows, part = outs[0].shape
-    mine = pl.ds(pl.multiple_of(info_ref[0] * rows, rows), rows)
-    for d, out_ref in enumerate(outs):
+    full = gots[0].shape[0]
+    mine = pl.ds(pl.multiple_of(info_ref[0] * full, full), full)
+    for c in range(2):
+        held[c * full : (c + 1) * full] = totals[c][mine]
+        held[(2 + c) * full : (3 + c) * full] = gots[c][...]
+    held[4 * full :] = jnp.zeros((full, held.shape[1]), BF)
+    for d in range(4):
 
         def one(j, carry):
             s = (info_ref[1] ^ d) * count + j
             lanes = pl.ds(pl.multiple_of(place_ref[s] * part, part), part)
-
-            @pl.when(side_ref[s] == 0)
-            def _():
-                out_ref[j] = total_ref[mine, lanes]
-
-            @pl.when(side_ref[s] == 1)
-            def _():
-                out_ref[j] = got_ref[:, lanes]
-
-            @pl.when(side_ref[s] == 2)
-            def _():
-                out_ref[j] = jnp.zeros((rows, part), BF)
-
+            for h, out_ref in enumerate(outs[d::4]):
+                start = pl.multiple_of(side_ref[s] * full + h * rows, rows)
+                out_ref[j] = held[pl.ds(start, rows), lanes]
             return carry
 
         lax.fori_loop(0, count, one, 0)
 
 
-def pack(place, side, info, summed, got, part):
-    rows, wide = got.shape
-    shape = (place.shape[0] // 4, rows, part)
-    return pl.pallas_call(
+def pack(place, side, info, totals, gots, part, halves):
+    rows, wide = gots[0].shape
+    shape = (place.shape[0] // 4, rows // halves, part)
+    outs = pl.pallas_call(
         pack_kernel,
         grid_spec=pltpu.PrefetchScalarGridSpec(
             num_scalar_prefetch=3,
             grid=(1,),
             in_specs=[
-                pl.BlockSpec((2 * rows, wide), lambda i, a, b, c: (0, 0)),
-                pl.BlockSpec((rows, wide), lambda i, a, b, c: (0, 0)),
+                *[pl.BlockSpec((2 * rows, wide), lambda i, a, b, c: (0, 0))] * 2,
+                *[pl.BlockSpec((rows, wide), lambda i, a, b, c: (0, 0))] * 2,
             ],
-            out_specs=[pl.BlockSpec(shape, lambda i, a, b, c: (0, 0, 0))] * 4,
+            out_specs=[pl.BlockSpec(shape, lambda i, a, b, c: (0, 0, 0))] * (4 * halves),
+            scratch_shapes=[pltpu.VMEM((5 * rows, wide), BF)],
         ),
-        out_shape=[jax.ShapeDtypeStruct(shape, BF)] * 4,
-        cost_estimate=took(4),
+        out_shape=[jax.ShapeDtypeStruct(shape, BF)] * (4 * halves),
+        cost_estimate=took(3),
         compiler_params=vmem(32),
-    )(place, side, info, summed, got)
+    )(place, side, info, *totals, *gots)
+    return [outs[4 * h : 4 * h + 4] for h in range(halves)]
 
 
 def update_kernel(info_ref, rate_ref, *refs):
@@ -407,7 +405,7 @@
         in_specs=[smem, smem] + [grad_spec] * len(grads) + [spec] * 3,
         out_specs=[spec] * 3,
         out_shape=[jax.ShapeDtypeStruct(masters.shape, F32)] * 3,
-        cost_estimate=took(14),
+        cost_estimate=took(6),
         compiler_params=vmem(62),
     )(info, rates, *grads, masters, first, second)
 
@@ -521,7 +519,7 @@
     return (key_pos <= query_pos) & (kseg == qseg_ref[0])
 
 
-def load_pairs(refs, tails, kv_all, kv_turned, marks, kseg):
+def load_pairs(refs, tails, kv_all, kv_turned, marks, kseg, reach):
     third = kv_all.shape[0] // 3
     for i, (ref, tail) in enumerate(zip(refs, tails)):
         kv_all[i * third : (i + 1) * third] = ref[...]
@@ -531,32 +529,46 @@
             at = i * third + j * 128
             kseg[at : at + 128] = columns[:, j : j + 1]
     kv_turned[...] = kv_all[...].T
+    seq = pl.program_id(0)
+    least = jnp.min(marks[0, seq][: third // 128])
+    far = jnp.max(marks[2, seq]) >= least
+    near = jnp.max(marks[1, seq]) >= least
+    reach[0] = jnp.where(far, 3, jnp.where(near, 2, 1)).astype(jnp.int32)
 
 
 def attend_kernel(info_ref, q_ref, k0_ref, k1_ref, k2_ref, t0_ref, t1_ref, t2_ref, qseg_ref,
-                  w_ref, mix_ref, stat_ref, low_ref, high_ref, kv_all, kv_turned, marks, kseg):
+                  w_ref, mix_ref, stat_ref, low_ref, high_ref, kv_all, kv_turned, marks, kseg, reach):
     block = q_ref.shape[0]
     span = kv_all.shape[0]
 
     @pl.when(pl.program_id(1) == 0)
     def _():
-        load_pairs((k0_ref, k1_ref, k2_ref), (t0_ref, t1_ref, t2_ref), kv_all, kv_turned, marks, kseg)
-
-    allowed = masks(info_ref, qseg_ref, kseg[...], block, span)
+        load_pairs((k0_ref, k1_ref, k2_ref), (t0_ref, t1_ref, t2_ref), kv_all, kv_turned, marks, kseg, reach)
+
     lane = lax.broadcasted_iota(jnp.int32, (block, 2 * HD), 1)
     query = q_ref[...] * jnp.asarray(HD**-0.5, BF)
-    mixed = []
-    for head in range(2):
-        scores = dot_nt(kv_all[...], head_rows(query, head, lane, False))
-        scores = jnp.where(allowed, scores, NEG_BIG)
-        top = jnp.max(scores, axis=0, keepdims=True)
-        powers = jnp.exp(scores - top)
-        total = jnp.sum(powers, axis=0, keepdims=True)
-        stat_ref[0, 0, head : head + 1, :] = top + jnp.log(total)
-        probs = (powers * (1.0 / total)).astype(BF)
-        mixed.append(dot_nn(kv_turned[...], probs)[HD:])
-    mix = jnp.concatenate(mixed, axis=0).T.astype(BF)
-    mix_ref[...] = mix
+
+    def attend_to(keys):
+        allowed = masks(info_ref, qseg_ref, kseg[:keys], block, keys)
+        mixed = []
+        for head in range(2):
+            scores = dot_nt(kv_all[:keys], head_rows(query, head, lane, False))
+            scores = jnp.where(allowed, scores, NEG_BIG)
+            top = jnp.max(scores, axis=0, keepdims=True)
+            powers = jnp.exp(scores - top)
+            total = jnp.sum(powers, axis=0, keepdims=True)
+            stat_ref[0, 0, head : head + 1, :] = top + jnp.log(total)
+            probs = (powers * (1.0 / total)).astype(BF)
+            mixed.append(dot_nn(kv_turned[:, :keys], probs)[HD:])
+        mix_ref[...] = jnp.concatenate(mixed, axis=0).T.astype(BF)
+
+    for blocks in range(1, 4):
+
+        @pl.when(reach[0] == blocks)
+        def _():
+            attend_to(blocks * span // 3)
+
+    mix = mix_ref[...]
     out = dot_nt(mix, w_ref[...]).astype(BF)
     early = pl.program_id(0) < pl.num_programs(0) // 2
 
@@ -606,6 +618,7 @@
             pltpu.VMEM((2 * HD, 6 * block), BF),
             pltpu.VMEM((3, seqs, 8, 128), F32),
             pltpu.VMEM((6 * block, 1), F32),
+            pltpu.SMEM((1,), jnp.int32),
         ],
         cost_estimate=took(24),
         compiler_params=vmem(62),
@@ -615,7 +628,7 @@
 def attend_back_kernel(info_ref, q_ref, k0_ref, k1_ref, k2_ref, t0_ref, t1_ref, t2_ref, qseg_ref,
                        stat_ref, dy_low, dy_high, mix_ref, w_ref, cos_ref, sin_ref,
                        dq_ref, dk0_ref, dk1_ref, dk2_ref, dw_ref,
-                       kv_all, kv_turned, marks, kseg, sums, dw_sum):
+                       kv_all, kv_turned, marks, kseg, reach, sums, dw_sum, turned_sum):
     block = q_ref.shape[0]
     span = kv_all.shape[0]
     third = span // 3
@@ -629,27 +642,37 @@
     @pl.when(chunk == 0)
     def _():
         sums[...] = jnp.zeros_like(sums)
-        load_pairs((k0_ref, k1_ref, k2_ref), (t0_ref, t1_ref, t2_ref), kv_all, kv_turned, marks, kseg)
-
-    allowed = masks(info_ref, qseg_ref, kseg[...], block, span)
+        load_pairs((k0_ref, k1_ref, k2_ref), (t0_ref, t1_ref, t2_ref), kv_all, kv_turned, marks, kseg, reach)
+
     lane = lax.broadcasted_iota(jnp.int32, (block, 2 * HD), 1)
     query = q_ref[...] * jnp.asarray(HD**-0.5, BF)
     grad_rows = choose(seq < pl.num_programs(0) // 2, dy_low, dy_high)
     dw_sum[...] += dot_tn(mix_ref[...], grad_rows)
     grad_mix = dot_nn(grad_rows, w_ref[...]).astype(BF)
-    grad_query = []
-    for head in range(2):
-        q_low = head_rows(query, head, lane, False)
-        g_high = head_rows(grad_mix, head, lane, True)
-        scores = dot_nt(kv_all[...], q_low)
-        stat = stat_ref[0, 0, head : head + 1, :]
-        probs = jnp.where(allowed, jnp.exp(scores - stat), 0.0)
-        grad_probs = dot_nt(kv_all[...], g_high)
-        delta = jnp.sum(probs * grad_probs, axis=0, keepdims=True)
-        grad_scores = (probs * (grad_probs - delta)).astype(BF)
-        sums[...] += dot_nn(grad_scores, q_low) + dot_nn(probs.astype(BF), g_high)
-        grad_query.append(dot_nn(kv_turned[...], grad_scores)[:HD])
-    grad_q = jnp.concatenate(grad_query, axis=0).T * HD**-0.5
+
+    def attend_to(keys):
+        allowed = masks(info_ref, qseg_ref, kseg[:keys], block, keys)
+        grad_query = []
+        for head in range(2):
+            q_low = head_rows(query, head, lane, False)
+            g_high = head_rows(grad_mix, head, lane, True)
+            scores = dot_nt(kv_all[:keys], q_low)
+            stat = stat_ref[0, 0, head : head + 1, :]
+            probs = jnp.where(allowed, jnp.exp(scores - stat), 0.0)
+            grad_probs = dot_nt(kv_all[:keys], g_high)
+            delta = jnp.sum(probs * grad_probs, axis=0, keepdims=True)
+            grad_scores = (probs * (grad_probs - delta)).astype(BF)
+            sums[:keys] += dot_nn(grad_scores, q_low) + dot_nn(probs.astype(BF), g_high)
+            grad_query.append(dot_nn(kv_turned[:, :keys], grad_scores)[:HD])
+        turned_sum[...] = jnp.concatenate(grad_query, axis=0)
+
+    for blocks in range(1, 4):
+
+        @pl.when(reach[0] == blocks)
+        def _():
+            attend_to(blocks * span // 3)
+
+    grad_q = turned_sum[...].T * HD**-0.5
     dq_ref[...] = (grad_q * cos_ref[0] - turn(grad_q * sin_ref[0], lane)).astype(BF)
 
     @pl.when(chunk == 1)
@@ -704,10 +727,12 @@
             pltpu.VMEM((2 * HD, 6 * block), BF),
             pltpu.VMEM((3, seqs, 8, 128), F32),
             pltpu.VMEM((6 * block, 1), F32),
+            pltpu.SMEM((1,), jnp.int32),
             pltpu.VMEM((6 * block, 2 * HD), F32),
             pltpu.VMEM((2 * HD, width), F32),
-        ],
-        cost_estimate=took(28),
+            pltpu.VMEM((2 * HD, block), F32),
+        ],
+        cost_estimate=took(12),
         compiler_params=vmem(62),
     )(info, query, *kv, *kv, qseg, stat, *grad_rows, mix, weights, cosine, sine)
 
@@ -780,10 +805,13 @@
     )(grad_q, here, arrived, *x_rows, weights, cosine, sine, grad_out)
 
 
-def expert_kernel(part, piece, halves, e_low, e_high, g_low, g_high, gate_ref, w_ref, *refs):
-    low_ref, high_ref, hidden_ref = refs[:3]
-    grads, (e_ref, g_ref, act_ref, sums) = refs[3 : 3 + halves], refs[3 + halves :]
-    rows, width = e_ref.shape
+def expert_kernel(part, start, more, e_low, e_high, g_low, g_high, gate_ref, w_ref, *refs):
+    before, (low_ref, high_ref, hidden_ref, grads_ref), (e_ref, g_ref, act_ref, sums) = (
+        refs[:more],
+        refs[more : more + 4],
+        refs[more + 4 :],
+    )
+    rows = e_ref.shape[0]
     step_id = pl.program_id(0)
     last = pl.num_programs(0) - 1
     early = step_id < pl.num_programs(0) // 2
@@ -794,7 +822,8 @@
     lane = lax.broadcasted_iota(jnp.int32, (rows, step), 1)
     for j in range(cols // step):
         at = j * step
-        gate = jnp.where(lane < part, gate_ref[:, 2 * j : 2 * j + 1], gate_ref[:, 2 * j + 1 : 2 * j + 2])
+        first = start + 2 * j
+        gate = jnp.where(lane < part, gate_ref[:, first : first + 1], gate_ref[:, first + 1 : first + 2])
         pre = dot_nn(e_ref[...], w_ref[:, at : at + step])
         up = dot_nn(e_ref[...], w_ref[:, cols + at : cols + at + step])
         grad = dot_nn(g_ref[...], w_ref[:, 2 * cols + at : 2 * cols + at + step]) * gate
@@ -806,77 +835,78 @@
         act_ref[:, cols + at : cols + at + step] = (grad * active).astype(BF)
         act_ref[:, 2 * cols + at : 2 * cols + at + step] = (active * up * gate).astype(BF)
     hidden_ref[...] = act_ref[:, 2 * cols :]
-    dx = dot_nt(act_ref[:, : 2 * cols], w_ref[:, : 2 * cols]).astype(BF)
+    dx = dot_nt(act_ref[:, : 2 * cols], w_ref[:, : 2 * cols])
+    if more:
+        dx = dx + choose(early, *before).astype(F32)
 
     @pl.when(early)
     def _():
-        low_ref[...] = dx
+        low_ref[...] = dx.astype(BF)
 
     @pl.when(jnp.logical_not(early))
     def _():
-        high_ref[...] = dx
+        high_ref[...] = dx.astype(BF)
 
     e_turned = e_ref[...].T
     g_turned = g_ref[...].T
     chunk = 2 * step
 
+    def part_sum(at):
+        left = e_turned if at < 2 * cols else g_turned
+        return dot_nn(left, act_ref[:, at : at + chunk])
+
     @pl.when(step_id == 0)
     def _():
         for at in range(0, 3 * cols, chunk):
-            left = e_turned if at < 2 * cols else g_turned
-            sums[:, at : at + chunk] = dot_nn(left, act_ref[:, at : at + chunk])
+            sums[:, at : at + chunk] = part_sum(at)
 
     @pl.when((step_id > 0) & (step_id < last))
     def _():
         for at in range(0, 3 * cols, chunk):
-            left = e_turned if at < 2 * cols else g_turned
-            sums[:, at : at + chunk] += dot_nn(left, act_ref[:, at : at + chunk])
+            sums[:, at : at + chunk] += part_sum(at)
 
     @pl.when(step_id == last)
     def _():
         for at in range(0, 3 * cols, chunk):
-            left = e_turned if at < 2 * cols else g_turned
-            total = (sums[:, at : at + chunk] + dot_nn(left, act_ref[:, at : at + chunk])).astype(BF)
-            for i in range(width // piece):
-                out_ref = grads[i % halves]
-                to = (i // halves) * piece
-                out_ref[to : to + piece, at : at + chunk] = total[i * piece : (i + 1) * piece]
-
-
-def expert_rows(e_rows, g_rows, gates, weights, part, piece, halves, block):
+            grads_ref[:, at : at + chunk] = (sums[:, at : at + chunk] + part_sum(at)).astype(BF)
+
+
+def expert_rows(e_rows, g_rows, gates, weights, part, start, before, block):
     rows, width = 2 * e_rows[0].shape[0], e_rows[0].shape[1]
-    wide = weights.shape[1]
+    wide = weights.shape[1] // 2
     once = pl.Buffered(1)
-    return pl.pallas_call(
-        lambda *refs: expert_kernel(part, piece, halves, *refs),
+    column = 1 if before else 0
+    return pl.pallas_call(
+        lambda *refs: expert_kernel(part, start, len(before), *refs),
         grid=(rows // block,),
         in_specs=[
             *half_specs(block, width, rows, lambda i: i) * 2,
             pl.BlockSpec((block, gates.shape[1]), lambda i: (i, 0)),
-            pl.BlockSpec(weights.shape, lambda i: (0, 0), pipeline_mode=once),
+            pl.BlockSpec((width, wide), lambda i: (0, column), pipeline_mode=once),
+            *half_specs(block, width, rows, lambda i: i)[: len(before)],
         ],
         out_specs=[
             *half_specs(block, width, rows, lambda i: i),
             pl.BlockSpec((block, wide // 3), lambda i: (i, 0)),
-            *[pl.BlockSpec((width // halves, wide), lambda i: (0, 0), pipeline_mode=once)] * halves,
+            pl.BlockSpec((width, wide), lambda i: (0, 0), pipeline_mode=once),
         ],
         out_shape=[
             *[jax.ShapeDtypeStruct((rows // 2, width), BF)] * 2,
             jax.ShapeDtypeStruct((rows, wide // 3), BF),
-            *[jax.ShapeDtypeStruct((width // halves, wide), BF)] * halves,
+            jax.ShapeDtypeStruct((width, wide), BF),
         ],
         scratch_shapes=[
             *[pltpu.VMEM((block, width), BF)] * 2,
             pltpu.VMEM((block, wide), BF),
             pltpu.VMEM((width, wide), F32),
         ],
-        cost_estimate=took(45),
+        cost_estimate=took(0.01),
         compiler_params=vmem(62),
-    )(*e_rows, *g_rows, gates, weights)
-
-
-def expert_out_kernel(act_ref, w_ref, low_ref, high_ref):
-    out = dot_nt(act_ref[...], w_ref[...]).astype(BF)
+    )(*e_rows, *g_rows, gates, weights, *before)
+
+
+def expert_out_kernel(h0_ref, h1_ref, w0_ref, w1_ref, low_ref, high_ref):
+    out = (dot_nt(h0_ref[...], w0_ref[...]) + dot_nt(h1_ref[...], w1_ref[...])).astype(BF)
     early = pl.program_id(0) < pl.num_programs(0) // 2
 
     @pl.when(early)
@@ -888,21 +918,22 @@
         high_ref[...] = out
 
 
-def expert_out(act, weights, block):
-    rows, cols = act.shape
+def expert_out(hidden, weights, block):
+    rows, cols = hidden[0].shape
     width = weights.shape[0]
     return pl.pallas_call(
         expert_out_kernel,
         grid=(rows // block,),
         in_specs=[
-            pl.BlockSpec((block, cols), lambda i: (i, 0)),
+            *[pl.BlockSpec((block, cols), lambda i: (i, 0))] * 2,
             pl.BlockSpec((width, cols), lambda i: (0, 2)),
+            pl.BlockSpec((width, cols), lambda i: (0, 5)),
         ],
         out_specs=half_specs(block, width, rows, lambda i: i),
         out_shape=[jax.ShapeDtypeStruct((rows // 2, width), BF)] * 2,
-        cost_estimate=took(8),
+        cost_estimate=took(2),
         compiler_params=vmem(62),
-    )(act, weights)
+    )(*hidden, weights, weights)
 
 
 def shards(
@@ -932,7 +963,7 @@
     group = experts // 2
     part = hidden // 4
     halves = 2 if row_count % 32 == 0 else 1
-    piece = row_count // halves
+    team = group // 2
     x_even = x_index == 0
     info = jnp.stack([x_index, w_index]).astype(jnp.int32)
 
@@ -949,7 +980,12 @@
     attn_mine = jnp.sum(attn_got.reshape(2, 4, 3, row_count, part).astype(F32), axis=1).astype(BF)
     attn_mine = jnp.transpose(attn_mine, (0, 2, 1, 3)).reshape(2 * row_count, 3 * part)
 
-    order = np.array([[6 + 3 * (group * g + e) + k for k in range(3) for e in range(group)] for g in range(2)])
+    order = np.array(
+        [
+            [6 + 3 * (group * g + team * c + e) + k for c in range(2) for k in range(3) for e in range(team)]
+            for g in range(2)
+        ]
+    )
     picks = jnp.take(owners, jnp.asarray(order))
     picks = jnp.stack([jnp.where(x_even, picks[0], picks[1]), jnp.where(x_even, picks[1], picks[0])])
     places = ((picks // slot_count) ^ w_index) * slot_count + picks % slot_count
@@ -1008,8 +1044,8 @@
 
     query, kv_low = project(*packed_all, attn_w, cosine, sine, seg_len)
     kv_zero = jnp.concatenate([kv_low, marks_tail], axis=0)
-    kv_one, got_rows = together(shift(kv_zero, 1), swap(picked[1], "x"))
-    joined = join(info, picked[:1], [got_rows])
+    kv_one = shift(kv_zero, 1)
+    joined = join(info, picked[:1], [swap(picked[1], "x")])
     expert_w = lax.all_gather(joined, "z", axis=0, tiled=True)
     kv_two = shift(after(kv_one, joined), 1)
     g_all = plane_gather(after(cot_low, joined))
@@ -1023,101 +1059,16 @@
     expert_in = (resid_one * scale_two * gains[1]).astype(BF)
     e_all = plane_gather(expert_in)
 
-    grad_in_low, grad_in_high, hidden_low, *parts = expert_rows(
-        e_all, g_all, my_gates, expert_w, part, piece, halves, 2 * seg_len
-    )
-    grad_expert_in = plane_reduce(grad_in_low, grad_in_high)
-
-    cot_rows = cot_low.astype(F32)
-    norm_grad_two = norm_back(resid_one, scale_two, gains[1], grad_expert_in)
-    gain_grad_two = jnp.sum(grad_expert_in * resid_one * scale_two, axis=0)
-    grad_resid = cot_rows + norm_grad_two
+    held, local_at, local_ok = together(*after((held, local_at, local_ok), expert_in))
     expert_of = (held - 6) // 3
     kind_of = (held - 6) % 3
-    place = jnp.where(held >= 6, kind_of * group + expert_of % group, 0)
-    side = jnp.where(held >= 6, (expert_of // group) ^ x_index, 2)
-
-    def over(total):
-        give = lax.dynamic_slice_in_dim(total, (1 - x_index) * piece, piece, axis=0)
-        return swap(give, "x")
+    place = jnp.where(held >= 6, kind_of * team + expert_of % team, 0)
+    side = jnp.where(held >= 6, 2 * ((expert_of // group) ^ x_index) + expert_of % group // team, 4)
 
     held_mine = lax.dynamic_slice_in_dim(held, w_index * slot_count, slot_count)
     table = jnp.asarray(np.array([7, 0, 0, 1, 2, 3, 3] + [4, 5, 6] * experts, np.int32))
     rates = jnp.take(jnp.asarray(kind_rates(width, hidden), F32), jnp.take(table, held_mine + 1))
 
-    sums = [lax.psum_scatter(parts[0], "z", scatter_dimension=0, tiled=True)]
-    dy = grad_resid.astype(BF)
-    over_x, over_y, moe = together(
-        swap(dy, "x"), swap(dy, "y"), expert_out(after(hidden_low, dy), expert_w, 2 * seg_len)
-    )
-    corner_top, corner_low, moe_got = together(
-        swap(over_x[:half], "y"), swap(over_y[half:], "x"), swap(moe[1], "c")
-    )
-    dy_mine = stack([dy, over_x, over_y, corner_top, corner_low])
-    dy_other, moe_corner = together(swap(dy_mine, "c"), corner_rows(moe[0], moe_got))
-    dy_all = after((dy_mine, dy_other), *sums)
-    if halves == 2:
-        sums.append(lax.psum_scatter(after(parts[1], *sums), "z", scatter_dimension=0, tiled=True))
-    back = attend_back(info, query, kv, qseg, stat, dy_all, attn_mix, attn_w, cosine, sine, seg_len)
-    (grad_q_low, dkv_zero, dkv_one, dkv_two, grad_w_out), got_rows, moe_x, moe_y = together(
-        back, over(sums[0]), swap(moe_corner[:half], "y"), swap(moe_corner[half:], "x")
-    )
-    to_x, to_y = edge_rows(moe[0], moe_got, moe_x, moe_y)
-
-    first_half = pack(place, side, info, sums[0], got_rows, part)
-    passed_one, slot_grads, out_x, out_y = together(
-        shift(dkv_two, -1), over_wsh(first_half), swap(to_x, "x"), swap(to_y, "y")
-    )
-    passing = (dkv_one + passed_one.astype(F32)).astype(BF)
-    passed, *got_rows = together(shift(passing, -1), *[over(total) for total in sums[1:]])
-    if halves == 2:
-        second_half = pack(place, side, info, sums[1], got_rows[0], part)
-        passed = after(passed, *second_half)
-        slot_grads = slot_grads + over_wsh(second_half)
-    grad_low, grad_high, attn_grads, gain_part = project_back(
-        grad_q_low, dkv_zero, passed, packed_all, attn_w, cosine, sine, grad_w_out, seg_len
-    )
-
-    hops = [("x", 1), ("z", 0), *[("z", k) for k in range(1, lax.axis_size("z").bit_length() - 1)], ("y", 1), ("c", 1)]
-
-    def hop(value, at):
-        axis, k = hops[at]
-        if axis != "z":
-            return value + swap(value, axis)
-        return value + lax.ppermute(value, "z", [(i, i ^ (1 << k)) for i in range(lax.axis_size("z"))])
-
-    gain_grad = jnp.stack([jnp.sum(gain_part, axis=0) / gains[0], gain_grad_two])
-    grad_got = swap(grad_high, "c")
-    grad_corner = corner_rows(grad_low, grad_got)
-    attn_sum, grad_x, grad_y, gain_grad, slot_grads = together(
-        lax.psum_scatter(attn_grads, "z", scatter_dimension=0, tiled=True),
-        swap(grad_corner[:half], "y"),
-        swap(grad_corner[half:], "x"),
-        hop(after(gain_grad, grad_corner), 0),
-        slot_grads,
-    )
-
-    attn_rows = jnp.broadcast_to(
-        attn_sum.reshape(2, 1, row_count, 3 * part), (2, 4, row_count, 3 * part)
-    ).reshape(8, row_count, 3 * part)
-    to_x, to_y = edge_rows(grad_low, grad_got, grad_x, grad_y)
-    attn_back, last_x, last_y, gain_grad, new = together(
-        lax.all_to_all(attn_rows, PLANE, split_axis=0, concat_axis=0, tiled=True),
-        swap(to_x, "x"),
-        swap(to_y, "y"),
-        hop(hop(gain_grad, 1), 2),
-        update(info, rates, slot_grads, masters, first_moments, second_moments),
-    )
-    for at in range(3, len(hops)):
-        gain_grad = hop(gain_grad, at)
-
-    def own(kept, got, *rest):
-        total = kept[:seg_len].astype(F32) + got[:seg_len].astype(F32)
-        return total + sum(value.astype(F32) for value in rest)
-
-    output = (resid_one + own(moe[0], moe_got, out_x, out_y)).astype(BF)
-    grad_in_one = own(grad_low, grad_got, last_x, last_y)
-    input_grad = grad_resid + norm_back(tokens_f, scale_one, gains[0], grad_in_one)
     rank = jnp.cumsum(local_ok.astype(jnp.int32)) - 1
     count = rank[5] + 1
     wanted = jnp.minimum(jnp.arange(6, dtype=jnp.int32), count - 1)
@@ -1125,6 +1076,103 @@
     attn_slots = jnp.sum(jnp.where(chosen, local_at[None, :], 0), axis=1)
     attn_held = jnp.sum(jnp.where(chosen, jnp.arange(6, dtype=jnp.int32)[None, :] + 1, 0), axis=1) - 1
     attn_rates = jnp.take(rates, attn_slots)
+    e_all, place, side, rates, attn_slots, attn_held, attn_rates = together(
+        e_all, place, side, rates, attn_slots, attn_held, attn_rates
+    )
+
+    before = ()
+    hidden_all = []
+    sums = []
+    for c in range(2):
+        *before, units, grads = expert_rows(
+            e_all, g_all, my_gates, expert_w, part, team * c, before, 2 * seg_len
+        )
+        hidden_all.append(units)
+        sums.append(lax.psum_scatter(after(grads, *sums), "z", scatter_dimension=0, tiled=True))
+    grad_expert_in = plane_reduce(*before)
+
+    cot_rows = cot_low.astype(F32)
+    norm_grad_two = norm_back(resid_one, scale_two, gains[1], grad_expert_in)
+    gain_grad_two = jnp.sum(grad_expert_in * resid_one * scale_two, axis=0)
+    grad_resid = cot_rows + norm_grad_two
+    def over(total):
+        give = lax.dynamic_slice_in_dim(total, (1 - x_index) * row_count, row_count, axis=0)
+        return swap(give, "x")
+
+    dy = after(grad_resid.astype(BF), sums[0])
+    over_x, over_y, moe = together(
+        swap(dy, "x"), swap(dy, "y"), expert_out([after(units, dy) for units in hidden_all], expert_w, 2 * seg_len)
+    )
+    corner_top, corner_low, moe_got = together(
+        swap(over_x[:half], "y"), swap(over_y[half:], "x"), swap(moe[1], "c")
+    )
+    dy_mine = stack([dy, over_x, over_y, corner_top, corner_low])
+    dy_other, moe_corner = together(swap(dy_mine, "c"), corner_rows(moe[0], moe_got))
+    dy_all = (dy_mine, dy_other)
+    back = attend_back(info, query, kv, qseg, stat, dy_all, attn_mix, attn_w, cosine, sine, seg_len)
+    (grad_q_low, dkv_zero, dkv_one, dkv_two, grad_w_out), got_one, moe_x, moe_y = together(
+        back, over(sums[0]), swap(moe_corner[:half], "y"), swap(moe_corner[half:], "x")
+    )
+    to_x, to_y = edge_rows(moe[0], moe_got, moe_x, moe_y)
+
+    passed_one, got_two, out_y = together(
+        shift(dkv_two, -1), over(after(sums[1], grad_q_low)), swap(to_y, "y")
+    )
+    passing = (dkv_one + passed_one.astype(F32)).astype(BF)
+    first_half, *second_half = pack(place, side, info, sums, [got_one, got_two], part, halves)
+    passed, slot_grads, out_x = together(shift(passing, -1), over_wsh(first_half), swap(to_x, "x"))
+    *grads, attn_grads, gain_part = project_back(
+        grad_q_low, dkv_zero, passed, packed_all, attn_w, cosine, sine, grad_w_out, seg_len
+    )
+    attn_sum = lax.psum_scatter(attn_grads, "z", scatter_dimension=0, tiled=True)
+    (grad_low, grad_high), *more = together(
+        grads,
+        *[over_wsh([after(array, passed) for array in arrays]) for arrays in second_half],
+    )
+    slot_grads = sum(more, slot_grads)
+
+    hops = [("x", 1), ("z", 0), *[("z", k) for k in range(1, lax.axis_size("z").bit_length() - 1)], ("y", 1), ("c", 1)]
+
+    def hop(value, at):
+        axis, k = hops[at]
+        if axis != "z":
+            return value + swap(value, axis)
+        return value + lax.ppermute(value, "z", [(i, i ^ (1 << k)) for i in range(lax.axis_size("z"))])
+
+    gain_grad = jnp.stack([jnp.sum(gain_part, axis=0) / gains[0], gain_grad_two])
+    grad_got = swap(grad_high, "c")
+    grad_corner = corner_rows(grad_low, grad_got)
+    grad_x, grad_y, gain_grad = together(
+        swap(grad_corner[:half], "y"),
+        swap(grad_corner[half:], "x"),
+        hop(after(gain_grad, grad_corner), 0),
+    )
+    to_x, to_y = edge_rows(grad_low, grad_got, grad_x, grad_y)
+    attn_sum, last_x, last_y, gain_grad, new = together(
+        attn_sum,
+        swap(to_x, "x"),
+        swap(to_y, "y"),
+        hop(gain_grad, 1),
+        update(after(info, to_x), rates, slot_grads, masters, first_moments, second_moments),
+    )
+
+    attn_rows = jnp.broadcast_to(
+        attn_sum.reshape(2, 1, row_count, 3 * part), (2, 4, row_count, 3 * part)
+    ).reshape(8, row_count, 3 * part)
+    attn_back, gain_grad = together(
+        lax.all_to_all(attn_rows, PLANE, split_axis=0, concat_axis=0, tiled=True),
+        hop(gain_grad, 2),
+    )
+    for at in range(3, len(hops)):
+        gain_grad = hop(gain_grad, at)
+
+    def own(kept, got, *rest):
+        total = kept[:seg_len].astype(F32) + got[:seg_len].astype(F32)
+        return total + sum(value.astype(F32) for value in rest)
+
+    output = (resid_one + own(moe[0], moe_got, out_x, out_y)).astype(BF)
+    grad_in_one = own(grad_low, grad_got, last_x, last_y)
+    input_grad = grad_resid + norm_back(tokens_f, scale_one, gains[0], grad_in_one)
     new_masters, new_first, new_second = update_attn(
         attn_slots, attn_held, attn_rates, attn_back, masters, first_moments, second_moments, new
     )

time: 538 us -> 518 us (0.963)
  Pallas kernels: 191 us -> 173 us
  waiting for transfers between devices: 189 us -> 175 us
  starting transfers between devices: 64.6 us -> 72.6 us
    ppermute x4, waiting for transfers between devices: 35.5 us -> 23.5 us  [shift(): return lax.ppermute(value, 'z', pairs)]
    pallas_call x1, Pallas kernels: 28.1 us -> 17.8 us  [attend(): pl.pallas_call(attend_kernel, grid=(seqs, 2), in_specs=[pl.BlockSpec(memo...]
    pallas_call x1, Pallas kernels: 31.5 us -> 21.3 us  [attend_back(): pl.pallas_call(attend_back_kernel, grid=(seqs, 2), in_specs=[pl.BlockSpec...]
    pallas_call x2 -> x3, Pallas kernels: 58.9 us -> 68.7 us  [the longest x2 59.5 us: expert_rows(): pl.pallas_call(lambda *refs: expert_kernel(part, start, len(before), *ref...]
    ppermute x2, starting transfers between devices: 1.89 us -> 10.4 us  [hop(): lax.ppermute(value, 'z', [(i, i ^ 1 << k) for i in range(lax.axis_size('z...]
    ppermute x51, waiting for transfers between devices: 126 us -> 119 us  [swap(): return lax.ppermute(value, axis, [(0, 1), (1, 0)])]
    all_gather x1, waiting for transfers between devices: 6.43 us -> 12.7 us  [shards(): expert_w = lax.all_gather(joined, 'z', axis=0, tiled=True)]
    pallas_call x2 -> x1, Pallas kernels: 8.22 us -> 2.44 us  [pack(): pl.pallas_call(pack_kernel, grid_spec=pltpu.PrefetchScalarGridSpec(num_sc...]
  transfers between devices with their start and end apart: 66 -> 66, of which waited for: 34 -> 37; matrix products, arithmetic and copies ran while one was open for 6% -> 7% of each run, Pallas kernels for 22% -> 27%
where the time goes in v4:
time: 518 us; the launch traced here: 511 us
  waiting for transfers between devices  175 us (34%)
  Pallas kernels  173 us (33%)
  starting transfers between devices  72.6 us (14%)
  local copies, waits for them, and re-layouts  30.2 us (6%)
  other arithmetic  24.8 us (5%)
  blocking collectives  19.8 us (4%)
  between operations  15.1 us (3%)
    ppermute x51, waiting for transfers between devices, swap(): return lax.ppermute(value, axis, [(0, 1), (1, 0)])  119 us
    pallas_call x2, Pallas kernels, expert_rows(): pl.pallas_call(lambda *refs: expert_kernel(part, start, len(before), *ref...  59.5 us
    ppermute x51, starting transfers between devices, swap(): return lax.ppermute(value, axis, [(0, 1), (1, 0)])  41.1 us
    ppermute x4, waiting for transfers between devices, shift(): return lax.ppermute(value, 'z', pairs)  23.5 us
    pallas_call x1, Pallas kernels, attend_back(): pl.pallas_call(attend_back_kernel, grid=(seqs, 2), in_specs=[pl.BlockSpec...  21.3 us
    all_gather x1, blocking collectives, shards(): lax.all_gather(attn_mine, 'z', axis=0, tiled=True)  19.8 us
    pallas_call x1, Pallas kernels, attend(): pl.pallas_call(attend_kernel, grid=(seqs, 2), in_specs=[pl.BlockSpec(memo...  17.8 us
    pallas_call x1, Pallas kernels, update(): pl.pallas_call(update_kernel, grid=(slots // step,), in_specs=[smem, smem...  15.6 us
  transfers between devices with their start and end apart: 66, of which 37 were waited for; matrix products, arithmetic and copies ran while one was open for 7% of the time, Pallas kernels for 27%

profile of v4, /device:TPU:0, one launch (start us, length us, event | category | flops | bytes accessed | tf_op | source)
XLA Modules:
  0.0 510.5 jit_solution(14857642392552801132)
XLA Ops:
  8.9 3.4 shard_map.206
  12.2 5.2 %all-to-all-start = ((bf16[8,3,128,128]{3,2,1,0:T(8,128)(2,1)}), bf16[8,3,128,128]{3,2,1,0:T(8,128)(2,1)S(1)}, u32[]{:S(2)}, u32[]{:S(2)}) async-start(bf16[8,3,128,128]{3,2,1,0:T(8,128)(2,1)} %shard_map.206), calls=%async_computation | async-start | bytes 1572864 | tf_op jit(solution)/shard_map/all_to_all | solution.py:978
  18.8 4.8 shard_map.207
  23.5 5.5 %all-to-all-done = bf16[8,3,128,128]{3,2,1,0:T(8,128)(2,1)S(1)} async-done(((bf16[8,3,128,128]{3,2,1,0:T(8,128)(2,1)}), bf16[8,3,128,128]{3,2,1,0:T(8,128)(2,1)S(1)}, u32[]{:S(2)}, u32[]{:S(2)}) %all-to-all-start) | async-done | bytes 786464 | tf_op jit(solution)/shard_map/all_to_all | solution.py:978
  33.7 19.8 %all_gather.6.w_ref = bf16[1024,384]{1,0:T(8,128)(2,1)S(1)} all-gather(bf16[256,384]{1,0:T(8,128)(2,1)S(1)} %bitcast.60), channel_id=1, replica_groups=mesh['z'=4,'x'=2,'y'=2,'c'=2] {'z'}, dimensions={0}, use_global_device_ids=true | all-gather | bytes 983040 | tf_op jit(solution)/shard_map/all_gather | solution.py:1016
  53.5 4.7 collective-permute-done.1.refs_2_
  59.0 15.0 %collective-permute-done.3.refs_3_ = bf16[256,1152]{1,0:T(8,128)(2,1)S(1)} collective-permute-done((bf16[256,1152]{1,0:T(8,128)(2,1)S(1)}, bf16[256,1152]{1,0:T(8,128)(2,1)S(1)}, u32[]{:S(2)}, u32[]{:S(2)}) %collective-permute-start.3) | collective-permute-done | bytes 589856 | tf_op jit(solution)/shard_map/ppermute | solution.py:30
  75.3 1.6 shard_map.208.low_ref.x_low
  80.5 4.1 shard_map.209
  86.5 6.8 %shard_map.210 = (bf16[2048,128]{1,0:T(8,128)(2,1)S(1)}, bf16[2048,128]{1,0:T(8,128)(2,1)S(1)}) custom-call(bf16[1024,1152]{1,0:T(8,128)(2,1)} %shard_map.208.low_ref.x_low, bf16[1024,1152]{1,0:T(8,128)(2,1)} %collective-permute-done.6.high_ref.x_high, bf16[1024,384]{1,0:T(8,128)(2,1)S(1)} %all_gather.6.w_ref, f32[2,256,128]{2,1,0:T(8,128)S(1)} %copy.74.cos_ref, ...), custom_call_target="tpu_custom_call" | custom-call | flops 6000000000 | bytes 1048576 | tf_op jit(solution)/shard_map/pallas_call | solution.py:488
  93.5 3.5 collective-permute-start.7
  97.0 8.6 %collective-permute-done.8.refs_1_ = bf16[128,3072]{1,0:T(8,128)(2,1)S(1)} collective-permute-done((bf16[128,3072]{1,0:T(8,128)(2,1)}, bf16[128,3072]{1,0:T(8,128)(2,1)S(1)}, u32[]{:S(2)}, u32[]{:S(2)}) %collective-permute-start.8) | collective-permute-done | bytes 786464 | tf_op jit(solution)/shard_map/ppermute | solution.py:30
  105.6 1.8 shard_map.211
  108.7 4.4 collective-permute-start.9
  114.4 11.5 %collective-permute-done.9.k2_ref.t2_ref = bf16[2080,128]{1,0:T(8,128)(2,1)S(1)} collective-permute-done((bf16[2080,128]{1,0:T(8,128)(2,1)S(1)}, bf16[2080,128]{1,0:T(8,128)(2,1)S(1)}, u32[]{:S(2)}, u32[]{:S(2)}) %collective-permute-start.9) | collective-permute-done | bytes 532512 | tf_op jit(solution)/shard_map/ppermute | solution.py:36
  126.6 17.8 %shard_map.212 = (bf16[2048,128]{1,0:T(8,128)(2,1)}, f32[4,2,2,256]{3,2,1,0:T(2,128)}, bf16[1024,1024]{1,0:T(8,128)(2,1)}, bf16[1024,1024]{1,0:T(8,128)(2,1)}) custom-call(s32[2]{0:T(128)} %pad_add_fusion.1.info_ref, bf16[2048,128]{1,0:T(8,128)(2,1)} %copy-done.26, bf16[2080,128]{1,0:T(8,128)(2,1)} %copy-done.44, bf16[2080,128]{1,0:T(8,128)(2,1)} %copy-done.58, ...), custom_call_target="tpu_custom_call" | custom-call | flops 24000000000 | bytes 1048576 | tf_op jit(solution)/shard_map/pallas_call | solution.py:591
  144.5 4.4 collective-permute-done.10.got_ref.gx_ref.gy_ref
  148.8 1.6 copy-done.9
  151.5 1.9 collective-permute-start.21
  153.4 1.5 collective-permute-start.20
  154.9 4.9 collective-permute-done.12.fy_ref
  164.4 7.2 %collective-permute-done.21.refs_2_ = bf16[256,1024]{1,0:T(8,128)(2,1)S(1)} collective-permute-done((bf16[256,1024]{1,0:T(8,128)(2,1)S(1)}, bf16[256,1024]{1,0:T(8,128)(2,1)S(1)}, u32[]{:S(2)}, u32[]{:S(2)}) %collective-permute-start.21) | collective-permute-done | bytes 524320 | tf_op jit(solution)/shard_map/ppermute | solution.py:30
  171.6 1.6 collective-permute-start.23
  174.3 8.1 %collective-permute-done.13 = bf16[256,1024]{1,0:T(8,128)(2,1)} collective-permute-done((bf16[256,1024]{1,0:T(8,128)(2,1)}, bf16[256,1024]{1,0:T(8,128)(2,1)}, u32[]{:S(2)}, u32[]{:S(2)}) %collective-permute-start.13) | collective-permute-done | bytes 524320 | tf_op jit(solution)/shard_map/ppermute | solution.py:30
  182.9 1.8 multiply_reduce_fusion.2
  185.0 1.6 collective-permute-start.15
  189.9 8.7 %collective-permute-done.16.refs_2_ = bf16[256,1024]{1,0:T(8,128)(2,1)} collective-permute-done((bf16[256,1024]{1,0:T(8,128)(2,1)S(1)}, bf16[256,1024]{1,0:T(8,128)(2,1)}, u32[]{:S(2)}, u32[]{:S(2)}) %collective-permute-start.16) | collective-permute-done | bytes 524320 | tf_op jit(solution)/shard_map/ppermute | solution.py:30
  199.6 1.6 collective-permute-start.18
  203.2 3.5 collective-permute-done.18.refs_4_
  206.7 2.3 collective-permute-done.17.refs_3_
  209.0 2.7 shard_map.215.refs_0_
  216.2 12.7 %all-gather.2.cloned.1.call-done.refs_5_.w0_ref.w1_ref = bf16[1024,3072]{1,0:T(8,128)(2,1)} async-done(((bf16[256,3072]{1,0:T(8,128)(2,1)}), bf16[1024,3072]{1,0:T(8,128)(2,1)}) %all-gather.2.cloned.1.call-update) | async-done | bytes 6291472 | tf_op jit(solution)/shard_map/all_gather | solution.py:1049
  228.9 29.0 %shard_map.217 = (bf16[1024,1024]{1,0:T(8,128)(2,1)}, bf16[1024,1024]{1,0:T(8,128)(2,1)}, bf16[2048,512]{1,0:T(8,128)(2,1)}, bf16[1024,1536]{1,0:T(8,128)(2,1)}) custom-call(bf16[1024,1024]{1,0:T(8,128)(2,1)} %shard_map.215.refs_0_, bf16[1024,1024]{1,0:T(8,128)(2,1)} %collective-permute-done.19.refs_1_, bf16[1024,1024]{1,0:T(8,128)(2,1)} %copy-done.10, ...), custom_call_target="tpu_custom_call" | custom-call | flops 10000000 | bytes 1048576 | tf_op jit(solution)/shard_map/pallas_call | solution.py:879
  258.0 30.5 %shard_map.218 = (bf16[1024,1024]{1,0:T(8,128)(2,1)}, bf16[1024,1024]{1,0:T(8,128)(2,1)}, bf16[2048,512]{1,0:T(8,128)(2,1)}, bf16[1024,1536]{1,0:T(8,128)(2,1)}) custom-call(bf16[1024,1024]{1,0:T(8,128)(2,1)} %shard_map.215.refs_0_, bf16[1024,1024]{1,0:T(8,128)(2,1)} %collective-permute-done.19.refs_1_, bf16[1024,1024]{1,0:T(8,128)(2,1)} %copy-done.10, ...), custom_call_target="tpu_custom_call" | custom-call | flops 10000000 | bytes 1048576 | tf_op jit(solution)/shard_map/pallas_call | solution.py:879
  288.6 4.4 collective-permute-done.25.got_ref.gx_ref.gy_ref
  293.0 1.6 copy-done.3
  297.4 5.7 %collective-permute-done.27.fy_ref = bf16[128,1024]{1,0:T(8,128)(2,1)S(1)} collective-permute-done((bf16[128,1024]{1,0:T(8,128)(2,1)S(1)}, bf16[128,1024]{1,0:T(8,128)(2,1)S(1)}, u32[]{:S(2)}, u32[]{:S(2)}) %collective-permute-start.27) | collective-permute-done | bytes 262176 | tf_op jit(solution)/shard_map/ppermute | solution.py:30
  306.4 10.9 %collective-permute-done.28 = bf16[256,1024]{1,0:T(8,128)(2,1)S(1)} collective-permute-done((bf16[256,1024]{1,0:T(8,128)(2,1)S(1)}, bf16[256,1024]{1,0:T(8,128)(2,1)S(1)}, u32[]{:S(2)}, u32[]{:S(2)}) %collective-permute-start.28) | collective-permute-done | bytes 524320 | tf_op jit(solution)/shard_map/ppermute | solution.py:30
  322.7 9.2 %shard_map.221 = (bf16[1024,1024]{1,0:T(8,128)(2,1)}, bf16[1024,1024]{1,0:T(8,128)(2,1)}) custom-call(bf16[2048,512]{1,0:T(8,128)(2,1)} %get-tuple-element.197.h0_ref, bf16[2048,512]{1,0:T(8,128)(2,1)} %get-tuple-element.199.h1_ref, bf16[1024,3072]{1,0:T(8,128)(2,1)} %all-gather.2.cloned.1.call-done.refs_5_.w0_ref.w1_ref, ...), custom_call_target="tpu_custom_call" | custom-call | flops 2000000000 | bytes 1048576 | tf_op jit(solution)/shard_map/pallas_call | solution.py:924
  335.5 6.0 %collective-permute-done.33.refs_4_ = bf16[128,1024]{1,0:T(8,128)(2,1)S(1)} collective-permute-done((bf16[128,1024]{1,0:T(8,128)(2,1)S(1)}, bf16[128,1024]{1,0:T(8,128)(2,1)S(1)}, u32[]{:S(2)}, u32[]{:S(2)}) %collective-permute-start.33) | collective-permute-done | bytes 262176 | tf_op jit(solution)/shard_map/ppermute | solution.py:30
  348.2 1.6 copy-done.7
  353.1 21.3 %shard_map.224 = (bf16[2048,128]{1,0:T(8,128)(2,1)}, f32[2048,128]{1,0:T(8,128)}, f32[2048,128]{1,0:T(8,128)}, bf16[2048,128]{1,0:T(8,128)(2,1)}, bf16[1024,128]{1,0:T(8,128)(2,1)}) custom-call(s32[2]{0:T(128)} %pad_add_fusion.1.info_ref, bf16[2048,128]{1,0:T(8,128)(2,1)} %copy-done.26, bf16[2080,128]{1,0:T(8,128)(2,1)} %copy-done.44, ...), custom_call_target="tpu_custom_call" | custom-call | flops 12000000000 | bytes 1048576 | tf_op jit(solution)/shard_map/pallas_call | solution.py:697
  375.8 1.6 copy-done.5
  377.4 1.6 copy-done.8
  383.8 10.8 %collective-permute-done.39 = bf16[2048,128]{1,0:T(8,128)(2,1)} collective-permute-done((bf16[2048,128]{1,0:T(8,128)(2,1)}, bf16[2048,128]{1,0:T(8,128)(2,1)}, u32[]{:S(2)}, u32[]{:S(2)}) %collective-permute-start.39) | collective-permute-done | bytes 524320 | tf_op jit(solution)/shard_map/ppermute | solution.py:36
  397.4 2.4 shard_map.226
  403.4 8.4 %collective-permute-done.44.refs_2_ = bf16[20,64,128]{2,1,0:T(8,128)(2,1)S(1)} collective-permute-done((bf16[20,64,128]{2,1,0:T(8,128)(2,1)S(1)}, bf16[20,64,128]{2,1,0:T(8,128)(2,1)S(1)}, u32[]{:S(2)}, u32[]{:S(2)}) %collective-permute-start.44) | collective-permute-done | bytes 327712 | tf_op jit(solution)/shard_map/ppermute | solution.py:30
  411.8 6.2 %collective-permute-done.45.refs_3_ = bf16[20,64,128]{2,1,0:T(8,128)(2,1)S(1)} collective-permute-done((bf16[20,64,128]{2,1,0:T(8,128)(2,1)S(1)}, bf16[20,64,128]{2,1,0:T(8,128)(2,1)S(1)}, u32[]{:S(2)}, u32[]{:S(2)}) %collective-permute-start.45) | collective-permute-done | bytes 327712 | tf_op jit(solution)/shard_map/ppermute | solution.py:271
  420.2 11.5 %shard_map.227 = (bf16[1024,1024]{1,0:T(8,128)(2,1)}, bf16[1024,1024]{1,0:T(8,128)(2,1)}, bf16[1024,384]{1,0:T(8,128)(2,1)}, f32[8,1024]{1,0:T(8,128)}) custom-call(bf16[2048,128]{1,0:T(8,128)(2,1)} %get-tuple-element.222.dq_ref, f32[2048,128]{1,0:T(8,128)} %get-tuple-element.239.a_ref, bf16[2048,128]{1,0:T(8,128)(2,1)} %copy-done.60, ...), custom_call_target="tpu_custom_call" | custom-call | flops 10000000000 | bytes 1048576 | tf_op jit(solution)/shard_map/pallas_call | solution.py:781
  431.7 3.0 collective-permute-done.49.refs_7_
  436.0 3.2 collective-permute-done.50.got_ref.gx_ref.gy_ref
  439.2 1.6 copy-done
  441.0 1.6 collective-permute-start.52
  444.6 5.1 %collective-permute-done.53 = f32[2,1024]{1,0:T(2,128)S(1)} collective-permute-done((f32[2,1024]{1,0:T(2,128)S(1)}, f32[2,1024]{1,0:T(2,128)S(1)}, u32[]{:S(2)}, u32[]{:S(2)}) %collective-permute-start.53) | collective-permute-done | bytes 8224 | tf_op jit(solution)/shard_map/ppermute | solution.py:30
  451.7 7.0 %collective-permute-start.56 = (f32[2,1024]{1,0:T(2,128)S(1)}, f32[2,1024]{1,0:T(2,128)S(1)}, u32[]{:S(2)}, u32[]{:S(2)}) collective-permute-start(f32[2,1024]{1,0:T(2,128)S(1)} %add.330), channel_id=1, source_target_pairs={{0,8},{8,0},{16,24},{24,16},{1,9},{9,1},{17,25},{25,17},{2,10},{10... | collective-permute-start | bytes 24584 | tf_op jit(solution)/shard_map/ppermute | solution.py:1140
  459.2 15.6 %shard_map.230 = (f32[20,128,512]{2,1,0:T(8,128)}, f32[20,128,512]{2,1,0:T(8,128)}, f32[20,128,512]{2,1,0:T(8,128)}) custom-call(s32[2]{0:T(128)} %pad_add_fusion.1.info_ref, f32[20]{0:T(128)} %copy-done.28, bf16[20,64,128]{2,1,0:T(8,128)(2,1)} %copy-done.24, bf16[20,64,128]{2,1,0:T(8,128)(2,1)} %copy-done.61, bf16[20,64,128]{2,1,0:T(8,128)(2,1)} %copy-done.62, ...), custom_call_target="tpu_custom_call" | custom-call | flops 6000000000 | bytes 1048576 | tf_op jit(solution)/shard_map/pallas_call | solution.py:402
  474.9 2.1 broadcast_in_dim.96
  477.0 4.2 all-to-all-start.1
  481.3 2.9 fusion.10
  484.2 3.5 collective-permute-start.57
  487.7 1.7 fusion.7
  489.4 3.5 all-to-all-done.1.attn_ref
  494.4 3.0 fusion.6
  497.5 5.6 %shard_map.231 = (f32[20,128,512]{2,1,0:T(8,128)}, f32[20,128,512]{2,1,0:T(8,128)}, f32[20,128,512]{2,1,0:T(8,128)}) custom-call(s32[6]{0:T(128)} %copy-done.51, s32[6]{0:T(128)} %broadcast_add_fusion.held_ref, f32[6]{0:T(128)} %and_select_fusion.rate_ref, ...), custom_call_target="tpu_custom_call", output_to_operand_aliasing={{0}: (7, {}), {1}: (8, {}), {2}: (9, {})} | custom-call | flops 5000000000 | bytes 1048576 | tf_op jit(solution)/shard_map/pallas_call | solution.py:452
  (329 shorter events, 84.5 us)
Async XLA Ops:
  12.2 16.8 %all-to-all-start = ((bf16[8,3,128,128]{3,2,1,0:T(8,128)(2,1)}), bf16[8,3,128,128]{3,2,1,0:T(8,128)(2,1)S(1)}, u32[]{:S(2)}, u32[]{:S(2)}) async-start(bf16[8,3,128,128]{3,2,1,0:T(8,128)(2,1)} %shard_map.206), calls=%async_computation | async-start | bytes 1572864 | tf_op jit(solution)/shard_map/all_to_all | solution.py:978
  17.4 211.5 %all-gather.2.cloned.1.call-start = ((), (), s32[]{:S(2)}) async-start(), calls=%async_computation.5 | async-start | bytes 7864320 | tf_op jit(solution)/shard_map/all_gather | solution.py:1049
  29.1 29.1 %collective-permute-start.2 = (bf16[20,128,128]{2,1,0:T(8,128)(2,1)}, bf16[20,128,128]{2,1,0:T(8,128)(2,1)S(1)}, u32[]{:S(2)}, u32[]{:S(2)}) collective-permute-start(bf16[20,128,128]{2,1,0:T(8,128)(2,1)} %get-tuple-element.155), channel_id=1, source_target_pairs={{0,2},{2,0},{1,3},{3,1},{4,6},{6,4},{5,7},{7,5},{8,10},{10,8},{9,1... | collective-permute-start | bytes 1966088 | tf_op jit(solution)/shard_map/ppermute | solution.py:30
  31.2 27.0 %collective-permute-start.1 = (bf16[256,1152]{1,0:T(8,128)(2,1)S(1)}, bf16[256,1152]{1,0:T(8,128)(2,1)S(1)}, u32[]{:S(2)}, u32[]{:S(2)}) collective-permute-start(bf16[256,1152]{1,0:T(8,128)(2,1)S(1)} %concatenate.13.refs_0_), channel_id=1, source_target_pairs={{0,2},{2,0},{1,3},{3,1},{4,6},{6,4},{5,7},{7,5},{8,10},{10,8},{9,1... | collective-permute-start | bytes 1769480 | tf_op jit(solution)/shard_map/ppermute | solution.py:30
  31.8 26.4 %collective-permute-start = (bf16[256,1152]{1,0:T(8,128)(2,1)S(1)}, bf16[256,1152]{1,0:T(8,128)(2,1)S(1)}, u32[]{:S(2)}, u32[]{:S(2)}) collective-permute-start(bf16[256,1152]{1,0:T(8,128)(2,1)S(1)} %concatenate.13.refs_0_), channel_id=1, source_target_pairs={{0,4},{4,0},{1,5},{5,1},{2,6},{6,2},{3,7},{7,3},{8,12},{12,8},{9,1... | collective-permute-start | bytes 1769480 | tf_op jit(solution)/shard_map/ppermute | solution.py:30
  33.6 25.5 %collective-permute-start.4 = (bf16[20,128,128]{2,1,0:T(8,128)(2,1)}, bf16[20,128,128]{2,1,0:T(8,128)(2,1)S(1)}, u32[]{:S(2)}, u32[]{:S(2)}) collective-permute-start(bf16[20,128,128]{2,1,0:T(8,128)(2,1)} %get-tuple-element.158), channel_id=1, source_target_pairs={{0,1},{1,0},{2,3},{3,2},{4,5},{5,4},{6,7},{7,6},{8,9},{9,8},{10,11... | collective-permute-start | bytes 1966088 | tf_op jit(solution)/shard_map/ppermute | solution.py:30
  58.2 17.1 %collective-permute-start.5 = (bf16[20,128,128]{2,1,0:T(8,128)(2,1)S(1)}, bf16[20,128,128]{2,1,0:T(8,128)(2,1)S(1)}, u32[]{:S(2)}, u32[]{:S(2)}) collective-permute-start(bf16[20,128,128]{2,1,0:T(8,128)(2,1)S(1)} %copy-done.57), channel_id=1, source_target_pairs={{0,3},{1,2},{2,1},{3,0},{4,7},{5,6},{6,5},{7,4},{8,11},{9,10},{10,... | collective-permute-start | bytes 1966088 | tf_op jit(solution)/shard_map/ppermute | solution.py:1021
  58.3 15.8 %collective-permute-start.3 = (bf16[256,1152]{1,0:T(8,128)(2,1)S(1)}, bf16[256,1152]{1,0:T(8,128)(2,1)S(1)}, u32[]{:S(2)}, u32[]{:S(2)}) collective-permute-start(bf16[256,1152]{1,0:T(8,128)(2,1)S(1)} %collective-permute-done.1.refs_2_), channel_id=1, source_target_pairs={{0,4},{4,0},{1,5},{5,1},{2,6},{6,2},{3,7},{7,3},{8,12},{12,8},{9,1... | collective-permute-start | bytes 1769480 | tf_op jit(solution)/shard_map/ppermute | solution.py:30
  76.9 7.6 %collective-permute-start.6 = (bf16[1024,1152]{1,0:T(8,128)(2,1)}, bf16[1024,1152]{1,0:T(8,128)(2,1)}, u32[]{:S(2)}, u32[]{:S(2)}) collective-permute-start(bf16[1024,1152]{1,0:T(8,128)(2,1)} %shard_map.208.low_ref.x_low), channel_id=1, source_target_pairs={{0,1},{1,0},{2,3},{3,2},{4,5},{5,4},{6,7},{7,6},{8,9},{9,8},{10,11... | collective-permute-start | bytes 7077896 | tf_op jit(solution)/shard_map/ppermute | solution.py:30
  85.5 20.1 %collective-permute-start.8 = (bf16[128,3072]{1,0:T(8,128)(2,1)}, bf16[128,3072]{1,0:T(8,128)(2,1)S(1)}, u32[]{:S(2)}, u32[]{:S(2)}) collective-permute-start(bf16[128,3072]{1,0:T(8,128)(2,1)} %get-tuple-element.173), channel_id=1, source_target_pairs={{0,4},{4,0},{1,5},{5,1},{2,6},{6,2},{3,7},{7,3},{8,12},{12,8},{9,1... | collective-permute-start | bytes 2359304 | tf_op jit(solution)/shard_map/ppermute | solution.py:30
  93.5 15.2 %collective-permute-start.7 = (bf16[2080,128]{1,0:T(8,128)(2,1)S(1)}, bf16[2080,128]{1,0:T(8,128)(2,1)S(1)}, u32[]{:S(2)}, u32[]{:S(2)}) collective-permute-start(bf16[2080,128]{1,0:T(8,128)(2,1)S(1)} %pad_maximum_fusion.k0_ref.t0_ref), channel_id=1, source_target_pairs={{0,8},{8,16},{16,24},{1,9},{9,17},{17,25},{2,10},{10,18},{18,26},{... | collective-permute-start | bytes 1597448 | tf_op jit(solution)/shard_map/ppermute | solution.py:36
  108.7 17.2 %collective-permute-start.9 = (bf16[2080,128]{1,0:T(8,128)(2,1)S(1)}, bf16[2080,128]{1,0:T(8,128)(2,1)S(1)}, u32[]{:S(2)}, u32[]{:S(2)}) collective-permute-start(bf16[2080,128]{1,0:T(8,128)(2,1)S(1)} %collective-permute-done.7.k1_ref.t1_ref), channel_id=1, source_target_pairs={{0,8},{8,16},{16,24},{1,9},{9,17},{17,25},{2,10},{10,18},{18,26},{... | collective-permute-start | bytes 1597448 | tf_op jit(solution)/shard_map/ppermute | solution.py:36
  114.1 205.9 %reduce-scatter.4.cloned.1.call-start = ((), (), s32[]{:S(2)}) async-start(), calls=%async_computation.6 | async-start | bytes 3932160 | tf_op jit(solution)/shard_map/reduce_scatter | solution.py:1091
  150.6 9.2 %collective-permute-start.12 = (bf16[128,1024]{1,0:T(8,128)(2,1)S(1)}, bf16[128,1024]{1,0:T(8,128)(2,1)S(1)}, u32[]{:S(2)}, u32[]{:S(2)}) collective-permute-start(bf16[128,1024]{1,0:T(8,128)(2,1)S(1)} %get-tuple-element.310), channel_id=1, source_target_pairs={{0,4},{4,0},{1,5},{5,1},{2,6},{6,2},{3,7},{7,3},{8,12},{12,8},{9,1... | collective-permute-start | bytes 786440 | tf_op jit(solution)/shard_map/ppermute | solution.py:30
  151.2 9.2 %collective-permute-start.11 = (bf16[128,1024]{1,0:T(8,128)(2,1)S(1)}, bf16[128,1024]{1,0:T(8,128)(2,1)S(1)}, u32[]{:S(2)}, u32[]{:S(2)}) collective-permute-start(bf16[128,1024]{1,0:T(8,128)(2,1)S(1)} %get-tuple-element.311), channel_id=1, source_target_pairs={{0,2},{2,0},{1,3},{3,1},{4,6},{6,4},{5,7},{7,5},{8,10},{10,8},{9,1... | collective-permute-start | bytes 786440 | tf_op jit(solution)/shard_map/ppermute | solution.py:30
  151.5 20.1 %collective-permute-start.21 = (bf16[256,1024]{1,0:T(8,128)(2,1)S(1)}, bf16[256,1024]{1,0:T(8,128)(2,1)S(1)}, u32[]{:S(2)}, u32[]{:S(2)}) collective-permute-start(bf16[256,1024]{1,0:T(8,128)(2,1)S(1)} %bitcast.54), channel_id=1, source_target_pairs={{0,2},{2,0},{1,3},{3,1},{4,6},{6,4},{5,7},{7,5},{8,10},{10,8},{9,1... | collective-permute-start | bytes 1572872 | tf_op jit(solution)/shard_map/ppermute | solution.py:30
  153.4 19.8 %collective-permute-start.20 = (bf16[256,1024]{1,0:T(8,128)(2,1)S(1)}, bf16[256,1024]{1,0:T(8,128)(2,1)}, u32[]{:S(2)}, u32[]{:S(2)}) collective-permute-start(bf16[256,1024]{1,0:T(8,128)(2,1)S(1)} %bitcast.55), channel_id=1, source_target_pairs={{0,4},{4,0},{1,5},{5,1},{2,6},{6,2},{3,7},{7,3},{8,12},{12,8},{9,1... | collective-permute-start | bytes 1572872 | tf_op jit(solution)/shard_map/ppermute | solution.py:30
  161.5 20.9 %collective-permute-start.13 = (bf16[256,1024]{1,0:T(8,128)(2,1)}, bf16[256,1024]{1,0:T(8,128)(2,1)}, u32[]{:S(2)}, u32[]{:S(2)}) collective-permute-start(bf16[256,1024]{1,0:T(8,128)(2,1)} %get-tuple-element.177), channel_id=1, source_target_pairs={{0,4},{4,0},{1,5},{5,1},{2,6},{6,2},{3,7},{7,3},{8,12},{12,8},{9,1... | collective-permute-start | bytes 1572872 | tf_op jit(solution)/shard_map/ppermute | solution.py:30
  163.0 19.9 %collective-permute-start.14 = (bf16[256,1024]{1,0:T(8,128)(2,1)}, bf16[256,1024]{1,0:T(8,128)(2,1)}, u32[]{:S(2)}, u32[]{:S(2)}) collective-permute-start(bf16[256,1024]{1,0:T(8,128)(2,1)} %get-tuple-element.178), channel_id=1, source_target_pairs={{0,2},{2,0},{1,3},{3,1},{4,6},{6,4},{5,7},{7,5},{8,10},{10,8},{9,1... | collective-permute-start | bytes 1572872 | tf_op jit(solution)/shard_map/ppermute | solution.py:30
  171.6 16.3 %collective-permute-start.23 = (bf16[128,1024]{1,0:T(8,128)(2,1)S(1)}, bf16[128,1024]{1,0:T(8,128)(2,1)S(1)}, u32[]{:S(2)}, u32[]{:S(2)}) collective-permute-start(bf16[128,1024]{1,0:T(8,128)(2,1)S(1)} %slice.165), channel_id=1, source_target_pairs={{0,4},{4,0},{1,5},{5,1},{2,6},{6,2},{3,7},{7,3},{8,12},{12,8},{9,1... | collective-permute-start | bytes 786440 | tf_op jit(solution)/shard_map/ppermute | solution.py:30
  174.2 14.3 %collective-permute-start.22 = (bf16[128,1024]{1,0:T(8,128)(2,1)S(1)}, bf16[128,1024]{1,0:T(8,128)(2,1)S(1)}, u32[]{:S(2)}, u32[]{:S(2)}) collective-permute-start(bf16[128,1024]{1,0:T(8,128)(2,1)S(1)} %slice.164), channel_id=1, source_target_pairs={{0,2},{2,0},{1,3},{3,1},{4,6},{6,4},{5,7},{7,5},{8,10},{10,8},{9,1... | collective-permute-start | bytes 786440 | tf_op jit(solution)/shard_map/ppermute | solution.py:30
  185.0 13.7 %collective-permute-start.16 = (bf16[256,1024]{1,0:T(8,128)(2,1)S(1)}, bf16[256,1024]{1,0:T(8,128)(2,1)}, u32[]{:S(2)}, u32[]{:S(2)}) collective-permute-start(bf16[256,1024]{1,0:T(8,128)(2,1)S(1)} %multiply_convert_fusion.refs_0_), channel_id=1, source_target_pairs={{0,2},{2,0},{1,3},{3,1},{4,6},{6,4},{5,7},{7,5},{8,10},{10,8},{9,1... | collective-permute-start | bytes 1572872 | tf_op jit(solution)/shard_map/ppermute | solution.py:30
  185.0 16.2 %collective-permute-start.15 = (bf16[256,1024]{1,0:T(8,128)(2,1)S(1)}, bf16[256,1024]{1,0:T(8,128)(2,1)}, u32[]{:S(2)}, u32[]{:S(2)}) collective-permute-start(bf16[256,1024]{1,0:T(8,128)(2,1)S(1)} %multiply_convert_fusion.refs_0_), channel_id=1, source_target_pairs={{0,4},{4,0},{1,5},{5,1},{2,6},{6,2},{3,7},{7,3},{8,12},{12,8},{9,1... | collective-permute-start | bytes 1572872 | tf_op jit(solution)/shard_map/ppermute | solution.py:30
  189.7 26.5 %collective-permute-start.24 = (bf16[1024,1024]{1,0:T(8,128)(2,1)S(1)}, bf16[1024,1024]{1,0:T(8,128)(2,1)}, u32[]{:S(2)}, u32[]{:S(2)}) collective-permute-start(bf16[1024,1024]{1,0:T(8,128)(2,1)S(1)} %shard_map.216.refs_2_), channel_id=1, source_target_pairs={{0,1},{1,0},{2,3},{3,2},{4,5},{5,4},{6,7},{7,6},{8,9},{9,8},{10,11... | collective-permute-start | bytes 6291464 | tf_op jit(solution)/shard_map/ppermute | solution.py:30
  199.6 7.1 %collective-permute-start.18 = (bf16[128,1024]{1,0:T(8,128)(2,1)S(1)}, bf16[128,1024]{1,0:T(8,128)(2,1)S(1)}, u32[]{:S(2)}, u32[]{:S(2)}) collective-permute-start(bf16[128,1024]{1,0:T(8,128)(2,1)S(1)} %slice.163), channel_id=1, source_target_pairs={{0,4},{4,0},{1,5},{5,1},{2,6},{6,2},{3,7},{7,3},{8,12},{12,8},{9,1... | collective-permute-start | bytes 786440 | tf_op jit(solution)/shard_map/ppermute | solution.py:30
  202.2 6.8 %collective-permute-start.17 = (bf16[128,1024]{1,0:T(8,128)(2,1)S(1)}, bf16[128,1024]{1,0:T(8,128)(2,1)S(1)}, u32[]{:S(2)}, u32[]{:S(2)}) collective-permute-start(bf16[128,1024]{1,0:T(8,128)(2,1)S(1)} %slice.162), channel_id=1, source_target_pairs={{0,2},{2,0},{1,3},{3,1},{4,6},{6,4},{5,7},{7,5},{8,10},{10,8},{9,1... | collective-permute-start | bytes 786440 | tf_op jit(solution)/shard_map/ppermute | solution.py:30
  211.6 4.5 collective-permute-start.19
  257.9 122.7 %reduce-scatter.6.cloned.1.call-start = ((), (), s32[]{:S(2)}) async-start(), calls=%async_computation.7 | async-start | bytes 3932160 | tf_op jit(solution)/shard_map/reduce_scatter | solution.py:1091
  288.5 4.4 collective-permute-start.25
  294.7 8.4 %collective-permute-start.27 = (bf16[128,1024]{1,0:T(8,128)(2,1)S(1)}, bf16[128,1024]{1,0:T(8,128)(2,1)S(1)}, u32[]{:S(2)}, u32[]{:S(2)}) collective-permute-start(bf16[128,1024]{1,0:T(8,128)(2,1)S(1)} %get-tuple-element.308), channel_id=1, source_target_pairs={{0,4},{4,0},{1,5},{5,1},{2,6},{6,2},{3,7},{7,3},{8,12},{12,8},{9,1... | collective-permute-start | bytes 786440 | tf_op jit(solution)/shard_map/ppermute | solution.py:30
  295.9 8.0 %collective-permute-start.26 = (bf16[128,1024]{1,0:T(8,128)(2,1)S(1)}, bf16[128,1024]{1,0:T(8,128)(2,1)S(1)}, u32[]{:S(2)}, u32[]{:S(2)}) collective-permute-start(bf16[128,1024]{1,0:T(8,128)(2,1)S(1)} %get-tuple-element.309), channel_id=1, source_target_pairs={{0,2},{2,0},{1,3},{3,1},{4,6},{6,4},{5,7},{7,5},{8,10},{10,8},{9,1... | collective-permute-start | bytes 786440 | tf_op jit(solution)/shard_map/ppermute | solution.py:30
  304.3 13.0 %collective-permute-start.28 = (bf16[256,1024]{1,0:T(8,128)(2,1)S(1)}, bf16[256,1024]{1,0:T(8,128)(2,1)S(1)}, u32[]{:S(2)}, u32[]{:S(2)}) collective-permute-start(bf16[256,1024]{1,0:T(8,128)(2,1)S(1)} %get-tuple-element.192), channel_id=1, source_target_pairs={{0,4},{4,0},{1,5},{5,1},{2,6},{6,2},{3,7},{7,3},{8,12},{12,8},{9,1... | collective-permute-start | bytes 1572872 | tf_op jit(solution)/shard_map/ppermute | solution.py:30
  305.3 12.6 %collective-permute-start.29 = (bf16[256,1024]{1,0:T(8,128)(2,1)S(1)}, bf16[256,1024]{1,0:T(8,128)(2,1)S(1)}, u32[]{:S(2)}, u32[]{:S(2)}) collective-permute-start(bf16[256,1024]{1,0:T(8,128)(2,1)S(1)} %get-tuple-element.193), channel_id=1, source_target_pairs={{0,2},{2,0},{1,3},{3,1},{4,6},{6,4},{5,7},{7,5},{8,10},{10,8},{9,1... | collective-permute-start | bytes 1572872 | tf_op jit(solution)/shard_map/ppermute | solution.py:30
  320.0 11.8 %collective-permute-start.31 = (bf16[256,1024]{1,0:T(8,128)(2,1)S(1)}, bf16[256,1024]{1,0:T(8,128)(2,1)S(1)}, u32[]{:S(2)}, u32[]{:S(2)}) collective-permute-start(bf16[256,1024]{1,0:T(8,128)(2,1)S(1)} %get-tuple-element.195.refs_0_), channel_id=1, source_target_pairs={{0,2},{2,0},{1,3},{3,1},{4,6},{6,4},{5,7},{7,5},{8,10},{10,8},{9,1... | collective-permute-start | bytes 1572872 | tf_op jit(solution)/shard_map/ppermute | solution.py:30
  321.2 11.5 %collective-permute-start.30 = (bf16[256,1024]{1,0:T(8,128)(2,1)S(1)}, bf16[256,1024]{1,0:T(8,128)(2,1)S(1)}, u32[]{:S(2)}, u32[]{:S(2)}) collective-permute-start(bf16[256,1024]{1,0:T(8,128)(2,1)S(1)} %get-tuple-element.195.refs_0_), channel_id=1, source_target_pairs={{0,4},{4,0},{1,5},{5,1},{2,6},{6,2},{3,7},{7,3},{8,12},{12,8},{9,1... | collective-permute-start | bytes 1572872 | tf_op jit(solution)/shard_map/ppermute | solution.py:30
  322.6 152.3 %reduce-scatter.8.cloned.1.call-start = ((), (), s32[]{:S(2)}) async-start(), calls=%async_computation.8 | async-start | bytes 983040 | tf_op jit(solution)/shard_map/reduce_scatter | solution.py:1127
  332.7 10.0 %collective-permute-start.34 = (bf16[1024,1024]{1,0:T(8,128)(2,1)}, bf16[1024,1024]{1,0:T(8,128)(2,1)S(1)}, u32[]{:S(2)}, u32[]{:S(2)}) collective-permute-start(bf16[1024,1024]{1,0:T(8,128)(2,1)} %get-tuple-element.205), channel_id=1, source_target_pairs={{0,1},{1,0},{2,3},{3,2},{4,5},{5,4},{6,7},{7,6},{8,9},{9,8},{10,11... | collective-permute-start | bytes 6291464 | tf_op jit(solution)/shard_map/ppermute | solution.py:30
  333.5 8.0 %collective-permute-start.33 = (bf16[128,1024]{1,0:T(8,128)(2,1)S(1)}, bf16[128,1024]{1,0:T(8,128)(2,1)S(1)}, u32[]{:S(2)}, u32[]{:S(2)}) collective-permute-start(bf16[128,1024]{1,0:T(8,128)(2,1)S(1)} %slice.138), channel_id=1, source_target_pairs={{0,4},{4,0},{1,5},{5,1},{2,6},{6,2},{3,7},{7,3},{8,12},{12,8},{9,1... | collective-permute-start | bytes 786440 | tf_op jit(solution)/shard_map/ppermute | solution.py:30
  335.0 7.7 %collective-permute-start.32 = (bf16[128,1024]{1,0:T(8,128)(2,1)S(1)}, bf16[128,1024]{1,0:T(8,128)(2,1)S(1)}, u32[]{:S(2)}, u32[]{:S(2)}) collective-permute-start(bf16[128,1024]{1,0:T(8,128)(2,1)S(1)} %slice.137), channel_id=1, source_target_pairs={{0,2},{2,0},{1,3},{3,1},{4,6},{6,4},{5,7},{7,5},{8,10},{10,8},{9,1... | collective-permute-start | bytes 786440 | tf_op jit(solution)/shard_map/ppermute | solution.py:30
  346.5 4.5 collective-permute-start.35
  347.5 27.0 %collective-permute-start.36 = (bf16[128,1536]{1,0:T(8,128)(2,1)S(1)}, bf16[128,1536]{1,0:T(8,128)(2,1)S(1)}, u32[]{:S(2)}, u32[]{:S(2)}) collective-permute-start(bf16[128,1536]{1,0:T(8,128)(2,1)S(1)} %constant_dynamic-slice_fusion), channel_id=1, source_target_pairs={{0,4},{4,0},{1,5},{5,1},{2,6},{6,2},{3,7},{7,3},{8,12},{12,8},{9,1... | collective-permute-start | bytes 1179656 | tf_op jit(solution)/shard_map/ppermute | solution.py:30
  351.7 22.8 %collective-permute-start.38 = (bf16[128,1024]{1,0:T(8,128)(2,1)}, bf16[128,1024]{1,0:T(8,128)(2,1)S(1)}, u32[]{:S(2)}, u32[]{:S(2)}) collective-permute-start(bf16[128,1024]{1,0:T(8,128)(2,1)} %get-tuple-element.306), channel_id=1, source_target_pairs={{0,4},{4,0},{1,5},{5,1},{2,6},{6,2},{3,7},{7,3},{8,12},{12,8},{9,1... | collective-permute-start | bytes 786440 | tf_op jit(solution)/shard_map/ppermute | solution.py:30
  352.3 22.2 %collective-permute-start.37 = (bf16[128,1024]{1,0:T(8,128)(2,1)S(1)}, bf16[128,1024]{1,0:T(8,128)(2,1)S(1)}, u32[]{:S(2)}, u32[]{:S(2)}) collective-permute-start(bf16[128,1024]{1,0:T(8,128)(2,1)S(1)} %get-tuple-element.307), channel_id=1, source_target_pairs={{0,2},{2,0},{1,3},{3,1},{4,6},{6,4},{5,7},{7,5},{8,10},{10,8},{9,1... | collective-permute-start | bytes 786440 | tf_op jit(solution)/shard_map/ppermute | solution.py:30
  374.5 20.1 %collective-permute-start.39 = (bf16[2048,128]{1,0:T(8,128)(2,1)}, bf16[2048,128]{1,0:T(8,128)(2,1)}, u32[]{:S(2)}, u32[]{:S(2)}) collective-permute-start(bf16[2048,128]{1,0:T(8,128)(2,1)} %get-tuple-element.219), channel_id=1, source_target_pairs={{8,0},{16,8},{24,16},{9,1},{17,9},{25,17},{10,2},{18,10},{26,18},{... | collective-permute-start | bytes 1572872 | tf_op jit(solution)/shard_map/ppermute | solution.py:36
  379.3 15.3 %collective-permute-start.41 = (bf16[256,1024]{1,0:T(8,128)(2,1)S(1)}, bf16[256,1024]{1,0:T(8,128)(2,1)}, u32[]{:S(2)}, u32[]{:S(2)}) collective-permute-start(bf16[256,1024]{1,0:T(8,128)(2,1)S(1)} %get-tuple-element.226), channel_id=1, source_target_pairs={{0,2},{2,0},{1,3},{3,1},{4,6},{6,4},{5,7},{7,5},{8,10},{10,8},{9,1... | collective-permute-start | bytes 1572872 | tf_op jit(solution)/shard_map/ppermute | solution.py:30
  381.7 12.9 %collective-permute-start.40 = (bf16[128,1536]{1,0:T(8,128)(2,1)S(1)}, bf16[128,1536]{1,0:T(8,128)(2,1)S(1)}, u32[]{:S(2)}, u32[]{:S(2)}) collective-permute-start(bf16[128,1536]{1,0:T(8,128)(2,1)S(1)} %constant_dynamic-slice_fusion.1), channel_id=1, source_target_pairs={{0,4},{4,0},{1,5},{5,1},{2,6},{6,2},{3,7},{7,3},{8,12},{12,8},{9,1... | collective-permute-start | bytes 1179656 | tf_op jit(solution)/shard_map/ppermute | solution.py:30
  383.2 20.1 %collective-permute-start.46 = (bf16[256,1024]{1,0:T(8,128)(2,1)S(1)}, bf16[256,1024]{1,0:T(8,128)(2,1)S(1)}, u32[]{:S(2)}, u32[]{:S(2)}) collective-permute-start(bf16[256,1024]{1,0:T(8,128)(2,1)S(1)} %get-tuple-element.236), channel_id=1, source_target_pairs={{0,4},{4,0},{1,5},{5,1},{2,6},{6,2},{3,7},{7,3},{8,12},{12,8},{9,1... | collective-permute-start | bytes 1572872 | tf_op jit(solution)/shard_map/ppermute | solution.py:30
  396.1 22.0 %collective-permute-start.42 = (bf16[2048,128]{1,0:T(8,128)(2,1)S(1)}, bf16[2048,128]{1,0:T(8,128)(2,1)S(1)}, u32[]{:S(2)}, u32[]{:S(2)}) collective-permute-start(bf16[2048,128]{1,0:T(8,128)(2,1)S(1)} %add_convert_fusion.1), channel_id=1, source_target_pairs={{8,0},{16,8},{24,16},{9,1},{17,9},{25,17},{10,2},{18,10},{26,18},{... | collective-permute-start | bytes 1572872 | tf_op jit(solution)/shard_map/ppermute | solution.py:36
  401.3 10.5 %collective-permute-start.44 = (bf16[20,64,128]{2,1,0:T(8,128)(2,1)S(1)}, bf16[20,64,128]{2,1,0:T(8,128)(2,1)S(1)}, u32[]{:S(2)}, u32[]{:S(2)}) collective-permute-start(bf16[20,64,128]{2,1,0:T(8,128)(2,1)S(1)} %get-tuple-element.234), channel_id=1, source_target_pairs={{0,2},{2,0},{1,3},{3,1},{4,6},{6,4},{5,7},{7,5},{8,10},{10,8},{9,1... | collective-permute-start | bytes 983048 | tf_op jit(solution)/shard_map/ppermute | solution.py:30
  402.8 15.3 %collective-permute-start.45 = (bf16[20,64,128]{2,1,0:T(8,128)(2,1)S(1)}, bf16[20,64,128]{2,1,0:T(8,128)(2,1)S(1)}, u32[]{:S(2)}, u32[]{:S(2)}) collective-permute-start(bf16[20,64,128]{2,1,0:T(8,128)(2,1)S(1)} %get-tuple-element.235), channel_id=1, source_target_pairs={{0,3},{1,2},{2,1},{3,0},{4,7},{5,6},{6,5},{7,4},{8,11},{9,10},{10,... | collective-permute-start | bytes 983048 | tf_op jit(solution)/shard_map/ppermute | solution.py:271
  418.1 13.7 %collective-permute-start.47 = (bf16[20,64,128]{2,1,0:T(8,128)(2,1)S(1)}, bf16[20,64,128]{2,1,0:T(8,128)(2,1)}, u32[]{:S(2)}, u32[]{:S(2)}) collective-permute-start(bf16[20,64,128]{2,1,0:T(8,128)(2,1)S(1)} %get-tuple-element.247), channel_id=1, source_target_pairs={{0,1},{1,0},{2,3},{3,2},{4,5},{5,4},{6,7},{7,6},{8,9},{9,8},{10,11... | collective-permute-start | bytes 983048 | tf_op jit(solution)/shard_map/ppermute | solution.py:30
  418.3 13.4 %collective-permute-start.48 = (bf16[20,64,128]{2,1,0:T(8,128)(2,1)S(1)}, bf16[20,64,128]{2,1,0:T(8,128)(2,1)}, u32[]{:S(2)}, u32[]{:S(2)}) collective-permute-start(bf16[20,64,128]{2,1,0:T(8,128)(2,1)S(1)} %get-tuple-element.249), channel_id=1, source_target_pairs={{0,2},{2,0},{1,3},{3,1},{4,6},{6,4},{5,7},{7,5},{8,10},{10,8},{9,1... | collective-permute-start | bytes 983048 | tf_op jit(solution)/shard_map/ppermute | solution.py:30
  419.8 14.9 %collective-permute-start.49 = (bf16[20,64,128]{2,1,0:T(8,128)(2,1)S(1)}, bf16[20,64,128]{2,1,0:T(8,128)(2,1)}, u32[]{:S(2)}, u32[]{:S(2)}) collective-permute-start(bf16[20,64,128]{2,1,0:T(8,128)(2,1)S(1)} %get-tuple-element.251), channel_id=1, source_target_pairs={{0,3},{1,2},{2,1},{3,0},{4,7},{5,6},{6,5},{7,4},{8,11},{9,10},{10,... | collective-permute-start | bytes 983048 | tf_op jit(solution)/shard_map/ppermute | solution.py:271
  434.7 4.4 collective-permute-start.50
  441.0 8.8 %collective-permute-start.52 = (bf16[128,1024]{1,0:T(8,128)(2,1)S(1)}, bf16[128,1024]{1,0:T(8,128)(2,1)S(1)}, u32[]{:S(2)}, u32[]{:S(2)}) collective-permute-start(bf16[128,1024]{1,0:T(8,128)(2,1)S(1)} %get-tuple-element.304), channel_id=1, source_target_pairs={{0,4},{4,0},{1,5},{5,1},{2,6},{6,2},{3,7},{7,3},{8,12},{12,8},{9,1... | collective-permute-start | bytes 786440 | tf_op jit(solution)/shard_map/ppermute | solution.py:30
  442.5 8.3 %collective-permute-start.51 = (bf16[128,1024]{1,0:T(8,128)(2,1)S(1)}, bf16[128,1024]{1,0:T(8,128)(2,1)S(1)}, u32[]{:S(2)}, u32[]{:S(2)}) collective-permute-start(bf16[128,1024]{1,0:T(8,128)(2,1)S(1)} %get-tuple-element.305), channel_id=1, source_target_pairs={{0,2},{2,0},{1,3},{3,1},{4,6},{6,4},{5,7},{7,5},{8,10},{10,8},{9,1... | collective-permute-start | bytes 786440 | tf_op jit(solution)/shard_map/ppermute | solution.py:30
  444.0 5.8 %collective-permute-start.53 = (f32[2,1024]{1,0:T(2,128)S(1)}, f32[2,1024]{1,0:T(2,128)S(1)}, u32[]{:S(2)}, u32[]{:S(2)}) collective-permute-start(f32[2,1024]{1,0:T(2,128)S(1)} %pad_maximum_fusion.2), channel_id=1, source_target_pairs={{0,4},{4,0},{1,5},{5,1},{2,6},{6,2},{3,7},{7,3},{8,12},{12,8},{9,1... | collective-permute-start | bytes 24584 | tf_op jit(solution)/shard_map/ppermute | solution.py:30
  451.1 23.8 %collective-permute-start.54 = (bf16[256,1024]{1,0:T(8,128)(2,1)S(1)}, bf16[256,1024]{1,0:T(8,128)(2,1)S(1)}, u32[]{:S(2)}, u32[]{:S(2)}) collective-permute-start(bf16[256,1024]{1,0:T(8,128)(2,1)S(1)} %get-tuple-element.259), channel_id=1, source_target_pairs={{0,4},{4,0},{1,5},{5,1},{2,6},{6,2},{3,7},{7,3},{8,12},{12,8},{9,1... | collective-permute-start | bytes 1572872 | tf_op jit(solution)/shard_map/ppermute | solution.py:30
  451.7 23.1 %collective-permute-start.56 = (f32[2,1024]{1,0:T(2,128)S(1)}, f32[2,1024]{1,0:T(2,128)S(1)}, u32[]{:S(2)}, u32[]{:S(2)}) collective-permute-start(f32[2,1024]{1,0:T(2,128)S(1)} %add.330), channel_id=1, source_target_pairs={{0,8},{8,0},{16,24},{24,16},{1,9},{9,1},{17,25},{25,17},{2,10},{10... | collective-permute-start | bytes 24584 | tf_op jit(solution)/shard_map/ppermute | solution.py:1140
  458.7 16.2 %collective-permute-start.55 = (bf16[256,1024]{1,0:T(8,128)(2,1)S(1)}, bf16[256,1024]{1,0:T(8,128)(2,1)}, u32[]{:S(2)}, u32[]{:S(2)}) collective-permute-start(bf16[256,1024]{1,0:T(8,128)(2,1)S(1)} %get-tuple-element.260), channel_id=1, source_target_pairs={{0,2},{2,0},{1,3},{3,1},{4,6},{6,4},{5,7},{7,5},{8,10},{10,8},{9,1... | collective-permute-start | bytes 1572872 | tf_op jit(solution)/shard_map/ppermute | solution.py:30
  477.0 15.9 %all-to-all-start.1 = ((bf16[8,128,384]{2,1,0:T(8,128)(2,1)}), bf16[8,128,384]{2,1,0:T(8,128)(2,1)}, u32[]{:S(2)}, u32[]{:S(2)}) async-start(bf16[8,128,384]{2,1,0:T(8,128)(2,1)} %bitcast.27), calls=%async_computation.4 | async-start | bytes 1572864 | tf_op jit(solution)/shard_map/all_to_all | solution.py:1163
  484.2 5.2 %collective-permute-start.57 = (f32[2,1024]{1,0:T(2,128)S(1)}, f32[2,1024]{1,0:T(2,128)S(1)}, u32[]{:S(2)}, u32[]{:S(2)}) collective-permute-start(f32[2,1024]{1,0:T(2,128)S(1)} %add.331), channel_id=1, source_target_pairs={{0,16},{8,24},{16,0},{24,8},{1,17},{9,25},{17,1},{25,9},{2,18},{10... | collective-permute-start | bytes 24584 | tf_op jit(solution)/shard_map/ppermute | solution.py:1140
  492.9 4.5 collective-permute-start.58
  497.4 5.7 %collective-permute-start.59 = (f32[2,1024]{1,0:T(2,128)S(1)}, f32[2,1024]{1,0:T(2,128)S(1)}, u32[]{:S(2)}, u32[]{:S(2)}) collective-permute-start(f32[2,1024]{1,0:T(2,128)S(1)} %add.336), channel_id=1, source_target_pairs={{0,1},{1,0},{2,3},{3,2},{4,5},{5,4},{6,7},{7,6},{8,9},{9,8},{10,11... | collective-permute-start | bytes 24584 | tf_op jit(solution)/shard_map/ppermute | solution.py:30
  (66 other events, 771.4 us)
Sparse Core Ops, SparseCore 0:
  114.2 114.6 all-gather.1
  258.1 58.4 reduce-scatter.3
  322.7 57.4 reduce-scatter.5
  435.3 29.8 reduce-scatter.7

commit v5 on v4

--- a/solution.py
+++ b/solution.py
@@ -621,7 +621,7 @@
             pltpu.SMEM((1,), jnp.int32),
         ],
         cost_estimate=took(24),
-        compiler_params=vmem(62),
+        compiler_params=vmem(32),
     )(info, query, *kv, *kv, qseg, weights)
 
 
@@ -733,7 +733,7 @@
             pltpu.VMEM((2 * HD, block), F32),
         ],
         cost_estimate=took(12),
-        compiler_params=vmem(62),
+        compiler_params=vmem(36),
     )(info, query, *kv, *kv, qseg, stat, *grad_rows, mix, weights, cosine, sine)
 
 
@@ -801,7 +801,7 @@
         ],
         scratch_shapes=[pltpu.VMEM((cols, width), F32)],
         cost_estimate=took(10),
-        compiler_params=vmem(62),
+        compiler_params=vmem(20),
     )(grad_q, here, arrived, *x_rows, weights, cosine, sine, grad_out)
 
 
@@ -932,7 +932,7 @@
         out_specs=half_specs(block, width, rows, lambda i: i),
         out_shape=[jax.ShapeDtypeStruct((rows // 2, width), BF)] * 2,
         cost_estimate=took(2),
-        compiler_params=vmem(62),
+        compiler_params=vmem(24),
     )(*hidden, weights, weights)
 
 

time: 518 us -> 518 us (level)
    unnamed x129 -> x179, local copies, waits for them, and re-layouts: 15.3 us -> 17.4 us
  transfers between devices with their start and end apart: 66 -> 66, of which waited for: 37 -> 37; matrix products, arithmetic and copies ran while one was open for 7% -> 6% of each run, Pallas kernels for 27% -> 27%
where the time goes in v5:
time: 518 us; the launch traced here: 511 us
  waiting for transfers between devices  178 us (34%)
  Pallas kernels  170 us (33%)
  starting transfers between devices  72.5 us (14%)
  local copies, waits for them, and re-layouts  32.7 us (6%)
  other arithmetic  23.2 us (4%)
  blocking collectives  19.8 us (4%)
  between operations  15.4 us (3%)
    ppermute x51, waiting for transfers between devices, swap(): return lax.ppermute(value, axis, [(0, 1), (1, 0)])  118 us
    pallas_call x2, Pallas kernels, expert_rows(): pl.pallas_call(lambda *refs: expert_kernel(part, start, len(before), *ref...  59.2 us
    ppermute x51, starting transfers between devices, swap(): return lax.ppermute(value, axis, [(0, 1), (1, 0)])  41.6 us
    ppermute x4, waiting for transfers between devices, shift(): return lax.ppermute(value, 'z', pairs)  26.3 us
    pallas_call x1, Pallas kernels, attend_back(): pl.pallas_call(attend_back_kernel, grid=(seqs, 2), in_specs=[pl.BlockSpec...  20 us
    all_gather x1, blocking collectives, shards(): lax.all_gather(attn_mine, 'z', axis=0, tiled=True)  19.8 us
    unnamed x179, local copies, waits for them, and re-layouts  17.4 us
    pallas_call x1, Pallas kernels, update(): pl.pallas_call(update_kernel, grid=(slots // step,), in_specs=[smem, smem...  15.6 us
  transfers between devices with their start and end apart: 66, of which 37 were waited for; matrix products, arithmetic and copies ran while one was open for 6% of the time, Pallas kernels for 27%

profile of v5, /device:TPU:0, one launch (start us, length us, event | category | flops | bytes accessed | tf_op | source)
XLA Modules:
  0.0 510.9 jit_solution(14325451546065442049)
XLA Ops:
  8.9 3.2 shard_map.206
  12.1 5.4 %all-to-all-start = ((bf16[8,3,128,128]{3,2,1,0:T(8,128)(2,1)}), bf16[8,3,128,128]{3,2,1,0:T(8,128)(2,1)S(1)}, u32[]{:S(2)}, u32[]{:S(2)}) async-start(bf16[8,3,128,128]{3,2,1,0:T(8,128)(2,1)} %shard_map.206), calls=%async_computation | async-start | bytes 1572864 | tf_op jit(solution)/shard_map/all_to_all | solution.py:978
  18.8 4.8 shard_map.207
  23.6 5.5 %all-to-all-done = bf16[8,3,128,128]{3,2,1,0:T(8,128)(2,1)S(1)} async-done(((bf16[8,3,128,128]{3,2,1,0:T(8,128)(2,1)}), bf16[8,3,128,128]{3,2,1,0:T(8,128)(2,1)S(1)}, u32[]{:S(2)}, u32[]{:S(2)}) %all-to-all-start) | async-done | bytes 786464 | tf_op jit(solution)/shard_map/all_to_all | solution.py:978
  33.7 19.8 %all_gather.6.w_ref = bf16[1024,384]{1,0:T(8,128)(2,1)S(1)} all-gather(bf16[256,384]{1,0:T(8,128)(2,1)S(1)} %bitcast.62), channel_id=1, replica_groups=mesh['z'=4,'x'=2,'y'=2,'c'=2] {'z'}, dimensions={0}, use_global_device_ids=true | all-gather | bytes 983040 | tf_op jit(solution)/shard_map/all_gather | solution.py:1016
  53.5 4.7 collective-permute-done.1.refs_2_
  59.1 15.0 %collective-permute-done.3.refs_3_ = bf16[256,1152]{1,0:T(8,128)(2,1)S(1)} collective-permute-done((bf16[256,1152]{1,0:T(8,128)(2,1)S(1)}, bf16[256,1152]{1,0:T(8,128)(2,1)S(1)}, u32[]{:S(2)}, u32[]{:S(2)}) %collective-permute-start.3) | collective-permute-done | bytes 589856 | tf_op jit(solution)/shard_map/ppermute | solution.py:30
  75.4 1.6 shard_map.208.low_ref.x_low
  80.6 4.1 shard_map.209
  86.6 6.8 %shard_map.210 = (bf16[2048,128]{1,0:T(8,128)(2,1)S(1)}, bf16[2048,128]{1,0:T(8,128)(2,1)S(1)}) custom-call(bf16[1024,1152]{1,0:T(8,128)(2,1)} %shard_map.208.low_ref.x_low, bf16[1024,1152]{1,0:T(8,128)(2,1)} %collective-permute-done.6.high_ref.x_high, bf16[1024,384]{1,0:T(8,128)(2,1)S(1)} %all_gather.6.w_ref, f32[2,256,128]{2,1,0:T(8,128)S(1)} %copy.74.cos_ref, ...), custom_call_target="tpu_custom_call" | custom-call | flops 6000000000 | bytes 1048576 | tf_op jit(solution)/shard_map/pallas_call | solution.py:488
  93.6 3.6 collective-permute-start.7
  97.2 8.5 %collective-permute-done.8.refs_1_ = bf16[128,3072]{1,0:T(8,128)(2,1)S(1)} collective-permute-done((bf16[128,3072]{1,0:T(8,128)(2,1)}, bf16[128,3072]{1,0:T(8,128)(2,1)S(1)}, u32[]{:S(2)}, u32[]{:S(2)}) %collective-permute-start.8) | collective-permute-done | bytes 786464 | tf_op jit(solution)/shard_map/ppermute | solution.py:30
  105.7 1.8 shard_map.211
  108.9 4.4 collective-permute-start.9
  114.0 13.3 %collective-permute-done.9.k2_ref.t2_ref = bf16[2080,128]{1,0:T(8,128)(2,1)S(1)} collective-permute-done((bf16[2080,128]{1,0:T(8,128)(2,1)S(1)}, bf16[2080,128]{1,0:T(8,128)(2,1)S(1)}, u32[]{:S(2)}, u32[]{:S(2)}) %collective-permute-start.9) | collective-permute-done | bytes 532512 | tf_op jit(solution)/shard_map/ppermute | solution.py:36
  131.2 15.3 %shard_map.212 = (bf16[2048,128]{1,0:T(8,128)(2,1)S(1)}, f32[4,2,2,256]{3,2,1,0:T(2,128)S(1)}, bf16[1024,1024]{1,0:T(8,128)(2,1)S(1)}, bf16[1024,1024]{1,0:T(8,128)(2,1)S(1)}) custom-call(s32[2]{0:T(128)S(1)} %copy-done.36, bf16[2048,128]{1,0:T(8,128)(2,1)S(1)} %copy-done.41, bf16[2080,128]{1,0:T(8,128)(2,1)S(1)} %pad_maximum_fusion.k0_ref.t0_ref, ...), custom_call_target="tpu_custom_call" | custom-call | flops 24000000000 | bytes 1048576 | tf_op jit(solution)/shard_map/pallas_call | solution.py:591
  146.6 4.1 collective-permute-done.10.got_ref.gx_ref.gy_ref
  155.3 4.9 collective-permute-done.12.fy_ref
  164.7 7.2 %collective-permute-done.21.refs_2_ = bf16[256,1024]{1,0:T(8,128)(2,1)S(1)} collective-permute-done((bf16[256,1024]{1,0:T(8,128)(2,1)S(1)}, bf16[256,1024]{1,0:T(8,128)(2,1)S(1)}, u32[]{:S(2)}, u32[]{:S(2)}) %collective-permute-start.21) | collective-permute-done | bytes 524320 | tf_op jit(solution)/shard_map/ppermute | solution.py:30
  172.0 1.6 collective-permute-start.23
  174.6 8.1 %collective-permute-done.13 = bf16[256,1024]{1,0:T(8,128)(2,1)} collective-permute-done((bf16[256,1024]{1,0:T(8,128)(2,1)}, bf16[256,1024]{1,0:T(8,128)(2,1)}, u32[]{:S(2)}, u32[]{:S(2)}) %collective-permute-start.13) | collective-permute-done | bytes 524320 | tf_op jit(solution)/shard_map/ppermute | solution.py:30
  183.3 1.8 multiply_reduce_fusion.2
  185.4 1.6 collective-permute-start.15
  190.3 8.7 %collective-permute-done.16.refs_2_ = bf16[256,1024]{1,0:T(8,128)(2,1)} collective-permute-done((bf16[256,1024]{1,0:T(8,128)(2,1)S(1)}, bf16[256,1024]{1,0:T(8,128)(2,1)}, u32[]{:S(2)}, u32[]{:S(2)}) %collective-permute-start.16) | collective-permute-done | bytes 524320 | tf_op jit(solution)/shard_map/ppermute | solution.py:30
  200.0 1.6 collective-permute-start.18
  203.6 3.5 collective-permute-done.18.refs_4_
  207.1 2.3 collective-permute-done.17.refs_3_
  209.4 2.6 shard_map.215.refs_0_
  216.5 12.0 %all-gather.2.cloned.1.call-done.refs_5_.w0_ref.w1_ref = bf16[1024,3072]{1,0:T(8,128)(2,1)} async-done(((bf16[256,3072]{1,0:T(8,128)(2,1)}), bf16[1024,3072]{1,0:T(8,128)(2,1)}) %all-gather.2.cloned.1.call-update) | async-done | bytes 6291472 | tf_op jit(solution)/shard_map/all_gather | solution.py:1049
  228.5 29.0 %shard_map.217 = (bf16[1024,1024]{1,0:T(8,128)(2,1)}, bf16[1024,1024]{1,0:T(8,128)(2,1)}, bf16[2048,512]{1,0:T(8,128)(2,1)}, bf16[1024,1536]{1,0:T(8,128)(2,1)}) custom-call(bf16[1024,1024]{1,0:T(8,128)(2,1)} %shard_map.215.refs_0_, bf16[1024,1024]{1,0:T(8,128)(2,1)} %collective-permute-done.19.refs_1_, bf16[1024,1024]{1,0:T(8,128)(2,1)} %copy-done.9, ...), custom_call_target="tpu_custom_call" | custom-call | flops 10000000 | bytes 1048576 | tf_op jit(solution)/shard_map/pallas_call | solution.py:879
  257.6 30.2 %shard_map.218 = (bf16[1024,1024]{1,0:T(8,128)(2,1)}, bf16[1024,1024]{1,0:T(8,128)(2,1)}, bf16[2048,512]{1,0:T(8,128)(2,1)}, bf16[1024,1536]{1,0:T(8,128)(2,1)}) custom-call(bf16[1024,1024]{1,0:T(8,128)(2,1)} %shard_map.215.refs_0_, bf16[1024,1024]{1,0:T(8,128)(2,1)} %collective-permute-done.19.refs_1_, bf16[1024,1024]{1,0:T(8,128)(2,1)} %copy-done.9, ...), custom_call_target="tpu_custom_call" | custom-call | flops 10000000 | bytes 1048576 | tf_op jit(solution)/shard_map/pallas_call | solution.py:879
  287.9 4.3 collective-permute-done.25.got_ref.gx_ref.gy_ref
  292.3 1.6 copy-done.3
  297.0 5.5 %collective-permute-done.27.fy_ref = bf16[128,1024]{1,0:T(8,128)(2,1)S(1)} collective-permute-done((bf16[128,1024]{1,0:T(8,128)(2,1)S(1)}, bf16[128,1024]{1,0:T(8,128)(2,1)S(1)}, u32[]{:S(2)}, u32[]{:S(2)}) %collective-permute-start.27) | collective-permute-done | bytes 262176 | tf_op jit(solution)/shard_map/ppermute | solution.py:30
  306.0 10.9 %collective-permute-done.28 = bf16[256,1024]{1,0:T(8,128)(2,1)S(1)} collective-permute-done((bf16[256,1024]{1,0:T(8,128)(2,1)S(1)}, bf16[256,1024]{1,0:T(8,128)(2,1)S(1)}, u32[]{:S(2)}, u32[]{:S(2)}) %collective-permute-start.28) | collective-permute-done | bytes 524320 | tf_op jit(solution)/shard_map/ppermute | solution.py:30
  322.4 2.8 copy-done
  325.2 2.1 copy-done.10
  327.3 1.6 copy-done.11
  328.8 5.9 %shard_map.221 = (bf16[1024,1024]{1,0:T(8,128)(2,1)S(1)}, bf16[1024,1024]{1,0:T(8,128)(2,1)S(1)}) custom-call(bf16[2048,512]{1,0:T(8,128)(2,1)S(1)} %copy-done.10, bf16[2048,512]{1,0:T(8,128)(2,1)S(1)} %copy-done.11, bf16[1024,3072]{1,0:T(8,128)(2,1)S(1)} %copy-done, bf16[1024,3072]{1,0:T(8,128)(2,1)S(1)} %copy-done), custom_call_target="tpu_custom_call" | custom-call | flops 2000000000 | bytes 1048576 | tf_op jit(solution)/shard_map/pallas_call | solution.py:924
  336.9 7.7 %collective-permute-done.33.refs_4_ = bf16[128,1024]{1,0:T(8,128)(2,1)S(1)} collective-permute-done((bf16[128,1024]{1,0:T(8,128)(2,1)S(1)}, bf16[128,1024]{1,0:T(8,128)(2,1)S(1)}, u32[]{:S(2)}, u32[]{:S(2)}) %collective-permute-start.33) | collective-permute-done | bytes 262176 | tf_op jit(solution)/shard_map/ppermute | solution.py:30
  346.2 2.5 shard_map.222.dy_low
  349.7 1.6 collective-permute-start.36
  351.3 1.6 copy-done.6
  353.2 1.6 collective-permute-start.38
  355.3 20.0 %shard_map.224 = (bf16[2048,128]{1,0:T(8,128)(2,1)S(1)}, f32[2048,128]{1,0:T(8,128)S(1)}, f32[2048,128]{1,0:T(8,128)S(1)}, bf16[2048,128]{1,0:T(8,128)(2,1)}, bf16[1024,128]{1,0:T(8,128)(2,1)S(1)}) custom-call(s32[2]{0:T(128)S(1)} %copy-done.36, bf16[2048,128]{1,0:T(8,128)(2,1)S(1)} %copy-done.42, bf16[2080,128]{1,0:T(8,128)(2,1)S(1)} %copy-done.16, ...), custom_call_target="tpu_custom_call" | custom-call | flops 12000000000 | bytes 1048576 | tf_op jit(solution)/shard_map/pallas_call | solution.py:697
  383.6 11.7 %collective-permute-done.39 = bf16[2048,128]{1,0:T(8,128)(2,1)} collective-permute-done((bf16[2048,128]{1,0:T(8,128)(2,1)}, bf16[2048,128]{1,0:T(8,128)(2,1)}, u32[]{:S(2)}, u32[]{:S(2)}) %collective-permute-start.39) | collective-permute-done | bytes 524320 | tf_op jit(solution)/shard_map/ppermute | solution.py:36
  396.5 1.6 collective-permute-start.42
  398.1 2.4 shard_map.226
  403.5 7.7 %collective-permute-done.44.refs_2_ = bf16[20,64,128]{2,1,0:T(8,128)(2,1)S(1)} collective-permute-done((bf16[20,64,128]{2,1,0:T(8,128)(2,1)S(1)}, bf16[20,64,128]{2,1,0:T(8,128)(2,1)S(1)}, u32[]{:S(2)}, u32[]{:S(2)}) %collective-permute-start.44) | collective-permute-done | bytes 327712 | tf_op jit(solution)/shard_map/ppermute | solution.py:30
  411.2 6.1 %collective-permute-done.45.refs_3_ = bf16[20,64,128]{2,1,0:T(8,128)(2,1)S(1)} collective-permute-done((bf16[20,64,128]{2,1,0:T(8,128)(2,1)S(1)}, bf16[20,64,128]{2,1,0:T(8,128)(2,1)S(1)}, u32[]{:S(2)}, u32[]{:S(2)}) %collective-permute-start.45) | collective-permute-done | bytes 327712 | tf_op jit(solution)/shard_map/ppermute | solution.py:271
  419.2 9.8 %shard_map.227 = (bf16[1024,1024]{1,0:T(8,128)(2,1)S(1)}, bf16[1024,1024]{1,0:T(8,128)(2,1)}, bf16[1024,384]{1,0:T(8,128)(2,1)}, f32[8,1024]{1,0:T(8,128)S(1)}) custom-call(bf16[2048,128]{1,0:T(8,128)(2,1)S(1)} %copy-done.46, f32[2048,128]{1,0:T(8,128)S(1)} %copy-done.44, bf16[2048,128]{1,0:T(8,128)(2,1)S(1)} %collective-permute-done.42.b_ref, ...), custom_call_target="tpu_custom_call" | custom-call | flops 10000000000 | bytes 1048576 | tf_op jit(solution)/shard_map/pallas_call | solution.py:781
  429.2 4.6 collective-permute-done.49.refs_7_
  435.1 4.1 collective-permute-done.50.got_ref.gx_ref.gy_ref
  443.4 5.8 %collective-permute-done.53 = f32[2,1024]{1,0:T(2,128)S(1)} collective-permute-done((f32[2,1024]{1,0:T(2,128)S(1)}, f32[2,1024]{1,0:T(2,128)S(1)}, u32[]{:S(2)}, u32[]{:S(2)}) %collective-permute-start.53) | collective-permute-done | bytes 8224 | tf_op jit(solution)/shard_map/ppermute | solution.py:30
  452.4 4.5 collective-permute-start.56
  458.1 15.6 %shard_map.230 = (f32[20,128,512]{2,1,0:T(8,128)}, f32[20,128,512]{2,1,0:T(8,128)}, f32[20,128,512]{2,1,0:T(8,128)}) custom-call(s32[2]{0:T(128)} %pad_add_fusion.1.info_ref, f32[20]{0:T(128)} %copy-done.52, bf16[20,64,128]{2,1,0:T(8,128)(2,1)} %copy-done.38, bf16[20,64,128]{2,1,0:T(8,128)(2,1)} %copy-done.83, bf16[20,64,128]{2,1,0:T(8,128)(2,1)} %copy-done.84, ...), custom_call_target="tpu_custom_call" | custom-call | flops 6000000000 | bytes 1048576 | tf_op jit(solution)/shard_map/pallas_call | solution.py:402
  473.7 2.1 broadcast_in_dim.96
  475.8 4.2 all-to-all-start.1
  480.1 2.9 fusion.10
  483.0 3.7 collective-permute-start.57
  486.7 1.7 fusion.7
  488.4 3.3 all-to-all-done.1.attn_ref
  493.2 3.0 fusion.6
  496.3 7.2 %shard_map.231 = (f32[20,128,512]{2,1,0:T(8,128)}, f32[20,128,512]{2,1,0:T(8,128)}, f32[20,128,512]{2,1,0:T(8,128)}) custom-call(s32[6]{0:T(128)} %copy-done.76, s32[6]{0:T(128)} %broadcast_add_fusion.held_ref, f32[6]{0:T(128)} %and_select_fusion.rate_ref, ...), custom_call_target="tpu_custom_call", output_to_operand_aliasing={{0}: (7, {}), {1}: (8, {}), {2}: (9, {})} | custom-call | flops 5000000000 | bytes 1048576 | tf_op jit(solution)/shard_map/pallas_call | solution.py:452
  (379 shorter events, 86.6 us)
Async XLA Ops:
  12.1 17.0 %all-to-all-start = ((bf16[8,3,128,128]{3,2,1,0:T(8,128)(2,1)}), bf16[8,3,128,128]{3,2,1,0:T(8,128)(2,1)S(1)}, u32[]{:S(2)}, u32[]{:S(2)}) async-start(bf16[8,3,128,128]{3,2,1,0:T(8,128)(2,1)} %shard_map.206), calls=%async_computation | async-start | bytes 1572864 | tf_op jit(solution)/shard_map/all_to_all | solution.py:978
  17.5 211.0 %all-gather.2.cloned.1.call-start = ((), (), s32[]{:S(2)}) async-start(), calls=%async_computation.5 | async-start | bytes 7864320 | tf_op jit(solution)/shard_map/all_gather | solution.py:1049
  29.1 29.1 %collective-permute-start.2 = (bf16[20,128,128]{2,1,0:T(8,128)(2,1)}, bf16[20,128,128]{2,1,0:T(8,128)(2,1)S(1)}, u32[]{:S(2)}, u32[]{:S(2)}) collective-permute-start(bf16[20,128,128]{2,1,0:T(8,128)(2,1)} %get-tuple-element.155), channel_id=1, source_target_pairs={{0,2},{2,0},{1,3},{3,1},{4,6},{6,4},{5,7},{7,5},{8,10},{10,8},{9,1... | collective-permute-start | bytes 1966088 | tf_op jit(solution)/shard_map/ppermute | solution.py:30
  31.2 27.0 %collective-permute-start.1 = (bf16[256,1152]{1,0:T(8,128)(2,1)S(1)}, bf16[256,1152]{1,0:T(8,128)(2,1)S(1)}, u32[]{:S(2)}, u32[]{:S(2)}) collective-permute-start(bf16[256,1152]{1,0:T(8,128)(2,1)S(1)} %concatenate.13.refs_0_), channel_id=1, source_target_pairs={{0,2},{2,0},{1,3},{3,1},{4,6},{6,4},{5,7},{7,5},{8,10},{10,8},{9,1... | collective-permute-start | bytes 1769480 | tf_op jit(solution)/shard_map/ppermute | solution.py:30
  31.9 26.4 %collective-permute-start = (bf16[256,1152]{1,0:T(8,128)(2,1)S(1)}, bf16[256,1152]{1,0:T(8,128)(2,1)S(1)}, u32[]{:S(2)}, u32[]{:S(2)}) collective-permute-start(bf16[256,1152]{1,0:T(8,128)(2,1)S(1)} %concatenate.13.refs_0_), channel_id=1, source_target_pairs={{0,4},{4,0},{1,5},{5,1},{2,6},{6,2},{3,7},{7,3},{8,12},{12,8},{9,1... | collective-permute-start | bytes 1769480 | tf_op jit(solution)/shard_map/ppermute | solution.py:30
  33.7 25.5 %collective-permute-start.4 = (bf16[20,128,128]{2,1,0:T(8,128)(2,1)}, bf16[20,128,128]{2,1,0:T(8,128)(2,1)S(1)}, u32[]{:S(2)}, u32[]{:S(2)}) collective-permute-start(bf16[20,128,128]{2,1,0:T(8,128)(2,1)} %get-tuple-element.158), channel_id=1, source_target_pairs={{0,1},{1,0},{2,3},{3,2},{4,5},{5,4},{6,7},{7,6},{8,9},{9,8},{10,11... | collective-permute-start | bytes 1966088 | tf_op jit(solution)/shard_map/ppermute | solution.py:30
  58.3 17.1 %collective-permute-start.5 = (bf16[20,128,128]{2,1,0:T(8,128)(2,1)S(1)}, bf16[20,128,128]{2,1,0:T(8,128)(2,1)S(1)}, u32[]{:S(2)}, u32[]{:S(2)}) collective-permute-start(bf16[20,128,128]{2,1,0:T(8,128)(2,1)S(1)} %copy-done.82), channel_id=1, source_target_pairs={{0,3},{1,2},{2,1},{3,0},{4,7},{5,6},{6,5},{7,4},{8,11},{9,10},{10,... | collective-permute-start | bytes 1966088 | tf_op jit(solution)/shard_map/ppermute | solution.py:1021
  58.4 15.8 %collective-permute-start.3 = (bf16[256,1152]{1,0:T(8,128)(2,1)S(1)}, bf16[256,1152]{1,0:T(8,128)(2,1)S(1)}, u32[]{:S(2)}, u32[]{:S(2)}) collective-permute-start(bf16[256,1152]{1,0:T(8,128)(2,1)S(1)} %collective-permute-done.1.refs_2_), channel_id=1, source_target_pairs={{0,4},{4,0},{1,5},{5,1},{2,6},{6,2},{3,7},{7,3},{8,12},{12,8},{9,1... | collective-permute-start | bytes 1769480 | tf_op jit(solution)/shard_map/ppermute | solution.py:30
  77.0 7.6 %collective-permute-start.6 = (bf16[1024,1152]{1,0:T(8,128)(2,1)}, bf16[1024,1152]{1,0:T(8,128)(2,1)}, u32[]{:S(2)}, u32[]{:S(2)}) collective-permute-start(bf16[1024,1152]{1,0:T(8,128)(2,1)} %shard_map.208.low_ref.x_low), channel_id=1, source_target_pairs={{0,1},{1,0},{2,3},{3,2},{4,5},{5,4},{6,7},{7,6},{8,9},{9,8},{10,11... | collective-permute-start | bytes 7077896 | tf_op jit(solution)/shard_map/ppermute | solution.py:30
  85.6 20.1 %collective-permute-start.8 = (bf16[128,3072]{1,0:T(8,128)(2,1)}, bf16[128,3072]{1,0:T(8,128)(2,1)S(1)}, u32[]{:S(2)}, u32[]{:S(2)}) collective-permute-start(bf16[128,3072]{1,0:T(8,128)(2,1)} %get-tuple-element.173), channel_id=1, source_target_pairs={{0,4},{4,0},{1,5},{5,1},{2,6},{6,2},{3,7},{7,3},{8,12},{12,8},{9,1... | collective-permute-start | bytes 2359304 | tf_op jit(solution)/shard_map/ppermute | solution.py:30
  93.6 15.3 %collective-permute-start.7 = (bf16[2080,128]{1,0:T(8,128)(2,1)S(1)}, bf16[2080,128]{1,0:T(8,128)(2,1)S(1)}, u32[]{:S(2)}, u32[]{:S(2)}) collective-permute-start(bf16[2080,128]{1,0:T(8,128)(2,1)S(1)} %pad_maximum_fusion.k0_ref.t0_ref), channel_id=1, source_target_pairs={{0,8},{8,16},{16,24},{1,9},{9,17},{17,25},{2,10},{10,18},{18,26},{... | collective-permute-start | bytes 1597448 | tf_op jit(solution)/shard_map/ppermute | solution.py:36
  108.9 18.4 %collective-permute-start.9 = (bf16[2080,128]{1,0:T(8,128)(2,1)S(1)}, bf16[2080,128]{1,0:T(8,128)(2,1)S(1)}, u32[]{:S(2)}, u32[]{:S(2)}) collective-permute-start(bf16[2080,128]{1,0:T(8,128)(2,1)S(1)} %collective-permute-done.7.k1_ref.t1_ref), channel_id=1, source_target_pairs={{0,8},{8,16},{16,24},{1,9},{9,17},{17,25},{2,10},{10,18},{18,26},{... | collective-permute-start | bytes 1597448 | tf_op jit(solution)/shard_map/ppermute | solution.py:36
  113.7 205.7 %reduce-scatter.4.cloned.1.call-start = ((), (), s32[]{:S(2)}) async-start(), calls=%async_computation.6 | async-start | bytes 3932160 | tf_op jit(solution)/shard_map/reduce_scatter | solution.py:1091
  151.0 9.2 %collective-permute-start.12 = (bf16[128,1024]{1,0:T(8,128)(2,1)S(1)}, bf16[128,1024]{1,0:T(8,128)(2,1)S(1)}, u32[]{:S(2)}, u32[]{:S(2)}) collective-permute-start(bf16[128,1024]{1,0:T(8,128)(2,1)S(1)} %get-tuple-element.310), channel_id=1, source_target_pairs={{0,4},{4,0},{1,5},{5,1},{2,6},{6,2},{3,7},{7,3},{8,12},{12,8},{9,1... | collective-permute-start | bytes 786440 | tf_op jit(solution)/shard_map/ppermute | solution.py:30
  151.5 9.2 %collective-permute-start.11 = (bf16[128,1024]{1,0:T(8,128)(2,1)S(1)}, bf16[128,1024]{1,0:T(8,128)(2,1)S(1)}, u32[]{:S(2)}, u32[]{:S(2)}) collective-permute-start(bf16[128,1024]{1,0:T(8,128)(2,1)S(1)} %get-tuple-element.311), channel_id=1, source_target_pairs={{0,2},{2,0},{1,3},{3,1},{4,6},{6,4},{5,7},{7,5},{8,10},{10,8},{9,1... | collective-permute-start | bytes 786440 | tf_op jit(solution)/shard_map/ppermute | solution.py:30
  152.2 19.8 %collective-permute-start.21 = (bf16[256,1024]{1,0:T(8,128)(2,1)S(1)}, bf16[256,1024]{1,0:T(8,128)(2,1)S(1)}, u32[]{:S(2)}, u32[]{:S(2)}) collective-permute-start(bf16[256,1024]{1,0:T(8,128)(2,1)S(1)} %bitcast.54), channel_id=1, source_target_pairs={{0,2},{2,0},{1,3},{3,1},{4,6},{6,4},{5,7},{7,5},{8,10},{10,8},{9,1... | collective-permute-start | bytes 1572872 | tf_op jit(solution)/shard_map/ppermute | solution.py:30
  153.7 19.8 %collective-permute-start.20 = (bf16[256,1024]{1,0:T(8,128)(2,1)S(1)}, bf16[256,1024]{1,0:T(8,128)(2,1)}, u32[]{:S(2)}, u32[]{:S(2)}) collective-permute-start(bf16[256,1024]{1,0:T(8,128)(2,1)S(1)} %bitcast.55), channel_id=1, source_target_pairs={{0,4},{4,0},{1,5},{5,1},{2,6},{6,2},{3,7},{7,3},{8,12},{12,8},{9,1... | collective-permute-start | bytes 1572872 | tf_op jit(solution)/shard_map/ppermute | solution.py:30
  161.8 20.9 %collective-permute-start.13 = (bf16[256,1024]{1,0:T(8,128)(2,1)}, bf16[256,1024]{1,0:T(8,128)(2,1)}, u32[]{:S(2)}, u32[]{:S(2)}) collective-permute-start(bf16[256,1024]{1,0:T(8,128)(2,1)} %get-tuple-element.177), channel_id=1, source_target_pairs={{0,4},{4,0},{1,5},{5,1},{2,6},{6,2},{3,7},{7,3},{8,12},{12,8},{9,1... | collective-permute-start | bytes 1572872 | tf_op jit(solution)/shard_map/ppermute | solution.py:30
  163.4 19.9 %collective-permute-start.14 = (bf16[256,1024]{1,0:T(8,128)(2,1)}, bf16[256,1024]{1,0:T(8,128)(2,1)}, u32[]{:S(2)}, u32[]{:S(2)}) collective-permute-start(bf16[256,1024]{1,0:T(8,128)(2,1)} %get-tuple-element.178), channel_id=1, source_target_pairs={{0,2},{2,0},{1,3},{3,1},{4,6},{6,4},{5,7},{7,5},{8,10},{10,8},{9,1... | collective-permute-start | bytes 1572872 | tf_op jit(solution)/shard_map/ppermute | solution.py:30
  172.0 16.4 %collective-permute-start.23 = (bf16[128,1024]{1,0:T(8,128)(2,1)S(1)}, bf16[128,1024]{1,0:T(8,128)(2,1)S(1)}, u32[]{:S(2)}, u32[]{:S(2)}) collective-permute-start(bf16[128,1024]{1,0:T(8,128)(2,1)S(1)} %slice.165), channel_id=1, source_target_pairs={{0,4},{4,0},{1,5},{5,1},{2,6},{6,2},{3,7},{7,3},{8,12},{12,8},{9,1... | collective-permute-start | bytes 786440 | tf_op jit(solution)/shard_map/ppermute | solution.py:30
  174.6 14.2 %collective-permute-start.22 = (bf16[128,1024]{1,0:T(8,128)(2,1)S(1)}, bf16[128,1024]{1,0:T(8,128)(2,1)S(1)}, u32[]{:S(2)}, u32[]{:S(2)}) collective-permute-start(bf16[128,1024]{1,0:T(8,128)(2,1)S(1)} %slice.164), channel_id=1, source_target_pairs={{0,2},{2,0},{1,3},{3,1},{4,6},{6,4},{5,7},{7,5},{8,10},{10,8},{9,1... | collective-permute-start | bytes 786440 | tf_op jit(solution)/shard_map/ppermute | solution.py:30
  185.3 13.7 %collective-permute-start.16 = (bf16[256,1024]{1,0:T(8,128)(2,1)S(1)}, bf16[256,1024]{1,0:T(8,128)(2,1)}, u32[]{:S(2)}, u32[]{:S(2)}) collective-permute-start(bf16[256,1024]{1,0:T(8,128)(2,1)S(1)} %multiply_convert_fusion.refs_0_), channel_id=1, source_target_pairs={{0,2},{2,0},{1,3},{3,1},{4,6},{6,4},{5,7},{7,5},{8,10},{10,8},{9,1... | collective-permute-start | bytes 1572872 | tf_op jit(solution)/shard_map/ppermute | solution.py:30
  185.4 16.2 %collective-permute-start.15 = (bf16[256,1024]{1,0:T(8,128)(2,1)S(1)}, bf16[256,1024]{1,0:T(8,128)(2,1)}, u32[]{:S(2)}, u32[]{:S(2)}) collective-permute-start(bf16[256,1024]{1,0:T(8,128)(2,1)S(1)} %multiply_convert_fusion.refs_0_), channel_id=1, source_target_pairs={{0,4},{4,0},{1,5},{5,1},{2,6},{6,2},{3,7},{7,3},{8,12},{12,8},{9,1... | collective-permute-start | bytes 1572872 | tf_op jit(solution)/shard_map/ppermute | solution.py:30
  190.0 26.5 %collective-permute-start.24 = (bf16[1024,1024]{1,0:T(8,128)(2,1)S(1)}, bf16[1024,1024]{1,0:T(8,128)(2,1)}, u32[]{:S(2)}, u32[]{:S(2)}) collective-permute-start(bf16[1024,1024]{1,0:T(8,128)(2,1)S(1)} %shard_map.216.refs_2_), channel_id=1, source_target_pairs={{0,1},{1,0},{2,3},{3,2},{4,5},{5,4},{6,7},{7,6},{8,9},{9,8},{10,11... | collective-permute-start | bytes 6291464 | tf_op jit(solution)/shard_map/ppermute | solution.py:30
  200.0 7.1 %collective-permute-start.18 = (bf16[128,1024]{1,0:T(8,128)(2,1)S(1)}, bf16[128,1024]{1,0:T(8,128)(2,1)S(1)}, u32[]{:S(2)}, u32[]{:S(2)}) collective-permute-start(bf16[128,1024]{1,0:T(8,128)(2,1)S(1)} %slice.163), channel_id=1, source_target_pairs={{0,4},{4,0},{1,5},{5,1},{2,6},{6,2},{3,7},{7,3},{8,12},{12,8},{9,1... | collective-permute-start | bytes 786440 | tf_op jit(solution)/shard_map/ppermute | solution.py:30
  202.6 6.8 %collective-permute-start.17 = (bf16[128,1024]{1,0:T(8,128)(2,1)S(1)}, bf16[128,1024]{1,0:T(8,128)(2,1)S(1)}, u32[]{:S(2)}, u32[]{:S(2)}) collective-permute-start(bf16[128,1024]{1,0:T(8,128)(2,1)S(1)} %slice.162), channel_id=1, source_target_pairs={{0,2},{2,0},{1,3},{3,1},{4,6},{6,4},{5,7},{7,5},{8,10},{10,8},{9,1... | collective-permute-start | bytes 786440 | tf_op jit(solution)/shard_map/ppermute | solution.py:30
  212.0 4.5 collective-permute-start.19
  257.6 122.8 %reduce-scatter.6.cloned.1.call-start = ((), (), s32[]{:S(2)}) async-start(), calls=%async_computation.7 | async-start | bytes 3932160 | tf_op jit(solution)/shard_map/reduce_scatter | solution.py:1091
  287.8 4.4 collective-permute-start.25
  294.1 8.4 %collective-permute-start.27 = (bf16[128,1024]{1,0:T(8,128)(2,1)S(1)}, bf16[128,1024]{1,0:T(8,128)(2,1)S(1)}, u32[]{:S(2)}, u32[]{:S(2)}) collective-permute-start(bf16[128,1024]{1,0:T(8,128)(2,1)S(1)} %get-tuple-element.308), channel_id=1, source_target_pairs={{0,4},{4,0},{1,5},{5,1},{2,6},{6,2},{3,7},{7,3},{8,12},{12,8},{9,1... | collective-permute-start | bytes 786440 | tf_op jit(solution)/shard_map/ppermute | solution.py:30
  295.6 8.1 %collective-permute-start.26 = (bf16[128,1024]{1,0:T(8,128)(2,1)S(1)}, bf16[128,1024]{1,0:T(8,128)(2,1)S(1)}, u32[]{:S(2)}, u32[]{:S(2)}) collective-permute-start(bf16[128,1024]{1,0:T(8,128)(2,1)S(1)} %get-tuple-element.309), channel_id=1, source_target_pairs={{0,2},{2,0},{1,3},{3,1},{4,6},{6,4},{5,7},{7,5},{8,10},{10,8},{9,1... | collective-permute-start | bytes 786440 | tf_op jit(solution)/shard_map/ppermute | solution.py:30
  304.0 13.0 %collective-permute-start.28 = (bf16[256,1024]{1,0:T(8,128)(2,1)S(1)}, bf16[256,1024]{1,0:T(8,128)(2,1)S(1)}, u32[]{:S(2)}, u32[]{:S(2)}) collective-permute-start(bf16[256,1024]{1,0:T(8,128)(2,1)S(1)} %get-tuple-element.192), channel_id=1, source_target_pairs={{0,4},{4,0},{1,5},{5,1},{2,6},{6,2},{3,7},{7,3},{8,12},{12,8},{9,1... | collective-permute-start | bytes 1572872 | tf_op jit(solution)/shard_map/ppermute | solution.py:30
  304.6 12.7 %collective-permute-start.29 = (bf16[256,1024]{1,0:T(8,128)(2,1)S(1)}, bf16[256,1024]{1,0:T(8,128)(2,1)S(1)}, u32[]{:S(2)}, u32[]{:S(2)}) collective-permute-start(bf16[256,1024]{1,0:T(8,128)(2,1)S(1)} %get-tuple-element.193), channel_id=1, source_target_pairs={{0,2},{2,0},{1,3},{3,1},{4,6},{6,4},{5,7},{7,5},{8,10},{10,8},{9,1... | collective-permute-start | bytes 1572872 | tf_op jit(solution)/shard_map/ppermute | solution.py:30
  319.4 15.3 %collective-permute-start.31 = (bf16[256,1024]{1,0:T(8,128)(2,1)S(1)}, bf16[256,1024]{1,0:T(8,128)(2,1)S(1)}, u32[]{:S(2)}, u32[]{:S(2)}) collective-permute-start(bf16[256,1024]{1,0:T(8,128)(2,1)S(1)} %get-tuple-element.195.refs_0_), channel_id=1, source_target_pairs={{0,2},{2,0},{1,3},{3,1},{4,6},{6,4},{5,7},{7,5},{8,10},{10,8},{9,1... | collective-permute-start | bytes 1572872 | tf_op jit(solution)/shard_map/ppermute | solution.py:30
  320.9 13.8 %collective-permute-start.30 = (bf16[256,1024]{1,0:T(8,128)(2,1)S(1)}, bf16[256,1024]{1,0:T(8,128)(2,1)}, u32[]{:S(2)}, u32[]{:S(2)}) collective-permute-start(bf16[256,1024]{1,0:T(8,128)(2,1)S(1)} %get-tuple-element.195.refs_0_), channel_id=1, source_target_pairs={{0,4},{4,0},{1,5},{5,1},{2,6},{6,2},{3,7},{7,3},{8,12},{12,8},{9,1... | collective-permute-start | bytes 1572872 | tf_op jit(solution)/shard_map/ppermute | solution.py:30
  322.3 151.4 %reduce-scatter.8.cloned.1.call-start = ((), (), s32[]{:S(2)}) async-start(), calls=%async_computation.8 | async-start | bytes 983040 | tf_op jit(solution)/shard_map/reduce_scatter | solution.py:1127
  334.8 10.1 %collective-permute-start.34 = (bf16[1024,1024]{1,0:T(8,128)(2,1)S(1)}, bf16[1024,1024]{1,0:T(8,128)(2,1)S(1)}, u32[]{:S(2)}, u32[]{:S(2)}) collective-permute-start(bf16[1024,1024]{1,0:T(8,128)(2,1)S(1)} %get-tuple-element.205), channel_id=1, source_target_pairs={{0,1},{1,0},{2,3},{3,2},{4,5},{5,4},{6,7},{7,6},{8,9},{9,8},{10,11... | collective-permute-start | bytes 6291464 | tf_op jit(solution)/shard_map/ppermute | solution.py:30
  336.0 8.6 %collective-permute-start.33 = (bf16[128,1024]{1,0:T(8,128)(2,1)S(1)}, bf16[128,1024]{1,0:T(8,128)(2,1)S(1)}, u32[]{:S(2)}, u32[]{:S(2)}) collective-permute-start(bf16[128,1024]{1,0:T(8,128)(2,1)S(1)} %slice.138), channel_id=1, source_target_pairs={{0,4},{4,0},{1,5},{5,1},{2,6},{6,2},{3,7},{7,3},{8,12},{12,8},{9,1... | collective-permute-start | bytes 786440 | tf_op jit(solution)/shard_map/ppermute | solution.py:30
  336.6 8.2 %collective-permute-start.32 = (bf16[128,1024]{1,0:T(8,128)(2,1)S(1)}, bf16[128,1024]{1,0:T(8,128)(2,1)S(1)}, u32[]{:S(2)}, u32[]{:S(2)}) collective-permute-start(bf16[128,1024]{1,0:T(8,128)(2,1)S(1)} %slice.137), channel_id=1, source_target_pairs={{0,2},{2,0},{1,3},{3,1},{4,6},{6,4},{5,7},{7,5},{8,10},{10,8},{9,1... | collective-permute-start | bytes 786440 | tf_op jit(solution)/shard_map/ppermute | solution.py:30
  348.7 4.5 collective-permute-start.35
  349.7 25.6 %collective-permute-start.36 = (bf16[128,1536]{1,0:T(8,128)(2,1)S(1)}, bf16[128,1536]{1,0:T(8,128)(2,1)S(1)}, u32[]{:S(2)}, u32[]{:S(2)}) collective-permute-start(bf16[128,1536]{1,0:T(8,128)(2,1)S(1)} %constant_dynamic-slice_fusion), channel_id=1, source_target_pairs={{0,4},{4,0},{1,5},{5,1},{2,6},{6,2},{3,7},{7,3},{8,12},{12,8},{9,1... | collective-permute-start | bytes 1179656 | tf_op jit(solution)/shard_map/ppermute | solution.py:30
  353.2 22.1 %collective-permute-start.38 = (bf16[128,1024]{1,0:T(8,128)(2,1)S(1)}, bf16[128,1024]{1,0:T(8,128)(2,1)S(1)}, u32[]{:S(2)}, u32[]{:S(2)}) collective-permute-start(bf16[128,1024]{1,0:T(8,128)(2,1)S(1)} %get-tuple-element.306), channel_id=1, source_target_pairs={{0,4},{4,0},{1,5},{5,1},{2,6},{6,2},{3,7},{7,3},{8,12},{12,8},{9,1... | collective-permute-start | bytes 786440 | tf_op jit(solution)/shard_map/ppermute | solution.py:30
  354.8 20.6 %collective-permute-start.37 = (bf16[128,1024]{1,0:T(8,128)(2,1)S(1)}, bf16[128,1024]{1,0:T(8,128)(2,1)S(1)}, u32[]{:S(2)}, u32[]{:S(2)}) collective-permute-start(bf16[128,1024]{1,0:T(8,128)(2,1)S(1)} %get-tuple-element.307), channel_id=1, source_target_pairs={{0,2},{2,0},{1,3},{3,1},{4,6},{6,4},{5,7},{7,5},{8,10},{10,8},{9,1... | collective-permute-start | bytes 786440 | tf_op jit(solution)/shard_map/ppermute | solution.py:30
  375.3 20.0 %collective-permute-start.39 = (bf16[2048,128]{1,0:T(8,128)(2,1)}, bf16[2048,128]{1,0:T(8,128)(2,1)}, u32[]{:S(2)}, u32[]{:S(2)}) collective-permute-start(bf16[2048,128]{1,0:T(8,128)(2,1)} %get-tuple-element.219), channel_id=1, source_target_pairs={{8,0},{16,8},{24,16},{9,1},{17,9},{25,17},{10,2},{18,10},{26,18},{... | collective-permute-start | bytes 1572872 | tf_op jit(solution)/shard_map/ppermute | solution.py:36
  378.4 16.9 %collective-permute-start.41 = (bf16[256,1024]{1,0:T(8,128)(2,1)}, bf16[256,1024]{1,0:T(8,128)(2,1)}, u32[]{:S(2)}, u32[]{:S(2)}) collective-permute-start(bf16[256,1024]{1,0:T(8,128)(2,1)} %get-tuple-element.226), channel_id=1, source_target_pairs={{0,2},{2,0},{1,3},{3,1},{4,6},{6,4},{5,7},{7,5},{8,10},{10,8},{9,1... | collective-permute-start | bytes 1572872 | tf_op jit(solution)/shard_map/ppermute | solution.py:30
  381.5 13.8 %collective-permute-start.40 = (bf16[128,1536]{1,0:T(8,128)(2,1)S(1)}, bf16[128,1536]{1,0:T(8,128)(2,1)S(1)}, u32[]{:S(2)}, u32[]{:S(2)}) collective-permute-start(bf16[128,1536]{1,0:T(8,128)(2,1)S(1)} %constant_dynamic-slice_fusion.1), channel_id=1, source_target_pairs={{0,4},{4,0},{1,5},{5,1},{2,6},{6,2},{3,7},{7,3},{8,12},{12,8},{9,1... | collective-permute-start | bytes 1179656 | tf_op jit(solution)/shard_map/ppermute | solution.py:30
  383.0 20.5 %collective-permute-start.46 = (bf16[256,1024]{1,0:T(8,128)(2,1)}, bf16[256,1024]{1,0:T(8,128)(2,1)S(1)}, u32[]{:S(2)}, u32[]{:S(2)}) collective-permute-start(bf16[256,1024]{1,0:T(8,128)(2,1)} %copy-done.33), channel_id=1, source_target_pairs={{0,4},{4,0},{1,5},{5,1},{2,6},{6,2},{3,7},{7,3},{8,12},{12,8},{9,1... | collective-permute-start | bytes 1572872 | tf_op jit(solution)/shard_map/ppermute | solution.py:30
  396.5 20.8 %collective-permute-start.42 = (bf16[2048,128]{1,0:T(8,128)(2,1)S(1)}, bf16[2048,128]{1,0:T(8,128)(2,1)S(1)}, u32[]{:S(2)}, u32[]{:S(2)}) collective-permute-start(bf16[2048,128]{1,0:T(8,128)(2,1)S(1)} %add_convert_fusion.1), channel_id=1, source_target_pairs={{8,0},{16,8},{24,16},{9,1},{17,9},{25,17},{10,2},{18,10},{26,18},{... | collective-permute-start | bytes 1572872 | tf_op jit(solution)/shard_map/ppermute | solution.py:36
  400.6 10.6 %collective-permute-start.44 = (bf16[20,64,128]{2,1,0:T(8,128)(2,1)S(1)}, bf16[20,64,128]{2,1,0:T(8,128)(2,1)S(1)}, u32[]{:S(2)}, u32[]{:S(2)}) collective-permute-start(bf16[20,64,128]{2,1,0:T(8,128)(2,1)S(1)} %get-tuple-element.234), channel_id=1, source_target_pairs={{0,2},{2,0},{1,3},{3,1},{4,6},{6,4},{5,7},{7,5},{8,10},{10,8},{9,1... | collective-permute-start | bytes 983048 | tf_op jit(solution)/shard_map/ppermute | solution.py:30
  401.6 15.8 %collective-permute-start.45 = (bf16[20,64,128]{2,1,0:T(8,128)(2,1)S(1)}, bf16[20,64,128]{2,1,0:T(8,128)(2,1)S(1)}, u32[]{:S(2)}, u32[]{:S(2)}) collective-permute-start(bf16[20,64,128]{2,1,0:T(8,128)(2,1)S(1)} %get-tuple-element.235), channel_id=1, source_target_pairs={{0,3},{1,2},{2,1},{3,0},{4,7},{5,6},{6,5},{7,4},{8,11},{9,10},{10,... | collective-permute-start | bytes 983048 | tf_op jit(solution)/shard_map/ppermute | solution.py:271
  417.3 11.8 %collective-permute-start.47 = (bf16[20,64,128]{2,1,0:T(8,128)(2,1)S(1)}, bf16[20,64,128]{2,1,0:T(8,128)(2,1)S(1)}, u32[]{:S(2)}, u32[]{:S(2)}) collective-permute-start(bf16[20,64,128]{2,1,0:T(8,128)(2,1)S(1)} %get-tuple-element.247), channel_id=1, source_target_pairs={{0,1},{1,0},{2,3},{3,2},{4,5},{5,4},{6,7},{7,6},{8,9},{9,8},{10,11... | collective-permute-start | bytes 983048 | tf_op jit(solution)/shard_map/ppermute | solution.py:30
  417.6 11.5 %collective-permute-start.48 = (bf16[20,64,128]{2,1,0:T(8,128)(2,1)S(1)}, bf16[20,64,128]{2,1,0:T(8,128)(2,1)S(1)}, u32[]{:S(2)}, u32[]{:S(2)}) collective-permute-start(bf16[20,64,128]{2,1,0:T(8,128)(2,1)S(1)} %get-tuple-element.249), channel_id=1, source_target_pairs={{0,2},{2,0},{1,3},{3,1},{4,6},{6,4},{5,7},{7,5},{8,10},{10,8},{9,1... | collective-permute-start | bytes 983048 | tf_op jit(solution)/shard_map/ppermute | solution.py:30
  418.5 15.3 %collective-permute-start.49 = (bf16[20,64,128]{2,1,0:T(8,128)(2,1)S(1)}, bf16[20,64,128]{2,1,0:T(8,128)(2,1)S(1)}, u32[]{:S(2)}, u32[]{:S(2)}) collective-permute-start(bf16[20,64,128]{2,1,0:T(8,128)(2,1)S(1)} %get-tuple-element.251), channel_id=1, source_target_pairs={{0,3},{1,2},{2,1},{3,0},{4,7},{5,6},{6,5},{7,4},{8,11},{9,10},{10,... | collective-permute-start | bytes 983048 | tf_op jit(solution)/shard_map/ppermute | solution.py:271
  434.5 4.7 collective-permute-start.50
  440.4 8.8 %collective-permute-start.52 = (bf16[128,1024]{1,0:T(8,128)(2,1)S(1)}, bf16[128,1024]{1,0:T(8,128)(2,1)S(1)}, u32[]{:S(2)}, u32[]{:S(2)}) collective-permute-start(bf16[128,1024]{1,0:T(8,128)(2,1)S(1)} %get-tuple-element.304), channel_id=1, source_target_pairs={{0,4},{4,0},{1,5},{5,1},{2,6},{6,2},{3,7},{7,3},{8,12},{12,8},{9,1... | collective-permute-start | bytes 786440 | tf_op jit(solution)/shard_map/ppermute | solution.py:30
  441.2 8.3 %collective-permute-start.51 = (bf16[128,1024]{1,0:T(8,128)(2,1)S(1)}, bf16[128,1024]{1,0:T(8,128)(2,1)S(1)}, u32[]{:S(2)}, u32[]{:S(2)}) collective-permute-start(bf16[128,1024]{1,0:T(8,128)(2,1)S(1)} %get-tuple-element.305), channel_id=1, source_target_pairs={{0,2},{2,0},{1,3},{3,1},{4,6},{6,4},{5,7},{7,5},{8,10},{10,8},{9,1... | collective-permute-start | bytes 786440 | tf_op jit(solution)/shard_map/ppermute | solution.py:30
  442.0 7.2 %collective-permute-start.53 = (f32[2,1024]{1,0:T(2,128)S(1)}, f32[2,1024]{1,0:T(2,128)S(1)}, u32[]{:S(2)}, u32[]{:S(2)}) collective-permute-start(f32[2,1024]{1,0:T(2,128)S(1)} %pad_maximum_fusion.2), channel_id=1, source_target_pairs={{0,4},{4,0},{1,5},{5,1},{2,6},{6,2},{3,7},{7,3},{8,12},{12,8},{9,1... | collective-permute-start | bytes 24584 | tf_op jit(solution)/shard_map/ppermute | solution.py:30
  451.0 22.7 %collective-permute-start.54 = (bf16[256,1024]{1,0:T(8,128)(2,1)S(1)}, bf16[256,1024]{1,0:T(8,128)(2,1)S(1)}, u32[]{:S(2)}, u32[]{:S(2)}) collective-permute-start(bf16[256,1024]{1,0:T(8,128)(2,1)S(1)} %get-tuple-element.259), channel_id=1, source_target_pairs={{0,4},{4,0},{1,5},{5,1},{2,6},{6,2},{3,7},{7,3},{8,12},{12,8},{9,1... | collective-permute-start | bytes 1572872 | tf_op jit(solution)/shard_map/ppermute | solution.py:30
  452.4 21.3 %collective-permute-start.56 = (f32[2,1024]{1,0:T(2,128)S(1)}, f32[2,1024]{1,0:T(2,128)S(1)}, u32[]{:S(2)}, u32[]{:S(2)}) collective-permute-start(f32[2,1024]{1,0:T(2,128)S(1)} %add.330), channel_id=1, source_target_pairs={{0,8},{8,0},{16,24},{24,16},{1,9},{9,1},{17,25},{25,17},{2,10},{10... | collective-permute-start | bytes 24584 | tf_op jit(solution)/shard_map/ppermute | solution.py:1140
  456.9 16.8 %collective-permute-start.55 = (bf16[256,1024]{1,0:T(8,128)(2,1)S(1)}, bf16[256,1024]{1,0:T(8,128)(2,1)}, u32[]{:S(2)}, u32[]{:S(2)}) collective-permute-start(bf16[256,1024]{1,0:T(8,128)(2,1)S(1)} %get-tuple-element.260), channel_id=1, source_target_pairs={{0,2},{2,0},{1,3},{3,1},{4,6},{6,4},{5,7},{7,5},{8,10},{10,8},{9,1... | collective-permute-start | bytes 1572872 | tf_op jit(solution)/shard_map/ppermute | solution.py:30
  475.8 15.9 %all-to-all-start.1 = ((bf16[8,128,384]{2,1,0:T(8,128)(2,1)}), bf16[8,128,384]{2,1,0:T(8,128)(2,1)}, u32[]{:S(2)}, u32[]{:S(2)}) async-start(bf16[8,128,384]{2,1,0:T(8,128)(2,1)} %bitcast.27), calls=%async_computation.4 | async-start | bytes 1572864 | tf_op jit(solution)/shard_map/all_to_all | solution.py:1163
  483.0 5.4 %collective-permute-start.57 = (f32[2,1024]{1,0:T(2,128)S(1)}, f32[2,1024]{1,0:T(2,128)S(1)}, u32[]{:S(2)}, u32[]{:S(2)}) collective-permute-start(f32[2,1024]{1,0:T(2,128)S(1)} %add.331), channel_id=1, source_target_pairs={{0,16},{8,24},{16,0},{24,8},{1,17},{9,25},{17,1},{25,9},{2,18},{10... | collective-permute-start | bytes 24584 | tf_op jit(solution)/shard_map/ppermute | solution.py:1140
  491.7 4.5 collective-permute-start.58
  496.2 7.3 %collective-permute-start.59 = (f32[2,1024]{1,0:T(2,128)S(1)}, f32[2,1024]{1,0:T(2,128)S(1)}, u32[]{:S(2)}, u32[]{:S(2)}) collective-permute-start(f32[2,1024]{1,0:T(2,128)S(1)} %add.336), channel_id=1, source_target_pairs={{0,1},{1,0},{2,3},{3,2},{4,5},{5,4},{6,7},{7,6},{8,9},{9,8},{10,11... | collective-permute-start | bytes 24584 | tf_op jit(solution)/shard_map/ppermute | solution.py:30
  (91 other events, 1131.6 us)
Sparse Core Ops, SparseCore 0:
  113.9 114.6 all-gather.1
  257.7 58.8 reduce-scatter.3
  322.5 57.9 reduce-scatter.5
  435.2 27.4 reduce-scatter.7

commit v6 on v5

--- a/solution.py
+++ b/solution.py
@@ -78,7 +78,7 @@
         out_specs=whole(shape),
         out_shape=jax.ShapeDtypeStruct(shape, BF),
         cost_estimate=took(2),
-        compiler_params=vmem(32),
+        compiler_params=vmem(12),
     )(*pieces)
 
 
@@ -107,7 +107,7 @@
         out_specs=whole((rows // 4, width)),
         out_shape=jax.ShapeDtypeStruct((rows // 4, width), BF),
         cost_estimate=took(1),
-        compiler_params=vmem(32),
+        compiler_params=vmem(8),
     )(kept, got)
 
 
@@ -132,7 +132,7 @@
         out_specs=[whole((step, width))] * 2,
         out_shape=[jax.ShapeDtypeStruct((step, width), BF)] * 2,
         cost_estimate=took(2),
-        compiler_params=vmem(32),
+        compiler_params=vmem(12),
     )(kept, got, kept, got, for_x, for_y)
 
 
@@ -297,7 +297,7 @@
         ),
         out_shape=[jax.ShapeDtypeStruct(wide, BF)] * parts,
         cost_estimate=took(3),
-        compiler_params=vmem(62),
+        compiler_params=vmem(24),
     )(places, *slots)
 
 
@@ -322,7 +322,7 @@
         out_specs=whole(shape),
         out_shape=jax.ShapeDtypeStruct(shape, BF),
         cost_estimate=took(1.5),
-        compiler_params=vmem(32),
+        compiler_params=vmem(12),
     )(info, *keeps, *gots)
 
 
@@ -365,7 +365,7 @@
         ),
         out_shape=[jax.ShapeDtypeStruct(shape, BF)] * (4 * halves),
         cost_estimate=took(3),
-        compiler_params=vmem(32),
+        compiler_params=vmem(16),
     )(place, side, info, *totals, *gots)
     return [outs[4 * h : 4 * h + 4] for h in range(halves)]
 
@@ -497,7 +497,7 @@
         out_specs=[pl.BlockSpec((block, 2 * HD), lambda i: (i, 0))] * 2,
         out_shape=[jax.ShapeDtypeStruct((rows, 2 * HD), BF)] * 2,
         cost_estimate=took(6),
-        compiler_params=vmem(32),
+        compiler_params=vmem(20),
     )(x_low, x_high, weights, cosine, sine)
 
 

time: 518 us -> 518 us (level)
    unnamed x179 -> x185, local copies, waits for them, and re-layouts: 17.4 us -> 21.4 us
  transfers between devices with their start and end apart: 66 -> 66, of which waited for: 37 -> 34; matrix products, arithmetic and copies ran while one was open for 6% -> 7% of each run, Pallas kernels for 27% -> 26%
where the time goes in v6:
time: 518 us; the launch traced here: 511 us
  waiting for transfers between devices  173 us (33%)
  Pallas kernels  166 us (32%)
  starting transfers between devices  75.3 us (15%)
  local copies, waits for them, and re-layouts  36.9 us (7%)
  other arithmetic  24.7 us (5%)
  blocking collectives  19.8 us (4%)
  between operations  15.3 us (3%)
    ppermute x51, waiting for transfers between devices, swap(): return lax.ppermute(value, axis, [(0, 1), (1, 0)])  116 us
    pallas_call x2, Pallas kernels, expert_rows(): pl.pallas_call(lambda *refs: expert_kernel(part, start, len(before), *ref...  59.5 us
    ppermute x51, starting transfers between devices, swap(): return lax.ppermute(value, axis, [(0, 1), (1, 0)])  43.3 us
    ppermute x4, waiting for transfers between devices, shift(): return lax.ppermute(value, 'z', pairs)  24.4 us
    unnamed x185, local copies, waits for them, and re-layouts  21.4 us
    pallas_call x1, Pallas kernels, attend_back(): pl.pallas_call(attend_back_kernel, grid=(seqs, 2), in_specs=[pl.BlockSpec...  20 us
    all_gather x1, blocking collectives, shards(): lax.all_gather(attn_mine, 'z', axis=0, tiled=True)  19.8 us
    pallas_call x1, Pallas kernels, update(): pl.pallas_call(update_kernel, grid=(slots // step,), in_specs=[smem, smem...  15.6 us
  transfers between devices with their start and end apart: 66, of which 34 were waited for; matrix products, arithmetic and copies ran while one was open for 7% of the time, Pallas kernels for 26%

profile of v6, /device:TPU:0, one launch (start us, length us, event | category | flops | bytes accessed | tf_op | source)
XLA Modules:
  0.0 510.5 jit_solution(5230478416357329313)
XLA Ops:
  9.4 3.3 shard_map.206
  12.7 5.4 %all-to-all-start = ((bf16[8,3,128,128]{3,2,1,0:T(8,128)(2,1)}), bf16[8,3,128,128]{3,2,1,0:T(8,128)(2,1)S(1)}, u32[]{:S(2)}, u32[]{:S(2)}) async-start(bf16[8,3,128,128]{3,2,1,0:T(8,128)(2,1)} %shard_map.206), calls=%async_computation | async-start | bytes 1572864 | tf_op jit(solution)/shard_map/all_to_all | solution.py:978
  19.9 4.8 shard_map.207
  24.8 4.9 all-to-all-done
  34.3 19.8 %all_gather.6.w_ref = bf16[1024,384]{1,0:T(8,128)(2,1)S(1)} all-gather(bf16[256,384]{1,0:T(8,128)(2,1)S(1)} %bitcast.62), channel_id=1, replica_groups=mesh['z'=4,'x'=2,'y'=2,'c'=2] {'z'}, dimensions={0}, use_global_device_ids=true | all-gather | bytes 983040 | tf_op jit(solution)/shard_map/all_gather | solution.py:1016
  54.1 4.7 collective-permute-done.1.refs_2_
  59.7 15.0 %collective-permute-done.3.refs_3_ = bf16[256,1152]{1,0:T(8,128)(2,1)S(1)} collective-permute-done((bf16[256,1152]{1,0:T(8,128)(2,1)S(1)}, bf16[256,1152]{1,0:T(8,128)(2,1)S(1)}, u32[]{:S(2)}, u32[]{:S(2)}) %collective-permute-start.3) | collective-permute-done | bytes 589856 | tf_op jit(solution)/shard_map/ppermute | solution.py:30
  75.9 1.6 shard_map.208.low_ref.x_low
  86.0 6.8 %shard_map.210 = (bf16[2048,128]{1,0:T(8,128)(2,1)S(1)}, bf16[2048,128]{1,0:T(8,128)(2,1)S(1)}) custom-call(bf16[1024,1152]{1,0:T(8,128)(2,1)} %shard_map.208.low_ref.x_low, bf16[1024,1152]{1,0:T(8,128)(2,1)} %collective-permute-done.6.high_ref.x_high, bf16[1024,384]{1,0:T(8,128)(2,1)S(1)} %all_gather.6.w_ref, f32[2,256,128]{2,1,0:T(8,128)S(1)} %copy.74.cos_ref, ...), custom_call_target="tpu_custom_call" | custom-call | flops 6000000000 | bytes 1048576 | tf_op jit(solution)/shard_map/pallas_call | solution.py:488
  92.8 3.5 collective-permute-start.7
  96.4 8.4 %collective-permute-done.8.refs_1_ = bf16[128,3072]{1,0:T(8,128)(2,1)S(1)} collective-permute-done((bf16[128,3072]{1,0:T(8,128)(2,1)S(1)}, bf16[128,3072]{1,0:T(8,128)(2,1)S(1)}, u32[]{:S(2)}, u32[]{:S(2)}) %collective-permute-start.8) | collective-permute-done | bytes 786464 | tf_op jit(solution)/shard_map/ppermute | solution.py:30
  104.8 1.8 shard_map.211
  106.6 1.7 collective-permute-done.7.k1_ref.t1_ref
  108.2 4.4 collective-permute-start.9
  114.3 11.4 %collective-permute-done.9.k2_ref.t2_ref = bf16[2080,128]{1,0:T(8,128)(2,1)S(1)} collective-permute-done((bf16[2080,128]{1,0:T(8,128)(2,1)S(1)}, bf16[2080,128]{1,0:T(8,128)(2,1)S(1)}, u32[]{:S(2)}, u32[]{:S(2)}) %collective-permute-start.9) | collective-permute-done | bytes 532512 | tf_op jit(solution)/shard_map/ppermute | solution.py:36
  129.7 15.3 %shard_map.212 = (bf16[2048,128]{1,0:T(8,128)(2,1)S(1)}, f32[4,2,2,256]{3,2,1,0:T(2,128)S(1)}, bf16[1024,1024]{1,0:T(8,128)(2,1)S(1)}, bf16[1024,1024]{1,0:T(8,128)(2,1)S(1)}) custom-call(s32[2]{0:T(128)S(1)} %copy-done.39, bf16[2048,128]{1,0:T(8,128)(2,1)S(1)} %copy-done.44, bf16[2080,128]{1,0:T(8,128)(2,1)S(1)} %pad_maximum_fusion.k0_ref.t0_ref, ...), custom_call_target="tpu_custom_call" | custom-call | flops 24000000000 | bytes 1048576 | tf_op jit(solution)/shard_map/pallas_call | solution.py:591
  145.1 4.1 collective-permute-done.10.got_ref.gx_ref.gy_ref
  151.8 1.9 collective-permute-start.20
  153.8 4.9 collective-permute-done.12.fy_ref
  159.9 2.0 collective-permute-start.13
  163.2 6.8 %collective-permute-done.21.refs_2_ = bf16[256,1024]{1,0:T(8,128)(2,1)S(1)} collective-permute-done((bf16[256,1024]{1,0:T(8,128)(2,1)S(1)}, bf16[256,1024]{1,0:T(8,128)(2,1)S(1)}, u32[]{:S(2)}, u32[]{:S(2)}) %collective-permute-start.21) | collective-permute-done | bytes 524320 | tf_op jit(solution)/shard_map/ppermute | solution.py:30
  170.0 2.1 collective-permute-start.23
  173.1 8.1 %collective-permute-done.13 = bf16[256,1024]{1,0:T(8,128)(2,1)} collective-permute-done((bf16[256,1024]{1,0:T(8,128)(2,1)}, bf16[256,1024]{1,0:T(8,128)(2,1)}, u32[]{:S(2)}, u32[]{:S(2)}) %collective-permute-start.13) | collective-permute-done | bytes 524320 | tf_op jit(solution)/shard_map/ppermute | solution.py:30
  181.3 1.8 multiply_reduce_fusion.2
  183.4 2.1 collective-permute-start.15
  188.3 9.1 %collective-permute-done.16.refs_2_ = bf16[256,1024]{1,0:T(8,128)(2,1)} collective-permute-done((bf16[256,1024]{1,0:T(8,128)(2,1)S(1)}, bf16[256,1024]{1,0:T(8,128)(2,1)}, u32[]{:S(2)}, u32[]{:S(2)}) %collective-permute-start.16) | collective-permute-done | bytes 524320 | tf_op jit(solution)/shard_map/ppermute | solution.py:30
  198.4 1.7 collective-permute-start.18
  202.1 3.7 collective-permute-done.18.refs_4_
  205.7 2.1 collective-permute-done.17.refs_3_
  207.8 2.7 shard_map.215.refs_0_
  215.0 13.5 %all-gather.2.cloned.1.call-done.refs_5_.w0_ref.w1_ref = bf16[1024,3072]{1,0:T(8,128)(2,1)} async-done(((bf16[256,3072]{1,0:T(8,128)(2,1)}), bf16[1024,3072]{1,0:T(8,128)(2,1)}) %all-gather.2.cloned.1.call-update) | async-done | bytes 6291472 | tf_op jit(solution)/shard_map/all_gather | solution.py:1049
  228.5 29.0 %shard_map.217 = (bf16[1024,1024]{1,0:T(8,128)(2,1)}, bf16[1024,1024]{1,0:T(8,128)(2,1)}, bf16[2048,512]{1,0:T(8,128)(2,1)}, bf16[1024,1536]{1,0:T(8,128)(2,1)}) custom-call(bf16[1024,1024]{1,0:T(8,128)(2,1)} %shard_map.215.refs_0_, bf16[1024,1024]{1,0:T(8,128)(2,1)} %collective-permute-done.19.refs_1_, bf16[1024,1024]{1,0:T(8,128)(2,1)} %copy-done.10, ...), custom_call_target="tpu_custom_call" | custom-call | flops 10000000 | bytes 1048576 | tf_op jit(solution)/shard_map/pallas_call | solution.py:879
  257.7 30.5 %shard_map.218 = (bf16[1024,1024]{1,0:T(8,128)(2,1)}, bf16[1024,1024]{1,0:T(8,128)(2,1)}, bf16[2048,512]{1,0:T(8,128)(2,1)}, bf16[1024,1536]{1,0:T(8,128)(2,1)}) custom-call(bf16[1024,1024]{1,0:T(8,128)(2,1)} %shard_map.215.refs_0_, bf16[1024,1024]{1,0:T(8,128)(2,1)} %collective-permute-done.19.refs_1_, bf16[1024,1024]{1,0:T(8,128)(2,1)} %copy-done.10, ...), custom_call_target="tpu_custom_call" | custom-call | flops 10000000 | bytes 1048576 | tf_op jit(solution)/shard_map/pallas_call | solution.py:879
  288.3 4.4 collective-permute-done.25.got_ref.gx_ref.gy_ref
  292.6 1.6 copy-done.3
  297.1 5.7 %collective-permute-done.27.fy_ref = bf16[128,1024]{1,0:T(8,128)(2,1)S(1)} collective-permute-done((bf16[128,1024]{1,0:T(8,128)(2,1)S(1)}, bf16[128,1024]{1,0:T(8,128)(2,1)S(1)}, u32[]{:S(2)}, u32[]{:S(2)}) %collective-permute-start.27) | collective-permute-done | bytes 262176 | tf_op jit(solution)/shard_map/ppermute | solution.py:30
  306.1 10.9 %collective-permute-done.28 = bf16[256,1024]{1,0:T(8,128)(2,1)S(1)} collective-permute-done((bf16[256,1024]{1,0:T(8,128)(2,1)S(1)}, bf16[256,1024]{1,0:T(8,128)(2,1)S(1)}, u32[]{:S(2)}, u32[]{:S(2)}) %collective-permute-start.28) | collective-permute-done | bytes 524320 | tf_op jit(solution)/shard_map/ppermute | solution.py:30
  322.4 2.8 copy-done
  325.1 2.0 copy-done.11
  328.7 5.9 %shard_map.221 = (bf16[1024,1024]{1,0:T(8,128)(2,1)S(1)}, bf16[1024,1024]{1,0:T(8,128)(2,1)S(1)}) custom-call(bf16[2048,512]{1,0:T(8,128)(2,1)S(1)} %copy-done.11, bf16[2048,512]{1,0:T(8,128)(2,1)S(1)} %copy-done.12, bf16[1024,3072]{1,0:T(8,128)(2,1)S(1)} %copy-done, bf16[1024,3072]{1,0:T(8,128)(2,1)S(1)} %copy-done), custom_call_target="tpu_custom_call" | custom-call | flops 2000000000 | bytes 1048576 | tf_op jit(solution)/shard_map/pallas_call | solution.py:924
  337.5 6.9 %collective-permute-done.33.refs_4_ = bf16[128,1024]{1,0:T(8,128)(2,1)S(1)} collective-permute-done((bf16[128,1024]{1,0:T(8,128)(2,1)S(1)}, bf16[128,1024]{1,0:T(8,128)(2,1)S(1)}, u32[]{:S(2)}, u32[]{:S(2)}) %collective-permute-start.33) | collective-permute-done | bytes 262176 | tf_op jit(solution)/shard_map/ppermute | solution.py:30
  345.9 2.5 shard_map.222.dy_low
  349.5 1.6 collective-permute-start.36
  351.1 1.6 copy-done.7
  353.0 1.6 collective-permute-start.38
  355.1 20.0 %shard_map.224 = (bf16[2048,128]{1,0:T(8,128)(2,1)S(1)}, f32[2048,128]{1,0:T(8,128)S(1)}, f32[2048,128]{1,0:T(8,128)S(1)}, bf16[2048,128]{1,0:T(8,128)(2,1)}, bf16[1024,128]{1,0:T(8,128)(2,1)S(1)}) custom-call(s32[2]{0:T(128)S(1)} %copy-done.39, bf16[2048,128]{1,0:T(8,128)(2,1)S(1)} %copy-done.45, bf16[2080,128]{1,0:T(8,128)(2,1)S(1)} %copy-done.17, ...), custom_call_target="tpu_custom_call" | custom-call | flops 12000000000 | bytes 1048576 | tf_op jit(solution)/shard_map/pallas_call | solution.py:697
  383.2 11.3 %collective-permute-done.39 = bf16[2048,128]{1,0:T(8,128)(2,1)} collective-permute-done((bf16[2048,128]{1,0:T(8,128)(2,1)}, bf16[2048,128]{1,0:T(8,128)(2,1)}, u32[]{:S(2)}, u32[]{:S(2)}) %collective-permute-start.39) | collective-permute-done | bytes 524320 | tf_op jit(solution)/shard_map/ppermute | solution.py:36
  397.2 2.4 shard_map.226
  403.1 8.6 %collective-permute-done.44.refs_2_ = bf16[20,64,128]{2,1,0:T(8,128)(2,1)S(1)} collective-permute-done((bf16[20,64,128]{2,1,0:T(8,128)(2,1)S(1)}, bf16[20,64,128]{2,1,0:T(8,128)(2,1)S(1)}, u32[]{:S(2)}, u32[]{:S(2)}) %collective-permute-start.44) | collective-permute-done | bytes 327712 | tf_op jit(solution)/shard_map/ppermute | solution.py:30
  411.7 6.2 %collective-permute-done.45.refs_3_ = bf16[20,64,128]{2,1,0:T(8,128)(2,1)S(1)} collective-permute-done((bf16[20,64,128]{2,1,0:T(8,128)(2,1)S(1)}, bf16[20,64,128]{2,1,0:T(8,128)(2,1)S(1)}, u32[]{:S(2)}, u32[]{:S(2)}) %collective-permute-start.45) | collective-permute-done | bytes 327712 | tf_op jit(solution)/shard_map/ppermute | solution.py:271
  419.9 9.9 %shard_map.227 = (bf16[1024,1024]{1,0:T(8,128)(2,1)S(1)}, bf16[1024,1024]{1,0:T(8,128)(2,1)}, bf16[1024,384]{1,0:T(8,128)(2,1)}, f32[8,1024]{1,0:T(8,128)S(1)}) custom-call(bf16[2048,128]{1,0:T(8,128)(2,1)S(1)} %copy-done.49, f32[2048,128]{1,0:T(8,128)S(1)} %copy-done.47, bf16[2048,128]{1,0:T(8,128)(2,1)S(1)} %collective-permute-done.42.b_ref, ...), custom_call_target="tpu_custom_call" | custom-call | flops 10000000000 | bytes 1048576 | tf_op jit(solution)/shard_map/pallas_call | solution.py:781
  429.8 4.6 collective-permute-done.49.refs_7_
  435.7 4.1 collective-permute-done.50.got_ref.gx_ref.gy_ref
  444.5 5.3 %collective-permute-done.53 = f32[2,1024]{1,0:T(2,128)S(1)} collective-permute-done((f32[2,1024]{1,0:T(2,128)S(1)}, f32[2,1024]{1,0:T(2,128)S(1)}, u32[]{:S(2)}, u32[]{:S(2)}) %collective-permute-start.53) | collective-permute-done | bytes 8224 | tf_op jit(solution)/shard_map/ppermute | solution.py:30
  453.0 5.0 collective-permute-start.56
  458.7 15.6 %shard_map.230 = (f32[20,128,512]{2,1,0:T(8,128)}, f32[20,128,512]{2,1,0:T(8,128)}, f32[20,128,512]{2,1,0:T(8,128)}) custom-call(s32[2]{0:T(128)} %pad_add_fusion.1.info_ref, f32[20]{0:T(128)} %copy-done.55, bf16[20,64,128]{2,1,0:T(8,128)(2,1)} %copy-done.40, bf16[20,64,128]{2,1,0:T(8,128)(2,1)} %copy-done.86, bf16[20,64,128]{2,1,0:T(8,128)(2,1)} %copy-done.87, ...), custom_call_target="tpu_custom_call" | custom-call | flops 6000000000 | bytes 1048576 | tf_op jit(solution)/shard_map/pallas_call | solution.py:402
  474.4 2.1 broadcast_in_dim.96
  476.6 4.2 all-to-all-start.1
  480.8 2.9 fusion.10
  483.7 5.2 %collective-permute-start.57 = (f32[2,1024]{1,0:T(2,128)S(1)}, f32[2,1024]{1,0:T(2,128)S(1)}, u32[]{:S(2)}, u32[]{:S(2)}) collective-permute-start(f32[2,1024]{1,0:T(2,128)S(1)} %add.331), channel_id=1, source_target_pairs={{0,16},{8,24},{16,0},{24,8},{1,17},{9,25},{17,1},{25,9},{2,18},{10... | collective-permute-start | bytes 24584 | tf_op jit(solution)/shard_map/ppermute | solution.py:1140
  489.0 1.7 fusion.7
  490.6 1.8 all-to-all-done.1.attn_ref
  493.9 3.0 fusion.6
  497.0 6.1 %shard_map.231 = (f32[20,128,512]{2,1,0:T(8,128)}, f32[20,128,512]{2,1,0:T(8,128)}, f32[20,128,512]{2,1,0:T(8,128)}) custom-call(s32[6]{0:T(128)} %copy-done.79, s32[6]{0:T(128)} %broadcast_add_fusion.held_ref, f32[6]{0:T(128)} %and_select_fusion.rate_ref, ...), custom_call_target="tpu_custom_call", output_to_operand_aliasing={{0}: (7, {}), {1}: (8, {}), {2}: (9, {})} | custom-call | flops 5000000000 | bytes 1048576 | tf_op jit(solution)/shard_map/pallas_call | solution.py:452
  (385 shorter events, 88.7 us)
Async XLA Ops:
  12.7 17.0 %all-to-all-start = ((bf16[8,3,128,128]{3,2,1,0:T(8,128)(2,1)}), bf16[8,3,128,128]{3,2,1,0:T(8,128)(2,1)S(1)}, u32[]{:S(2)}, u32[]{:S(2)}) async-start(bf16[8,3,128,128]{3,2,1,0:T(8,128)(2,1)} %shard_map.206), calls=%async_computation | async-start | bytes 1572864 | tf_op jit(solution)/shard_map/all_to_all | solution.py:978
  18.0 210.5 %all-gather.2.cloned.1.call-start = ((), (), s32[]{:S(2)}) async-start(), calls=%async_computation.5 | async-start | bytes 7864320 | tf_op jit(solution)/shard_map/all_gather | solution.py:1049
  29.7 29.1 %collective-permute-start.2 = (bf16[20,128,128]{2,1,0:T(8,128)(2,1)}, bf16[20,128,128]{2,1,0:T(8,128)(2,1)S(1)}, u32[]{:S(2)}, u32[]{:S(2)}) collective-permute-start(bf16[20,128,128]{2,1,0:T(8,128)(2,1)} %get-tuple-element.155), channel_id=1, source_target_pairs={{0,2},{2,0},{1,3},{3,1},{4,6},{6,4},{5,7},{7,5},{8,10},{10,8},{9,1... | collective-permute-start | bytes 1966088 | tf_op jit(solution)/shard_map/ppermute | solution.py:30
  31.8 27.0 %collective-permute-start.1 = (bf16[256,1152]{1,0:T(8,128)(2,1)S(1)}, bf16[256,1152]{1,0:T(8,128)(2,1)S(1)}, u32[]{:S(2)}, u32[]{:S(2)}) collective-permute-start(bf16[256,1152]{1,0:T(8,128)(2,1)S(1)} %concatenate.13.refs_0_), channel_id=1, source_target_pairs={{0,2},{2,0},{1,3},{3,1},{4,6},{6,4},{5,7},{7,5},{8,10},{10,8},{9,1... | collective-permute-start | bytes 1769480 | tf_op jit(solution)/shard_map/ppermute | solution.py:30
  32.4 26.4 %collective-permute-start = (bf16[256,1152]{1,0:T(8,128)(2,1)S(1)}, bf16[256,1152]{1,0:T(8,128)(2,1)S(1)}, u32[]{:S(2)}, u32[]{:S(2)}) collective-permute-start(bf16[256,1152]{1,0:T(8,128)(2,1)S(1)} %concatenate.13.refs_0_), channel_id=1, source_target_pairs={{0,4},{4,0},{1,5},{5,1},{2,6},{6,2},{3,7},{7,3},{8,12},{12,8},{9,1... | collective-permute-start | bytes 1769480 | tf_op jit(solution)/shard_map/ppermute | solution.py:30
  34.2 25.5 %collective-permute-start.4 = (bf16[20,128,128]{2,1,0:T(8,128)(2,1)}, bf16[20,128,128]{2,1,0:T(8,128)(2,1)S(1)}, u32[]{:S(2)}, u32[]{:S(2)}) collective-permute-start(bf16[20,128,128]{2,1,0:T(8,128)(2,1)} %get-tuple-element.158), channel_id=1, source_target_pairs={{0,1},{1,0},{2,3},{3,2},{4,5},{5,4},{6,7},{7,6},{8,9},{9,8},{10,11... | collective-permute-start | bytes 1966088 | tf_op jit(solution)/shard_map/ppermute | solution.py:30
  58.8 17.1 %collective-permute-start.5 = (bf16[20,128,128]{2,1,0:T(8,128)(2,1)S(1)}, bf16[20,128,128]{2,1,0:T(8,128)(2,1)S(1)}, u32[]{:S(2)}, u32[]{:S(2)}) collective-permute-start(bf16[20,128,128]{2,1,0:T(8,128)(2,1)S(1)} %copy-done.85), channel_id=1, source_target_pairs={{0,3},{1,2},{2,1},{3,0},{4,7},{5,6},{6,5},{7,4},{8,11},{9,10},{10,... | collective-permute-start | bytes 1966088 | tf_op jit(solution)/shard_map/ppermute | solution.py:1021
  58.9 15.8 %collective-permute-start.3 = (bf16[256,1152]{1,0:T(8,128)(2,1)S(1)}, bf16[256,1152]{1,0:T(8,128)(2,1)S(1)}, u32[]{:S(2)}, u32[]{:S(2)}) collective-permute-start(bf16[256,1152]{1,0:T(8,128)(2,1)S(1)} %collective-permute-done.1.refs_2_), channel_id=1, source_target_pairs={{0,4},{4,0},{1,5},{5,1},{2,6},{6,2},{3,7},{7,3},{8,12},{12,8},{9,1... | collective-permute-start | bytes 1769480 | tf_op jit(solution)/shard_map/ppermute | solution.py:30
  77.5 6.3 %collective-permute-start.6 = (bf16[1024,1152]{1,0:T(8,128)(2,1)}, bf16[1024,1152]{1,0:T(8,128)(2,1)}, u32[]{:S(2)}, u32[]{:S(2)}) collective-permute-start(bf16[1024,1152]{1,0:T(8,128)(2,1)} %shard_map.208.low_ref.x_low), channel_id=1, source_target_pairs={{0,1},{1,0},{2,3},{3,2},{4,5},{5,4},{6,7},{7,6},{8,9},{9,8},{10,11... | collective-permute-start | bytes 7077896 | tf_op jit(solution)/shard_map/ppermute | solution.py:30
  84.9 19.9 %collective-permute-start.8 = (bf16[128,3072]{1,0:T(8,128)(2,1)S(1)}, bf16[128,3072]{1,0:T(8,128)(2,1)S(1)}, u32[]{:S(2)}, u32[]{:S(2)}) collective-permute-start(bf16[128,3072]{1,0:T(8,128)(2,1)S(1)} %get-tuple-element.173), channel_id=1, source_target_pairs={{0,4},{4,0},{1,5},{5,1},{2,6},{6,2},{3,7},{7,3},{8,12},{12,8},{9,1... | collective-permute-start | bytes 2359304 | tf_op jit(solution)/shard_map/ppermute | solution.py:30
  92.8 15.4 %collective-permute-start.7 = (bf16[2080,128]{1,0:T(8,128)(2,1)S(1)}, bf16[2080,128]{1,0:T(8,128)(2,1)S(1)}, u32[]{:S(2)}, u32[]{:S(2)}) collective-permute-start(bf16[2080,128]{1,0:T(8,128)(2,1)S(1)} %pad_maximum_fusion.k0_ref.t0_ref), channel_id=1, source_target_pairs={{0,8},{8,16},{16,24},{1,9},{9,17},{17,25},{2,10},{10,18},{18,26},{... | collective-permute-start | bytes 1597448 | tf_op jit(solution)/shard_map/ppermute | solution.py:36
  108.2 17.6 %collective-permute-start.9 = (bf16[2080,128]{1,0:T(8,128)(2,1)S(1)}, bf16[2080,128]{1,0:T(8,128)(2,1)S(1)}, u32[]{:S(2)}, u32[]{:S(2)}) collective-permute-start(bf16[2080,128]{1,0:T(8,128)(2,1)S(1)} %collective-permute-done.7.k1_ref.t1_ref), channel_id=1, source_target_pairs={{0,8},{8,16},{16,24},{1,9},{9,17},{17,25},{2,10},{10,18},{18,26},{... | collective-permute-start | bytes 1597448 | tf_op jit(solution)/shard_map/ppermute | solution.py:36
  114.1 205.6 %reduce-scatter.4.cloned.1.call-start = ((), (), s32[]{:S(2)}) async-start(), calls=%async_computation.6 | async-start | bytes 3932160 | tf_op jit(solution)/shard_map/reduce_scatter | solution.py:1091
  149.5 9.2 %collective-permute-start.12 = (bf16[128,1024]{1,0:T(8,128)(2,1)S(1)}, bf16[128,1024]{1,0:T(8,128)(2,1)S(1)}, u32[]{:S(2)}, u32[]{:S(2)}) collective-permute-start(bf16[128,1024]{1,0:T(8,128)(2,1)S(1)} %get-tuple-element.310), channel_id=1, source_target_pairs={{0,4},{4,0},{1,5},{5,1},{2,6},{6,2},{3,7},{7,3},{8,12},{12,8},{9,1... | collective-permute-start | bytes 786440 | tf_op jit(solution)/shard_map/ppermute | solution.py:30
  149.5 9.2 %collective-permute-start.11 = (bf16[128,1024]{1,0:T(8,128)(2,1)S(1)}, bf16[128,1024]{1,0:T(8,128)(2,1)S(1)}, u32[]{:S(2)}, u32[]{:S(2)}) collective-permute-start(bf16[128,1024]{1,0:T(8,128)(2,1)S(1)} %get-tuple-element.311), channel_id=1, source_target_pairs={{0,2},{2,0},{1,3},{3,1},{4,6},{6,4},{5,7},{7,5},{8,10},{10,8},{9,1... | collective-permute-start | bytes 786440 | tf_op jit(solution)/shard_map/ppermute | solution.py:30
  150.7 19.3 %collective-permute-start.21 = (bf16[256,1024]{1,0:T(8,128)(2,1)S(1)}, bf16[256,1024]{1,0:T(8,128)(2,1)S(1)}, u32[]{:S(2)}, u32[]{:S(2)}) collective-permute-start(bf16[256,1024]{1,0:T(8,128)(2,1)S(1)} %bitcast.54), channel_id=1, source_target_pairs={{0,2},{2,0},{1,3},{3,1},{4,6},{6,4},{5,7},{7,5},{8,10},{10,8},{9,1... | collective-permute-start | bytes 1572872 | tf_op jit(solution)/shard_map/ppermute | solution.py:30
  151.8 20.3 %collective-permute-start.20 = (bf16[256,1024]{1,0:T(8,128)(2,1)S(1)}, bf16[256,1024]{1,0:T(8,128)(2,1)}, u32[]{:S(2)}, u32[]{:S(2)}) collective-permute-start(bf16[256,1024]{1,0:T(8,128)(2,1)S(1)} %bitcast.55), channel_id=1, source_target_pairs={{0,4},{4,0},{1,5},{5,1},{2,6},{6,2},{3,7},{7,3},{8,12},{12,8},{9,1... | collective-permute-start | bytes 1572872 | tf_op jit(solution)/shard_map/ppermute | solution.py:30
  159.9 21.4 %collective-permute-start.13 = (bf16[256,1024]{1,0:T(8,128)(2,1)}, bf16[256,1024]{1,0:T(8,128)(2,1)}, u32[]{:S(2)}, u32[]{:S(2)}) collective-permute-start(bf16[256,1024]{1,0:T(8,128)(2,1)} %get-tuple-element.177), channel_id=1, source_target_pairs={{0,4},{4,0},{1,5},{5,1},{2,6},{6,2},{3,7},{7,3},{8,12},{12,8},{9,1... | collective-permute-start | bytes 1572872 | tf_op jit(solution)/shard_map/ppermute | solution.py:30
  161.9 19.5 %collective-permute-start.14 = (bf16[256,1024]{1,0:T(8,128)(2,1)}, bf16[256,1024]{1,0:T(8,128)(2,1)}, u32[]{:S(2)}, u32[]{:S(2)}) collective-permute-start(bf16[256,1024]{1,0:T(8,128)(2,1)} %get-tuple-element.178), channel_id=1, source_target_pairs={{0,2},{2,0},{1,3},{3,1},{4,6},{6,4},{5,7},{7,5},{8,10},{10,8},{9,1... | collective-permute-start | bytes 1572872 | tf_op jit(solution)/shard_map/ppermute | solution.py:30
  170.0 16.8 %collective-permute-start.23 = (bf16[128,1024]{1,0:T(8,128)(2,1)S(1)}, bf16[128,1024]{1,0:T(8,128)(2,1)S(1)}, u32[]{:S(2)}, u32[]{:S(2)}) collective-permute-start(bf16[128,1024]{1,0:T(8,128)(2,1)S(1)} %slice.165), channel_id=1, source_target_pairs={{0,4},{4,0},{1,5},{5,1},{2,6},{6,2},{3,7},{7,3},{8,12},{12,8},{9,1... | collective-permute-start | bytes 786440 | tf_op jit(solution)/shard_map/ppermute | solution.py:30
  173.1 13.8 %collective-permute-start.22 = (bf16[128,1024]{1,0:T(8,128)(2,1)S(1)}, bf16[128,1024]{1,0:T(8,128)(2,1)S(1)}, u32[]{:S(2)}, u32[]{:S(2)}) collective-permute-start(bf16[128,1024]{1,0:T(8,128)(2,1)S(1)} %slice.164), channel_id=1, source_target_pairs={{0,2},{2,0},{1,3},{3,1},{4,6},{6,4},{5,7},{7,5},{8,10},{10,8},{9,1... | collective-permute-start | bytes 786440 | tf_op jit(solution)/shard_map/ppermute | solution.py:30
  183.4 14.0 %collective-permute-start.16 = (bf16[256,1024]{1,0:T(8,128)(2,1)S(1)}, bf16[256,1024]{1,0:T(8,128)(2,1)}, u32[]{:S(2)}, u32[]{:S(2)}) collective-permute-start(bf16[256,1024]{1,0:T(8,128)(2,1)S(1)} %multiply_convert_fusion.refs_0_), channel_id=1, source_target_pairs={{0,2},{2,0},{1,3},{3,1},{4,6},{6,4},{5,7},{7,5},{8,10},{10,8},{9,1... | collective-permute-start | bytes 1572872 | tf_op jit(solution)/shard_map/ppermute | solution.py:30
  183.4 16.6 %collective-permute-start.15 = (bf16[256,1024]{1,0:T(8,128)(2,1)S(1)}, bf16[256,1024]{1,0:T(8,128)(2,1)}, u32[]{:S(2)}, u32[]{:S(2)}) collective-permute-start(bf16[256,1024]{1,0:T(8,128)(2,1)S(1)} %multiply_convert_fusion.refs_0_), channel_id=1, source_target_pairs={{0,4},{4,0},{1,5},{5,1},{2,6},{6,2},{3,7},{7,3},{8,12},{12,8},{9,1... | collective-permute-start | bytes 1572872 | tf_op jit(solution)/shard_map/ppermute | solution.py:30
  188.0 27.0 %collective-permute-start.24 = (bf16[1024,1024]{1,0:T(8,128)(2,1)S(1)}, bf16[1024,1024]{1,0:T(8,128)(2,1)}, u32[]{:S(2)}, u32[]{:S(2)}) collective-permute-start(bf16[1024,1024]{1,0:T(8,128)(2,1)S(1)} %shard_map.216.refs_2_), channel_id=1, source_target_pairs={{0,1},{1,0},{2,3},{3,2},{4,5},{5,4},{6,7},{7,6},{8,9},{9,8},{10,11... | collective-permute-start | bytes 6291464 | tf_op jit(solution)/shard_map/ppermute | solution.py:30
  198.4 7.4 %collective-permute-start.18 = (bf16[128,1024]{1,0:T(8,128)(2,1)S(1)}, bf16[128,1024]{1,0:T(8,128)(2,1)S(1)}, u32[]{:S(2)}, u32[]{:S(2)}) collective-permute-start(bf16[128,1024]{1,0:T(8,128)(2,1)S(1)} %slice.163), channel_id=1, source_target_pairs={{0,4},{4,0},{1,5},{5,1},{2,6},{6,2},{3,7},{7,3},{8,12},{12,8},{9,1... | collective-permute-start | bytes 786440 | tf_op jit(solution)/shard_map/ppermute | solution.py:30
  201.1 6.8 %collective-permute-start.17 = (bf16[128,1024]{1,0:T(8,128)(2,1)S(1)}, bf16[128,1024]{1,0:T(8,128)(2,1)S(1)}, u32[]{:S(2)}, u32[]{:S(2)}) collective-permute-start(bf16[128,1024]{1,0:T(8,128)(2,1)S(1)} %slice.162), channel_id=1, source_target_pairs={{0,2},{2,0},{1,3},{3,1},{4,6},{6,4},{5,7},{7,5},{8,10},{10,8},{9,1... | collective-permute-start | bytes 786440 | tf_op jit(solution)/shard_map/ppermute | solution.py:30
  210.5 4.5 collective-permute-start.19
  257.6 122.4 %reduce-scatter.6.cloned.1.call-start = ((), (), s32[]{:S(2)}) async-start(), calls=%async_computation.7 | async-start | bytes 3932160 | tf_op jit(solution)/shard_map/reduce_scatter | solution.py:1091
  288.2 4.4 collective-permute-start.25
  294.4 8.4 %collective-permute-start.27 = (bf16[128,1024]{1,0:T(8,128)(2,1)S(1)}, bf16[128,1024]{1,0:T(8,128)(2,1)S(1)}, u32[]{:S(2)}, u32[]{:S(2)}) collective-permute-start(bf16[128,1024]{1,0:T(8,128)(2,1)S(1)} %get-tuple-element.308), channel_id=1, source_target_pairs={{0,4},{4,0},{1,5},{5,1},{2,6},{6,2},{3,7},{7,3},{8,12},{12,8},{9,1... | collective-permute-start | bytes 786440 | tf_op jit(solution)/shard_map/ppermute | solution.py:30
  295.6 8.0 %collective-permute-start.26 = (bf16[128,1024]{1,0:T(8,128)(2,1)S(1)}, bf16[128,1024]{1,0:T(8,128)(2,1)S(1)}, u32[]{:S(2)}, u32[]{:S(2)}) collective-permute-start(bf16[128,1024]{1,0:T(8,128)(2,1)S(1)} %get-tuple-element.309), channel_id=1, source_target_pairs={{0,2},{2,0},{1,3},{3,1},{4,6},{6,4},{5,7},{7,5},{8,10},{10,8},{9,1... | collective-permute-start | bytes 786440 | tf_op jit(solution)/shard_map/ppermute | solution.py:30
  304.0 13.0 %collective-permute-start.28 = (bf16[256,1024]{1,0:T(8,128)(2,1)S(1)}, bf16[256,1024]{1,0:T(8,128)(2,1)S(1)}, u32[]{:S(2)}, u32[]{:S(2)}) collective-permute-start(bf16[256,1024]{1,0:T(8,128)(2,1)S(1)} %get-tuple-element.192), channel_id=1, source_target_pairs={{0,4},{4,0},{1,5},{5,1},{2,6},{6,2},{3,7},{7,3},{8,12},{12,8},{9,1... | collective-permute-start | bytes 1572872 | tf_op jit(solution)/shard_map/ppermute | solution.py:30
  304.9 12.6 %collective-permute-start.29 = (bf16[256,1024]{1,0:T(8,128)(2,1)S(1)}, bf16[256,1024]{1,0:T(8,128)(2,1)S(1)}, u32[]{:S(2)}, u32[]{:S(2)}) collective-permute-start(bf16[256,1024]{1,0:T(8,128)(2,1)S(1)} %get-tuple-element.193), channel_id=1, source_target_pairs={{0,2},{2,0},{1,3},{3,1},{4,6},{6,4},{5,7},{7,5},{8,10},{10,8},{9,1... | collective-permute-start | bytes 1572872 | tf_op jit(solution)/shard_map/ppermute | solution.py:30
  319.7 14.9 %collective-permute-start.31 = (bf16[256,1024]{1,0:T(8,128)(2,1)S(1)}, bf16[256,1024]{1,0:T(8,128)(2,1)S(1)}, u32[]{:S(2)}, u32[]{:S(2)}) collective-permute-start(bf16[256,1024]{1,0:T(8,128)(2,1)S(1)} %get-tuple-element.195.refs_0_), channel_id=1, source_target_pairs={{0,2},{2,0},{1,3},{3,1},{4,6},{6,4},{5,7},{7,5},{8,10},{10,8},{9,1... | collective-permute-start | bytes 1572872 | tf_op jit(solution)/shard_map/ppermute | solution.py:30
  320.9 13.7 %collective-permute-start.30 = (bf16[256,1024]{1,0:T(8,128)(2,1)S(1)}, bf16[256,1024]{1,0:T(8,128)(2,1)}, u32[]{:S(2)}, u32[]{:S(2)}) collective-permute-start(bf16[256,1024]{1,0:T(8,128)(2,1)S(1)} %get-tuple-element.195.refs_0_), channel_id=1, source_target_pairs={{0,4},{4,0},{1,5},{5,1},{2,6},{6,2},{3,7},{7,3},{8,12},{12,8},{9,1... | collective-permute-start | bytes 1572872 | tf_op jit(solution)/shard_map/ppermute | solution.py:30
  322.3 152.1 %reduce-scatter.8.cloned.1.call-start = ((), (), s32[]{:S(2)}) async-start(), calls=%async_computation.8 | async-start | bytes 983040 | tf_op jit(solution)/shard_map/reduce_scatter | solution.py:1127
  334.6 10.0 %collective-permute-start.34 = (bf16[1024,1024]{1,0:T(8,128)(2,1)S(1)}, bf16[1024,1024]{1,0:T(8,128)(2,1)S(1)}, u32[]{:S(2)}, u32[]{:S(2)}) collective-permute-start(bf16[1024,1024]{1,0:T(8,128)(2,1)S(1)} %get-tuple-element.205), channel_id=1, source_target_pairs={{0,1},{1,0},{2,3},{3,2},{4,5},{5,4},{6,7},{7,6},{8,9},{9,8},{10,11... | collective-permute-start | bytes 6291464 | tf_op jit(solution)/shard_map/ppermute | solution.py:30
  335.9 8.6 %collective-permute-start.33 = (bf16[128,1024]{1,0:T(8,128)(2,1)S(1)}, bf16[128,1024]{1,0:T(8,128)(2,1)S(1)}, u32[]{:S(2)}, u32[]{:S(2)}) collective-permute-start(bf16[128,1024]{1,0:T(8,128)(2,1)S(1)} %slice.138), channel_id=1, source_target_pairs={{0,4},{4,0},{1,5},{5,1},{2,6},{6,2},{3,7},{7,3},{8,12},{12,8},{9,1... | collective-permute-start | bytes 786440 | tf_op jit(solution)/shard_map/ppermute | solution.py:30
  336.4 8.2 %collective-permute-start.32 = (bf16[128,1024]{1,0:T(8,128)(2,1)S(1)}, bf16[128,1024]{1,0:T(8,128)(2,1)S(1)}, u32[]{:S(2)}, u32[]{:S(2)}) collective-permute-start(bf16[128,1024]{1,0:T(8,128)(2,1)S(1)} %slice.137), channel_id=1, source_target_pairs={{0,2},{2,0},{1,3},{3,1},{4,6},{6,4},{5,7},{7,5},{8,10},{10,8},{9,1... | collective-permute-start | bytes 786440 | tf_op jit(solution)/shard_map/ppermute | solution.py:30
  348.4 4.5 collective-permute-start.35
  349.5 25.7 %collective-permute-start.36 = (bf16[128,1536]{1,0:T(8,128)(2,1)S(1)}, bf16[128,1536]{1,0:T(8,128)(2,1)S(1)}, u32[]{:S(2)}, u32[]{:S(2)}) collective-permute-start(bf16[128,1536]{1,0:T(8,128)(2,1)S(1)} %constant_dynamic-slice_fusion), channel_id=1, source_target_pairs={{0,4},{4,0},{1,5},{5,1},{2,6},{6,2},{3,7},{7,3},{8,12},{12,8},{9,1... | collective-permute-start | bytes 1179656 | tf_op jit(solution)/shard_map/ppermute | solution.py:30
  353.0 22.1 %collective-permute-start.38 = (bf16[128,1024]{1,0:T(8,128)(2,1)S(1)}, bf16[128,1024]{1,0:T(8,128)(2,1)S(1)}, u32[]{:S(2)}, u32[]{:S(2)}) collective-permute-start(bf16[128,1024]{1,0:T(8,128)(2,1)S(1)} %get-tuple-element.306), channel_id=1, source_target_pairs={{0,4},{4,0},{1,5},{5,1},{2,6},{6,2},{3,7},{7,3},{8,12},{12,8},{9,1... | collective-permute-start | bytes 786440 | tf_op jit(solution)/shard_map/ppermute | solution.py:30
  354.6 20.5 %collective-permute-start.37 = (bf16[128,1024]{1,0:T(8,128)(2,1)S(1)}, bf16[128,1024]{1,0:T(8,128)(2,1)S(1)}, u32[]{:S(2)}, u32[]{:S(2)}) collective-permute-start(bf16[128,1024]{1,0:T(8,128)(2,1)S(1)} %get-tuple-element.307), channel_id=1, source_target_pairs={{0,2},{2,0},{1,3},{3,1},{4,6},{6,4},{5,7},{7,5},{8,10},{10,8},{9,1... | collective-permute-start | bytes 786440 | tf_op jit(solution)/shard_map/ppermute | solution.py:30
  375.1 19.3 %collective-permute-start.39 = (bf16[2048,128]{1,0:T(8,128)(2,1)}, bf16[2048,128]{1,0:T(8,128)(2,1)}, u32[]{:S(2)}, u32[]{:S(2)}) collective-permute-start(bf16[2048,128]{1,0:T(8,128)(2,1)} %get-tuple-element.219), channel_id=1, source_target_pairs={{8,0},{16,8},{24,16},{9,1},{17,9},{25,17},{10,2},{18,10},{26,18},{... | collective-permute-start | bytes 1572872 | tf_op jit(solution)/shard_map/ppermute | solution.py:36
  378.3 16.2 %collective-permute-start.41 = (bf16[256,1024]{1,0:T(8,128)(2,1)}, bf16[256,1024]{1,0:T(8,128)(2,1)}, u32[]{:S(2)}, u32[]{:S(2)}) collective-permute-start(bf16[256,1024]{1,0:T(8,128)(2,1)} %get-tuple-element.226), channel_id=1, source_target_pairs={{0,2},{2,0},{1,3},{3,1},{4,6},{6,4},{5,7},{7,5},{8,10},{10,8},{9,1... | collective-permute-start | bytes 1572872 | tf_op jit(solution)/shard_map/ppermute | solution.py:30
  381.1 13.4 %collective-permute-start.40 = (bf16[128,1536]{1,0:T(8,128)(2,1)S(1)}, bf16[128,1536]{1,0:T(8,128)(2,1)S(1)}, u32[]{:S(2)}, u32[]{:S(2)}) collective-permute-start(bf16[128,1536]{1,0:T(8,128)(2,1)S(1)} %constant_dynamic-slice_fusion.1), channel_id=1, source_target_pairs={{0,4},{4,0},{1,5},{5,1},{2,6},{6,2},{3,7},{7,3},{8,12},{12,8},{9,1... | collective-permute-start | bytes 1179656 | tf_op jit(solution)/shard_map/ppermute | solution.py:30
  382.6 20.5 %collective-permute-start.46 = (bf16[256,1024]{1,0:T(8,128)(2,1)}, bf16[256,1024]{1,0:T(8,128)(2,1)S(1)}, u32[]{:S(2)}, u32[]{:S(2)}) collective-permute-start(bf16[256,1024]{1,0:T(8,128)(2,1)} %copy-done.36), channel_id=1, source_target_pairs={{0,4},{4,0},{1,5},{5,1},{2,6},{6,2},{3,7},{7,3},{8,12},{12,8},{9,1... | collective-permute-start | bytes 1572872 | tf_op jit(solution)/shard_map/ppermute | solution.py:30
  395.7 22.3 %collective-permute-start.42 = (bf16[2048,128]{1,0:T(8,128)(2,1)S(1)}, bf16[2048,128]{1,0:T(8,128)(2,1)S(1)}, u32[]{:S(2)}, u32[]{:S(2)}) collective-permute-start(bf16[2048,128]{1,0:T(8,128)(2,1)S(1)} %add_convert_fusion.1), channel_id=1, source_target_pairs={{8,0},{16,8},{24,16},{9,1},{17,9},{25,17},{10,2},{18,10},{26,18},{... | collective-permute-start | bytes 1572872 | tf_op jit(solution)/shard_map/ppermute | solution.py:36
  401.2 10.5 %collective-permute-start.44 = (bf16[20,64,128]{2,1,0:T(8,128)(2,1)S(1)}, bf16[20,64,128]{2,1,0:T(8,128)(2,1)S(1)}, u32[]{:S(2)}, u32[]{:S(2)}) collective-permute-start(bf16[20,64,128]{2,1,0:T(8,128)(2,1)S(1)} %get-tuple-element.234), channel_id=1, source_target_pairs={{0,2},{2,0},{1,3},{3,1},{4,6},{6,4},{5,7},{7,5},{8,10},{10,8},{9,1... | collective-permute-start | bytes 983048 | tf_op jit(solution)/shard_map/ppermute | solution.py:30
  402.5 15.4 %collective-permute-start.45 = (bf16[20,64,128]{2,1,0:T(8,128)(2,1)S(1)}, bf16[20,64,128]{2,1,0:T(8,128)(2,1)S(1)}, u32[]{:S(2)}, u32[]{:S(2)}) collective-permute-start(bf16[20,64,128]{2,1,0:T(8,128)(2,1)S(1)} %get-tuple-element.235), channel_id=1, source_target_pairs={{0,3},{1,2},{2,1},{3,0},{4,7},{5,6},{6,5},{7,4},{8,11},{9,10},{10,... | collective-permute-start | bytes 983048 | tf_op jit(solution)/shard_map/ppermute | solution.py:271
  417.9 11.8 %collective-permute-start.47 = (bf16[20,64,128]{2,1,0:T(8,128)(2,1)S(1)}, bf16[20,64,128]{2,1,0:T(8,128)(2,1)S(1)}, u32[]{:S(2)}, u32[]{:S(2)}) collective-permute-start(bf16[20,64,128]{2,1,0:T(8,128)(2,1)S(1)} %get-tuple-element.247), channel_id=1, source_target_pairs={{0,1},{1,0},{2,3},{3,2},{4,5},{5,4},{6,7},{7,6},{8,9},{9,8},{10,11... | collective-permute-start | bytes 983048 | tf_op jit(solution)/shard_map/ppermute | solution.py:30
  418.1 11.6 %collective-permute-start.48 = (bf16[20,64,128]{2,1,0:T(8,128)(2,1)S(1)}, bf16[20,64,128]{2,1,0:T(8,128)(2,1)S(1)}, u32[]{:S(2)}, u32[]{:S(2)}) collective-permute-start(bf16[20,64,128]{2,1,0:T(8,128)(2,1)S(1)} %get-tuple-element.249), channel_id=1, source_target_pairs={{0,2},{2,0},{1,3},{3,1},{4,6},{6,4},{5,7},{7,5},{8,10},{10,8},{9,1... | collective-permute-start | bytes 983048 | tf_op jit(solution)/shard_map/ppermute | solution.py:30
  419.5 15.0 %collective-permute-start.49 = (bf16[20,64,128]{2,1,0:T(8,128)(2,1)S(1)}, bf16[20,64,128]{2,1,0:T(8,128)(2,1)S(1)}, u32[]{:S(2)}, u32[]{:S(2)}) collective-permute-start(bf16[20,64,128]{2,1,0:T(8,128)(2,1)S(1)} %get-tuple-element.251), channel_id=1, source_target_pairs={{0,3},{1,2},{2,1},{3,0},{4,7},{5,6},{6,5},{7,4},{8,11},{9,10},{10,... | collective-permute-start | bytes 983048 | tf_op jit(solution)/shard_map/ppermute | solution.py:271
  435.2 4.6 collective-permute-start.50
  441.0 8.8 %collective-permute-start.52 = (bf16[128,1024]{1,0:T(8,128)(2,1)S(1)}, bf16[128,1024]{1,0:T(8,128)(2,1)S(1)}, u32[]{:S(2)}, u32[]{:S(2)}) collective-permute-start(bf16[128,1024]{1,0:T(8,128)(2,1)S(1)} %get-tuple-element.304), channel_id=1, source_target_pairs={{0,4},{4,0},{1,5},{5,1},{2,6},{6,2},{3,7},{7,3},{8,12},{12,8},{9,1... | collective-permute-start | bytes 786440 | tf_op jit(solution)/shard_map/ppermute | solution.py:30
  442.2 8.3 %collective-permute-start.51 = (bf16[128,1024]{1,0:T(8,128)(2,1)S(1)}, bf16[128,1024]{1,0:T(8,128)(2,1)S(1)}, u32[]{:S(2)}, u32[]{:S(2)}) collective-permute-start(bf16[128,1024]{1,0:T(8,128)(2,1)S(1)} %get-tuple-element.305), channel_id=1, source_target_pairs={{0,2},{2,0},{1,3},{3,1},{4,6},{6,4},{5,7},{7,5},{8,10},{10,8},{9,1... | collective-permute-start | bytes 786440 | tf_op jit(solution)/shard_map/ppermute | solution.py:30
  443.1 6.7 %collective-permute-start.53 = (f32[2,1024]{1,0:T(2,128)S(1)}, f32[2,1024]{1,0:T(2,128)S(1)}, u32[]{:S(2)}, u32[]{:S(2)}) collective-permute-start(f32[2,1024]{1,0:T(2,128)S(1)} %pad_maximum_fusion.2), channel_id=1, source_target_pairs={{0,4},{4,0},{1,5},{5,1},{2,6},{6,2},{3,7},{7,3},{8,12},{12,8},{9,1... | collective-permute-start | bytes 24584 | tf_op jit(solution)/shard_map/ppermute | solution.py:30
  452.0 22.4 %collective-permute-start.54 = (bf16[256,1024]{1,0:T(8,128)(2,1)S(1)}, bf16[256,1024]{1,0:T(8,128)(2,1)S(1)}, u32[]{:S(2)}, u32[]{:S(2)}) collective-permute-start(bf16[256,1024]{1,0:T(8,128)(2,1)S(1)} %get-tuple-element.259), channel_id=1, source_target_pairs={{0,4},{4,0},{1,5},{5,1},{2,6},{6,2},{3,7},{7,3},{8,12},{12,8},{9,1... | collective-permute-start | bytes 1572872 | tf_op jit(solution)/shard_map/ppermute | solution.py:30
  453.0 21.4 %collective-permute-start.56 = (f32[2,1024]{1,0:T(2,128)S(1)}, f32[2,1024]{1,0:T(2,128)S(1)}, u32[]{:S(2)}, u32[]{:S(2)}) collective-permute-start(f32[2,1024]{1,0:T(2,128)S(1)} %add.330), channel_id=1, source_target_pairs={{0,8},{8,0},{16,24},{24,16},{1,9},{9,1},{17,25},{25,17},{2,10},{10... | collective-permute-start | bytes 24584 | tf_op jit(solution)/shard_map/ppermute | solution.py:1140
  458.0 16.4 %collective-permute-start.55 = (bf16[256,1024]{1,0:T(8,128)(2,1)S(1)}, bf16[256,1024]{1,0:T(8,128)(2,1)}, u32[]{:S(2)}, u32[]{:S(2)}) collective-permute-start(bf16[256,1024]{1,0:T(8,128)(2,1)S(1)} %get-tuple-element.260), channel_id=1, source_target_pairs={{0,2},{2,0},{1,3},{3,1},{4,6},{6,4},{5,7},{7,5},{8,10},{10,8},{9,1... | collective-permute-start | bytes 1572872 | tf_op jit(solution)/shard_map/ppermute | solution.py:30
  476.6 15.9 %all-to-all-start.1 = ((bf16[8,128,384]{2,1,0:T(8,128)(2,1)}), bf16[8,128,384]{2,1,0:T(8,128)(2,1)}, u32[]{:S(2)}, u32[]{:S(2)}) async-start(bf16[8,128,384]{2,1,0:T(8,128)(2,1)} %bitcast.27), calls=%async_computation.4 | async-start | bytes 1572864 | tf_op jit(solution)/shard_map/all_to_all | solution.py:1163
  483.7 6.9 %collective-permute-start.57 = (f32[2,1024]{1,0:T(2,128)S(1)}, f32[2,1024]{1,0:T(2,128)S(1)}, u32[]{:S(2)}, u32[]{:S(2)}) collective-permute-start(f32[2,1024]{1,0:T(2,128)S(1)} %add.331), channel_id=1, source_target_pairs={{0,16},{8,24},{16,0},{24,8},{1,17},{9,25},{17,1},{25,9},{2,18},{10... | collective-permute-start | bytes 24584 | tf_op jit(solution)/shard_map/ppermute | solution.py:1140
  492.4 4.5 collective-permute-start.58
  496.9 6.1 %collective-permute-start.59 = (f32[2,1024]{1,0:T(2,128)S(1)}, f32[2,1024]{1,0:T(2,128)S(1)}, u32[]{:S(2)}, u32[]{:S(2)}) collective-permute-start(f32[2,1024]{1,0:T(2,128)S(1)} %add.336), channel_id=1, source_target_pairs={{0,1},{1,0},{2,3},{3,2},{4,5},{5,4},{6,7},{7,6},{8,9},{9,8},{10,11... | collective-permute-start | bytes 24584 | tf_op jit(solution)/shard_map/ppermute | solution.py:30
  (94 other events, 987.3 us)
Sparse Core Ops, SparseCore 0:
  114.2 114.2 all-gather.1
  257.7 58.4 reduce-scatter.3
  322.4 57.4 reduce-scatter.5
  435.8 29.5 reduce-scatter.7
